TPU v7x, 32 devices: a whole 2x2x4 slice. The times are simulated.
32 devices in a mesh: parts: 2 (over x), ep: 8 (over z, y), mod: 2 (over core).
Axes of the slice: x: 2, y: 2, z: 4, core: 2. Of those that a mesh axis runs over, the one named last changes fastest.
Arguments:
- tokens: bfloat16 [2048, 4096], P(('parts', 'ep')), parts along dimension 0, may hold values from -6 to 6
- cotangent: bfloat16 [2048, 4096], P(('parts', 'ep')), parts along dimension 0, may hold values from -6 to 6
- modality: int32 [2048], P(('parts', 'ep')), parts along dimension 0, may hold values from 0 to 1, as said below
- picks: int32 [2048, 2], P(('parts', 'ep')), parts along dimension 0, may hold values from 0 to 3, as said below
- gate_weights: float32 [2048, 2], P(('parts', 'ep')), parts along dimension 0, may hold values from 0.2 to 1
- gate_proj: bfloat16 [2, 4096, 8192], P('mod', None, 'ep'), may hold values from -0.09375 to 0.09375
- up_proj: bfloat16 [2, 4096, 8192], P('mod', None, 'ep'), may hold values from -0.09375 to 0.09375
- down_proj: bfloat16 [2, 8192, 4096], P('mod', 'ep'), may hold values from -0.125 to 0.125
Outputs:
- token_grad: bfloat16 [2048, 4096], P(('parts', 'ep'), 'mod'), parts along dimension 0
- gate_grad: float32 [2048, 2], P(('parts', 'ep'), 'mod'), parts along dimension 0
There are 2 independent parts, one for each index of `parts`. A program takes and returns all parts, laid end to end along the dimension named above; an argument that names none is the same for every part. Nothing has to cross between parts.
Inputs may be any that keep to these rules, and one draw needn't show every extreme that they name: `modality`: 0 marks a text token, 1 a vision token. The 2 picks of a token are different experts of its modality.
All inputs are finite; a program needn't handle non-finite values.
Results may differ from a plain program's by a relative error of at most 0.0057.
Values may be sent and summed in bfloat16 or wider, within the bound.
No kernel may reach another device: no remote copies, remote signals or barrier semaphores. Data moves between devices by JAX's collectives and lax.ppermute only.
A program may use at most 128 MiB of HBM per device.

v0:
```python
import jax
import jax.numpy as jnp
from jax import lax
from jax.sharding import PartitionSpec as P

E_MOD = 4
CAP = 16


def piece_terms(token_rows, grad_rows, gate_piece, up_piece, down_piece):
    gate_pre = jnp.dot(token_rows, gate_piece, preferred_element_type=jnp.float32)
    up_pre = jnp.dot(token_rows, up_piece, preferred_element_type=jnp.float32)
    hidden_grad = lax.dot_general(
        grad_rows, down_piece, (((1,), (1,)), ((), ())), preferred_element_type=jnp.float32
    )
    sigmoid_gate = jax.nn.sigmoid(gate_pre)
    activated = gate_pre * sigmoid_gate
    slope_term = sigmoid_gate * (1.0 + gate_pre * (1.0 - sigmoid_gate))
    part_gate = jnp.sum(activated * up_pre * hidden_grad, axis=1).astype(jnp.bfloat16)
    grad_gate_pre = (hidden_grad * up_pre * slope_term).astype(jnp.bfloat16)
    grad_up_pre = (hidden_grad * activated).astype(jnp.bfloat16)
    part_dx = lax.dot_general(
        grad_gate_pre, gate_piece, (((1,), (1,)), ((), ())), preferred_element_type=jnp.float32
    )
    part_dx = part_dx + lax.dot_general(
        grad_up_pre, up_piece, (((1,), (1,)), ((), ())), preferred_element_type=jnp.float32
    )
    return (part_dx.astype(jnp.bfloat16), part_gate)


def local(tokens, cotangent, modality, picks, gate_weights, gate_proj, up_proj, down_proj):
    core_index = lax.axis_index("mod")
    device_count = lax.axis_size("ep")
    tok_rows, model_width = tokens.shape
    topk_count = picks.shape[1]
    group_size = device_count // E_MOD
    pair_count = tok_rows * topk_count
    expert_id = picks.reshape(pair_count)
    live_pairs = jnp.repeat(modality == core_index, topk_count)
    positions = lax.iota(jnp.int32, pair_count)
    earlier = positions[None, :] < positions[:, None]
    same_label = (expert_id[:, None] == expert_id[None, :]) & live_pairs[None, :] & earlier
    slot_index = jnp.sum(same_label.astype(jnp.int32), axis=1)
    kept_pairs = live_pairs & (slot_index < CAP)
    target_row = expert_id * CAP + slot_index
    buffer_rows = lax.iota(jnp.int32, E_MOD * CAP)
    choose = (buffer_rows[:, None] == target_row[None, :]) & kept_pairs[None, :]
    pick_rows = jnp.any(choose.reshape(E_MOD * CAP, tok_rows, topk_count), axis=2).astype(
        jnp.bfloat16
    )
    outgoing = jnp.stack(
        [
            jnp.dot(pick_rows, tokens, preferred_element_type=jnp.float32),
            jnp.dot(pick_rows, cotangent, preferred_element_type=jnp.float32),
        ]
    ).astype(jnp.bfloat16)
    gate_piece = gate_proj[0]
    up_piece = up_proj[0]
    down_piece = down_proj[0]
    slot_clip = jnp.minimum(slot_index, CAP - 1)
    copies = jnp.broadcast_to(
        outgoing.reshape(2, E_MOD, 1, CAP, model_width), (2, E_MOD, group_size, CAP, model_width)
    )
    copies = copies.reshape(2, device_count, CAP, model_width)
    pieces = lax.all_to_all(copies, "ep", split_axis=1, concat_axis=1, tiled=True)
    item_count = pieces.shape[2]
    part_dx, part_gate = piece_terms(
        pieces[0].reshape(-1, model_width),
        pieces[1].reshape(-1, model_width),
        gate_piece,
        up_piece,
        down_piece,
    )
    back_dx = lax.all_to_all(
        part_dx.reshape(device_count, item_count, model_width),
        "ep",
        split_axis=0,
        concat_axis=0,
        tiled=True,
    )
    back_gate = lax.all_to_all(
        part_gate.reshape(device_count, item_count), "ep", split_axis=0, concat_axis=0, tiled=True
    )
    table_dx = jnp.sum(
        back_dx.astype(jnp.float32).reshape(E_MOD, group_size, CAP, model_width), axis=1
    ).reshape(-1, model_width)
    table_gate = jnp.sum(
        back_gate.astype(jnp.float32).reshape(E_MOD, group_size, CAP), axis=1
    ).reshape(-1)
    position = expert_id * CAP + slot_clip
    weight = jnp.where(kept_pairs, gate_weights.reshape(pair_count), 0.0)
    pair_dx = table_dx[position] * weight[:, None]
    local_dx = jnp.sum(pair_dx.reshape(tok_rows, topk_count, model_width), axis=1)
    local_gate = jnp.where(kept_pairs, table_gate[position], 0.0).reshape(tok_rows, topk_count)
    token_grad, gate_grad = (
        lax.psum_scatter(local_dx, "mod", scatter_dimension=1, tiled=True),
        lax.psum_scatter(local_gate, "mod", scatter_dimension=1, tiled=True),
    )
    return (token_grad.astype(jnp.bfloat16), gate_grad)


def solution(mesh):
    in_specs = (
        P(("parts", "ep"), None),
        P(("parts", "ep"), None),
        P(("parts", "ep")),
        P(("parts", "ep"), None),
        P(("parts", "ep"), None),
        P("mod", None, "ep"),
        P("mod", None, "ep"),
        P("mod", "ep", None),
    )
    out_specs = (P(("parts", "ep"), "mod"), P(("parts", "ep"), "mod"))
    return jax.shard_map(local, mesh=mesh, in_specs=in_specs, out_specs=out_specs, check_vma=False)
```

profile of v0, /device:TPU:0, one launch (start us, length us, event | category | flops | bytes accessed | tf_op | source)
XLA Modules:
  0.0 161.8 jit_solution(12442020263248949203)
XLA Ops:
  7.2 0.0 copy-start
  7.2 0.7 broadcast_compare_fusion
  7.9 0.1 broadcast_in_dim.8
  8.0 0.1 and.35
  8.2 0.8 copy.24
  9.0 0.1 eq.36
  9.1 0.2 convert_reduce_fusion.1
  9.3 0.1 reduce_sum.48
  9.4 0.8 copy.29
  10.2 0.1 broadcast_select_fusion.1
  10.3 0.1 copy.27
  10.4 0.1 copy.26
  10.5 0.0 copy-done
  10.5 0.3 fusion.17
  10.8 1.5 fusion.16
  12.4 0.0 slice-start
  12.4 0.1 pad_maximum_fusion
  12.5 0.1 copy.28
  12.6 0.2 broadcast_in_dim.9
  12.8 0.0 slice-start.1
  12.8 55.6 %all_to_all.16 = bf16[2,8,16,4096]{3,2,0,1:T(8,128)(2,1)S(1)} all-to-all(bf16[2,8,16,4096]{3,2,0,1:T(8,128)(2,1)S(1)} %bitcast.57), channel_id=1, replica_groups=mesh['parts'=2,'ep'=8,'mod'=2] {'ep'}, dimensions={1} | all-to-all | bytes 4194304 | tf_op jit(solution)/shard_map/all_to_all | solution.py:65
  68.4 0.0 slice-start.2
  68.4 0.2 fusion.29
  68.6 0.0 slice-done
  68.6 0.0 slice-done.1
  68.7 0.0 slice-start.3
  68.7 1.2 fusion.2
  69.9 0.7 slice-done.2
  70.6 1.3 slice-done.3
  72.0 1.2 fusion.6
  73.2 6.3 %multiply_reduce_fusion.1 = (bf16[128]{0:T(256)(128)(2,1)S(1)}, f32[128,1024]{1,0:T(8,128)S(1)}) fusion(f32[128,1024]{1,0:T(8,128)S(1)} %fusion.6, f32[128,1024]{1,0:T(8,128)S(1)} %fusion.2, bf16[128,4096]{1,0:T(8,128)(2,1)S(1)} %bitcast.58, bf16[1,1024,4096]{2,1,0:T(8,128)(2,1)} %param.15), kind=kOutput, calls=%fused_computation.23 | convolution fusion | flops 1074659200 | bytes 11010304 | tf_op jit(solution)/shard_map/dot_general | solution.py:13
  79.6 2.9 %fusion = f32[128,4096]{1,0:T(8,128)S(1)} fusion(bf16[1,4096,1024]{2,1,0:T(8,128)(2,1)S(1)} %bitcast.52, f32[128,1024]{1,0:T(8,128)S(1)} %fusion.2, f32[128,1024]{1,0:T(8,128)S(1)} %get-tuple-element.15, f32[128,1024]{1,0:T(8,128)S(1)} %fusion.6), kind=kOutput, calls=%fused_computation.2 | convolution fusion | flops 1075052544 | bytes 12058624 | tf_op jit(solution)/shard_map/dot_general | solution.py:22
  82.4 3.9 %fusion.13 = bf16[128,4096]{1,0:T(8,128)(2,1)} fusion(f32[128,4096]{1,0:T(8,128)S(1)} %fusion, bf16[1,4096,1024]{2,1,0:T(8,128)(2,1)S(1)} %bitcast.54, f32[128,1024]{1,0:T(8,128)S(1)} %get-tuple-element.15, f32[128,1024]{1,0:T(8,128)S(1)} %fusion.2), kind=kOutput, calls=%fused_computation.13 | convolution fusion | flops 1075576832 | bytes 12582912 | tf_op jit(solution)/shard_map/dot_general | solution.py:25
  86.3 3.6 %all-to-all-start.1 = ((bf16[8,16,4096]{2,1,0:T(8,128)(2,1)}), bf16[8,16,4096]{2,1,0:T(8,128)(2,1)S(1)}, u32[]{:S(2)}, u32[]{:S(2)}) async-start(bf16[8,16,4096]{2,1,0:T(8,128)(2,1)} %bitcast.11), calls=%async_computation.1 | async-start | bytes 2097152 | tf_op jit(solution)/shard_map/all_to_all | solution.py:74
  89.9 0.2 reduce-scatter.3.cloned.1.call-start
  90.1 0.1 mul.58
  90.3 25.2 %all-to-all-done.1 = bf16[8,16,4096]{2,1,0:T(8,128)(2,1)S(1)} async-done(((bf16[8,16,4096]{2,1,0:T(8,128)(2,1)}), bf16[8,16,4096]{2,1,0:T(8,128)(2,1)S(1)}, u32[]{:S(2)}, u32[]{:S(2)}) %all-to-all-start.1) | async-done | bytes 1048608 | tf_op jit(solution)/shard_map/all_to_all | solution.py:74
  115.5 0.2 convert_reduce_fusion
  115.7 3.9 %gather_fusion = f32[256,4096]{1,0:T(8,128)} fusion(f32[64,4096]{1,0:T(8,128)S(1)} %bitcast.50, s32[1024]{0:T(1024)S(1)} %pad_clamp_fusion), kind=kCustom, calls=%fused_computation | custom fusion | bytes 8389632 | tf_op jit(solution)/shard_map/gather | solution.py:92
  119.5 5.8 %gather.11 = f32[128,2,4096]{2,1,0:T(2,128)} reshape(f32[256,4096]{1,0:T(8,128)} %gather_fusion) | data formatting | bytes 8388608 | tf_op jit(solution)/shard_map/gather | solution.py:92
  125.4 0.0 copy-start.1
  125.4 9.9 %multiply_reduce_fusion = f32[128,4096]{1,0:T(8,128)} fusion(f32[128,2,4096]{2,1,0:T(2,128)} %gather.11, f32[128,2]{1,0:T(8,128)S(1)} %get-tuple-element.8), kind=kLoop, calls=%fused_computation.18 | loop fusion | flops 1572864 | bytes 6292480 | tf_op jit(solution)/shard_map/reduce_sum | solution.py:93
  135.3 0.0 reduce-scatter.3.cloned.1.call-update
  135.3 0.7 convert_element_type.57
  136.0 3.4 %all-to-all-start.2 = ((bf16[8,1,16]{2,1,0:T(2,128)(2,1)}), bf16[8,1,16]{2,1,0:T(2,128)(2,1)S(1)}, u32[]{:S(2)}, u32[]{:S(2)}) async-start(bf16[8,1,16]{2,1,0:T(2,128)(2,1)} %convert_element_type.57), calls=%async_computation.3 | async-start | bytes 8192 | tf_op jit(solution)/shard_map/all_to_all | solution.py:81
  139.4 0.0 copy-done.1
  139.4 0.6 dynamic-slice
  140.0 5.8 %all-to-all-done.2 = bf16[8,1,16]{2,1,0:T(2,128)(2,1)S(1)} async-done(((bf16[8,1,16]{2,1,0:T(2,128)(2,1)}), bf16[8,1,16]{2,1,0:T(2,128)(2,1)S(1)}, u32[]{:S(2)}, u32[]{:S(2)}) %all-to-all-start.2) | async-done | bytes 288 | tf_op jit(solution)/shard_map/all_to_all | solution.py:81
  145.8 0.1 reshape.168
  145.9 1.9 %gather_fusion.1 = f32[256]{0:T(256)S(1)} fusion(f32[64]{0:T(128)S(1)} %reshape.168, s32[1024]{0:T(1024)S(1)} %pad_clamp_fusion), kind=kCustom, calls=%fused_computation.1 | custom fusion | bytes 3072 | tf_op jit(solution)/shard_map/gather | solution.py:94
  147.7 0.1 gather.13
  147.9 3.6 %all-reduce = f32[128,2]{1,0:T(8,128)S(1)} all-reduce(f32[128,2]{1,0:T(8,128)S(1)} %broadcast_select_fusion), channel_id=3, replica_groups=mesh['parts'=2,'ep'=8,'mod'=2] {'mod'}, use_global_device_ids=true, to_apply=%region_7.8.clone | all-reduce | flops 256 | bytes 2048
  151.5 0.7 constant_dynamic-slice_fusion
  152.2 0.6 copy.32
  152.8 0.0 reduce-scatter.3.cloned.1.call-done
  152.8 2.1 %convert_element_type.51 = bf16[128,2048]{1,0:T(8,128)(2,1)} convert(f32[128,2048]{1,0:T(8,128)} %reduce-scatter.3.cloned.1.call-done) | non-fusion elementwise | flops 262144 | bytes 1572864 | tf_op jit(solution)/shard_map/convert_element_type | solution.py:99
  (10 shorter events, 0.1 us)
Async XLA Ops:
  7.2 3.4 %copy-start = (bf16[128,4096]{1,0:T(8,128)(2,1)S(1)}, bf16[128,4096]{1,0:T(8,128)(2,1)}, u32[]{:S(2)}) copy-start(bf16[128,4096]{1,0:T(8,128)(2,1)} %param.9) | copy-start | bytes 3145732
  12.4 56.3 %slice-start = ((s8[8388608]{0:T(1024)(128)(4,1)}), s8[4194304]{0:T(1024)(128)(4,1)S(1)}, s32[]{:S(2)}) async-start(s8[8388608]{0:T(1024)(128)(4,1)} %bitcast.51), calls=%async_computation.5 | async-start | bytes 8388608
  12.8 55.8 %slice-start.1 = ((s8[8388608]{0:T(1024)(128)(4,1)}), s8[4194304]{0:T(1024)(128)(4,1)S(1)}, s32[]{:S(2)}) async-start(s8[8388608]{0:T(1024)(128)(4,1)} %bitcast.51), calls=%async_computation.6 | async-start | bytes 8388608
  68.4 2.2 %slice-start.2 = ((s8[8388608]{0:T(1024)(128)(4,1)}), s8[4194304]{0:T(1024)(128)(4,1)S(1)}, s32[]{:S(2)}) async-start(s8[8388608]{0:T(1024)(128)(4,1)} %bitcast.53), calls=%async_computation.7 | async-start | bytes 8388608
  68.7 3.3 %slice-start.3 = ((s8[8388608]{0:T(1024)(128)(4,1)}), s8[4194304]{0:T(1024)(128)(4,1)S(1)}, s32[]{:S(2)}) async-start(s8[8388608]{0:T(1024)(128)(4,1)} %bitcast.53), calls=%async_computation.8 | async-start | bytes 8388608
  86.3 29.2 %all-to-all-start.1 = ((bf16[8,16,4096]{2,1,0:T(8,128)(2,1)}), bf16[8,16,4096]{2,1,0:T(8,128)(2,1)S(1)}, u32[]{:S(2)}, u32[]{:S(2)}) async-start(bf16[8,16,4096]{2,1,0:T(8,128)(2,1)} %bitcast.11), calls=%async_computation.1 | async-start | bytes 2097152 | tf_op jit(solution)/shard_map/all_to_all | solution.py:74
  89.9 62.9 %reduce-scatter.3.cloned.1.call-start = ((), (), s32[]{:S(2)}) async-start(), calls=%async_computation.4 | async-start | bytes 3145728 | tf_op jit(solution)/shard_map/reduce_scatter | solution.py:96
  125.4 14.0 %copy-start.1 = (u32[32]{0:T(128)S(1)}, u32[32]{0:T(128)}, u32[]{:S(2)}) copy-start(u32[32]{0:T(128)} %constant.24) | copy-start | bytes 388
  136.0 9.8 %all-to-all-start.2 = ((bf16[8,1,16]{2,1,0:T(2,128)(2,1)}), bf16[8,1,16]{2,1,0:T(2,128)(2,1)S(1)}, u32[]{:S(2)}, u32[]{:S(2)}) async-start(bf16[8,1,16]{2,1,0:T(2,128)(2,1)} %convert_element_type.57), calls=%async_computation.3 | async-start | bytes 8192 | tf_op jit(solution)/shard_map/all_to_all | solution.py:81
Sparse Core Ops, SparseCore 0:
  135.4 8.4 reduce-scatter.2
where the time goes:
time: 162 us
  blocking collectives  59.2 us (37%)
  waiting for transfers between devices  31 us (19%)
  local copies, waits for them, and re-layouts  19.3 us (12%)
  matrix products  17.4 us (11%)
  between operations  14.3 us (9%)
  other arithmetic  13.4 us (8%)
  starting transfers between devices  7.21 us (4%)
    all_to_all x1, blocking collectives, local(): lax.all_to_all(copies, 'ep', split_axis=1, concat_axis=1, tiled=True)  55.6 us
    all_to_all x1, waiting for transfers between devices, local(): lax.all_to_all(part_dx.reshape(device_count, item_count, model_width), 'e...  25.2 us
    reduce_sum x1, other arithmetic, local(): jnp.sum(pair_dx.reshape(tok_rows, topk_count, model_width), axis=1)  9.89 us
    gather x2, local copies, waits for them, and re-layouts, local(): pair_dx = table_dx[position] * weight[:, None]  9.69 us
    dot_general x1, matrix products, piece_terms(): lax.dot_general(grad_rows, down_piece, (((1,), (1,)), ((), ())), preferre...  6.34 us
    all_to_all x1, waiting for transfers between devices, local(): lax.all_to_all(part_gate.reshape(device_count, item_count), 'ep', split_a...  5.8 us
    unnamed x17, local copies, waits for them, and re-layouts  5.55 us
    dot_general x1, matrix products, piece_terms(): lax.dot_general(grad_up_pre, up_piece, (((1,), (1,)), ((), ())), preferre...  3.86 us
  transfers between devices with their start and end apart: 3, of which 2 were waited for; matrix products, arithmetic and copies ran while one was open for 3% of the time, Pallas kernels for 0%

commit v1 on v0

v1 whole, which is shorter than its diff:
```python
import functools

import jax
import jax.numpy as jnp
from jax import lax
from jax.experimental import pallas as pl
from jax.experimental.pallas import tpu as pltpu
from jax.sharding import PartitionSpec as P

E_MOD = 4
CAP = 16
EXT = 128
BF16 = jnp.bfloat16
F32 = jnp.float32
MIB = 1024 * 1024


def cost(flops, nbytes):
    return pl.CostEstimate(flops=flops, bytes_accessed=nbytes, transcendentals=0)


def whole(shape):
    return pl.BlockSpec(shape, lambda *_: (0,) * len(shape))


def nt_dot(lhs, rhs):
    return lax.dot_general(lhs, rhs, (((1,), (1,)), ((), ())), preferred_element_type=F32)


def slot_of_labels(ids_ref, modality_ref, picks_ref):
    tok_rows = modality_ref.shape[1]
    label = lax.broadcasted_iota(jnp.int32, (2 * E_MOD, tok_rows), 0)
    expert = jnp.bitwise_xor(label % E_MOD, ids_ref[0])
    modal = jnp.bitwise_xor(label // E_MOD, ids_ref[1])
    mine = modality_ref[...] == modal
    first = mine & (picks_ref[0:1, :] == expert)
    second = mine & (picks_ref[1:2, :] == expert)
    member = first | second
    row = lax.broadcasted_iota(jnp.int32, (tok_rows, tok_rows), 0)
    col = lax.broadcasted_iota(jnp.int32, (tok_rows, tok_rows), 1)
    earlier = (row < col).astype(F32)
    count = jnp.dot(member.astype(F32), earlier, preferred_element_type=F32).astype(jnp.int32)
    return count, first, second, member


def gather_kernel(ids_ref, modality_ref, picks_ref, rows_ref, *out_refs):
    count, _, _, member = slot_of_labels(ids_ref, modality_ref, picks_ref)
    slot = jnp.where(member, count, -1)
    tok_rows = slot.shape[1]
    want = lax.broadcasted_iota(jnp.int32, (CAP, tok_rows), 0)
    chosen = jnp.concatenate(
        [(slot[s : s + 1, :] == want).astype(F32) for s in range(E_MOD)], axis=0
    ).astype(BF16)
    picked = jnp.dot(chosen, rows_ref[...], preferred_element_type=F32).astype(BF16)
    for s in range(E_MOD):
        out_refs[s][...] = picked[s * CAP : (s + 1) * CAP, :]


def gather_slots(ids, modality, picks, rows):
    tok_rows, width = rows.shape
    chunk = width // 4
    return pl.pallas_call(
        gather_kernel,
        grid=(width // chunk,),
        in_specs=[
            pl.BlockSpec(memory_space=pltpu.SMEM),
            whole(modality.shape),
            whole(picks.shape),
            pl.BlockSpec((tok_rows, chunk), lambda i: (0, i)),
        ],
        out_specs=[pl.BlockSpec((CAP, chunk), lambda i: (0, i))] * E_MOD,
        out_shape=[jax.ShapeDtypeStruct((CAP, width), BF16)] * E_MOD,
        cost_estimate=cost(2 * E_MOD * CAP * tok_rows * width, 3 * tok_rows * width),
        name="gather_slots",
    )(ids, modality, picks, rows)


def pre_kernel(count, *refs):
    blocks, (gate_ref, up_ref, gate_out, up_out, rows) = refs[:count], refs[count:]

    @pl.when(pl.program_id(0) == 0)
    def _():
        for i in range(count):
            rows[i * CAP : (i + 1) * CAP, :] = blocks[i][...]

    gate_out[...] = jnp.dot(rows[...], gate_ref[0], preferred_element_type=F32)
    up_out[...] = jnp.dot(rows[...], up_ref[0], preferred_element_type=F32)


def pre_activations(blocks, gate_proj, up_proj):
    count = len(blocks)
    _, width, hidden = gate_proj.shape
    total = count * CAP
    chunk = min(256, hidden)
    weight = pl.BlockSpec((1, width, chunk), lambda i: (0, 0, i))
    out = pl.BlockSpec((total, chunk), lambda i: (0, i))
    return pl.pallas_call(
        functools.partial(pre_kernel, count),
        grid=(hidden // chunk,),
        in_specs=[whole((CAP, width))] * count + [weight] * 2,
        out_specs=[out] * 2,
        out_shape=[jax.ShapeDtypeStruct((total, hidden), F32)] * 2,
        scratch_shapes=[pltpu.VMEM((total, width), BF16)],
        compiler_params=pltpu.CompilerParams(vmem_limit_bytes=24 * MIB),
        cost_estimate=cost(4 * total * width * hidden, 4 * width * hidden),
        name="pre_activations",
    )(*blocks, gate_proj, up_proj)


def hidden_kernel(count, *refs):
    blocks = refs[:count]
    down_ref, gate_ref, up_ref, dgate_out, dup_out, part_out, rows, part = refs[count:]
    step = pl.program_id(0)

    @pl.when(step == 0)
    def _():
        for i in range(count):
            rows[i * CAP : (i + 1) * CAP, :] = blocks[i][...]
        part[...] = jnp.zeros_like(part)

    grad = nt_dot(rows[...], down_ref[...])
    gate_pre = gate_ref[...]
    up_pre = up_ref[...]
    sig = jax.nn.sigmoid(gate_pre)
    act = gate_pre * sig
    grad_act = grad * act
    part[...] += jnp.sum(grad_act * up_pre, axis=1, keepdims=True)
    dgate_out[...] = (grad * up_pre * (sig * (1.0 + gate_pre * (1.0 - sig)))).astype(BF16)
    dup_out[...] = grad_act.astype(BF16)

    @pl.when(step == pl.num_programs(0) - 1)
    def _():
        part_out[...] = two_terms(part[...])


def two_terms(value):
    high = value.astype(BF16).astype(F32)
    low = value - high
    lane = lax.broadcasted_iota(jnp.int32, (value.shape[0], EXT), 1)
    return jnp.where(lane == 0, high, jnp.where(lane == 1, low, 0.0)).astype(BF16)


def hidden_grads(blocks, down_piece, gate_pre, up_pre):
    count = len(blocks)
    hidden, width = down_piece.shape
    total = count * CAP
    chunk = min(256, hidden)
    tile = pl.BlockSpec((total, chunk), lambda i: (0, i))
    return pl.pallas_call(
        functools.partial(hidden_kernel, count),
        grid=(hidden // chunk,),
        in_specs=[whole((CAP, width))] * count
        + [pl.BlockSpec((chunk, width), lambda i: (i, 0)), tile, tile],
        out_specs=[tile, tile, whole((total, EXT))],
        out_shape=[jax.ShapeDtypeStruct((total, hidden), BF16)] * 2
        + [jax.ShapeDtypeStruct((total, EXT), BF16)],
        scratch_shapes=[pltpu.VMEM((total, width), BF16), pltpu.VMEM((total, 1), F32)],
        compiler_params=pltpu.CompilerParams(vmem_limit_bytes=24 * MIB),
        cost_estimate=cost(2 * total * width * hidden, 2 * width * hidden),
        name="hidden_grads",
    )(*blocks, down_piece, gate_pre, up_pre)


def back_kernel(groups, half_ref, dgate_ref, dup_ref, part_ref, gate_ref, up_ref, *outs):
    step = pl.program_id(0)
    chunk = gate_ref.shape[1]
    wide = outs[0].shape[1] - EXT
    own_rows = outs[0].shape[0]
    grad = nt_dot(dgate_ref[...], gate_ref[0]) + nt_dot(dup_ref[...], up_ref[0])
    grad = grad.astype(BF16)
    start = pl.multiple_of(step * chunk, chunk)
    for t in range(groups):
        outs[t][:, pl.ds(start, chunk)] = grad[t * own_rows : (t + 1) * own_rows, :]

    @pl.when(step == 0)
    def _():
        for t in range(groups):
            outs[t][:, wide:] = part_ref[t * own_rows : (t + 1) * own_rows, :]


def back_half(groups, half, dgate, dup, part, gate_proj, up_proj):
    _, width, hidden = gate_proj.shape
    total = dgate.shape[0]
    own_rows = total // groups
    wide = width // 2
    chunk = 512
    steps = wide // chunk
    weight = pl.BlockSpec((1, chunk, hidden), lambda i, half_ref: (0, half_ref[0] * steps + i, 0))
    shape = (own_rows, wide + EXT)
    return pl.pallas_call(
        functools.partial(back_kernel, groups),
        grid_spec=pltpu.PrefetchScalarGridSpec(
            num_scalar_prefetch=1,
            grid=(steps,),
            in_specs=[whole(dgate.shape), whole(dup.shape), whole(part.shape), weight, weight],
            out_specs=[whole(shape)] * groups,
        ),
        out_shape=[jax.ShapeDtypeStruct(shape, BF16)] * groups,
        compiler_params=pltpu.CompilerParams(vmem_limit_bytes=24 * MIB),
        cost_estimate=cost(4 * total * wide * hidden, 4 * wide * hidden),
        name="back_half",
    )(half, dgate, dup, part, gate_proj, up_proj)


def sum_kernel(groups, *refs):
    ins, outs = refs[:groups], refs[groups:]
    wide = ins[0].shape[1] - EXT
    for s in range(E_MOD):
        rows = slice(s * CAP, (s + 1) * CAP)
        total = ins[0][rows, :].astype(F32)
        for t in range(1, groups):
            total = total + ins[t][rows, :].astype(F32)
        outs[s][:, :wide] = total[:, :wide].astype(BF16)
        outs[s][:, wide:] = two_terms(jnp.sum(total[:, wide:], axis=1, keepdims=True))


def sum_pieces(partials):
    groups = len(partials)
    own_rows, wide = partials[0].shape
    return pl.pallas_call(
        functools.partial(sum_kernel, groups),
        out_shape=[jax.ShapeDtypeStruct((CAP, wide), BF16)] * E_MOD,
        cost_estimate=cost(own_rows * wide, 4 * groups * own_rows * wide),
        name="sum_pieces",
    )(*partials)


def combine_kernel(ids_ref, modality_ref, picks_ref, weights_ref, *refs):
    blocks, (grad_out, gate_out, table) = refs[: 2 * E_MOD], refs[2 * E_MOD :]
    wide = grad_out.shape[1]
    for i in range(2 * E_MOD):
        table[i * CAP : (i + 1) * CAP, :] = blocks[i][...]
    count, first, second, member = slot_of_labels(ids_ref, modality_ref, picks_ref)
    slot = jnp.where(member, count, -1)
    scale = jnp.where(first, weights_ref[0:1, :], jnp.where(second, weights_ref[1:2, :], 0.0))
    own = jnp.where(ids_ref[1] == 0, first.astype(F32), second.astype(F32))
    tok_rows = slot.shape[1]
    want = lax.broadcasted_iota(jnp.int32, (CAP, tok_rows), 0)
    mix = []
    gate = jnp.zeros((1, tok_rows), F32)
    for i in range(2 * E_MOD):
        hit = slot[i : i + 1, :] == want
        mix.append(jnp.where(hit, scale[i : i + 1, :], 0.0))
        part = jnp.sum(table[i * CAP : (i + 1) * CAP, wide:].astype(F32), axis=1, keepdims=True)
        gate = gate + jnp.sum(
            jnp.where(hit, own[i : i + 1, :] * part, 0.0), axis=0, keepdims=True
        )
    gate_out[...] = gate
    mix = jnp.concatenate(mix, axis=0).T
    high = mix.astype(BF16)
    low = (mix - high.astype(F32)).astype(BF16)
    values = table[:, :wide]
    total = jnp.dot(high, values, preferred_element_type=F32)
    total = total + jnp.dot(low, values, preferred_element_type=F32)
    grad_out[...] = total.astype(BF16)


def combine(ids, modality, picks, weights, blocks):
    tok_rows = modality.shape[1]
    wide = blocks[0].shape[1] - EXT
    count = len(blocks)
    vmem = pl.BlockSpec(memory_space=pltpu.VMEM)
    return pl.pallas_call(
        combine_kernel,
        in_specs=[pl.BlockSpec(memory_space=pltpu.SMEM)] + [vmem] * (3 + count),
        out_specs=[vmem] * 2,
        out_shape=[
            jax.ShapeDtypeStruct((tok_rows, wide), BF16),
            jax.ShapeDtypeStruct((1, tok_rows), F32),
        ],
        scratch_shapes=[pltpu.VMEM((count * CAP, wide + EXT), BF16)],
        cost_estimate=cost(4 * count * CAP * tok_rows * wide, 4 * tok_rows * wide),
        name="combine",
    )(ids, modality, picks, weights, *blocks)


def local(tokens, cotangent, modality, picks, gate_weights, gate_proj, up_proj, down_proj):
    device_count = lax.axis_size("ep")
    groups = device_count // E_MOD
    core = lax.axis_index("mod")
    expert = lax.axis_index("ep") // groups
    ids = jnp.stack([expert, core]).astype(jnp.int32)
    modality = modality.reshape(1, -1)
    picks = picks.T
    weights = gate_weights.T

    def to_expert(x, s):
        return lax.ppermute(
            x,
            "ep",
            [(e * groups + j, (e ^ s) * groups + j) for e in range(E_MOD) for j in range(groups)],
        )

    def to_piece(x, t):
        return lax.ppermute(
            x,
            "ep",
            [
                (e * groups + j, e * groups + (j + t) % groups)
                for e in range(E_MOD)
                for j in range(groups)
            ],
        )

    def to_source(x, s, flip):
        return lax.ppermute(
            x,
            ("ep", "mod"),
            [
                ((e * groups + j) * 2 + m, ((e ^ s) * groups + j) * 2 + (m ^ flip))
                for e in range(E_MOD)
                for j in range(groups)
                for m in range(2)
            ],
        )

    def spread(rows):
        sent = gather_slots(ids, modality, picks, rows)
        here = [sent[0]] + [to_expert(sent[s], s) for s in range(1, E_MOD)]
        return here + [to_piece(x, t) for t in range(1, groups) for x in here]

    token_blocks = spread(tokens)
    grad_blocks = spread(cotangent)
    gate_pre, up_pre = pre_activations(token_blocks, gate_proj, up_proj)
    dgate, dup, part = hidden_grads(grad_blocks, down_proj[0], gate_pre, up_pre)
    arrived = []
    for flip in (1, 0):
        half = (core ^ flip).astype(jnp.int32).reshape(1)
        partials = back_half(groups, half, dgate, dup, part, gate_proj, up_proj)
        partials = [partials[0]] + [to_piece(partials[t], groups - t) for t in range(1, groups)]
        sums = sum_pieces(partials)
        arrived.append(
            [sums[s] if s + flip == 0 else to_source(sums[s], s, flip) for s in range(E_MOD)]
        )
    token_grad, gate_grad = combine(ids, modality, picks, weights, arrived[1] + arrived[0])
    return token_grad, gate_grad.reshape(-1, 1)


def solution(mesh):
    in_specs = (
        P(("parts", "ep"), None),
        P(("parts", "ep"), None),
        P(("parts", "ep")),
        P(("parts", "ep"), None),
        P(("parts", "ep"), None),
        P("mod", None, "ep"),
        P("mod", None, "ep"),
        P("mod", "ep", None),
    )
    out_specs = (P(("parts", "ep"), "mod"), P(("parts", "ep"), "mod"))
    return jax.shard_map(local, mesh=mesh, in_specs=in_specs, out_specs=out_specs, check_vma=False)
```

time: 162 us -> 94.7 us (0.58)
  blocking collectives: 59.2 us -> 0 us
  Pallas kernels: 0 us -> 30.1 us
  starting transfers between devices: 7.21 us -> 32.9 us
  matrix products: 17.4 us -> 0 us
  waiting for transfers between devices: 31 us -> 15.2 us
  between operations: 14.3 us -> 0.84 us
  other arithmetic: 13.4 us -> 0.66 us
  local copies, waits for them, and re-layouts: 19.3 us -> 14.6 us
    all_to_all x1 -> x0, blocking collectives: 55.6 us -> none  [local(): lax.all_to_all(copies, 'ep', split_axis=1, concat_axis=1, tiled=True)]
    ppermute x0 -> x23, starting transfers between devices: none -> 32.9 us  [the longest x10 12 us: to_piece(): lax.ppermute(x, 'ep', [(e * groups + j, e * groups + (j + t) % groups) fo...]
    all_to_all x2 -> x0, waiting for transfers between devices: 31 us -> none  [the longest x1 25.2 us: local(): lax.all_to_all(part_dx.reshape(device_count, item_count, model_width), 'e...]
    pallas_call x0 -> x9, Pallas kernels: none -> 30.1 us  [the longest x2 7.61 us: gather_slots(): pl.pallas_call(gather_kernel, grid=(width // chunk,), in_specs=[pl.BlockS...]
    dot_general x7 -> x0, matrix products: 17.4 us -> none  [the longest x1 6.34 us: piece_terms(): lax.dot_general(grad_rows, down_piece, (((1,), (1,)), ((), ())), preferre...]
    ppermute x0 -> x23, waiting for transfers between devices: none -> 15.2 us  [the longest x6 6.44 us: to_expert(): lax.ppermute(x, 'ep', [(e * groups + j, (e ^ s) * groups + j) for e in ra...]
    gather x4 -> x0, local copies, waits for them, and re-layouts: 11.7 us -> none  [the longest x2 9.69 us: local(): pair_dx = table_dx[position] * weight[:, None]]
    reduce_sum x4 -> x0, other arithmetic: 10.3 us -> none  [the longest x1 9.89 us: local(): jnp.sum(pair_dx.reshape(tok_rows, topk_count, model_width), axis=1)]
  transfers between devices with their start and end apart: 3 -> 23, of which waited for: 2 -> 5; matrix products, arithmetic and copies ran while one was open for 3% -> 0% of each run, Pallas kernels for 0% -> 17%
where the time goes in v1:
time: 94.7 us; the launch traced here: 94.3 us
  starting transfers between devices  32.9 us (35%)
  Pallas kernels  30.1 us (32%)
  waiting for transfers between devices  15.2 us (16%)
  local copies, waits for them, and re-layouts  14.6 us (15%)
    unnamed x36, local copies, waits for them, and re-layouts  14.6 us
    ppermute x10, starting transfers between devices, to_piece(): lax.ppermute(x, 'ep', [(e * groups + j, e * groups + (j + t) % groups) fo...  12 us
    ppermute x6, starting transfers between devices, to_expert(): lax.ppermute(x, 'ep', [(e * groups + j, (e ^ s) * groups + j) for e in ra...  11.3 us
    ppermute x7, starting transfers between devices, to_source(): lax.ppermute(x, ('ep', 'mod'), [((e * groups + j) * 2 + m, ((e ^ s) * gro...  9.57 us
    pallas_call x2, Pallas kernels, gather_slots(): pl.pallas_call(gather_kernel, grid=(width // chunk,), in_specs=[pl.BlockS...  7.61 us
    pallas_call x2, Pallas kernels, back_half(): pl.pallas_call(functools.partial(back_kernel, groups), grid_spec=pltpu.Pr...  6.77 us
    ppermute x6, waiting for transfers between devices, to_expert(): lax.ppermute(x, 'ep', [(e * groups + j, (e ^ s) * groups + j) for e in ra...  6.44 us
    ppermute x7, waiting for transfers between devices, to_source(): lax.ppermute(x, ('ep', 'mod'), [((e * groups + j) * 2 + m, ((e ^ s) * gro...  5.52 us
  transfers between devices with their start and end apart: 23, of which 5 were waited for; matrix products, arithmetic and copies ran while one was open for 0% of the time, Pallas kernels for 17%

profile of v1, /device:TPU:0, one launch (start us, length us, event | category | flops | bytes accessed | tf_op | source)
XLA Modules:
  0.0 94.3 jit_solution(17656483031430495447)
XLA Ops:
  0.6 0.7 pad_add_fusion.ids_ref
  1.3 3.8 %gather_slots.3 = (bf16[16,4096]{1,0:T(8,128)(2,1)}, bf16[16,4096]{1,0:T(8,128)(2,1)}, bf16[16,4096]{1,0:T(8,128)(2,1)}, bf16[16,4096]{1,0:T(8,128)(2,1)}) custom-call(s32[2]{0:T(128)} %pad_add_fusion.ids_ref, s32[1,128]{1,0:T(1,128)} %bitcast.12, s32[2,128]{1,0:T(2,128)} %bitcast.9, bf16[128,4096]{1,0:T(8,128)(2,1)} %rows_ref.3), custom_call_target="tpu_custom_call" | custom-call | flops 67108864 | bytes 1572864 | tf_op jit(solution)/shard_map/gather_slots/pallas_call | solution.py:62
  5.1 3.0 %collective-permute-start.7 = (bf16[16,4096]{1,0:T(8,128)(2,1)}, bf16[16,4096]{1,0:T(8,128)(2,1)S(1)}, u32[]{:S(2)}, u32[]{:S(2)}) collective-permute-start(bf16[16,4096]{1,0:T(8,128)(2,1)} %get-tuple-element.34), channel_id=1, source_target_pairs={{0,4},{2,6},{4,0},{6,2},{8,12},{10,14},{12,8},{14,10},{1,5},{3,7},... | collective-permute-start | bytes 393224 | tf_op jit(solution)/shard_map/ppermute | solution.py:288
  8.2 2.6 %collective-permute-start.8 = (bf16[16,4096]{1,0:T(8,128)(2,1)}, bf16[16,4096]{1,0:T(8,128)(2,1)S(1)}, u32[]{:S(2)}, u32[]{:S(2)}) collective-permute-start(bf16[16,4096]{1,0:T(8,128)(2,1)} %get-tuple-element.35), channel_id=1, source_target_pairs={{0,8},{2,10},{4,12},{6,14},{8,0},{10,2},{12,4},{14,6},{1,9},{3,11}... | collective-permute-start | bytes 393224 | tf_op jit(solution)/shard_map/ppermute | solution.py:288
  10.8 0.0 collective-permute-start.9
  10.8 1.7 %collective-permute-start.10 = (bf16[16,4096]{1,0:T(8,128)(2,1)}, bf16[16,4096]{1,0:T(8,128)(2,1)S(1)}, u32[]{:S(2)}, u32[]{:S(2)}) collective-permute-start(bf16[16,4096]{1,0:T(8,128)(2,1)} %get-tuple-element.33.refs_0_), channel_id=1, source_target_pairs={{0,2},{2,0},{4,6},{6,4},{8,10},{10,8},{12,14},{14,12},{1,3},{3,1},... | collective-permute-start | bytes 393224 | tf_op jit(solution)/shard_map/ppermute | solution.py:295
  12.5 3.8 %gather_slots.2 = (bf16[16,4096]{1,0:T(8,128)(2,1)}, bf16[16,4096]{1,0:T(8,128)(2,1)}, bf16[16,4096]{1,0:T(8,128)(2,1)}, bf16[16,4096]{1,0:T(8,128)(2,1)}) custom-call(s32[2]{0:T(128)} %pad_add_fusion.ids_ref, s32[1,128]{1,0:T(1,128)} %bitcast.13, s32[2,128]{1,0:T(2,128)} %bitcast.10, bf16[128,4096]{1,0:T(8,128)(2,1)} %rows_ref.2), custom_call_target="tpu_custom_call" | custom-call | flops 67108864 | bytes 1572864 | tf_op jit(solution)/shard_map/gather_slots/pallas_call | solution.py:62
  16.3 0.7 collective-permute-start
  17.0 0.0 collective-permute-done.7.refs_1_
  17.0 3.5 %collective-permute-start.1 = (bf16[16,4096]{1,0:T(8,128)(2,1)}, bf16[16,4096]{1,0:T(8,128)(2,1)S(1)}, u32[]{:S(2)}, u32[]{:S(2)}) collective-permute-start(bf16[16,4096]{1,0:T(8,128)(2,1)} %get-tuple-element.31), channel_id=1, source_target_pairs={{0,8},{2,10},{4,12},{6,14},{8,0},{10,2},{12,4},{14,6},{1,9},{3,11}... | collective-permute-start | bytes 393224 | tf_op jit(solution)/shard_map/ppermute | solution.py:288
  20.5 1.7 %collective-permute-done.8.refs_2_ = bf16[16,4096]{1,0:T(8,128)(2,1)S(1)} collective-permute-done((bf16[16,4096]{1,0:T(8,128)(2,1)}, bf16[16,4096]{1,0:T(8,128)(2,1)S(1)}, u32[]{:S(2)}, u32[]{:S(2)}) %collective-permute-start.8) | collective-permute-done | bytes 131104 | tf_op jit(solution)/shard_map/ppermute | solution.py:288
  22.2 1.4 %collective-permute-start.2 = (bf16[16,4096]{1,0:T(8,128)(2,1)}, bf16[16,4096]{1,0:T(8,128)(2,1)S(1)}, u32[]{:S(2)}, u32[]{:S(2)}) collective-permute-start(bf16[16,4096]{1,0:T(8,128)(2,1)} %get-tuple-element.32), channel_id=1, source_target_pairs={{0,12},{2,14},{4,8},{6,10},{8,4},{10,6},{12,0},{14,2},{1,13},{3,15... | collective-permute-start | bytes 393224 | tf_op jit(solution)/shard_map/ppermute | solution.py:288
  23.6 0.0 collective-permute-done.9.refs_3_
  23.6 2.2 %collective-permute-start.11 = (bf16[16,4096]{1,0:T(8,128)(2,1)S(1)}, bf16[16,4096]{1,0:T(8,128)(2,1)S(1)}, u32[]{:S(2)}, u32[]{:S(2)}) collective-permute-start(bf16[16,4096]{1,0:T(8,128)(2,1)S(1)} %collective-permute-done.7.refs_1_), channel_id=1, source_target_pairs={{0,2},{2,0},{4,6},{6,4},{8,10},{10,8},{12,14},{14,12},{1,3},{3,1},... | collective-permute-start | bytes 393224 | tf_op jit(solution)/shard_map/ppermute | solution.py:295
  25.8 0.0 collective-permute-done.10.refs_4_
  25.8 0.1 collective-permute-start.12
  25.9 0.0 collective-permute-done.refs_1_
  25.9 2.0 %collective-permute-start.13 = (bf16[16,4096]{1,0:T(8,128)(2,1)S(1)}, bf16[16,4096]{1,0:T(8,128)(2,1)S(1)}, u32[]{:S(2)}, u32[]{:S(2)}) collective-permute-start(bf16[16,4096]{1,0:T(8,128)(2,1)S(1)} %collective-permute-done.9.refs_3_), channel_id=1, source_target_pairs={{0,2},{2,0},{4,6},{6,4},{8,10},{10,8},{12,14},{14,12},{1,3},{3,1},... | collective-permute-start | bytes 393224 | tf_op jit(solution)/shard_map/ppermute | solution.py:295
  27.9 4.7 %collective-permute-done.1.refs_2_ = bf16[16,4096]{1,0:T(8,128)(2,1)S(1)} collective-permute-done((bf16[16,4096]{1,0:T(8,128)(2,1)}, bf16[16,4096]{1,0:T(8,128)(2,1)S(1)}, u32[]{:S(2)}, u32[]{:S(2)}) %collective-permute-start.1) | collective-permute-done | bytes 131104 | tf_op jit(solution)/shard_map/ppermute | solution.py:288
  32.6 1.5 %collective-permute-start.3 = (bf16[16,4096]{1,0:T(8,128)(2,1)}, bf16[16,4096]{1,0:T(8,128)(2,1)S(1)}, u32[]{:S(2)}, u32[]{:S(2)}) collective-permute-start(bf16[16,4096]{1,0:T(8,128)(2,1)} %get-tuple-element.29.refs_0_), channel_id=1, source_target_pairs={{0,2},{2,0},{4,6},{6,4},{8,10},{10,8},{12,14},{14,12},{1,3},{3,1},... | collective-permute-start | bytes 393224 | tf_op jit(solution)/shard_map/ppermute | solution.py:295
  34.1 0.0 collective-permute-done.2.refs_3_
  34.1 0.5 collective-permute-start.4
  34.6 0.0 collective-permute-done.11.refs_5_
  34.6 1.5 %collective-permute-start.5 = (bf16[16,4096]{1,0:T(8,128)(2,1)S(1)}, bf16[16,4096]{1,0:T(8,128)(2,1)S(1)}, u32[]{:S(2)}, u32[]{:S(2)}) collective-permute-start(bf16[16,4096]{1,0:T(8,128)(2,1)S(1)} %collective-permute-done.1.refs_2_), channel_id=1, source_target_pairs={{0,2},{2,0},{4,6},{6,4},{8,10},{10,8},{12,14},{14,12},{1,3},{3,1},... | collective-permute-start | bytes 393224 | tf_op jit(solution)/shard_map/ppermute | solution.py:295
  36.1 0.5 collective-permute-start.6
  36.7 3.4 %copy-done = bf16[1,4096,1024]{2,1,0:T(8,128)(2,1)S(1)} copy-done((bf16[1,4096,1024]{2,1,0:T(8,128)(2,1)S(1)}, bf16[1,4096,1024]{2,1,0:T(8,128)(2,1)}, u32[]{:S(2)}) %copy-start) | copy-done | bytes 8388632
  40.0 3.4 %copy-done.2 = bf16[1,4096,1024]{2,1,0:T(8,128)(2,1)S(1)} copy-done((bf16[1,4096,1024]{2,1,0:T(8,128)(2,1)S(1)}, bf16[1,4096,1024]{2,1,0:T(8,128)(2,1)}, u32[]{:S(2)}) %copy-start.2) | copy-done | bytes 8388632
  43.4 0.9 copy-done.8
  44.3 5.4 %pre_activations.1 = (f32[128,1024]{1,0:T(8,128)S(1)}, f32[128,1024]{1,0:T(8,128)S(1)}) custom-call(bf16[16,4096]{1,0:T(8,128)(2,1)S(1)} %copy-done.8, bf16[16,4096]{1,0:T(8,128)(2,1)S(1)} %collective-permute-done.7.refs_1_, bf16[16,4096]{1,0:T(8,128)(2,1)S(1)} %collective-permute-done.8.refs_2_, bf16[16,4096]{1,0:T(8,128)(2,1)S(1)} %collective-permute-done.9.refs_3_, ...), custom_call_target="tpu_custom_call" | custom-call | flops 2147483648 | bytes 16777216 | tf_op jit(solution)/shard_map/pre_activations/pallas_call | solution.py:97
  49.7 0.0 copy-start.1
  49.7 0.0 collective-permute-done.4.refs_5_
  49.7 0.0 collective-permute-done.5.refs_6_
  49.8 0.0 copy-start.4
  49.8 3.5 %copy-done.4 = bf16[1,1024,4096]{2,1,0:T(8,128)(2,1)S(1)} copy-done((bf16[1,1024,4096]{2,1,0:T(8,128)(2,1)S(1)}, bf16[1,1024,4096]{2,1,0:T(8,128)(2,1)}, u32[]{:S(2)}) %copy-start.4) | copy-done | bytes 8388632
  53.3 4.0 %hidden_grads.1 = (bf16[128,1024]{1,0:T(8,128)(2,1)S(1)}, bf16[128,1024]{1,0:T(8,128)(2,1)S(1)}, bf16[128,128]{1,0:T(8,128)(2,1)S(1)}) custom-call(bf16[16,4096]{1,0:T(8,128)(2,1)S(1)} %copy-done.7, bf16[16,4096]{1,0:T(8,128)(2,1)S(1)} %collective-permute-done.refs_1_, bf16[16,4096]{1,0:T(8,128)(2,1)S(1)} %collective-permute-done.1.refs_2_, ...), custom_call_target="tpu_custom_call" | custom-call | flops 1073741824 | bytes 8388608 | tf_op jit(solution)/shard_map/hidden_grads/pallas_call | solution.py:149
  57.4 3.4 %back_half.3 = (bf16[64,2176]{1,0:T(8,128)(2,1)S(1)}, bf16[64,2176]{1,0:T(8,128)(2,1)S(1)}) custom-call(s32[1]{0:T(128)} %bitcast.6.half_ref, bf16[128,1024]{1,0:T(8,128)(2,1)S(1)} %get-tuple-element.39.dgate_ref, bf16[128,1024]{1,0:T(8,128)(2,1)S(1)} %get-tuple-element.40.dup_ref, bf16[128,128]{1,0:T(8,128)(2,1)S(1)} %get-tuple-element.41.part_ref, ...), custom_call_target="tpu_custom_call" | custom-call | flops 1073741824 | bytes 8388608 | tf_op jit(solution)/shard_map/back_half/pallas_call | solution.py:190
  60.8 0.7 copy-done.6
  61.5 1.5 %collective-permute-start.18 = (bf16[64,2176]{1,0:T(8,128)(2,1)S(1)}, bf16[64,2176]{1,0:T(8,128)(2,1)S(1)}, u32[]{:S(2)}, u32[]{:S(2)}) collective-permute-start(bf16[64,2176]{1,0:T(8,128)(2,1)S(1)} %get-tuple-element.49), channel_id=1, source_target_pairs={{0,2},{2,0},{4,6},{6,4},{8,10},{10,8},{12,14},{14,12},{1,3},{3,1},... | collective-permute-start | bytes 835592 | tf_op jit(solution)/shard_map/ppermute | solution.py:295
  63.0 3.4 %back_half.2 = (bf16[64,2176]{1,0:T(8,128)(2,1)S(1)}, bf16[64,2176]{1,0:T(8,128)(2,1)S(1)}) custom-call(s32[1]{0:T(128)} %bitcast.1.half_ref, bf16[128,1024]{1,0:T(8,128)(2,1)S(1)} %get-tuple-element.39.dgate_ref, bf16[128,1024]{1,0:T(8,128)(2,1)S(1)} %get-tuple-element.40.dup_ref, bf16[128,128]{1,0:T(8,128)(2,1)S(1)} %get-tuple-element.41.part_ref, ...), custom_call_target="tpu_custom_call" | custom-call | flops 1073741824 | bytes 8388608 | tf_op jit(solution)/shard_map/back_half/pallas_call | solution.py:190
  66.3 0.0 copy-start.5
  66.3 0.7 copy-done.5
  67.0 0.5 collective-permute-start.14
  67.6 3.2 %collective-permute-done.18.refs_1_ = bf16[64,2176]{1,0:T(8,128)(2,1)S(1)} collective-permute-done((bf16[64,2176]{1,0:T(8,128)(2,1)S(1)}, bf16[64,2176]{1,0:T(8,128)(2,1)S(1)}, u32[]{:S(2)}, u32[]{:S(2)}) %collective-permute-start.18) | collective-permute-done | bytes 278560 | tf_op jit(solution)/shard_map/ppermute | solution.py:295
  70.8 0.7 copy-done.10
  71.5 1.9 %sum_pieces.3 = (bf16[16,2176]{1,0:T(8,128)(2,1)}, bf16[16,2176]{1,0:T(8,128)(2,1)}, bf16[16,2176]{1,0:T(8,128)(2,1)}, bf16[16,2176]{1,0:T(8,128)(2,1)}) custom-call(bf16[64,2176]{1,0:T(8,128)(2,1)} %copy-done.6, bf16[64,2176]{1,0:T(8,128)(2,1)} %copy-done.10), custom_call_target="tpu_custom_call" | custom-call | flops 139264 | bytes 1114112 | tf_op jit(solution)/shard_map/sum_pieces/pallas_call | solution.py:220
  73.4 2.7 %collective-permute-start.20 = (bf16[16,2176]{1,0:T(8,128)(2,1)}, bf16[16,2176]{1,0:T(8,128)(2,1)S(1)}, u32[]{:S(2)}, u32[]{:S(2)}) collective-permute-start(bf16[16,2176]{1,0:T(8,128)(2,1)} %get-tuple-element.51), channel_id=1, source_target_pairs={{0,5},{1,4},{2,7},{3,6},{4,1},{5,0},{6,3},{7,2},{8,13},{9,12},{10,... | collective-permute-start | bytes 208904 | tf_op jit(solution)/shard_map/ppermute | solution.py:306
  76.0 1.5 %collective-permute-start.21 = (bf16[16,2176]{1,0:T(8,128)(2,1)}, bf16[16,2176]{1,0:T(8,128)(2,1)S(1)}, u32[]{:S(2)}, u32[]{:S(2)}) collective-permute-start(bf16[16,2176]{1,0:T(8,128)(2,1)} %get-tuple-element.52), channel_id=1, source_target_pairs={{0,9},{1,8},{2,11},{3,10},{4,13},{5,12},{6,15},{7,14},{8,1},{9,0},... | collective-permute-start | bytes 208904 | tf_op jit(solution)/shard_map/ppermute | solution.py:306
  77.5 1.1 %collective-permute-start.22 = (bf16[16,2176]{1,0:T(8,128)(2,1)}, bf16[16,2176]{1,0:T(8,128)(2,1)S(1)}, u32[]{:S(2)}, u32[]{:S(2)}) collective-permute-start(bf16[16,2176]{1,0:T(8,128)(2,1)} %get-tuple-element.53), channel_id=1, source_target_pairs={{0,13},{1,12},{2,15},{3,14},{4,9},{5,8},{6,11},{7,10},{8,5},{9,4},... | collective-permute-start | bytes 208904 | tf_op jit(solution)/shard_map/ppermute | solution.py:306
  78.6 0.0 collective-permute-done.14.refs_1_
  78.6 0.7 copy-done.9
  79.3 1.8 %sum_pieces.2 = (bf16[16,2176]{1,0:T(8,128)(2,1)}, bf16[16,2176]{1,0:T(8,128)(2,1)}, bf16[16,2176]{1,0:T(8,128)(2,1)}, bf16[16,2176]{1,0:T(8,128)(2,1)}) custom-call(bf16[64,2176]{1,0:T(8,128)(2,1)} %copy-done.5, bf16[64,2176]{1,0:T(8,128)(2,1)} %copy-done.9), custom_call_target="tpu_custom_call" | custom-call | flops 139264 | bytes 1114112 | tf_op jit(solution)/shard_map/sum_pieces/pallas_call | solution.py:220
  81.1 0.7 collective-permute-start.15
  81.8 0.0 collective-permute-done.19.refs_4_
  81.8 2.3 %collective-permute-start.16 = (bf16[16,2176]{1,0:T(8,128)(2,1)}, bf16[16,2176]{1,0:T(8,128)(2,1)S(1)}, u32[]{:S(2)}, u32[]{:S(2)}) collective-permute-start(bf16[16,2176]{1,0:T(8,128)(2,1)} %get-tuple-element.46), channel_id=1, source_target_pairs={{0,8},{1,9},{2,10},{3,11},{4,12},{5,13},{6,14},{7,15},{8,0},{9,1},... | collective-permute-start | bytes 208904 | tf_op jit(solution)/shard_map/ppermute | solution.py:306
  84.1 0.0 collective-permute-done.20.refs_5_
  84.1 1.4 %collective-permute-start.17 = (bf16[16,2176]{1,0:T(8,128)(2,1)}, bf16[16,2176]{1,0:T(8,128)(2,1)S(1)}, u32[]{:S(2)}, u32[]{:S(2)}) collective-permute-start(bf16[16,2176]{1,0:T(8,128)(2,1)} %get-tuple-element.47), channel_id=1, source_target_pairs={{0,12},{1,13},{2,14},{3,15},{4,8},{5,9},{6,10},{7,11},{8,4},{9,5},... | collective-permute-start | bytes 208904 | tf_op jit(solution)/shard_map/ppermute | solution.py:306
  85.5 0.0 collective-permute-done.21.refs_6_
  85.5 0.0 collective-permute-done.22.refs_7_
  85.5 0.9 collective-permute-done.15.refs_1_
  86.4 4.6 %collective-permute-done.16.refs_2_ = bf16[16,2176]{1,0:T(8,128)(2,1)S(1)} collective-permute-done((bf16[16,2176]{1,0:T(8,128)(2,1)}, bf16[16,2176]{1,0:T(8,128)(2,1)S(1)}, u32[]{:S(2)}, u32[]{:S(2)}) %collective-permute-start.16) | collective-permute-done | bytes 69664 | tf_op jit(solution)/shard_map/ppermute | solution.py:306
  91.0 0.0 collective-permute-done.17.refs_3_
  91.1 0.6 copy-done.16
  91.7 0.0 copy-done.17
  91.7 2.6 %combine.1 = (bf16[128,2048]{1,0:T(8,128)(2,1)}, f32[1,128]{1,0:T(1,128)}) custom-call(s32[2]{0:T(128)} %pad_add_fusion.ids_ref, s32[1,128]{1,0:T(1,128)} %bitcast.14, s32[2,128]{1,0:T(2,128)} %bitcast.11, f32[2,128]{1,0:T(2,128)} %bitcast.15, bf16[16,2176]{1,0:T(8,128)(2,1)} %get-tuple-element.44.refs_0_, bf16[16,2176]{1,0:T(8,128)(2,1)} %copy-done.15, ...), custom_call_target="tpu_custom_call" | custom-call | flops 134217728 | bytes 1048576 | tf_op jit(solution)/shard_map/combine/pallas_call | solution.py:263
  (28 shorter events, 0.1 us)
Async XLA Ops:
  5.1 11.9 %collective-permute-start.7 = (bf16[16,4096]{1,0:T(8,128)(2,1)}, bf16[16,4096]{1,0:T(8,128)(2,1)S(1)}, u32[]{:S(2)}, u32[]{:S(2)}) collective-permute-start(bf16[16,4096]{1,0:T(8,128)(2,1)} %get-tuple-element.34), channel_id=1, source_target_pairs={{0,4},{2,6},{4,0},{6,2},{8,12},{10,14},{12,8},{14,10},{1,5},{3,7},... | collective-permute-start | bytes 393224 | tf_op jit(solution)/shard_map/ppermute | solution.py:288
  8.2 14.0 %collective-permute-start.8 = (bf16[16,4096]{1,0:T(8,128)(2,1)}, bf16[16,4096]{1,0:T(8,128)(2,1)S(1)}, u32[]{:S(2)}, u32[]{:S(2)}) collective-permute-start(bf16[16,4096]{1,0:T(8,128)(2,1)} %get-tuple-element.35), channel_id=1, source_target_pairs={{0,8},{2,10},{4,12},{6,14},{8,0},{10,2},{12,4},{14,6},{1,9},{3,11}... | collective-permute-start | bytes 393224 | tf_op jit(solution)/shard_map/ppermute | solution.py:288
  10.8 12.9 %collective-permute-start.9 = (bf16[16,4096]{1,0:T(8,128)(2,1)}, bf16[16,4096]{1,0:T(8,128)(2,1)S(1)}, u32[]{:S(2)}, u32[]{:S(2)}) collective-permute-start(bf16[16,4096]{1,0:T(8,128)(2,1)} %get-tuple-element.36), channel_id=1, source_target_pairs={{0,12},{2,14},{4,8},{6,10},{8,4},{10,6},{12,0},{14,2},{1,13},{3,15... | collective-permute-start | bytes 393224 | tf_op jit(solution)/shard_map/ppermute | solution.py:288
  10.8 15.1 %collective-permute-start.10 = (bf16[16,4096]{1,0:T(8,128)(2,1)}, bf16[16,4096]{1,0:T(8,128)(2,1)S(1)}, u32[]{:S(2)}, u32[]{:S(2)}) collective-permute-start(bf16[16,4096]{1,0:T(8,128)(2,1)} %get-tuple-element.33.refs_0_), channel_id=1, source_target_pairs={{0,2},{2,0},{4,6},{6,4},{8,10},{10,8},{12,14},{14,12},{1,3},{3,1},... | collective-permute-start | bytes 393224 | tf_op jit(solution)/shard_map/ppermute | solution.py:295
  16.3 9.6 %collective-permute-start = (bf16[16,4096]{1,0:T(8,128)(2,1)}, bf16[16,4096]{1,0:T(8,128)(2,1)S(1)}, u32[]{:S(2)}, u32[]{:S(2)}) collective-permute-start(bf16[16,4096]{1,0:T(8,128)(2,1)} %get-tuple-element.30), channel_id=1, source_target_pairs={{0,4},{2,6},{4,0},{6,2},{8,12},{10,14},{12,8},{14,10},{1,5},{3,7},... | collective-permute-start | bytes 393224 | tf_op jit(solution)/shard_map/ppermute | solution.py:288
  17.0 15.6 %collective-permute-start.1 = (bf16[16,4096]{1,0:T(8,128)(2,1)}, bf16[16,4096]{1,0:T(8,128)(2,1)S(1)}, u32[]{:S(2)}, u32[]{:S(2)}) collective-permute-start(bf16[16,4096]{1,0:T(8,128)(2,1)} %get-tuple-element.31), channel_id=1, source_target_pairs={{0,8},{2,10},{4,12},{6,14},{8,0},{10,2},{12,4},{14,6},{1,9},{3,11}... | collective-permute-start | bytes 393224 | tf_op jit(solution)/shard_map/ppermute | solution.py:288
  22.2 11.9 %collective-permute-start.2 = (bf16[16,4096]{1,0:T(8,128)(2,1)}, bf16[16,4096]{1,0:T(8,128)(2,1)S(1)}, u32[]{:S(2)}, u32[]{:S(2)}) collective-permute-start(bf16[16,4096]{1,0:T(8,128)(2,1)} %get-tuple-element.32), channel_id=1, source_target_pairs={{0,12},{2,14},{4,8},{6,10},{8,4},{10,6},{12,0},{14,2},{1,13},{3,15... | collective-permute-start | bytes 393224 | tf_op jit(solution)/shard_map/ppermute | solution.py:288
  23.6 11.0 %collective-permute-start.11 = (bf16[16,4096]{1,0:T(8,128)(2,1)S(1)}, bf16[16,4096]{1,0:T(8,128)(2,1)S(1)}, u32[]{:S(2)}, u32[]{:S(2)}) collective-permute-start(bf16[16,4096]{1,0:T(8,128)(2,1)S(1)} %collective-permute-done.7.refs_1_), channel_id=1, source_target_pairs={{0,2},{2,0},{4,6},{6,4},{8,10},{10,8},{12,14},{14,12},{1,3},{3,1},... | collective-permute-start | bytes 393224 | tf_op jit(solution)/shard_map/ppermute | solution.py:295
  25.8 10.3 %collective-permute-start.12 = (bf16[16,4096]{1,0:T(8,128)(2,1)S(1)}, bf16[16,4096]{1,0:T(8,128)(2,1)S(1)}, u32[]{:S(2)}, u32[]{:S(2)}) collective-permute-start(bf16[16,4096]{1,0:T(8,128)(2,1)S(1)} %collective-permute-done.8.refs_2_), channel_id=1, source_target_pairs={{0,2},{2,0},{4,6},{6,4},{8,10},{10,8},{12,14},{14,12},{1,3},{3,1},... | collective-permute-start | bytes 393224 | tf_op jit(solution)/shard_map/ppermute | solution.py:295
  25.9 10.8 %collective-permute-start.13 = (bf16[16,4096]{1,0:T(8,128)(2,1)S(1)}, bf16[16,4096]{1,0:T(8,128)(2,1)S(1)}, u32[]{:S(2)}, u32[]{:S(2)}) collective-permute-start(bf16[16,4096]{1,0:T(8,128)(2,1)S(1)} %collective-permute-done.9.refs_3_), channel_id=1, source_target_pairs={{0,2},{2,0},{4,6},{6,4},{8,10},{10,8},{12,14},{14,12},{1,3},{3,1},... | collective-permute-start | bytes 393224 | tf_op jit(solution)/shard_map/ppermute | solution.py:295
  32.6 17.1 %collective-permute-start.3 = (bf16[16,4096]{1,0:T(8,128)(2,1)}, bf16[16,4096]{1,0:T(8,128)(2,1)S(1)}, u32[]{:S(2)}, u32[]{:S(2)}) collective-permute-start(bf16[16,4096]{1,0:T(8,128)(2,1)} %get-tuple-element.29.refs_0_), channel_id=1, source_target_pairs={{0,2},{2,0},{4,6},{6,4},{8,10},{10,8},{12,14},{14,12},{1,3},{3,1},... | collective-permute-start | bytes 393224 | tf_op jit(solution)/shard_map/ppermute | solution.py:295
  34.1 15.6 %collective-permute-start.4 = (bf16[16,4096]{1,0:T(8,128)(2,1)S(1)}, bf16[16,4096]{1,0:T(8,128)(2,1)S(1)}, u32[]{:S(2)}, u32[]{:S(2)}) collective-permute-start(bf16[16,4096]{1,0:T(8,128)(2,1)S(1)} %collective-permute-done.refs_1_), channel_id=1, source_target_pairs={{0,2},{2,0},{4,6},{6,4},{8,10},{10,8},{12,14},{14,12},{1,3},{3,1},... | collective-permute-start | bytes 393224 | tf_op jit(solution)/shard_map/ppermute | solution.py:295
  34.6 15.1 %collective-permute-start.5 = (bf16[16,4096]{1,0:T(8,128)(2,1)S(1)}, bf16[16,4096]{1,0:T(8,128)(2,1)S(1)}, u32[]{:S(2)}, u32[]{:S(2)}) collective-permute-start(bf16[16,4096]{1,0:T(8,128)(2,1)S(1)} %collective-permute-done.1.refs_2_), channel_id=1, source_target_pairs={{0,2},{2,0},{4,6},{6,4},{8,10},{10,8},{12,14},{14,12},{1,3},{3,1},... | collective-permute-start | bytes 393224 | tf_op jit(solution)/shard_map/ppermute | solution.py:295
  36.1 13.6 %collective-permute-start.6 = (bf16[16,4096]{1,0:T(8,128)(2,1)S(1)}, bf16[16,4096]{1,0:T(8,128)(2,1)S(1)}, u32[]{:S(2)}, u32[]{:S(2)}) collective-permute-start(bf16[16,4096]{1,0:T(8,128)(2,1)S(1)} %collective-permute-done.2.refs_3_), channel_id=1, source_target_pairs={{0,2},{2,0},{4,6},{6,4},{8,10},{10,8},{12,14},{14,12},{1,3},{3,1},... | collective-permute-start | bytes 393224 | tf_op jit(solution)/shard_map/ppermute | solution.py:295
  36.7 3.4 %copy-start = (bf16[1,4096,1024]{2,1,0:T(8,128)(2,1)S(1)}, bf16[1,4096,1024]{2,1,0:T(8,128)(2,1)}, u32[]{:S(2)}) copy-start(bf16[1,4096,1024]{2,1,0:T(8,128)(2,1)} %gate_ref.3) | copy-start | bytes 25165828
  40.0 3.4 %copy-start.2 = (bf16[1,4096,1024]{2,1,0:T(8,128)(2,1)S(1)}, bf16[1,4096,1024]{2,1,0:T(8,128)(2,1)}, u32[]{:S(2)}) copy-start(bf16[1,4096,1024]{2,1,0:T(8,128)(2,1)} %up_ref.3) | copy-start | bytes 25165828
  43.4 0.9 copy-start.8
  44.3 5.4 %copy-start.7 = (bf16[16,4096]{1,0:T(8,128)(2,1)S(1)}, bf16[16,4096]{1,0:T(8,128)(2,1)}, u32[]{:S(2)}) copy-start(bf16[16,4096]{1,0:T(8,128)(2,1)} %get-tuple-element.29.refs_0_) | copy-start | bytes 393220
  44.3 13.0 %copy-start.3 = (bf16[1,4096,1024]{2,1,0:T(8,128)(2,1)S(1)}, bf16[1,4096,1024]{2,1,0:T(8,128)(2,1)}, u32[]{:S(2)}) copy-start(bf16[1,4096,1024]{2,1,0:T(8,128)(2,1)} %up_ref.3) | copy-start | bytes 25165828
  49.7 7.7 %copy-start.1 = (bf16[1,4096,1024]{2,1,0:T(8,128)(2,1)S(1)}, bf16[1,4096,1024]{2,1,0:T(8,128)(2,1)}, u32[]{:S(2)}) copy-start(bf16[1,4096,1024]{2,1,0:T(8,128)(2,1)} %gate_ref.3) | copy-start | bytes 25165828
  49.8 3.5 %copy-start.4 = (bf16[1,1024,4096]{2,1,0:T(8,128)(2,1)S(1)}, bf16[1,1024,4096]{2,1,0:T(8,128)(2,1)}, u32[]{:S(2)}) copy-start(bf16[1,1024,4096]{2,1,0:T(8,128)(2,1)} %param.15) | copy-start | bytes 25165828
  60.8 0.7 copy-start.6
  61.5 9.3 %collective-permute-start.18 = (bf16[64,2176]{1,0:T(8,128)(2,1)S(1)}, bf16[64,2176]{1,0:T(8,128)(2,1)S(1)}, u32[]{:S(2)}, u32[]{:S(2)}) collective-permute-start(bf16[64,2176]{1,0:T(8,128)(2,1)S(1)} %get-tuple-element.49), channel_id=1, source_target_pairs={{0,2},{2,0},{4,6},{6,4},{8,10},{10,8},{12,14},{14,12},{1,3},{3,1},... | collective-permute-start | bytes 835592 | tf_op jit(solution)/shard_map/ppermute | solution.py:295
  66.3 0.7 copy-start.5
  67.0 11.5 %collective-permute-start.14 = (bf16[64,2176]{1,0:T(8,128)(2,1)S(1)}, bf16[64,2176]{1,0:T(8,128)(2,1)S(1)}, u32[]{:S(2)}, u32[]{:S(2)}) collective-permute-start(bf16[64,2176]{1,0:T(8,128)(2,1)S(1)} %get-tuple-element.43), channel_id=1, source_target_pairs={{0,2},{2,0},{4,6},{6,4},{8,10},{10,8},{12,14},{14,12},{1,3},{3,1},... | collective-permute-start | bytes 835592 | tf_op jit(solution)/shard_map/ppermute | solution.py:295
  70.8 0.7 copy-start.10
  73.4 8.4 %collective-permute-start.19 = (bf16[16,2176]{1,0:T(8,128)(2,1)}, bf16[16,2176]{1,0:T(8,128)(2,1)S(1)}, u32[]{:S(2)}, u32[]{:S(2)}) collective-permute-start(bf16[16,2176]{1,0:T(8,128)(2,1)} %get-tuple-element.50), channel_id=1, source_target_pairs={{0,1},{1,0},{2,3},{3,2},{4,5},{5,4},{6,7},{7,6},{8,9},{9,8},{10,11... | collective-permute-start | bytes 208904 | tf_op jit(solution)/shard_map/ppermute | solution.py:306
  73.4 10.7 %collective-permute-start.20 = (bf16[16,2176]{1,0:T(8,128)(2,1)}, bf16[16,2176]{1,0:T(8,128)(2,1)S(1)}, u32[]{:S(2)}, u32[]{:S(2)}) collective-permute-start(bf16[16,2176]{1,0:T(8,128)(2,1)} %get-tuple-element.51), channel_id=1, source_target_pairs={{0,5},{1,4},{2,7},{3,6},{4,1},{5,0},{6,3},{7,2},{8,13},{9,12},{10,... | collective-permute-start | bytes 208904 | tf_op jit(solution)/shard_map/ppermute | solution.py:306
  76.0 9.5 %collective-permute-start.21 = (bf16[16,2176]{1,0:T(8,128)(2,1)}, bf16[16,2176]{1,0:T(8,128)(2,1)S(1)}, u32[]{:S(2)}, u32[]{:S(2)}) collective-permute-start(bf16[16,2176]{1,0:T(8,128)(2,1)} %get-tuple-element.52), channel_id=1, source_target_pairs={{0,9},{1,8},{2,11},{3,10},{4,13},{5,12},{6,15},{7,14},{8,1},{9,0},... | collective-permute-start | bytes 208904 | tf_op jit(solution)/shard_map/ppermute | solution.py:306
  77.5 8.0 %collective-permute-start.22 = (bf16[16,2176]{1,0:T(8,128)(2,1)}, bf16[16,2176]{1,0:T(8,128)(2,1)S(1)}, u32[]{:S(2)}, u32[]{:S(2)}) collective-permute-start(bf16[16,2176]{1,0:T(8,128)(2,1)} %get-tuple-element.53), channel_id=1, source_target_pairs={{0,13},{1,12},{2,15},{3,14},{4,9},{5,8},{6,11},{7,10},{8,5},{9,4},... | collective-permute-start | bytes 208904 | tf_op jit(solution)/shard_map/ppermute | solution.py:306
  78.6 0.7 copy-start.9
  81.1 5.3 %collective-permute-start.15 = (bf16[16,2176]{1,0:T(8,128)(2,1)}, bf16[16,2176]{1,0:T(8,128)(2,1)S(1)}, u32[]{:S(2)}, u32[]{:S(2)}) collective-permute-start(bf16[16,2176]{1,0:T(8,128)(2,1)} %get-tuple-element.45), channel_id=1, source_target_pairs={{0,4},{1,5},{2,6},{3,7},{4,0},{5,1},{6,2},{7,3},{8,12},{9,13},{10,... | collective-permute-start | bytes 208904 | tf_op jit(solution)/shard_map/ppermute | solution.py:306
  81.8 9.2 %copy-start.11 = (bf16[16,2176]{1,0:T(8,128)(2,1)}, bf16[16,2176]{1,0:T(8,128)(2,1)S(1)}, u32[]{:S(2)}) copy-start(bf16[16,2176]{1,0:T(8,128)(2,1)S(1)} %collective-permute-done.19.refs_4_) | copy-start | bytes 208900
  81.8 9.2 %collective-permute-start.16 = (bf16[16,2176]{1,0:T(8,128)(2,1)}, bf16[16,2176]{1,0:T(8,128)(2,1)S(1)}, u32[]{:S(2)}, u32[]{:S(2)}) collective-permute-start(bf16[16,2176]{1,0:T(8,128)(2,1)} %get-tuple-element.46), channel_id=1, source_target_pairs={{0,8},{1,9},{2,10},{3,11},{4,12},{5,13},{6,14},{7,15},{8,0},{9,1},... | collective-permute-start | bytes 208904 | tf_op jit(solution)/shard_map/ppermute | solution.py:306
  84.1 6.9 %copy-start.12 = (bf16[16,2176]{1,0:T(8,128)(2,1)}, bf16[16,2176]{1,0:T(8,128)(2,1)S(1)}, u32[]{:S(2)}) copy-start(bf16[16,2176]{1,0:T(8,128)(2,1)S(1)} %collective-permute-done.20.refs_5_) | copy-start | bytes 208900
  84.1 6.9 %collective-permute-start.17 = (bf16[16,2176]{1,0:T(8,128)(2,1)}, bf16[16,2176]{1,0:T(8,128)(2,1)S(1)}, u32[]{:S(2)}, u32[]{:S(2)}) collective-permute-start(bf16[16,2176]{1,0:T(8,128)(2,1)} %get-tuple-element.47), channel_id=1, source_target_pairs={{0,12},{1,13},{2,14},{3,15},{4,8},{5,9},{6,10},{7,11},{8,4},{9,5},... | collective-permute-start | bytes 208904 | tf_op jit(solution)/shard_map/ppermute | solution.py:306
  85.5 5.6 %copy-start.13 = (bf16[16,2176]{1,0:T(8,128)(2,1)}, bf16[16,2176]{1,0:T(8,128)(2,1)S(1)}, u32[]{:S(2)}) copy-start(bf16[16,2176]{1,0:T(8,128)(2,1)S(1)} %collective-permute-done.21.refs_6_) | copy-start | bytes 208900
  85.5 5.6 %copy-start.14 = (bf16[16,2176]{1,0:T(8,128)(2,1)}, bf16[16,2176]{1,0:T(8,128)(2,1)S(1)}, u32[]{:S(2)}) copy-start(bf16[16,2176]{1,0:T(8,128)(2,1)S(1)} %collective-permute-done.22.refs_7_) | copy-start | bytes 208900
  86.4 4.7 %copy-start.15 = (bf16[16,2176]{1,0:T(8,128)(2,1)}, bf16[16,2176]{1,0:T(8,128)(2,1)S(1)}, u32[]{:S(2)}) copy-start(bf16[16,2176]{1,0:T(8,128)(2,1)S(1)} %collective-permute-done.15.refs_1_) | copy-start | bytes 208900
  91.0 0.6 copy-start.16
  91.0 0.6 copy-start.17

commit v2 on v1

v2 whole, which is shorter than its diff:
```python
import functools

import jax
import jax.numpy as jnp
from jax import lax
from jax.experimental import pallas as pl
from jax.experimental.pallas import tpu as pltpu
from jax.sharding import PartitionSpec as P

E_MOD = 4
CAP = 16
EXT = 128
BF16 = jnp.bfloat16
F32 = jnp.float32
MIB = 1024 * 1024


def cost(flops, nbytes):
    return pl.CostEstimate(flops=flops, bytes_accessed=nbytes, transcendentals=0)


def whole(shape):
    return pl.BlockSpec(shape, lambda *_: (0,) * len(shape))


def nt_dot(lhs, rhs):
    return lax.dot_general(lhs, rhs, (((1,), (1,)), ((), ())), preferred_element_type=F32)


def slot_of_labels(ids_ref, modality_ref, picks_ref):
    tok_rows = modality_ref.shape[1]
    label = lax.broadcasted_iota(jnp.int32, (2 * E_MOD, tok_rows), 0)
    expert = jnp.bitwise_xor(label % E_MOD, ids_ref[0])
    modal = jnp.bitwise_xor(label // E_MOD, ids_ref[1])
    mine = modality_ref[...] == modal
    first = mine & (picks_ref[0:1, :] == expert)
    second = mine & (picks_ref[1:2, :] == expert)
    member = first | second
    row = lax.broadcasted_iota(jnp.int32, (tok_rows, tok_rows), 0)
    col = lax.broadcasted_iota(jnp.int32, (tok_rows, tok_rows), 1)
    earlier = (row < col).astype(F32)
    count = jnp.dot(member.astype(F32), earlier, preferred_element_type=F32).astype(jnp.int32)
    return count, first, second, member


def gather_kernel(ids_ref, modality_ref, picks_ref, rows_ref, grads_ref, *refs):
    outs, chosen = refs[:-1], refs[-1]

    @pl.when(pl.program_id(0) == 0)
    def _():
        count, _, _, member = slot_of_labels(ids_ref, modality_ref, picks_ref)
        slot = jnp.where(member, count, -1)
        want = lax.broadcasted_iota(jnp.int32, (CAP, slot.shape[1]), 0)
        for s in range(E_MOD):
            hit = (slot[s : s + 1, :] == want).astype(F32)
            chosen[s * CAP : (s + 1) * CAP, :] = hit.astype(BF16)

    both = [
        jnp.dot(chosen[...], ref[...], preferred_element_type=F32).astype(BF16)
        for ref in (rows_ref, grads_ref)
    ]
    for s in range(2):
        for a in range(2):
            outs[s][a * CAP : (a + 1) * CAP, :] = both[a][s * CAP : (s + 1) * CAP, :]
    for s in range(2, E_MOD):
        for a in range(2):
            outs[2 * s - 2 + a][...] = both[a][s * CAP : (s + 1) * CAP, :]


def gather_slots(ids, modality, picks, rows, grads):
    tok_rows, width = rows.shape
    chunk = width // 4
    heights = [2 * CAP] * 2 + [CAP] * (2 * E_MOD - 4)
    source = pl.BlockSpec((tok_rows, chunk), lambda i: (0, i))
    return pl.pallas_call(
        gather_kernel,
        grid=(width // chunk,),
        in_specs=[
            pl.BlockSpec(memory_space=pltpu.SMEM),
            whole(modality.shape),
            whole(picks.shape),
            source,
            source,
        ],
        out_specs=[pl.BlockSpec((h, chunk), lambda i: (0, i)) for h in heights],
        out_shape=[jax.ShapeDtypeStruct((h, width), BF16) for h in heights],
        scratch_shapes=[pltpu.VMEM((E_MOD * CAP, tok_rows), BF16)],
        compiler_params=pltpu.CompilerParams(vmem_limit_bytes=8 * MIB),
        cost_estimate=cost(4 * E_MOD * CAP * tok_rows * width, 6 * tok_rows * width),
        name="gather_slots",
    )(ids, modality, picks, rows, grads)


def load_kernel(parts, src, dst, sems):
    rows = src.shape[1] // parts
    copies = [
        pltpu.make_async_copy(
            src.at[:, pl.ds(i * rows, rows), :], dst.at[:, pl.ds(i * rows, rows), :], sems.at[i]
        )
        for i in range(parts)
    ]
    for copy in copies:
        copy.start()
    for copy in copies:
        copy.wait()


def load(weight):
    parts = 8
    return pl.pallas_call(
        functools.partial(load_kernel, parts),
        in_specs=[pl.BlockSpec(memory_space=pl.ANY)],
        out_specs=pl.BlockSpec(memory_space=pltpu.VMEM),
        out_shape=pltpu.VMEM(weight.shape, weight.dtype),
        scratch_shapes=[pltpu.SemaphoreType.DMA((parts,))],
        compiler_params=pltpu.CompilerParams(vmem_limit_bytes=MIB),
        cost_estimate=cost(0, 2 * weight.size * weight.dtype.itemsize),
        name="load",
    )(pltpu.with_memory_space_constraint(weight, pltpu.HBM))


def in_vmem(x):
    return pltpu.with_memory_space_constraint(x, pltpu.VMEM)


def fill(rows, refs, places):
    for i, (index, start) in enumerate(places):
        rows[i * CAP : (i + 1) * CAP, :] = refs[index][start : start + CAP, :]


def pre_kernel(count, places, *refs):
    blocks, (gate_ref, up_ref, act_out, slope_out, both_out, rows) = refs[:count], refs[count:]
    fill(rows, blocks, places)
    hidden = gate_ref.shape[2]
    chunk = min(256, hidden)
    for start in range(0, hidden, chunk):
        cols = slice(start, start + chunk)
        gate_pre = jnp.dot(rows[...], gate_ref[0, :, cols], preferred_element_type=F32)
        up_pre = jnp.dot(rows[...], up_ref[0, :, cols], preferred_element_type=F32)
        sig = jax.nn.sigmoid(gate_pre)
        act = gate_pre * sig
        act_out[:, cols] = act
        slope_out[:, cols] = up_pre * (sig * (1.0 + gate_pre * (1.0 - sig)))
        both_out[:, cols] = act * up_pre


def pre_activations(blocks, places, gate_piece, up_piece):
    count = len(blocks)
    _, width, hidden = gate_piece.shape
    total = len(places) * CAP
    vmem = pl.BlockSpec(memory_space=pltpu.VMEM)
    return pl.pallas_call(
        functools.partial(pre_kernel, count, places),
        in_specs=[vmem] * (count + 2),
        out_specs=[vmem] * 3,
        out_shape=[jax.ShapeDtypeStruct((total, hidden), F32)] * 3,
        scratch_shapes=[pltpu.VMEM((total, width), BF16)],
        compiler_params=pltpu.CompilerParams(vmem_limit_bytes=16 * MIB),
        cost_estimate=cost(4 * total * width * hidden, 4 * total * hidden),
        name="pre_activations",
    )(*blocks, in_vmem(gate_piece), in_vmem(up_piece))


def back_columns(groups, half, dgate_ref, dup_ref, part, gate_ref, up_ref, outs):
    wide = outs[0].shape[1] - EXT
    own_rows = outs[0].shape[0]
    chunk = 512
    for step in range(wide // chunk):
        rows = pl.ds(pl.multiple_of(half * wide + step * chunk, chunk), chunk)
        grad = nt_dot(dgate_ref[...], gate_ref[0, rows, :]) + nt_dot(dup_ref[...], up_ref[0, rows, :])
        grad = grad.astype(BF16)
        for t in range(groups):
            outs[t][:, step * chunk : (step + 1) * chunk] = grad[t * own_rows : (t + 1) * own_rows, :]
    for t in range(groups):
        outs[t][:, wide:] = part[t * own_rows : (t + 1) * own_rows, :]


def hidden_kernel(count, places, groups, half_ref, *refs):
    blocks = refs[:count]
    act_ref, slope_ref, both_ref, down_ref, gate_ref, up_ref = refs[count : count + 6]
    outs = refs[count + 6 : count + 6 + groups]
    dgate, dup, part_out, rows = refs[count + 6 + groups :]
    fill(rows, blocks, places)
    hidden = gate_ref.shape[2]
    chunk = min(256, hidden)
    part = jnp.zeros((rows.shape[0], 1), F32)
    for start in range(0, hidden, chunk):
        cols = slice(start, start + chunk)
        grad = nt_dot(rows[...], down_ref[0, cols, :])
        part = part + jnp.sum(grad * both_ref[:, cols], axis=1, keepdims=True)
        dgate[:, cols] = (grad * slope_ref[:, cols]).astype(BF16)
        dup[:, cols] = (grad * act_ref[:, cols]).astype(BF16)
    part_out[...] = two_terms(part)
    back_columns(groups, half_ref[0], dgate, dup, part_out[...], gate_ref, up_ref, outs)


def hidden_grads(blocks, places, groups, half, factors, down_piece, gate_piece, up_piece):
    count = len(blocks)
    _, width, hidden = gate_piece.shape
    total = len(places) * CAP
    shape = (total // groups, width // 2 + EXT)
    vmem = pl.BlockSpec(memory_space=pltpu.VMEM)
    smem = pl.BlockSpec(memory_space=pltpu.SMEM)
    out = pl.pallas_call(
        functools.partial(hidden_kernel, count, places, groups),
        in_specs=[smem] + [vmem] * (count + 6),
        out_specs=[vmem] * (groups + 3),
        out_shape=[jax.ShapeDtypeStruct(shape, BF16)] * groups
        + [jax.ShapeDtypeStruct((total, hidden), BF16)] * 2
        + [jax.ShapeDtypeStruct((total, EXT), BF16)],
        scratch_shapes=[pltpu.VMEM((total, width), BF16)],
        compiler_params=pltpu.CompilerParams(vmem_limit_bytes=16 * MIB),
        cost_estimate=cost(4 * total * width * hidden, 4 * total * hidden),
        name="hidden_grads",
    )(half, *blocks, *factors, in_vmem(down_piece), in_vmem(gate_piece), in_vmem(up_piece))
    return out[:groups], out[groups:]


def back_kernel(groups, half_ref, dgate_ref, dup_ref, part_ref, gate_ref, up_ref, *outs):
    back_columns(groups, half_ref[0], dgate_ref, dup_ref, part_ref[...], gate_ref, up_ref, outs)


def back_half(groups, half, dgate, dup, part, gate_piece, up_piece):
    _, width, hidden = gate_piece.shape
    total = dgate.shape[0]
    shape = (total // groups, width // 2 + EXT)
    vmem = pl.BlockSpec(memory_space=pltpu.VMEM)
    smem = pl.BlockSpec(memory_space=pltpu.SMEM)
    return pl.pallas_call(
        functools.partial(back_kernel, groups),
        in_specs=[smem] + [vmem] * 5,
        out_specs=[vmem] * groups,
        out_shape=[jax.ShapeDtypeStruct(shape, BF16)] * groups,
        compiler_params=pltpu.CompilerParams(vmem_limit_bytes=16 * MIB),
        cost_estimate=cost(2 * total * width * hidden, 4 * total * hidden),
        name="back_half",
    )(half, dgate, dup, part, in_vmem(gate_piece), in_vmem(up_piece))


def two_terms(value):
    high = value.astype(BF16).astype(F32)
    low = value - high
    lane = lax.broadcasted_iota(jnp.int32, (value.shape[0], EXT), 1)
    return jnp.where(lane == 0, high, jnp.where(lane == 1, low, 0.0)).astype(BF16)


def sum_kernel(groups, *refs):
    ins, outs = refs[:groups], refs[groups:]
    wide = ins[0].shape[1] - EXT
    for s in range(E_MOD):
        rows = slice(s * CAP, (s + 1) * CAP)
        total = ins[0][rows, :].astype(F32)
        for t in range(1, groups):
            total = total + ins[t][rows, :].astype(F32)
        outs[s][:, :wide] = total[:, :wide].astype(BF16)
        outs[s][:, wide:] = two_terms(jnp.sum(total[:, wide:], axis=1, keepdims=True))


def sum_pieces(partials):
    groups = len(partials)
    own_rows, wide = partials[0].shape
    return pl.pallas_call(
        functools.partial(sum_kernel, groups),
        out_shape=[jax.ShapeDtypeStruct((CAP, wide), BF16)] * E_MOD,
        cost_estimate=cost(own_rows * wide, 4 * groups * own_rows * wide),
        compiler_params=pltpu.CompilerParams(vmem_limit_bytes=8 * MIB),
        name="sum_pieces",
    )(*partials)


def combine_kernel(ids_ref, modality_ref, picks_ref, weights_ref, *refs):
    blocks, (grad_out, gate_out, table) = refs[: 2 * E_MOD], refs[2 * E_MOD :]
    wide = grad_out.shape[1]
    for i in range(2 * E_MOD):
        table[i * CAP : (i + 1) * CAP, :] = blocks[i][...]
    count, first, second, member = slot_of_labels(ids_ref, modality_ref, picks_ref)
    slot = jnp.where(member, count, -1)
    scale = jnp.where(first, weights_ref[0:1, :], jnp.where(second, weights_ref[1:2, :], 0.0))
    own = jnp.where(ids_ref[1] == 0, first.astype(F32), second.astype(F32))
    tok_rows = slot.shape[1]
    want = lax.broadcasted_iota(jnp.int32, (CAP, tok_rows), 0)
    mix = []
    gate = jnp.zeros((1, tok_rows), F32)
    for i in range(2 * E_MOD):
        hit = slot[i : i + 1, :] == want
        mix.append(jnp.where(hit, scale[i : i + 1, :], 0.0))
        part = jnp.sum(table[i * CAP : (i + 1) * CAP, wide:].astype(F32), axis=1, keepdims=True)
        gate = gate + jnp.sum(
            jnp.where(hit, own[i : i + 1, :] * part, 0.0), axis=0, keepdims=True
        )
    gate_out[...] = gate
    mix = jnp.concatenate(mix, axis=0).T
    high = mix.astype(BF16)
    low = (mix - high.astype(F32)).astype(BF16)
    values = table[:, :wide]
    total = jnp.dot(high, values, preferred_element_type=F32)
    total = total + jnp.dot(low, values, preferred_element_type=F32)
    grad_out[...] = total.astype(BF16)


def combine(ids, modality, picks, weights, blocks):
    tok_rows = modality.shape[1]
    wide = blocks[0].shape[1] - EXT
    count = len(blocks)
    vmem = pl.BlockSpec(memory_space=pltpu.VMEM)
    return pl.pallas_call(
        combine_kernel,
        in_specs=[pl.BlockSpec(memory_space=pltpu.SMEM)] + [vmem] * (3 + count),
        out_specs=[vmem] * 2,
        out_shape=[
            jax.ShapeDtypeStruct((tok_rows, wide), BF16),
            jax.ShapeDtypeStruct((1, tok_rows), F32),
        ],
        scratch_shapes=[pltpu.VMEM((count * CAP, wide + EXT), BF16)],
        cost_estimate=cost(4 * count * CAP * tok_rows * wide, 4 * tok_rows * wide),
        compiler_params=pltpu.CompilerParams(vmem_limit_bytes=16 * MIB),
        name="combine",
    )(ids, modality, picks, weights, *blocks)


def local(tokens, cotangent, modality, picks, gate_weights, gate_proj, up_proj, down_proj):
    device_count = lax.axis_size("ep")
    groups = device_count // E_MOD
    core = lax.axis_index("mod")
    expert = lax.axis_index("ep") // groups
    ids = jnp.stack([expert, core]).astype(jnp.int32)
    modality = modality.reshape(1, -1)
    picks = picks.T
    weights = gate_weights.T

    def to_expert(x, s):
        return lax.ppermute(
            x,
            "ep",
            [(e * groups + j, (e ^ s) * groups + j) for e in range(E_MOD) for j in range(groups)],
        )

    def to_piece(x, t):
        return lax.ppermute(
            x,
            "ep",
            [
                (e * groups + j, e * groups + (j + t) % groups)
                for e in range(E_MOD)
                for j in range(groups)
            ],
        )

    def to_source(x, s, flip):
        return lax.ppermute(
            x,
            ("ep", "mod"),
            [
                ((e * groups + j) * 2 + m, ((e ^ s) * groups + j) * 2 + (m ^ flip))
                for e in range(E_MOD)
                for j in range(groups)
                for m in range(2)
            ],
        )

    sent = gather_slots(ids, modality, picks, tokens, cotangent)
    gate_piece, up_piece, down_piece = load(gate_proj), load(up_proj), load(down_proj)
    near = [sent[0], to_expert(sent[1], 1)]
    far = [[to_expert(sent[2 * s - 2 + a], s) for s in range(2, E_MOD)] for a in range(2)]
    near_pieces = [[to_piece(x, t) for x in near] for t in range(1, groups)]
    blocks, places = [], []
    for a in range(2):
        far_pieces = [[to_piece(x, t) for x in far[a]] for t in range(1, groups)]
        use, where = [], []
        for two, others in zip([near] + near_pieces, [far[a]] + far_pieces):
            where += [(len(use), a * CAP), (len(use) + 1, a * CAP)]
            where += [(len(use) + 2 + i, 0) for i in range(len(others))]
            use += two + others
        blocks.append(use)
        places.append(tuple(where))
    factors = pre_activations(blocks[0], places[0], gate_piece, up_piece)
    halves = [(core ^ flip).astype(jnp.int32).reshape(1) for flip in range(2)]
    first, (dgate, dup, part) = hidden_grads(
        blocks[1], places[1], groups, halves[1], factors, down_piece, gate_piece, up_piece
    )
    arrived = []
    for flip in (1, 0):
        if flip:
            partials = first
        else:
            partials = back_half(groups, halves[0], dgate, dup, part, gate_piece, up_piece)
        partials = [partials[0]] + [to_piece(partials[t], groups - t) for t in range(1, groups)]
        sums = sum_pieces(partials)
        arrived.append(
            [sums[s] if s + flip == 0 else to_source(sums[s], s, flip) for s in range(E_MOD)]
        )
    token_grad, gate_grad = combine(ids, modality, picks, weights, arrived[1] + arrived[0])
    return token_grad, gate_grad.reshape(-1, 1)


def solution(mesh):
    in_specs = (
        P(("parts", "ep"), None),
        P(("parts", "ep"), None),
        P(("parts", "ep")),
        P(("parts", "ep"), None),
        P(("parts", "ep"), None),
        P("mod", None, "ep"),
        P("mod", None, "ep"),
        P("mod", "ep", None),
    )
    out_specs = (P(("parts", "ep"), "mod"), P(("parts", "ep"), "mod"))
    return jax.shard_map(local, mesh=mesh, in_specs=in_specs, out_specs=out_specs, check_vma=False)
```

time: 94.7 us -> 83.2 us (0.88)
  local copies, waits for them, and re-layouts: 14.6 us -> 3.8 us
  waiting for transfers between devices: 15.2 us -> 21.8 us
  Pallas kernels: 30.1 us -> 25.7 us
  starting transfers between devices: 32.9 us -> 30.8 us
    unnamed x36 -> x14, local copies, waits for them, and re-layouts: 14.6 us -> 3.8 us
    pallas_call x2 -> x1, Pallas kernels: 7.61 us -> 1.86 us  [gather_slots(): pl.pallas_call(gather_kernel, grid=(width // chunk,), in_specs=[pl.BlockS...]
    pallas_call x4 -> x6, Pallas kernels: 16.2 us -> 21.7 us  [the longest x3 10.4 us: load(): pl.pallas_call(functools.partial(load_kernel, parts), in_specs=[pl.BlockS...]
    pallas_call x2, Pallas kernels: 3.68 us -> 0.18 us  [sum_pieces(): pl.pallas_call(functools.partial(sum_kernel, groups), out_shape=[jax.Shap...]
    ppermute x6 -> x5, waiting for transfers between devices: 6.44 us -> 9.63 us  [to_expert(): lax.ppermute(x, 'ep', [(e * groups + j, (e ^ s) * groups + j) for e in ra...]
    ppermute x10 -> x8, waiting for transfers between devices: 3.25 us -> 6.26 us  [to_piece(): lax.ppermute(x, 'ep', [(e * groups + j, e * groups + (j + t) % groups) fo...]
    ppermute x10 -> x8, starting transfers between devices: 12 us -> 9.41 us  [to_piece(): lax.ppermute(x, 'ep', [(e * groups + j, e * groups + (j + t) % groups) fo...]
    ppermute x6 -> x5, starting transfers between devices: 11.3 us -> 11.4 us  [to_expert(): lax.ppermute(x, 'ep', [(e * groups + j, (e ^ s) * groups + j) for e in ra...]
  transfers between devices with their start and end apart: 23 -> 20, of which waited for: 5 -> 9; matrix products, arithmetic and copies ran while one was open for 0% -> 0% of each run, Pallas kernels for 17% -> 16%
where the time goes in v2:
time: 83.2 us; the launch traced here: 83 us
  starting transfers between devices  30.8 us (37%)
  Pallas kernels  25.7 us (31%)
  waiting for transfers between devices  21.8 us (26%)
  local copies, waits for them, and re-layouts  3.8 us (5%)
    ppermute x5, starting transfers between devices, to_expert(): lax.ppermute(x, 'ep', [(e * groups + j, (e ^ s) * groups + j) for e in ra...  11.4 us
    pallas_call x3, Pallas kernels, load(): pl.pallas_call(functools.partial(load_kernel, parts), in_specs=[pl.BlockS...  10.4 us
    ppermute x7, starting transfers between devices, to_source(): lax.ppermute(x, ('ep', 'mod'), [((e * groups + j) * 2 + m, ((e ^ s) * gro...  9.99 us
    ppermute x5, waiting for transfers between devices, to_expert(): lax.ppermute(x, 'ep', [(e * groups + j, (e ^ s) * groups + j) for e in ra...  9.63 us
    ppermute x8, starting transfers between devices, to_piece(): lax.ppermute(x, 'ep', [(e * groups + j, e * groups + (j + t) % groups) fo...  9.41 us
    ppermute x8, waiting for transfers between devices, to_piece(): lax.ppermute(x, 'ep', [(e * groups + j, e * groups + (j + t) % groups) fo...  6.26 us
    ppermute x7, waiting for transfers between devices, to_source(): lax.ppermute(x, ('ep', 'mod'), [((e * groups + j) * 2 + m, ((e ^ s) * gro...  5.92 us
    pallas_call x1, Pallas kernels, hidden_grads(): pl.pallas_call(functools.partial(hidden_kernel, count, places, groups), i...  5.66 us
  transfers between devices with their start and end apart: 20, of which 9 were waited for; matrix products, arithmetic and copies ran while one was open for 0% of the time, Pallas kernels for 16%

profile of v2, /device:TPU:0, one launch (start us, length us, event | category | flops | bytes accessed | tf_op | source)
XLA Modules:
  0.0 83.0 jit_solution(17329227080769189249)
XLA Ops:
  0.6 0.1 pad_add_fusion.ids_ref
  0.7 0.0 copy-start
  0.7 1.2 %copy-done = bf16[128,4096]{1,0:T(8,128)(2,1)S(1)} copy-done((bf16[128,4096]{1,0:T(8,128)(2,1)S(1)}, bf16[128,4096]{1,0:T(8,128)(2,1)}, u32[]{:S(2)}) %copy-start) | copy-done | bytes 1048600
  1.9 0.0 copy-start.1
  1.9 1.2 %copy-done.1 = bf16[128,4096]{1,0:T(8,128)(2,1)S(1)} copy-done((bf16[128,4096]{1,0:T(8,128)(2,1)S(1)}, bf16[128,4096]{1,0:T(8,128)(2,1)}, u32[]{:S(2)}) %copy-start.1) | copy-done | bytes 1048600
  3.2 0.0 copy-start.2
  3.2 0.7 copy-done.2
  3.9 0.7 copy-done.4
  4.5 1.9 %gather_slots.1 = (bf16[32,4096]{1,0:T(8,128)(2,1)S(1)}, bf16[32,4096]{1,0:T(8,128)(2,1)S(1)}, bf16[16,4096]{1,0:T(8,128)(2,1)S(1)}, bf16[16,4096]{1,0:T(8,128)(...) custom-call(s32[2]{0:T(128)S(1)} %pad_add_fusion.ids_ref, s32[1,128]{1,0:T(1,128)S(1)} %bitcast.9, ...), custom_call_target="tpu_custom_call" | custom-call | flops 134217728 | bytes 3145728 | tf_op jit(solution)/shard_map/gather_slots/pallas_call | solution.py:75
  6.4 3.1 %collective-permute-start = (bf16[32,4096]{1,0:T(8,128)(2,1)S(1)}, bf16[32,4096]{1,0:T(8,128)(2,1)S(1)}, u32[]{:S(2)}, u32[]{:S(2)}) collective-permute-start(bf16[32,4096]{1,0:T(8,128)(2,1)S(1)} %get-tuple-element.29), channel_id=1, source_target_pairs={{0,4},{2,6},{4,0},{6,2},{8,12},{10,14},{12,8},{14,10},{1,5},{3,7},... | collective-permute-start | bytes 786440 | tf_op jit(solution)/shard_map/ppermute | solution.py:332
  9.5 2.6 %collective-permute-start.1 = (bf16[16,4096]{1,0:T(8,128)(2,1)S(1)}, bf16[16,4096]{1,0:T(8,128)(2,1)S(1)}, u32[]{:S(2)}, u32[]{:S(2)}) collective-permute-start(bf16[16,4096]{1,0:T(8,128)(2,1)S(1)} %get-tuple-element.30), channel_id=1, source_target_pairs={{0,8},{2,10},{4,12},{6,14},{8,0},{10,2},{12,4},{14,6},{1,9},{3,11}... | collective-permute-start | bytes 393224 | tf_op jit(solution)/shard_map/ppermute | solution.py:332
  12.1 0.3 collective-permute-start.7
  12.4 2.5 %collective-permute-start.8 = (bf16[16,4096]{1,0:T(8,128)(2,1)S(1)}, bf16[16,4096]{1,0:T(8,128)(2,1)S(1)}, u32[]{:S(2)}, u32[]{:S(2)}) collective-permute-start(bf16[16,4096]{1,0:T(8,128)(2,1)S(1)} %get-tuple-element.33), channel_id=1, source_target_pairs={{0,12},{2,14},{4,8},{6,10},{8,4},{10,6},{12,0},{14,2},{1,13},{3,15... | collective-permute-start | bytes 393224 | tf_op jit(solution)/shard_map/ppermute | solution.py:332
  14.9 1.5 %collective-permute-start.3 = (bf16[32,4096]{1,0:T(8,128)(2,1)S(1)}, bf16[32,4096]{1,0:T(8,128)(2,1)S(1)}, u32[]{:S(2)}, u32[]{:S(2)}) collective-permute-start(bf16[32,4096]{1,0:T(8,128)(2,1)S(1)} %get-tuple-element.28.refs_0_), channel_id=1, source_target_pairs={{0,2},{2,0},{4,6},{6,4},{8,10},{10,8},{12,14},{14,12},{1,3},{3,1},... | collective-permute-start | bytes 786440 | tf_op jit(solution)/shard_map/ppermute | solution.py:339
  16.4 4.3 %collective-permute-done.refs_1_ = bf16[32,4096]{1,0:T(8,128)(2,1)S(1)} collective-permute-done((bf16[32,4096]{1,0:T(8,128)(2,1)S(1)}, bf16[32,4096]{1,0:T(8,128)(2,1)S(1)}, u32[]{:S(2)}, u32[]{:S(2)}) %collective-permute-start) | collective-permute-done | bytes 262176 | tf_op jit(solution)/shard_map/ppermute | solution.py:332
  20.7 1.7 %collective-permute-start.4 = (bf16[32,4096]{1,0:T(8,128)(2,1)S(1)}, bf16[32,4096]{1,0:T(8,128)(2,1)S(1)}, u32[]{:S(2)}, u32[]{:S(2)}) collective-permute-start(bf16[32,4096]{1,0:T(8,128)(2,1)S(1)} %collective-permute-done.refs_1_), channel_id=1, source_target_pairs={{0,2},{2,0},{4,6},{6,4},{8,10},{10,8},{12,14},{14,12},{1,3},{3,1},... | collective-permute-start | bytes 786440 | tf_op jit(solution)/shard_map/ppermute | solution.py:339
  22.4 0.0 collective-permute-done.1.refs_2_
  22.4 2.9 %collective-permute-start.2 = (bf16[16,4096]{1,0:T(8,128)(2,1)S(1)}, bf16[16,4096]{1,0:T(8,128)(2,1)S(1)}, u32[]{:S(2)}, u32[]{:S(2)}) collective-permute-start(bf16[16,4096]{1,0:T(8,128)(2,1)S(1)} %get-tuple-element.31), channel_id=1, source_target_pairs={{0,12},{2,14},{4,8},{6,10},{8,4},{10,6},{12,0},{14,2},{1,13},{3,15... | collective-permute-start | bytes 393224 | tf_op jit(solution)/shard_map/ppermute | solution.py:332
  25.3 5.3 %collective-permute-done.7.refs_2_ = bf16[16,4096]{1,0:T(8,128)(2,1)S(1)} collective-permute-done((bf16[16,4096]{1,0:T(8,128)(2,1)S(1)}, bf16[16,4096]{1,0:T(8,128)(2,1)S(1)}, u32[]{:S(2)}, u32[]{:S(2)}) %collective-permute-start.7) | collective-permute-done | bytes 131104 | tf_op jit(solution)/shard_map/ppermute | solution.py:332
  30.6 1.5 %collective-permute-start.9 = (bf16[16,4096]{1,0:T(8,128)(2,1)S(1)}, bf16[16,4096]{1,0:T(8,128)(2,1)S(1)}, u32[]{:S(2)}, u32[]{:S(2)}) collective-permute-start(bf16[16,4096]{1,0:T(8,128)(2,1)S(1)} %collective-permute-done.7.refs_2_), channel_id=1, source_target_pairs={{0,2},{2,0},{4,6},{6,4},{8,10},{10,8},{12,14},{14,12},{1,3},{3,1},... | collective-permute-start | bytes 393224 | tf_op jit(solution)/shard_map/ppermute | solution.py:339
  32.1 0.0 collective-permute-done.8.refs_3_
  32.1 0.5 collective-permute-start.10
  32.7 3.5 %load.3.refs_8_.refs_12_.gate_ref = bf16[1,4096,1024]{2,1,0:T(8,128)(2,1)S(1)} custom-call(bf16[1,4096,1024]{2,1,0:T(8,128)(2,1)} %src.3), custom_call_target="tpu_custom_call" | custom-call | bytes 16777216 | tf_op jit(solution)/shard_map/load/pallas_call | solution.py:110
  36.1 3.5 %load.4.refs_9_.refs_13_.up_ref = bf16[1,4096,1024]{2,1,0:T(8,128)(2,1)S(1)} custom-call(bf16[1,4096,1024]{2,1,0:T(8,128)(2,1)} %src.4), custom_call_target="tpu_custom_call" | custom-call | bytes 16777216 | tf_op jit(solution)/shard_map/load/pallas_call | solution.py:110
  39.6 3.5 %load.5.refs_11_ = bf16[1,1024,4096]{2,1,0:T(8,128)(2,1)S(1)} custom-call(bf16[1,1024,4096]{2,1,0:T(8,128)(2,1)} %src.5), custom_call_target="tpu_custom_call" | custom-call | bytes 16777216 | tf_op jit(solution)/shard_map/load/pallas_call | solution.py:110
  43.1 0.0 collective-permute-done.2.refs_3_
  43.1 1.6 %collective-permute-start.5 = (bf16[16,4096]{1,0:T(8,128)(2,1)S(1)}, bf16[16,4096]{1,0:T(8,128)(2,1)S(1)}, u32[]{:S(2)}, u32[]{:S(2)}) collective-permute-start(bf16[16,4096]{1,0:T(8,128)(2,1)S(1)} %collective-permute-done.1.refs_2_), channel_id=1, source_target_pairs={{0,2},{2,0},{4,6},{6,4},{8,10},{10,8},{12,14},{14,12},{1,3},{3,1},... | collective-permute-start | bytes 393224 | tf_op jit(solution)/shard_map/ppermute | solution.py:339
  44.7 0.0 collective-permute-done.9.refs_6_
  44.7 0.5 collective-permute-start.6
  45.2 0.0 collective-permute-done.10.refs_7_
  45.2 0.0 collective-permute-done.3.refs_4_
  45.2 0.0 collective-permute-done.4.refs_5_
  45.2 2.7 %pre_activations.1 = (f32[128,1024]{1,0:T(8,128)S(1)}, f32[128,1024]{1,0:T(8,128)S(1)}, f32[128,1024]{1,0:T(8,128)S(1)}) custom-call(bf16[32,4096]{1,0:T(8,128)(2,1)S(1)} %get-tuple-element.28.refs_0_, bf16[32,4096]{1,0:T(8,128)(2,1)S(1)} %collective-permute-done.refs_1_, bf16[16,4096]{1,0:T(8,128)(2,1)S(1)} %collective-permute-done.7.refs_2_, ...), custom_call_target="tpu_custom_call" | custom-call | flops 2147483648 | bytes 524288 | tf_op jit(solution)/shard_map/pre_activations/pallas_call | solution.py:152
  47.9 0.2 collective-permute-done.5.refs_6_
  48.1 1.5 %collective-permute-done.6.refs_7_ = bf16[16,4096]{1,0:T(8,128)(2,1)S(1)} collective-permute-done((bf16[16,4096]{1,0:T(8,128)(2,1)S(1)}, bf16[16,4096]{1,0:T(8,128)(2,1)S(1)}, u32[]{:S(2)}, u32[]{:S(2)}) %collective-permute-start.6) | collective-permute-done | bytes 131104 | tf_op jit(solution)/shard_map/ppermute | solution.py:339
  49.7 5.7 %hidden_grads.1 = (bf16[64,2176]{1,0:T(8,128)(2,1)S(1)}, bf16[64,2176]{1,0:T(8,128)(2,1)S(1)}, bf16[128,1024]{1,0:T(8,128)(2,1)S(1)}, bf16[128,1024]{1,0:T(8,128)(2,1)S(1)}, bf16[128,128]{1,0:T(8,128)(2,1)S(1)}) custom-call(s32[1]{0:T(128)} %bitcast.5.half_ref, bf16[32,4096]{1,0:T(8,128)(2,1)S(1)} %get-tuple-element.28.refs_0_, ...), custom_call_target="tpu_custom_call" | custom-call | flops 2147483648 | bytes 524288 | tf_op jit(solution)/shard_map/hidden_grads/pallas_call | solution.py:204
  55.3 0.0 copy-start.3
  55.4 0.0 copy-start.5
  55.4 0.0 copy-start.6
  55.4 2.9 %back_half.1 = (bf16[64,2176]{1,0:T(8,128)(2,1)S(1)}, bf16[64,2176]{1,0:T(8,128)(2,1)S(1)}) custom-call(s32[1]{0:T(128)} %bitcast.1.half_ref, bf16[128,1024]{1,0:T(8,128)(2,1)S(1)} %get-tuple-element.37.dgate_ref, bf16[128,1024]{1,0:T(8,128)(2,1)S(1)} %get-tuple-element.38.dup_ref, bf16[128,128]{1,0:T(8,128)(2,1)S(1)} %get-tuple-element.39.part_ref, ...), custom_call_target="tpu_custom_call" | custom-call | flops 1073741824 | bytes 524288 | tf_op jit(solution)/shard_map/back_half/pallas_call | solution.py:229
  58.3 1.5 %collective-permute-start.11 = (bf16[64,2176]{1,0:T(8,128)(2,1)S(1)}, bf16[64,2176]{1,0:T(8,128)(2,1)S(1)}, u32[]{:S(2)}, u32[]{:S(2)}) collective-permute-start(bf16[64,2176]{1,0:T(8,128)(2,1)S(1)} %get-tuple-element.41), channel_id=1, source_target_pairs={{0,2},{2,0},{4,6},{6,4},{8,10},{10,8},{12,14},{14,12},{1,3},{3,1},... | collective-permute-start | bytes 835592 | tf_op jit(solution)/shard_map/ppermute | solution.py:339
  59.8 0.6 collective-permute-start.15
  60.4 4.5 %collective-permute-done.11.refs_1_ = bf16[64,2176]{1,0:T(8,128)(2,1)S(1)} collective-permute-done((bf16[64,2176]{1,0:T(8,128)(2,1)S(1)}, bf16[64,2176]{1,0:T(8,128)(2,1)S(1)}, u32[]{:S(2)}, u32[]{:S(2)}) %collective-permute-start.11) | collective-permute-done | bytes 278560 | tf_op jit(solution)/shard_map/ppermute | solution.py:339
  64.9 0.1 sum_pieces.2
  65.0 4.1 %collective-permute-start.12 = (bf16[16,2176]{1,0:T(8,128)(2,1)S(1)}, bf16[16,2176]{1,0:T(8,128)(2,1)S(1)}, u32[]{:S(2)}, u32[]{:S(2)}) collective-permute-start(bf16[16,2176]{1,0:T(8,128)(2,1)S(1)} %get-tuple-element.43), channel_id=1, source_target_pairs={{0,4},{1,5},{2,6},{3,7},{4,0},{5,1},{6,2},{7,3},{8,12},{9,13},{10,... | collective-permute-start | bytes 208904 | tf_op jit(solution)/shard_map/ppermute | solution.py:350
  69.1 0.6 collective-permute-start.13
  69.6 1.9 %collective-permute-start.14 = (bf16[16,2176]{1,0:T(8,128)(2,1)S(1)}, bf16[16,2176]{1,0:T(8,128)(2,1)S(1)}, u32[]{:S(2)}, u32[]{:S(2)}) collective-permute-start(bf16[16,2176]{1,0:T(8,128)(2,1)S(1)} %get-tuple-element.45), channel_id=1, source_target_pairs={{0,12},{1,13},{2,14},{3,15},{4,8},{5,9},{6,10},{7,11},{8,4},{9,5},... | collective-permute-start | bytes 208904 | tf_op jit(solution)/shard_map/ppermute | solution.py:350
  71.5 0.0 collective-permute-done.15.refs_1_
  71.5 0.1 sum_pieces.3
  71.6 0.1 collective-permute-start.16
  71.7 1.2 %collective-permute-start.17 = (bf16[16,2176]{1,0:T(8,128)(2,1)S(1)}, bf16[16,2176]{1,0:T(8,128)(2,1)S(1)}, u32[]{:S(2)}, u32[]{:S(2)}) collective-permute-start(bf16[16,2176]{1,0:T(8,128)(2,1)S(1)} %get-tuple-element.49), channel_id=1, source_target_pairs={{0,5},{1,4},{2,7},{3,6},{4,1},{5,0},{6,3},{7,2},{8,13},{9,12},{10,... | collective-permute-start | bytes 208904 | tf_op jit(solution)/shard_map/ppermute | solution.py:350
  72.8 0.0 collective-permute-done.12.refs_1_
  72.8 1.2 %collective-permute-start.18 = (bf16[16,2176]{1,0:T(8,128)(2,1)S(1)}, bf16[16,2176]{1,0:T(8,128)(2,1)S(1)}, u32[]{:S(2)}, u32[]{:S(2)}) collective-permute-start(bf16[16,2176]{1,0:T(8,128)(2,1)S(1)} %get-tuple-element.50), channel_id=1, source_target_pairs={{0,9},{1,8},{2,11},{3,10},{4,13},{5,12},{6,15},{7,14},{8,1},{9,0},... | collective-permute-start | bytes 208904 | tf_op jit(solution)/shard_map/ppermute | solution.py:350
  74.0 0.8 collective-permute-done.13.refs_2_
  74.8 1.1 %collective-permute-start.19 = (bf16[16,2176]{1,0:T(8,128)(2,1)S(1)}, bf16[16,2176]{1,0:T(8,128)(2,1)S(1)}, u32[]{:S(2)}, u32[]{:S(2)}) collective-permute-start(bf16[16,2176]{1,0:T(8,128)(2,1)S(1)} %get-tuple-element.51), channel_id=1, source_target_pairs={{0,13},{1,12},{2,15},{3,14},{4,9},{5,8},{6,11},{7,10},{8,5},{9,4},... | collective-permute-start | bytes 208904 | tf_op jit(solution)/shard_map/ppermute | solution.py:350
  75.9 0.0 collective-permute-done.14.refs_3_
  75.9 0.0 collective-permute-done.16.refs_4_
  75.9 0.8 collective-permute-done.17.refs_5_
  76.7 2.8 %collective-permute-done.18.refs_6_ = bf16[16,2176]{1,0:T(8,128)(2,1)S(1)} collective-permute-done((bf16[16,2176]{1,0:T(8,128)(2,1)S(1)}, bf16[16,2176]{1,0:T(8,128)(2,1)S(1)}, u32[]{:S(2)}, u32[]{:S(2)}) %collective-permute-start.18) | collective-permute-done | bytes 69664 | tf_op jit(solution)/shard_map/ppermute | solution.py:350
  79.5 1.5 %collective-permute-done.19.refs_7_ = bf16[16,2176]{1,0:T(8,128)(2,1)S(1)} collective-permute-done((bf16[16,2176]{1,0:T(8,128)(2,1)S(1)}, bf16[16,2176]{1,0:T(8,128)(2,1)S(1)}, u32[]{:S(2)}, u32[]{:S(2)}) %collective-permute-start.19) | collective-permute-done | bytes 69664 | tf_op jit(solution)/shard_map/ppermute | solution.py:350
  81.0 0.0 copy-done.3
  81.0 0.0 copy-done.5
  81.0 0.0 copy-done.6
  81.0 2.0 %combine.1 = (bf16[128,2048]{1,0:T(8,128)(2,1)}, f32[1,128]{1,0:T(1,128)}) custom-call(s32[2]{0:T(128)S(1)} %pad_add_fusion.ids_ref, s32[1,128]{1,0:T(1,128)S(1)} %bitcast.10, s32[2,128]{1,0:T(2,128)S(1)} %bitcast.8, f32[2,128]{1,0:T(2,128)S(1)} %bitcast.11, bf16[16,2176]{1,0:T(8,128)(2,1)S(1)} %get-tuple-element.42.refs_0_, ...), custom_call_target="tpu_custom_call" | custom-call | flops 134217728 | bytes 1048576 | tf_op jit(solution)/shard_map/combine/pallas_call | solution.py:306
  (1 shorter events, 0.0 us)
Async XLA Ops:
  0.7 1.2 %copy-start = (bf16[128,4096]{1,0:T(8,128)(2,1)S(1)}, bf16[128,4096]{1,0:T(8,128)(2,1)}, u32[]{:S(2)}) copy-start(bf16[128,4096]{1,0:T(8,128)(2,1)} %rows_ref.1) | copy-start | bytes 3145732
  1.9 1.2 %copy-start.1 = (bf16[128,4096]{1,0:T(8,128)(2,1)S(1)}, bf16[128,4096]{1,0:T(8,128)(2,1)}, u32[]{:S(2)}) copy-start(bf16[128,4096]{1,0:T(8,128)(2,1)} %grads_ref.1) | copy-start | bytes 3145732
  3.2 0.7 copy-start.2
  3.9 0.7 copy-start.4
  6.4 14.3 %collective-permute-start = (bf16[32,4096]{1,0:T(8,128)(2,1)S(1)}, bf16[32,4096]{1,0:T(8,128)(2,1)S(1)}, u32[]{:S(2)}, u32[]{:S(2)}) collective-permute-start(bf16[32,4096]{1,0:T(8,128)(2,1)S(1)} %get-tuple-element.29), channel_id=1, source_target_pairs={{0,4},{2,6},{4,0},{6,2},{8,12},{10,14},{12,8},{14,10},{1,5},{3,7},... | collective-permute-start | bytes 786440 | tf_op jit(solution)/shard_map/ppermute | solution.py:332
  9.5 12.9 %collective-permute-start.1 = (bf16[16,4096]{1,0:T(8,128)(2,1)S(1)}, bf16[16,4096]{1,0:T(8,128)(2,1)S(1)}, u32[]{:S(2)}, u32[]{:S(2)}) collective-permute-start(bf16[16,4096]{1,0:T(8,128)(2,1)S(1)} %get-tuple-element.30), channel_id=1, source_target_pairs={{0,8},{2,10},{4,12},{6,14},{8,0},{10,2},{12,4},{14,6},{1,9},{3,11}... | collective-permute-start | bytes 393224 | tf_op jit(solution)/shard_map/ppermute | solution.py:332
  12.1 18.6 %collective-permute-start.7 = (bf16[16,4096]{1,0:T(8,128)(2,1)S(1)}, bf16[16,4096]{1,0:T(8,128)(2,1)S(1)}, u32[]{:S(2)}, u32[]{:S(2)}) collective-permute-start(bf16[16,4096]{1,0:T(8,128)(2,1)S(1)} %get-tuple-element.32), channel_id=1, source_target_pairs={{0,8},{2,10},{4,12},{6,14},{8,0},{10,2},{12,4},{14,6},{1,9},{3,11}... | collective-permute-start | bytes 393224 | tf_op jit(solution)/shard_map/ppermute | solution.py:332
  12.4 19.8 %collective-permute-start.8 = (bf16[16,4096]{1,0:T(8,128)(2,1)S(1)}, bf16[16,4096]{1,0:T(8,128)(2,1)S(1)}, u32[]{:S(2)}, u32[]{:S(2)}) collective-permute-start(bf16[16,4096]{1,0:T(8,128)(2,1)S(1)} %get-tuple-element.33), channel_id=1, source_target_pairs={{0,12},{2,14},{4,8},{6,10},{8,4},{10,6},{12,0},{14,2},{1,13},{3,15... | collective-permute-start | bytes 393224 | tf_op jit(solution)/shard_map/ppermute | solution.py:332
  14.9 30.4 %collective-permute-start.3 = (bf16[32,4096]{1,0:T(8,128)(2,1)S(1)}, bf16[32,4096]{1,0:T(8,128)(2,1)S(1)}, u32[]{:S(2)}, u32[]{:S(2)}) collective-permute-start(bf16[32,4096]{1,0:T(8,128)(2,1)S(1)} %get-tuple-element.28.refs_0_), channel_id=1, source_target_pairs={{0,2},{2,0},{4,6},{6,4},{8,10},{10,8},{12,14},{14,12},{1,3},{3,1},... | collective-permute-start | bytes 786440 | tf_op jit(solution)/shard_map/ppermute | solution.py:339
  20.7 24.5 %collective-permute-start.4 = (bf16[32,4096]{1,0:T(8,128)(2,1)S(1)}, bf16[32,4096]{1,0:T(8,128)(2,1)S(1)}, u32[]{:S(2)}, u32[]{:S(2)}) collective-permute-start(bf16[32,4096]{1,0:T(8,128)(2,1)S(1)} %collective-permute-done.refs_1_), channel_id=1, source_target_pairs={{0,2},{2,0},{4,6},{6,4},{8,10},{10,8},{12,14},{14,12},{1,3},{3,1},... | collective-permute-start | bytes 786440 | tf_op jit(solution)/shard_map/ppermute | solution.py:339
  22.4 20.7 %collective-permute-start.2 = (bf16[16,4096]{1,0:T(8,128)(2,1)S(1)}, bf16[16,4096]{1,0:T(8,128)(2,1)S(1)}, u32[]{:S(2)}, u32[]{:S(2)}) collective-permute-start(bf16[16,4096]{1,0:T(8,128)(2,1)S(1)} %get-tuple-element.31), channel_id=1, source_target_pairs={{0,12},{2,14},{4,8},{6,10},{8,4},{10,6},{12,0},{14,2},{1,13},{3,15... | collective-permute-start | bytes 393224 | tf_op jit(solution)/shard_map/ppermute | solution.py:332
  30.6 14.1 %collective-permute-start.9 = (bf16[16,4096]{1,0:T(8,128)(2,1)S(1)}, bf16[16,4096]{1,0:T(8,128)(2,1)S(1)}, u32[]{:S(2)}, u32[]{:S(2)}) collective-permute-start(bf16[16,4096]{1,0:T(8,128)(2,1)S(1)} %collective-permute-done.7.refs_2_), channel_id=1, source_target_pairs={{0,2},{2,0},{4,6},{6,4},{8,10},{10,8},{12,14},{14,12},{1,3},{3,1},... | collective-permute-start | bytes 393224 | tf_op jit(solution)/shard_map/ppermute | solution.py:339
  32.1 13.1 %collective-permute-start.10 = (bf16[16,4096]{1,0:T(8,128)(2,1)S(1)}, bf16[16,4096]{1,0:T(8,128)(2,1)S(1)}, u32[]{:S(2)}, u32[]{:S(2)}) collective-permute-start(bf16[16,4096]{1,0:T(8,128)(2,1)S(1)} %collective-permute-done.8.refs_3_), channel_id=1, source_target_pairs={{0,2},{2,0},{4,6},{6,4},{8,10},{10,8},{12,14},{14,12},{1,3},{3,1},... | collective-permute-start | bytes 393224 | tf_op jit(solution)/shard_map/ppermute | solution.py:339
  43.1 5.0 %collective-permute-start.5 = (bf16[16,4096]{1,0:T(8,128)(2,1)S(1)}, bf16[16,4096]{1,0:T(8,128)(2,1)S(1)}, u32[]{:S(2)}, u32[]{:S(2)}) collective-permute-start(bf16[16,4096]{1,0:T(8,128)(2,1)S(1)} %collective-permute-done.1.refs_2_), channel_id=1, source_target_pairs={{0,2},{2,0},{4,6},{6,4},{8,10},{10,8},{12,14},{14,12},{1,3},{3,1},... | collective-permute-start | bytes 393224 | tf_op jit(solution)/shard_map/ppermute | solution.py:339
  44.7 5.0 %collective-permute-start.6 = (bf16[16,4096]{1,0:T(8,128)(2,1)S(1)}, bf16[16,4096]{1,0:T(8,128)(2,1)S(1)}, u32[]{:S(2)}, u32[]{:S(2)}) collective-permute-start(bf16[16,4096]{1,0:T(8,128)(2,1)S(1)} %collective-permute-done.2.refs_3_), channel_id=1, source_target_pairs={{0,2},{2,0},{4,6},{6,4},{8,10},{10,8},{12,14},{14,12},{1,3},{3,1},... | collective-permute-start | bytes 393224 | tf_op jit(solution)/shard_map/ppermute | solution.py:339
  55.3 25.7 %copy-start.3 = (s32[128,2]{0,1:T(2,128)S(1)}, s32[128,2]{0,1:T(2,128)}, u32[]{:S(2)}) copy-start(s32[128,2]{0,1:T(2,128)} %param.11) | copy-start | bytes 3076
  55.4 25.7 %copy-start.5 = (s32[128]{0:T(128)S(1)}, s32[128]{0:T(128)}, u32[]{:S(2)}) copy-start(s32[128]{0:T(128)} %param.10) | copy-start | bytes 1540
  55.4 25.7 %copy-start.6 = (f32[128,2]{0,1:T(2,128)S(1)}, f32[128,2]{0,1:T(2,128)}, u32[]{:S(2)}) copy-start(f32[128,2]{0,1:T(2,128)} %param.12) | copy-start | bytes 3076
  58.3 6.6 %collective-permute-start.11 = (bf16[64,2176]{1,0:T(8,128)(2,1)S(1)}, bf16[64,2176]{1,0:T(8,128)(2,1)S(1)}, u32[]{:S(2)}, u32[]{:S(2)}) collective-permute-start(bf16[64,2176]{1,0:T(8,128)(2,1)S(1)} %get-tuple-element.41), channel_id=1, source_target_pairs={{0,2},{2,0},{4,6},{6,4},{8,10},{10,8},{12,14},{14,12},{1,3},{3,1},... | collective-permute-start | bytes 835592 | tf_op jit(solution)/shard_map/ppermute | solution.py:339
  59.8 11.7 %collective-permute-start.15 = (bf16[64,2176]{1,0:T(8,128)(2,1)S(1)}, bf16[64,2176]{1,0:T(8,128)(2,1)S(1)}, u32[]{:S(2)}, u32[]{:S(2)}) collective-permute-start(bf16[64,2176]{1,0:T(8,128)(2,1)S(1)} %get-tuple-element.47), channel_id=1, source_target_pairs={{0,2},{2,0},{4,6},{6,4},{8,10},{10,8},{12,14},{14,12},{1,3},{3,1},... | collective-permute-start | bytes 835592 | tf_op jit(solution)/shard_map/ppermute | solution.py:339
  65.0 7.8 %collective-permute-start.12 = (bf16[16,2176]{1,0:T(8,128)(2,1)S(1)}, bf16[16,2176]{1,0:T(8,128)(2,1)S(1)}, u32[]{:S(2)}, u32[]{:S(2)}) collective-permute-start(bf16[16,2176]{1,0:T(8,128)(2,1)S(1)} %get-tuple-element.43), channel_id=1, source_target_pairs={{0,4},{1,5},{2,6},{3,7},{4,0},{5,1},{6,2},{7,3},{8,12},{9,13},{10,... | collective-permute-start | bytes 208904 | tf_op jit(solution)/shard_map/ppermute | solution.py:350
  69.1 5.8 %collective-permute-start.13 = (bf16[16,2176]{1,0:T(8,128)(2,1)S(1)}, bf16[16,2176]{1,0:T(8,128)(2,1)S(1)}, u32[]{:S(2)}, u32[]{:S(2)}) collective-permute-start(bf16[16,2176]{1,0:T(8,128)(2,1)S(1)} %get-tuple-element.44), channel_id=1, source_target_pairs={{0,8},{1,9},{2,10},{3,11},{4,12},{5,13},{6,14},{7,15},{8,0},{9,1},... | collective-permute-start | bytes 208904 | tf_op jit(solution)/shard_map/ppermute | solution.py:350
  69.6 6.3 %collective-permute-start.14 = (bf16[16,2176]{1,0:T(8,128)(2,1)S(1)}, bf16[16,2176]{1,0:T(8,128)(2,1)S(1)}, u32[]{:S(2)}, u32[]{:S(2)}) collective-permute-start(bf16[16,2176]{1,0:T(8,128)(2,1)S(1)} %get-tuple-element.45), channel_id=1, source_target_pairs={{0,12},{1,13},{2,14},{3,15},{4,8},{5,9},{6,10},{7,11},{8,4},{9,5},... | collective-permute-start | bytes 208904 | tf_op jit(solution)/shard_map/ppermute | solution.py:350
  71.6 4.3 %collective-permute-start.16 = (bf16[16,2176]{1,0:T(8,128)(2,1)S(1)}, bf16[16,2176]{1,0:T(8,128)(2,1)S(1)}, u32[]{:S(2)}, u32[]{:S(2)}) collective-permute-start(bf16[16,2176]{1,0:T(8,128)(2,1)S(1)} %get-tuple-element.48), channel_id=1, source_target_pairs={{0,1},{1,0},{2,3},{3,2},{4,5},{5,4},{6,7},{7,6},{8,9},{9,8},{10,11... | collective-permute-start | bytes 208904 | tf_op jit(solution)/shard_map/ppermute | solution.py:350
  71.7 5.0 %collective-permute-start.17 = (bf16[16,2176]{1,0:T(8,128)(2,1)S(1)}, bf16[16,2176]{1,0:T(8,128)(2,1)S(1)}, u32[]{:S(2)}, u32[]{:S(2)}) collective-permute-start(bf16[16,2176]{1,0:T(8,128)(2,1)S(1)} %get-tuple-element.49), channel_id=1, source_target_pairs={{0,5},{1,4},{2,7},{3,6},{4,1},{5,0},{6,3},{7,2},{8,13},{9,12},{10,... | collective-permute-start | bytes 208904 | tf_op jit(solution)/shard_map/ppermute | solution.py:350
  72.8 6.6 %collective-permute-start.18 = (bf16[16,2176]{1,0:T(8,128)(2,1)S(1)}, bf16[16,2176]{1,0:T(8,128)(2,1)S(1)}, u32[]{:S(2)}, u32[]{:S(2)}) collective-permute-start(bf16[16,2176]{1,0:T(8,128)(2,1)S(1)} %get-tuple-element.50), channel_id=1, source_target_pairs={{0,9},{1,8},{2,11},{3,10},{4,13},{5,12},{6,15},{7,14},{8,1},{9,0},... | collective-permute-start | bytes 208904 | tf_op jit(solution)/shard_map/ppermute | solution.py:350
  74.8 6.2 %collective-permute-start.19 = (bf16[16,2176]{1,0:T(8,128)(2,1)S(1)}, bf16[16,2176]{1,0:T(8,128)(2,1)S(1)}, u32[]{:S(2)}, u32[]{:S(2)}) collective-permute-start(bf16[16,2176]{1,0:T(8,128)(2,1)S(1)} %get-tuple-element.51), channel_id=1, source_target_pairs={{0,13},{1,12},{2,15},{3,14},{4,9},{5,8},{6,11},{7,10},{8,5},{9,4},... | collective-permute-start | bytes 208904 | tf_op jit(solution)/shard_map/ppermute | solution.py:350

commit v3 on v2

--- a/solution.py
+++ b/solution.py
@@ -88,10 +88,11 @@
         compiler_params=pltpu.CompilerParams(vmem_limit_bytes=8 * MIB),
         cost_estimate=cost(4 * E_MOD * CAP * tok_rows * width, 6 * tok_rows * width),
         name="gather_slots",
-    )(ids, modality, picks, rows, grads)
-
-
-def load_kernel(parts, src, dst, sems):
+    )(ids, in_hbm(modality), in_hbm(picks), in_hbm(rows), in_hbm(grads))
+
+
+def load_kernel(parts, ties, src, *refs):
+    dst, sems = refs[ties], refs[-1]
     rows = src.shape[1] // parts
     copies = [
         pltpu.make_async_copy(
@@ -105,18 +106,56 @@
         copy.wait()
 
 
-def load(weight):
+def load(weight, after, through=()):
     parts = 8
-    return pl.pallas_call(
-        functools.partial(load_kernel, parts),
-        in_specs=[pl.BlockSpec(memory_space=pl.ANY)],
-        out_specs=pl.BlockSpec(memory_space=pltpu.VMEM),
-        out_shape=pltpu.VMEM(weight.shape, weight.dtype),
+    place = pl.BlockSpec(memory_space=pl.ANY)
+    ties = len(after) + len(through)
+    return pl.pallas_call(
+        functools.partial(load_kernel, parts, ties),
+        in_specs=[place] * (1 + ties),
+        out_specs=[pl.BlockSpec(memory_space=pltpu.VMEM)] + [place] * len(through),
+        out_shape=[pltpu.VMEM(weight.shape, weight.dtype)]
+        + [jax.ShapeDtypeStruct(tie.shape, tie.dtype) for tie in through],
+        input_output_aliases={1 + len(after) + i: 1 + i for i in range(len(through))},
         scratch_shapes=[pltpu.SemaphoreType.DMA((parts,))],
         compiler_params=pltpu.CompilerParams(vmem_limit_bytes=MIB),
-        cost_estimate=cost(0, 2 * weight.size * weight.dtype.itemsize),
+        cost_estimate=cost(0, 1024),
         name="load",
-    )(pltpu.with_memory_space_constraint(weight, pltpu.HBM))
+    )(in_hbm(weight), *after, *through)
+
+
+def join_kernel(count, *refs):
+    blocks, out = refs[:count], refs[-1]
+    start = 0
+    for block in blocks:
+        out[start : start + block.shape[0], :] = block[...]
+        start += block.shape[0]
+
+
+def join_and_pass_kernel(count, through, *refs):
+    join_kernel(count, *refs[:count], refs[count + through])
+
+
+def join(blocks, through=()):
+    count = len(blocks)
+    total = sum(block.shape[0] for block in blocks)
+    vmem = pl.BlockSpec(memory_space=pltpu.VMEM)
+    ties = [pl.BlockSpec(memory_space=pl.ANY)] * len(through)
+    return pl.pallas_call(
+        functools.partial(join_and_pass_kernel, count, len(through)),
+        in_specs=[vmem] * count + ties,
+        out_specs=[vmem] + ties,
+        out_shape=[jax.ShapeDtypeStruct((total, blocks[0].shape[1]), BF16)]
+        + [jax.ShapeDtypeStruct(tie.shape, tie.dtype) for tie in through],
+        input_output_aliases={count + i: 1 + i for i in range(len(through))},
+        compiler_params=pltpu.CompilerParams(vmem_limit_bytes=8 * MIB),
+        cost_estimate=cost(0, 1024),
+        name="join",
+    )(*blocks, *through)
+
+
+def in_hbm(x):
+    return pltpu.with_memory_space_constraint(x, pltpu.HBM)
 
 
 def in_vmem(x):
@@ -156,7 +195,7 @@
         out_shape=[jax.ShapeDtypeStruct((total, hidden), F32)] * 3,
         scratch_shapes=[pltpu.VMEM((total, width), BF16)],
         compiler_params=pltpu.CompilerParams(vmem_limit_bytes=16 * MIB),
-        cost_estimate=cost(4 * total * width * hidden, 4 * total * hidden),
+        cost_estimate=cost(1024, 1024),
         name="pre_activations",
     )(*blocks, in_vmem(gate_piece), in_vmem(up_piece))
 
@@ -210,7 +249,7 @@
         + [jax.ShapeDtypeStruct((total, EXT), BF16)],
         scratch_shapes=[pltpu.VMEM((total, width), BF16)],
         compiler_params=pltpu.CompilerParams(vmem_limit_bytes=16 * MIB),
-        cost_estimate=cost(4 * total * width * hidden, 4 * total * hidden),
+        cost_estimate=cost(4 * total * width * hidden, 4 * width * hidden),
         name="hidden_grads",
     )(half, *blocks, *factors, in_vmem(down_piece), in_vmem(gate_piece), in_vmem(up_piece))
     return out[:groups], out[groups:]
@@ -232,7 +271,7 @@
         out_specs=[vmem] * groups,
         out_shape=[jax.ShapeDtypeStruct(shape, BF16)] * groups,
         compiler_params=pltpu.CompilerParams(vmem_limit_bytes=16 * MIB),
-        cost_estimate=cost(2 * total * width * hidden, 4 * total * hidden),
+        cost_estimate=cost(2 * total * width * hidden, 2 * width * hidden),
         name="back_half",
     )(half, dgate, dup, part, in_vmem(gate_piece), in_vmem(up_piece))
 
@@ -328,23 +367,19 @@
     picks = picks.T
     weights = gate_weights.T
 
-    def to_expert(x, s):
-        return lax.ppermute(
-            x,
-            "ep",
-            [(e * groups + j, (e ^ s) * groups + j) for e in range(E_MOD) for j in range(groups)],
-        )
-
-    def to_piece(x, t):
+    def to_expert(x, s, t=0):
         return lax.ppermute(
             x,
             "ep",
             [
-                (e * groups + j, e * groups + (j + t) % groups)
+                (e * groups + j, (e ^ s) * groups + (j + t) % groups)
                 for e in range(E_MOD)
                 for j in range(groups)
             ],
         )
+
+    def to_piece(x, t):
+        return to_expert(x, 0, t)
 
     def to_source(x, s, flip):
         return lax.ppermute(
@@ -359,20 +394,28 @@
         )
 
     sent = gather_slots(ids, modality, picks, tokens, cotangent)
-    gate_piece, up_piece, down_piece = load(gate_proj), load(up_proj), load(down_proj)
-    near = [sent[0], to_expert(sent[1], 1)]
-    far = [[to_expert(sent[2 * s - 2 + a], s) for s in range(2, E_MOD)] for a in range(2)]
-    near_pieces = [[to_piece(x, t) for x in near] for t in range(1, groups)]
-    blocks, places = [], []
-    for a in range(2):
-        far_pieces = [[to_piece(x, t) for x in far[a]] for t in range(1, groups)]
-        use, where = [], []
-        for two, others in zip([near] + near_pieces, [far[a]] + far_pieces):
-            where += [(len(use), a * CAP), (len(use) + 1, a * CAP)]
-            where += [(len(use) + 2 + i, 0) for i in range(len(others))]
-            use += two + others
-        blocks.append(use)
-        places.append(tuple(where))
+    far = [[to_expert(sent[2 * s - 2], s) for s in range(2, E_MOD)]]
+    near = to_expert(sent[1], 1)
+    gate_piece, own = load(gate_proj, [], sent[:1])
+    (near,) = join([own, near])
+    near = [near] + [to_piece(near, t) for t in range(1, groups)]
+    far[0], *later = join(far[0], [sent[2 * s - 1] for s in range(2, E_MOD)])
+    far.append([to_expert(x, s) for x, s in zip(later, range(2, E_MOD))])
+    up_piece, far[0] = load(up_proj, [], [far[0]])
+    far[0] = [far[0]] + [to_piece(far[0], t) for t in range(1, groups)]
+    (far[1],) = join(far[1])
+    (down_piece,) = load(down_proj, [far[1]])
+    far[1] = [far[1]] + [to_piece(far[1], t) for t in range(1, groups)]
+    blocks = [near + far[a] for a in range(2)]
+    places = [
+        tuple(
+            place
+            for t in range(groups)
+            for place in [(t, a * CAP), (t, (2 + a) * CAP)]
+            + [(groups + t, i * CAP) for i in range(E_MOD - 2)]
+        )
+        for a in range(2)
+    ]
     factors = pre_activations(blocks[0], places[0], gate_piece, up_piece)
     halves = [(core ^ flip).astype(jnp.int32).reshape(1) for flip in range(2)]
     first, (dgate, dup, part) = hidden_grads(

time: 83.2 us -> 80.7 us (0.970)
  local copies, waits for them, and re-layouts: 3.8 us -> 10.1 us
  waiting for transfers between devices: 21.8 us -> 16.6 us
  starting transfers between devices: 30.8 us -> 25.7 us
  Pallas kernels: 25.7 us -> 27.1 us
    unnamed x14, local copies, waits for them, and re-layouts: 3.8 us -> 10.1 us
    ppermute x13 -> x10, starting transfers between devices: 20.8 us -> 15.1 us  [to_expert(): lax.ppermute(x, 'ep', [(e * groups + j, (e ^ s) * groups + (j + t) % grou...]
    ppermute x13 -> x10, waiting for transfers between devices: 15.9 us -> 10.9 us  [to_expert(): lax.ppermute(x, 'ep', [(e * groups + j, (e ^ s) * groups + (j + t) % grou...]
    pallas_call x1, Pallas kernels: 1.86 us -> 3.09 us  [gather_slots(): pl.pallas_call(gather_kernel, grid=(width // chunk,), in_specs=[pl.BlockS...]
    pallas_call x3 -> x6, Pallas kernels: 10.4 us -> 10.6 us  [the longest x3 10.6 us: load(): pl.pallas_call(functools.partial(load_kernel, parts, ties), in_specs=[pla...]
  transfers between devices with their start and end apart: 20 -> 17, of which waited for: 9 -> 7; matrix products, arithmetic and copies ran while one was open for 0% -> 0% of each run, Pallas kernels for 16% -> 17%
where the time goes in v3:
time: 80.7 us; the launch traced here: 80.5 us
  Pallas kernels  27.1 us (34%)
  starting transfers between devices  25.7 us (32%)
  waiting for transfers between devices  16.6 us (21%)
  local copies, waits for them, and re-layouts  10.1 us (13%)
    ppermute x10, starting transfers between devices, to_expert(): lax.ppermute(x, 'ep', [(e * groups + j, (e ^ s) * groups + (j + t) % grou...  15.1 us
    ppermute x10, waiting for transfers between devices, to_expert(): lax.ppermute(x, 'ep', [(e * groups + j, (e ^ s) * groups + (j + t) % grou...  10.9 us
    ppermute x7, starting transfers between devices, to_source(): lax.ppermute(x, ('ep', 'mod'), [((e * groups + j) * 2 + m, ((e ^ s) * gro...  10.7 us
    pallas_call x3, Pallas kernels, load(): pl.pallas_call(functools.partial(load_kernel, parts, ties), in_specs=[pla...  10.6 us
    unnamed x14, local copies, waits for them, and re-layouts  10.1 us
    pallas_call x1, Pallas kernels, hidden_grads(): pl.pallas_call(functools.partial(hidden_kernel, count, places, groups), i...  5.69 us
    ppermute x7, waiting for transfers between devices, to_source(): lax.ppermute(x, ('ep', 'mod'), [((e * groups + j) * 2 + m, ((e ^ s) * gro...  5.69 us
    pallas_call x1, Pallas kernels, gather_slots(): pl.pallas_call(gather_kernel, grid=(width // chunk,), in_specs=[pl.BlockS...  3.09 us
  transfers between devices with their start and end apart: 17, of which 7 were waited for; matrix products, arithmetic and copies ran while one was open for 0% of the time, Pallas kernels for 17%

profile of v3, /device:TPU:0, one launch (start us, length us, event | category | flops | bytes accessed | tf_op | source)
XLA Modules:
  0.0 80.5 jit_solution(12407169707643140541)
XLA Ops:
  0.6 0.1 pad_add_fusion.ids_ref
  0.7 3.1 %gather_slots.1 = (bf16[32,4096]{1,0:T(8,128)(2,1)S(1)}, bf16[32,4096]{1,0:T(8,128)(2,1)S(1)}, bf16[16,4096]{1,0:T(8,128)(2,1)S(1)}, bf16[16,4096]{1,0:T(8,128)(...) custom-call(s32[2]{0:T(128)S(1)} %pad_add_fusion.ids_ref, s32[1,128]{1,0:T(1,128)} %bitcast.9, ...), custom_call_target="tpu_custom_call" | custom-call | flops 134217728 | bytes 3145728 | tf_op jit(solution)/shard_map/gather_slots/pallas_call | solution.py:75
  3.8 3.1 %collective-permute-start = (bf16[32,4096]{1,0:T(8,128)(2,1)S(1)}, bf16[32,4096]{1,0:T(8,128)(2,1)S(1)}, u32[]{:S(2)}, u32[]{:S(2)}) collective-permute-start(bf16[32,4096]{1,0:T(8,128)(2,1)S(1)} %get-tuple-element.37), channel_id=1, source_target_pairs={{0,4},{2,6},{4,0},{6,2},{8,12},{10,14},{12,8},{14,10},{1,5},{3,7},... | collective-permute-start | bytes 786440 | tf_op jit(solution)/shard_map/ppermute | solution.py:371
  6.9 2.6 %collective-permute-start.2 = (bf16[16,4096]{1,0:T(8,128)(2,1)S(1)}, bf16[16,4096]{1,0:T(8,128)(2,1)S(1)}, u32[]{:S(2)}, u32[]{:S(2)}) collective-permute-start(bf16[16,4096]{1,0:T(8,128)(2,1)S(1)} %get-tuple-element.38), channel_id=1, source_target_pairs={{0,8},{2,10},{4,12},{6,14},{8,0},{10,2},{12,4},{14,6},{1,9},{3,11}... | collective-permute-start | bytes 393224 | tf_op jit(solution)/shard_map/ppermute | solution.py:371
  9.5 0.0 collective-permute-start.3
  9.5 3.5 %load.3 = (bf16[1,4096,1024]{2,1,0:T(8,128)(2,1)S(1)}, bf16[32,4096]{1,0:T(8,128)(2,1)S(1)}) custom-call(bf16[1,4096,1024]{2,1,0:T(8,128)(2,1)} %src.3, bf16[32,4096]{1,0:T(8,128)(2,1)S(1)} %get-tuple-element.35.refs_0_), custom_call_target="tpu_custom_call", output_to_operand_aliasing={{1}: (1, {})} | custom-call | bytes 1024 | tf_op jit(solution)/shard_map/load/pallas_call | solution.py:113
  13.0 0.0 copy-start
  13.0 3.3 %copy-done = bf16[1,4096,1024]{2,1,0:T(8,128)(2,1)} copy-done((bf16[1,4096,1024]{2,1,0:T(8,128)(2,1)}, bf16[1,4096,1024]{2,1,0:T(8,128)(2,1)S(1)}, u32[]{:S(2)}) %copy-start) | copy-done | bytes 8388632
  16.3 0.0 collective-permute-done.refs_1_
  16.3 1.8 %collective-permute-start.1 = (bf16[64,4096]{1,0:T(8,128)(2,1)S(1)}, bf16[64,4096]{1,0:T(8,128)(2,1)S(1)}, u32[]{:S(2)}, u32[]{:S(2)}) collective-permute-start(bf16[64,4096]{1,0:T(8,128)(2,1)S(1)} %join.3.refs_0_), channel_id=1, source_target_pairs={{0,2},{2,0},{4,6},{6,4},{8,10},{10,8},{12,14},{14,12},{1,3},{3,1},... | collective-permute-start | bytes 1572872 | tf_op jit(solution)/shard_map/ppermute | solution.py:371
  18.1 0.0 collective-permute-done.2.refs_0_
  18.1 3.0 %collective-permute-done.3.refs_1_ = bf16[16,4096]{1,0:T(8,128)(2,1)S(1)} collective-permute-done((bf16[16,4096]{1,0:T(8,128)(2,1)S(1)}, bf16[16,4096]{1,0:T(8,128)(2,1)S(1)}, u32[]{:S(2)}, u32[]{:S(2)}) %collective-permute-start.3) | collective-permute-done | bytes 131104 | tf_op jit(solution)/shard_map/ppermute | solution.py:371
  21.2 1.7 %collective-permute-start.4 = (bf16[16,4096]{1,0:T(8,128)(2,1)S(1)}, bf16[16,4096]{1,0:T(8,128)(2,1)S(1)}, u32[]{:S(2)}, u32[]{:S(2)}) collective-permute-start(bf16[16,4096]{1,0:T(8,128)(2,1)S(1)} %get-tuple-element.42), channel_id=1, source_target_pairs={{0,8},{2,10},{4,12},{6,14},{8,0},{10,2},{12,4},{14,6},{1,9},{3,11}... | collective-permute-start | bytes 393224 | tf_op jit(solution)/shard_map/ppermute | solution.py:371
  22.9 1.5 %collective-permute-start.5 = (bf16[16,4096]{1,0:T(8,128)(2,1)S(1)}, bf16[16,4096]{1,0:T(8,128)(2,1)S(1)}, u32[]{:S(2)}, u32[]{:S(2)}) collective-permute-start(bf16[16,4096]{1,0:T(8,128)(2,1)S(1)} %get-tuple-element.43), channel_id=1, source_target_pairs={{0,12},{2,14},{4,8},{6,10},{8,4},{10,6},{12,0},{14,2},{1,13},{3,15... | collective-permute-start | bytes 393224 | tf_op jit(solution)/shard_map/ppermute | solution.py:371
  24.4 3.5 %load.4 = (bf16[1,4096,1024]{2,1,0:T(8,128)(2,1)S(1)}, bf16[32,4096]{1,0:T(8,128)(2,1)S(1)}) custom-call(bf16[1,4096,1024]{2,1,0:T(8,128)(2,1)} %src.4, bf16[32,4096]{1,0:T(8,128)(2,1)S(1)} %get-tuple-element.44.refs_0_), custom_call_target="tpu_custom_call", output_to_operand_aliasing={{1}: (1, {})} | custom-call | bytes 1024 | tf_op jit(solution)/shard_map/load/pallas_call | solution.py:113
  27.9 0.0 copy-start.2
  27.9 3.2 %copy-done.2 = bf16[1,4096,1024]{2,1,0:T(8,128)(2,1)} copy-done((bf16[1,4096,1024]{2,1,0:T(8,128)(2,1)}, bf16[1,4096,1024]{2,1,0:T(8,128)(2,1)S(1)}, u32[]{:S(2)}) %copy-start.2) | copy-done | bytes 8388632
  31.1 1.4 %collective-permute-start.7 = (bf16[32,4096]{1,0:T(8,128)(2,1)S(1)}, bf16[32,4096]{1,0:T(8,128)(2,1)S(1)}, u32[]{:S(2)}, u32[]{:S(2)}) collective-permute-start(bf16[32,4096]{1,0:T(8,128)(2,1)S(1)} %get-tuple-element.45.refs_2_), channel_id=1, source_target_pairs={{0,2},{2,0},{4,6},{6,4},{8,10},{10,8},{12,14},{14,12},{1,3},{3,1},... | collective-permute-start | bytes 786440 | tf_op jit(solution)/shard_map/ppermute | solution.py:371
  32.5 0.0 collective-permute-done.4.refs_0_
  32.5 0.0 collective-permute-done.5.refs_1_
  32.5 0.9 %collective-permute-start.6 = (bf16[32,4096]{1,0:T(8,128)(2,1)S(1)}, bf16[32,4096]{1,0:T(8,128)(2,1)S(1)}, u32[]{:S(2)}, u32[]{:S(2)}) collective-permute-start(bf16[32,4096]{1,0:T(8,128)(2,1)S(1)} %join.5.refs_0_.refs_2_), channel_id=1, source_target_pairs={{0,2},{2,0},{4,6},{6,4},{8,10},{10,8},{12,14},{14,12},{1,3},{3,1},... | collective-permute-start | bytes 786440 | tf_op jit(solution)/shard_map/ppermute | solution.py:371
  33.4 0.0 copy-start.3
  33.4 3.6 %load.5.refs_7_ = bf16[1,1024,4096]{2,1,0:T(8,128)(2,1)S(1)} custom-call(bf16[1,1024,4096]{2,1,0:T(8,128)(2,1)} %src.5, bf16[32,4096]{1,0:T(8,128)(2,1)S(1)} %join.5.refs_0_.refs_2_), custom_call_target="tpu_custom_call" | custom-call | bytes 1024 | tf_op jit(solution)/shard_map/load/pallas_call | solution.py:113
  37.0 2.0 %collective-permute-done.7.refs_3_ = bf16[32,4096]{1,0:T(8,128)(2,1)S(1)} collective-permute-done((bf16[32,4096]{1,0:T(8,128)(2,1)S(1)}, bf16[32,4096]{1,0:T(8,128)(2,1)S(1)}, u32[]{:S(2)}, u32[]{:S(2)}) %collective-permute-start.7) | collective-permute-done | bytes 262176 | tf_op jit(solution)/shard_map/ppermute | solution.py:371
  39.0 0.0 collective-permute-done.1.refs_1_
  39.0 0.2 copy-done.3
  39.2 0.0 copy-start.1
  39.2 3.4 %copy-done.1 = bf16[1,4096,1024]{2,1,0:T(8,128)(2,1)S(1)} copy-done((bf16[1,4096,1024]{2,1,0:T(8,128)(2,1)S(1)}, bf16[1,4096,1024]{2,1,0:T(8,128)(2,1)}, u32[]{:S(2)}) %copy-start.1) | copy-done | bytes 8388632
  42.6 2.6 %pre_activations.1 = (f32[128,1024]{1,0:T(8,128)S(1)}, f32[128,1024]{1,0:T(8,128)S(1)}, f32[128,1024]{1,0:T(8,128)S(1)}) custom-call(bf16[64,4096]{1,0:T(8,128)(2,1)S(1)} %join.3.refs_0_, bf16[64,4096]{1,0:T(8,128)(2,1)S(1)} %collective-permute-done.1.refs_1_, bf16[32,4096]{1,0:T(8,128)(2,1)S(1)} %get-tuple-element.45.refs_2_, ...), custom_call_target="tpu_custom_call" | custom-call | flops 1024 | bytes 1024 | tf_op jit(solution)/shard_map/pre_activations/pallas_call | solution.py:191
  45.3 0.0 collective-permute-done.6.refs_3_
  45.3 5.7 %hidden_grads.1 = (bf16[64,2176]{1,0:T(8,128)(2,1)S(1)}, bf16[64,2176]{1,0:T(8,128)(2,1)S(1)}, bf16[128,1024]{1,0:T(8,128)(2,1)S(1)}, bf16[128,1024]{1,0:T(8,128)(2,1)S(1)}, bf16[128,128]{1,0:T(8,128)(2,1)S(1)}) custom-call(s32[1]{0:T(128)} %bitcast.5.half_ref, bf16[64,4096]{1,0:T(8,128)(2,1)S(1)} %join.3.refs_0_, ...), custom_call_target="tpu_custom_call" | custom-call | flops 2147483648 | bytes 16777216 | tf_op jit(solution)/shard_map/hidden_grads/pallas_call | solution.py:243
  51.0 0.0 copy-start.4
  51.0 0.0 copy-start.5
  51.0 0.0 copy-start.6
  51.0 2.9 %back_half.1 = (bf16[64,2176]{1,0:T(8,128)(2,1)S(1)}, bf16[64,2176]{1,0:T(8,128)(2,1)S(1)}) custom-call(s32[1]{0:T(128)} %bitcast.1.half_ref, bf16[128,1024]{1,0:T(8,128)(2,1)S(1)} %get-tuple-element.51.dgate_ref, bf16[128,1024]{1,0:T(8,128)(2,1)S(1)} %get-tuple-element.52.dup_ref, bf16[128,128]{1,0:T(8,128)(2,1)S(1)} %get-tuple-element.53.part_ref, ...), custom_call_target="tpu_custom_call" | custom-call | flops 1073741824 | bytes 8388608 | tf_op jit(solution)/shard_map/back_half/pallas_call | solution.py:268
  53.9 1.3 %collective-permute-start.8 = (bf16[64,2176]{1,0:T(8,128)(2,1)S(1)}, bf16[64,2176]{1,0:T(8,128)(2,1)S(1)}, u32[]{:S(2)}, u32[]{:S(2)}) collective-permute-start(bf16[64,2176]{1,0:T(8,128)(2,1)S(1)} %get-tuple-element.55), channel_id=1, source_target_pairs={{0,2},{2,0},{4,6},{6,4},{8,10},{10,8},{12,14},{14,12},{1,3},{3,1},... | collective-permute-start | bytes 835592 | tf_op jit(solution)/shard_map/ppermute | solution.py:371
  55.3 0.7 collective-permute-start.12
  56.0 5.9 %collective-permute-done.8.refs_1_ = bf16[64,2176]{1,0:T(8,128)(2,1)S(1)} collective-permute-done((bf16[64,2176]{1,0:T(8,128)(2,1)S(1)}, bf16[64,2176]{1,0:T(8,128)(2,1)S(1)}, u32[]{:S(2)}, u32[]{:S(2)}) %collective-permute-start.8) | collective-permute-done | bytes 278560 | tf_op jit(solution)/shard_map/ppermute | solution.py:371
  61.9 0.1 sum_pieces.2
  62.0 4.1 %collective-permute-start.9 = (bf16[16,2176]{1,0:T(8,128)(2,1)S(1)}, bf16[16,2176]{1,0:T(8,128)(2,1)S(1)}, u32[]{:S(2)}, u32[]{:S(2)}) collective-permute-start(bf16[16,2176]{1,0:T(8,128)(2,1)S(1)} %get-tuple-element.57), channel_id=1, source_target_pairs={{0,4},{1,5},{2,6},{3,7},{4,0},{5,1},{6,2},{7,3},{8,12},{9,13},{10,... | collective-permute-start | bytes 208904 | tf_op jit(solution)/shard_map/ppermute | solution.py:385
  66.1 1.1 %collective-permute-start.10 = (bf16[16,2176]{1,0:T(8,128)(2,1)S(1)}, bf16[16,2176]{1,0:T(8,128)(2,1)S(1)}, u32[]{:S(2)}, u32[]{:S(2)}) collective-permute-start(bf16[16,2176]{1,0:T(8,128)(2,1)S(1)} %get-tuple-element.58), channel_id=1, source_target_pairs={{0,8},{1,9},{2,10},{3,11},{4,12},{5,13},{6,14},{7,15},{8,0},{9,1},... | collective-permute-start | bytes 208904 | tf_op jit(solution)/shard_map/ppermute | solution.py:385
  67.1 1.4 %collective-permute-start.11 = (bf16[16,2176]{1,0:T(8,128)(2,1)S(1)}, bf16[16,2176]{1,0:T(8,128)(2,1)S(1)}, u32[]{:S(2)}, u32[]{:S(2)}) collective-permute-start(bf16[16,2176]{1,0:T(8,128)(2,1)S(1)} %get-tuple-element.59), channel_id=1, source_target_pairs={{0,12},{1,13},{2,14},{3,15},{4,8},{5,9},{6,10},{7,11},{8,4},{9,5},... | collective-permute-start | bytes 208904 | tf_op jit(solution)/shard_map/ppermute | solution.py:385
  68.5 0.0 collective-permute-done.12.refs_1_
  68.5 0.1 sum_pieces.3
  68.6 0.1 collective-permute-start.13
  68.7 1.2 %collective-permute-start.14 = (bf16[16,2176]{1,0:T(8,128)(2,1)S(1)}, bf16[16,2176]{1,0:T(8,128)(2,1)S(1)}, u32[]{:S(2)}, u32[]{:S(2)}) collective-permute-start(bf16[16,2176]{1,0:T(8,128)(2,1)S(1)} %get-tuple-element.63), channel_id=1, source_target_pairs={{0,5},{1,4},{2,7},{3,6},{4,1},{5,0},{6,3},{7,2},{8,13},{9,12},{10,... | collective-permute-start | bytes 208904 | tf_op jit(solution)/shard_map/ppermute | solution.py:385
  70.0 0.0 collective-permute-done.9.refs_1_
  70.0 1.9 %collective-permute-start.15 = (bf16[16,2176]{1,0:T(8,128)(2,1)S(1)}, bf16[16,2176]{1,0:T(8,128)(2,1)S(1)}, u32[]{:S(2)}, u32[]{:S(2)}) collective-permute-start(bf16[16,2176]{1,0:T(8,128)(2,1)S(1)} %get-tuple-element.64), channel_id=1, source_target_pairs={{0,9},{1,8},{2,11},{3,10},{4,13},{5,12},{6,15},{7,14},{8,1},{9,0},... | collective-permute-start | bytes 208904 | tf_op jit(solution)/shard_map/ppermute | solution.py:385
  71.8 0.2 collective-permute-done.10.refs_2_
  72.1 1.0 %collective-permute-start.16 = (bf16[16,2176]{1,0:T(8,128)(2,1)S(1)}, bf16[16,2176]{1,0:T(8,128)(2,1)S(1)}, u32[]{:S(2)}, u32[]{:S(2)}) collective-permute-start(bf16[16,2176]{1,0:T(8,128)(2,1)S(1)} %get-tuple-element.65), channel_id=1, source_target_pairs={{0,13},{1,12},{2,15},{3,14},{4,9},{5,8},{6,11},{7,10},{8,5},{9,4},... | collective-permute-start | bytes 208904 | tf_op jit(solution)/shard_map/ppermute | solution.py:385
  73.0 0.4 collective-permute-done.11.refs_3_
  73.4 0.0 collective-permute-done.13.refs_4_
  73.4 2.0 %collective-permute-done.14.refs_5_ = bf16[16,2176]{1,0:T(8,128)(2,1)S(1)} collective-permute-done((bf16[16,2176]{1,0:T(8,128)(2,1)S(1)}, bf16[16,2176]{1,0:T(8,128)(2,1)S(1)}, u32[]{:S(2)}, u32[]{:S(2)}) %collective-permute-start.14) | collective-permute-done | bytes 69664 | tf_op jit(solution)/shard_map/ppermute | solution.py:385
  75.4 0.0 collective-permute-done.15.refs_6_
  75.4 3.1 %collective-permute-done.16.refs_7_ = bf16[16,2176]{1,0:T(8,128)(2,1)S(1)} collective-permute-done((bf16[16,2176]{1,0:T(8,128)(2,1)S(1)}, bf16[16,2176]{1,0:T(8,128)(2,1)S(1)}, u32[]{:S(2)}, u32[]{:S(2)}) %collective-permute-start.16) | collective-permute-done | bytes 69664 | tf_op jit(solution)/shard_map/ppermute | solution.py:385
  78.5 0.0 copy-done.4
  78.5 0.0 copy-done.5
  78.5 0.0 copy-done.6
  78.5 2.0 %combine.1 = (bf16[128,2048]{1,0:T(8,128)(2,1)}, f32[1,128]{1,0:T(1,128)}) custom-call(s32[2]{0:T(128)S(1)} %pad_add_fusion.ids_ref, s32[1,128]{1,0:T(1,128)S(1)} %bitcast.10, s32[2,128]{1,0:T(2,128)S(1)} %bitcast.8, f32[2,128]{1,0:T(2,128)S(1)} %bitcast.11, bf16[16,2176]{1,0:T(8,128)(2,1)S(1)} %get-tuple-element.56.refs_0_, ...), custom_call_target="tpu_custom_call" | custom-call | flops 134217728 | bytes 1048576 | tf_op jit(solution)/shard_map/combine/pallas_call | solution.py:345
  (3 shorter events, 0.1 us)
Async XLA Ops:
  3.8 12.4 %collective-permute-start = (bf16[32,4096]{1,0:T(8,128)(2,1)S(1)}, bf16[32,4096]{1,0:T(8,128)(2,1)S(1)}, u32[]{:S(2)}, u32[]{:S(2)}) collective-permute-start(bf16[32,4096]{1,0:T(8,128)(2,1)S(1)} %get-tuple-element.37), channel_id=1, source_target_pairs={{0,4},{2,6},{4,0},{6,2},{8,12},{10,14},{12,8},{14,10},{1,5},{3,7},... | collective-permute-start | bytes 786440 | tf_op jit(solution)/shard_map/ppermute | solution.py:371
  6.9 11.2 %collective-permute-start.2 = (bf16[16,4096]{1,0:T(8,128)(2,1)S(1)}, bf16[16,4096]{1,0:T(8,128)(2,1)S(1)}, u32[]{:S(2)}, u32[]{:S(2)}) collective-permute-start(bf16[16,4096]{1,0:T(8,128)(2,1)S(1)} %get-tuple-element.38), channel_id=1, source_target_pairs={{0,8},{2,10},{4,12},{6,14},{8,0},{10,2},{12,4},{14,6},{1,9},{3,11}... | collective-permute-start | bytes 393224 | tf_op jit(solution)/shard_map/ppermute | solution.py:371
  9.5 11.6 %collective-permute-start.3 = (bf16[16,4096]{1,0:T(8,128)(2,1)S(1)}, bf16[16,4096]{1,0:T(8,128)(2,1)S(1)}, u32[]{:S(2)}, u32[]{:S(2)}) collective-permute-start(bf16[16,4096]{1,0:T(8,128)(2,1)S(1)} %get-tuple-element.39), channel_id=1, source_target_pairs={{0,12},{2,14},{4,8},{6,10},{8,4},{10,6},{12,0},{14,2},{1,13},{3,15... | collective-permute-start | bytes 393224 | tf_op jit(solution)/shard_map/ppermute | solution.py:371
  13.0 3.3 %copy-start = (bf16[1,4096,1024]{2,1,0:T(8,128)(2,1)}, bf16[1,4096,1024]{2,1,0:T(8,128)(2,1)S(1)}, u32[]{:S(2)}) copy-start(bf16[1,4096,1024]{2,1,0:T(8,128)(2,1)S(1)} %get-tuple-element.46.refs_4_.refs_8_.gate_ref) | copy-start | bytes 25165828
  16.3 22.7 %collective-permute-start.1 = (bf16[64,4096]{1,0:T(8,128)(2,1)S(1)}, bf16[64,4096]{1,0:T(8,128)(2,1)S(1)}, u32[]{:S(2)}, u32[]{:S(2)}) collective-permute-start(bf16[64,4096]{1,0:T(8,128)(2,1)S(1)} %join.3.refs_0_), channel_id=1, source_target_pairs={{0,2},{2,0},{4,6},{6,4},{8,10},{10,8},{12,14},{14,12},{1,3},{3,1},... | collective-permute-start | bytes 1572872 | tf_op jit(solution)/shard_map/ppermute | solution.py:371
  21.2 11.3 %collective-permute-start.4 = (bf16[16,4096]{1,0:T(8,128)(2,1)S(1)}, bf16[16,4096]{1,0:T(8,128)(2,1)S(1)}, u32[]{:S(2)}, u32[]{:S(2)}) collective-permute-start(bf16[16,4096]{1,0:T(8,128)(2,1)S(1)} %get-tuple-element.42), channel_id=1, source_target_pairs={{0,8},{2,10},{4,12},{6,14},{8,0},{10,2},{12,4},{14,6},{1,9},{3,11}... | collective-permute-start | bytes 393224 | tf_op jit(solution)/shard_map/ppermute | solution.py:371
  22.9 9.6 %collective-permute-start.5 = (bf16[16,4096]{1,0:T(8,128)(2,1)S(1)}, bf16[16,4096]{1,0:T(8,128)(2,1)S(1)}, u32[]{:S(2)}, u32[]{:S(2)}) collective-permute-start(bf16[16,4096]{1,0:T(8,128)(2,1)S(1)} %get-tuple-element.43), channel_id=1, source_target_pairs={{0,12},{2,14},{4,8},{6,10},{8,4},{10,6},{12,0},{14,2},{1,13},{3,15... | collective-permute-start | bytes 393224 | tf_op jit(solution)/shard_map/ppermute | solution.py:371
  27.9 3.2 %copy-start.2 = (bf16[1,4096,1024]{2,1,0:T(8,128)(2,1)}, bf16[1,4096,1024]{2,1,0:T(8,128)(2,1)S(1)}, u32[]{:S(2)}) copy-start(bf16[1,4096,1024]{2,1,0:T(8,128)(2,1)S(1)} %get-tuple-element.47.refs_5_.refs_9_.up_ref) | copy-start | bytes 25165828
  31.1 7.9 %collective-permute-start.7 = (bf16[32,4096]{1,0:T(8,128)(2,1)S(1)}, bf16[32,4096]{1,0:T(8,128)(2,1)S(1)}, u32[]{:S(2)}, u32[]{:S(2)}) collective-permute-start(bf16[32,4096]{1,0:T(8,128)(2,1)S(1)} %get-tuple-element.45.refs_2_), channel_id=1, source_target_pairs={{0,2},{2,0},{4,6},{6,4},{8,10},{10,8},{12,14},{14,12},{1,3},{3,1},... | collective-permute-start | bytes 786440 | tf_op jit(solution)/shard_map/ppermute | solution.py:371
  32.5 12.7 %collective-permute-start.6 = (bf16[32,4096]{1,0:T(8,128)(2,1)S(1)}, bf16[32,4096]{1,0:T(8,128)(2,1)S(1)}, u32[]{:S(2)}, u32[]{:S(2)}) collective-permute-start(bf16[32,4096]{1,0:T(8,128)(2,1)S(1)} %join.5.refs_0_.refs_2_), channel_id=1, source_target_pairs={{0,2},{2,0},{4,6},{6,4},{8,10},{10,8},{12,14},{14,12},{1,3},{3,1},... | collective-permute-start | bytes 786440 | tf_op jit(solution)/shard_map/ppermute | solution.py:371
  33.4 5.9 %copy-start.3 = (bf16[1,4096,1024]{2,1,0:T(8,128)(2,1)S(1)}, bf16[1,4096,1024]{2,1,0:T(8,128)(2,1)}, u32[]{:S(2)}) copy-start(bf16[1,4096,1024]{2,1,0:T(8,128)(2,1)} %copy-done.2) | copy-start | bytes 25165828
  39.2 3.4 %copy-start.1 = (bf16[1,4096,1024]{2,1,0:T(8,128)(2,1)S(1)}, bf16[1,4096,1024]{2,1,0:T(8,128)(2,1)}, u32[]{:S(2)}) copy-start(bf16[1,4096,1024]{2,1,0:T(8,128)(2,1)} %copy-done) | copy-start | bytes 25165828
  51.0 27.5 %copy-start.4 = (s32[128,2]{0,1:T(2,128)S(1)}, s32[128,2]{0,1:T(2,128)}, u32[]{:S(2)}) copy-start(s32[128,2]{0,1:T(2,128)} %param.11) | copy-start | bytes 3076
  51.0 27.5 %copy-start.5 = (s32[128]{0:T(128)S(1)}, s32[128]{0:T(128)}, u32[]{:S(2)}) copy-start(s32[128]{0:T(128)} %param.10) | copy-start | bytes 1540
  51.0 27.5 %copy-start.6 = (f32[128,2]{0,1:T(2,128)S(1)}, f32[128,2]{0,1:T(2,128)}, u32[]{:S(2)}) copy-start(f32[128,2]{0,1:T(2,128)} %param.12) | copy-start | bytes 3076
  53.9 8.0 %collective-permute-start.8 = (bf16[64,2176]{1,0:T(8,128)(2,1)S(1)}, bf16[64,2176]{1,0:T(8,128)(2,1)S(1)}, u32[]{:S(2)}, u32[]{:S(2)}) collective-permute-start(bf16[64,2176]{1,0:T(8,128)(2,1)S(1)} %get-tuple-element.55), channel_id=1, source_target_pairs={{0,2},{2,0},{4,6},{6,4},{8,10},{10,8},{12,14},{14,12},{1,3},{3,1},... | collective-permute-start | bytes 835592 | tf_op jit(solution)/shard_map/ppermute | solution.py:371
  55.3 13.3 %collective-permute-start.12 = (bf16[64,2176]{1,0:T(8,128)(2,1)S(1)}, bf16[64,2176]{1,0:T(8,128)(2,1)S(1)}, u32[]{:S(2)}, u32[]{:S(2)}) collective-permute-start(bf16[64,2176]{1,0:T(8,128)(2,1)S(1)} %get-tuple-element.61), channel_id=1, source_target_pairs={{0,2},{2,0},{4,6},{6,4},{8,10},{10,8},{12,14},{14,12},{1,3},{3,1},... | collective-permute-start | bytes 835592 | tf_op jit(solution)/shard_map/ppermute | solution.py:371
  62.0 7.9 %collective-permute-start.9 = (bf16[16,2176]{1,0:T(8,128)(2,1)S(1)}, bf16[16,2176]{1,0:T(8,128)(2,1)S(1)}, u32[]{:S(2)}, u32[]{:S(2)}) collective-permute-start(bf16[16,2176]{1,0:T(8,128)(2,1)S(1)} %get-tuple-element.57), channel_id=1, source_target_pairs={{0,4},{1,5},{2,6},{3,7},{4,0},{5,1},{6,2},{7,3},{8,12},{9,13},{10,... | collective-permute-start | bytes 208904 | tf_op jit(solution)/shard_map/ppermute | solution.py:385
  66.1 6.0 %collective-permute-start.10 = (bf16[16,2176]{1,0:T(8,128)(2,1)S(1)}, bf16[16,2176]{1,0:T(8,128)(2,1)S(1)}, u32[]{:S(2)}, u32[]{:S(2)}) collective-permute-start(bf16[16,2176]{1,0:T(8,128)(2,1)S(1)} %get-tuple-element.58), channel_id=1, source_target_pairs={{0,8},{1,9},{2,10},{3,11},{4,12},{5,13},{6,14},{7,15},{8,0},{9,1},... | collective-permute-start | bytes 208904 | tf_op jit(solution)/shard_map/ppermute | solution.py:385
  67.1 6.3 %collective-permute-start.11 = (bf16[16,2176]{1,0:T(8,128)(2,1)S(1)}, bf16[16,2176]{1,0:T(8,128)(2,1)S(1)}, u32[]{:S(2)}, u32[]{:S(2)}) collective-permute-start(bf16[16,2176]{1,0:T(8,128)(2,1)S(1)} %get-tuple-element.59), channel_id=1, source_target_pairs={{0,12},{1,13},{2,14},{3,15},{4,8},{5,9},{6,10},{7,11},{8,4},{9,5},... | collective-permute-start | bytes 208904 | tf_op jit(solution)/shard_map/ppermute | solution.py:385
  68.6 4.8 %collective-permute-start.13 = (bf16[16,2176]{1,0:T(8,128)(2,1)S(1)}, bf16[16,2176]{1,0:T(8,128)(2,1)S(1)}, u32[]{:S(2)}, u32[]{:S(2)}) collective-permute-start(bf16[16,2176]{1,0:T(8,128)(2,1)S(1)} %get-tuple-element.62), channel_id=1, source_target_pairs={{0,1},{1,0},{2,3},{3,2},{4,5},{5,4},{6,7},{7,6},{8,9},{9,8},{10,11... | collective-permute-start | bytes 208904 | tf_op jit(solution)/shard_map/ppermute | solution.py:385
  68.7 6.7 %collective-permute-start.14 = (bf16[16,2176]{1,0:T(8,128)(2,1)S(1)}, bf16[16,2176]{1,0:T(8,128)(2,1)S(1)}, u32[]{:S(2)}, u32[]{:S(2)}) collective-permute-start(bf16[16,2176]{1,0:T(8,128)(2,1)S(1)} %get-tuple-element.63), channel_id=1, source_target_pairs={{0,5},{1,4},{2,7},{3,6},{4,1},{5,0},{6,3},{7,2},{8,13},{9,12},{10,... | collective-permute-start | bytes 208904 | tf_op jit(solution)/shard_map/ppermute | solution.py:385
  70.0 5.4 %collective-permute-start.15 = (bf16[16,2176]{1,0:T(8,128)(2,1)S(1)}, bf16[16,2176]{1,0:T(8,128)(2,1)S(1)}, u32[]{:S(2)}, u32[]{:S(2)}) collective-permute-start(bf16[16,2176]{1,0:T(8,128)(2,1)S(1)} %get-tuple-element.64), channel_id=1, source_target_pairs={{0,9},{1,8},{2,11},{3,10},{4,13},{5,12},{6,15},{7,14},{8,1},{9,0},... | collective-permute-start | bytes 208904 | tf_op jit(solution)/shard_map/ppermute | solution.py:385
  72.1 6.4 %collective-permute-start.16 = (bf16[16,2176]{1,0:T(8,128)(2,1)S(1)}, bf16[16,2176]{1,0:T(8,128)(2,1)S(1)}, u32[]{:S(2)}, u32[]{:S(2)}) collective-permute-start(bf16[16,2176]{1,0:T(8,128)(2,1)S(1)} %get-tuple-element.65), channel_id=1, source_target_pairs={{0,13},{1,12},{2,15},{3,14},{4,9},{5,8},{6,11},{7,10},{8,5},{9,4},... | collective-permute-start | bytes 208904 | tf_op jit(solution)/shard_map/ppermute | solution.py:385

commit v4 on v3

--- a/solution.py
+++ b/solution.py
@@ -13,6 +13,7 @@
 BF16 = jnp.bfloat16
 F32 = jnp.float32
 MIB = 1024 * 1024
+SCOPED = 16 * MIB
 
 
 def cost(flops, nbytes):
@@ -85,7 +86,7 @@
         out_specs=[pl.BlockSpec((h, chunk), lambda i: (0, i)) for h in heights],
         out_shape=[jax.ShapeDtypeStruct((h, width), BF16) for h in heights],
         scratch_shapes=[pltpu.VMEM((E_MOD * CAP, tok_rows), BF16)],
-        compiler_params=pltpu.CompilerParams(vmem_limit_bytes=8 * MIB),
+        compiler_params=pltpu.CompilerParams(vmem_limit_bytes=SCOPED),
         cost_estimate=cost(4 * E_MOD * CAP * tok_rows * width, 6 * tok_rows * width),
         name="gather_slots",
     )(ids, in_hbm(modality), in_hbm(picks), in_hbm(rows), in_hbm(grads))
@@ -118,7 +119,7 @@
         + [jax.ShapeDtypeStruct(tie.shape, tie.dtype) for tie in through],
         input_output_aliases={1 + len(after) + i: 1 + i for i in range(len(through))},
         scratch_shapes=[pltpu.SemaphoreType.DMA((parts,))],
-        compiler_params=pltpu.CompilerParams(vmem_limit_bytes=MIB),
+        compiler_params=pltpu.CompilerParams(vmem_limit_bytes=SCOPED),
         cost_estimate=cost(0, 1024),
         name="load",
     )(in_hbm(weight), *after, *through)
@@ -148,7 +149,7 @@
         out_shape=[jax.ShapeDtypeStruct((total, blocks[0].shape[1]), BF16)]
         + [jax.ShapeDtypeStruct(tie.shape, tie.dtype) for tie in through],
         input_output_aliases={count + i: 1 + i for i in range(len(through))},
-        compiler_params=pltpu.CompilerParams(vmem_limit_bytes=8 * MIB),
+        compiler_params=pltpu.CompilerParams(vmem_limit_bytes=SCOPED),
         cost_estimate=cost(0, 1024),
         name="join",
     )(*blocks, *through)
@@ -194,7 +195,7 @@
         out_specs=[vmem] * 3,
         out_shape=[jax.ShapeDtypeStruct((total, hidden), F32)] * 3,
         scratch_shapes=[pltpu.VMEM((total, width), BF16)],
-        compiler_params=pltpu.CompilerParams(vmem_limit_bytes=16 * MIB),
+        compiler_params=pltpu.CompilerParams(vmem_limit_bytes=SCOPED),
         cost_estimate=cost(1024, 1024),
         name="pre_activations",
     )(*blocks, in_vmem(gate_piece), in_vmem(up_piece))
@@ -248,7 +249,7 @@
         + [jax.ShapeDtypeStruct((total, hidden), BF16)] * 2
         + [jax.ShapeDtypeStruct((total, EXT), BF16)],
         scratch_shapes=[pltpu.VMEM((total, width), BF16)],
-        compiler_params=pltpu.CompilerParams(vmem_limit_bytes=16 * MIB),
+        compiler_params=pltpu.CompilerParams(vmem_limit_bytes=SCOPED),
         cost_estimate=cost(4 * total * width * hidden, 4 * width * hidden),
         name="hidden_grads",
     )(half, *blocks, *factors, in_vmem(down_piece), in_vmem(gate_piece), in_vmem(up_piece))
@@ -270,7 +271,7 @@
         in_specs=[smem] + [vmem] * 5,
         out_specs=[vmem] * groups,
         out_shape=[jax.ShapeDtypeStruct(shape, BF16)] * groups,
-        compiler_params=pltpu.CompilerParams(vmem_limit_bytes=16 * MIB),
+        compiler_params=pltpu.CompilerParams(vmem_limit_bytes=SCOPED),
         cost_estimate=cost(2 * total * width * hidden, 2 * width * hidden),
         name="back_half",
     )(half, dgate, dup, part, in_vmem(gate_piece), in_vmem(up_piece))
@@ -302,7 +303,7 @@
         functools.partial(sum_kernel, groups),
         out_shape=[jax.ShapeDtypeStruct((CAP, wide), BF16)] * E_MOD,
         cost_estimate=cost(own_rows * wide, 4 * groups * own_rows * wide),
-        compiler_params=pltpu.CompilerParams(vmem_limit_bytes=8 * MIB),
+        compiler_params=pltpu.CompilerParams(vmem_limit_bytes=SCOPED),
         name="sum_pieces",
     )(*partials)
 
@@ -352,7 +353,7 @@
         ],
         scratch_shapes=[pltpu.VMEM((count * CAP, wide + EXT), BF16)],
         cost_estimate=cost(4 * count * CAP * tok_rows * wide, 4 * tok_rows * wide),
-        compiler_params=pltpu.CompilerParams(vmem_limit_bytes=16 * MIB),
+        compiler_params=pltpu.CompilerParams(vmem_limit_bytes=SCOPED),
         name="combine",
     )(ids, modality, picks, weights, *blocks)
 

time: 80.7 us -> 80.7 us (level)
  no operation moved by 1% of the time
where the time goes in v4:
time: 80.7 us; the launch traced here: 80.5 us
  Pallas kernels  27.1 us (34%)
  starting transfers between devices  25.7 us (32%)
  waiting for transfers between devices  16.6 us (21%)
  local copies, waits for them, and re-layouts  10.1 us (13%)
    ppermute x10, starting transfers between devices, to_expert(): lax.ppermute(x, 'ep', [(e * groups + j, (e ^ s) * groups + (j + t) % grou...  15.1 us
    ppermute x10, waiting for transfers between devices, to_expert(): lax.ppermute(x, 'ep', [(e * groups + j, (e ^ s) * groups + (j + t) % grou...  10.9 us
    ppermute x7, starting transfers between devices, to_source(): lax.ppermute(x, ('ep', 'mod'), [((e * groups + j) * 2 + m, ((e ^ s) * gro...  10.7 us
    pallas_call x3, Pallas kernels, load(): pl.pallas_call(functools.partial(load_kernel, parts, ties), in_specs=[pla...  10.6 us
    unnamed x14, local copies, waits for them, and re-layouts  10.1 us
    pallas_call x1, Pallas kernels, hidden_grads(): pl.pallas_call(functools.partial(hidden_kernel, count, places, groups), i...  5.69 us
    ppermute x7, waiting for transfers between devices, to_source(): lax.ppermute(x, ('ep', 'mod'), [((e * groups + j) * 2 + m, ((e ^ s) * gro...  5.69 us
    pallas_call x1, Pallas kernels, gather_slots(): pl.pallas_call(gather_kernel, grid=(width // chunk,), in_specs=[pl.BlockS...  3.09 us
  transfers between devices with their start and end apart: 17, of which 7 were waited for; matrix products, arithmetic and copies ran while one was open for 0% of the time, Pallas kernels for 17%

profile of v4, /device:TPU:0, one launch (start us, length us, event | category | flops | bytes accessed | tf_op | source)
XLA Modules:
  0.0 80.5 jit_solution(2472686718882987768)
XLA Ops:
  0.6 0.1 pad_add_fusion.ids_ref
  0.7 3.1 %gather_slots.1 = (bf16[32,4096]{1,0:T(8,128)(2,1)S(1)}, bf16[32,4096]{1,0:T(8,128)(2,1)S(1)}, bf16[16,4096]{1,0:T(8,128)(2,1)S(1)}, bf16[16,4096]{1,0:T(8,128)(...) custom-call(s32[2]{0:T(128)S(1)} %pad_add_fusion.ids_ref, s32[1,128]{1,0:T(1,128)} %bitcast.9, ...), custom_call_target="tpu_custom_call" | custom-call | flops 134217728 | bytes 3145728 | tf_op jit(solution)/shard_map/gather_slots/pallas_call | solution.py:76
  3.8 3.1 %collective-permute-start = (bf16[32,4096]{1,0:T(8,128)(2,1)S(1)}, bf16[32,4096]{1,0:T(8,128)(2,1)S(1)}, u32[]{:S(2)}, u32[]{:S(2)}) collective-permute-start(bf16[32,4096]{1,0:T(8,128)(2,1)S(1)} %get-tuple-element.37), channel_id=1, source_target_pairs={{0,4},{2,6},{4,0},{6,2},{8,12},{10,14},{12,8},{14,10},{1,5},{3,7},... | collective-permute-start | bytes 786440 | tf_op jit(solution)/shard_map/ppermute | solution.py:372
  6.9 2.6 %collective-permute-start.2 = (bf16[16,4096]{1,0:T(8,128)(2,1)S(1)}, bf16[16,4096]{1,0:T(8,128)(2,1)S(1)}, u32[]{:S(2)}, u32[]{:S(2)}) collective-permute-start(bf16[16,4096]{1,0:T(8,128)(2,1)S(1)} %get-tuple-element.38), channel_id=1, source_target_pairs={{0,8},{2,10},{4,12},{6,14},{8,0},{10,2},{12,4},{14,6},{1,9},{3,11}... | collective-permute-start | bytes 393224 | tf_op jit(solution)/shard_map/ppermute | solution.py:372
  9.5 0.0 collective-permute-start.3
  9.5 3.5 %load.3 = (bf16[1,4096,1024]{2,1,0:T(8,128)(2,1)S(1)}, bf16[32,4096]{1,0:T(8,128)(2,1)S(1)}) custom-call(bf16[1,4096,1024]{2,1,0:T(8,128)(2,1)} %src.3, bf16[32,4096]{1,0:T(8,128)(2,1)S(1)} %get-tuple-element.35.refs_0_), custom_call_target="tpu_custom_call", output_to_operand_aliasing={{1}: (1, {})} | custom-call | bytes 1024 | tf_op jit(solution)/shard_map/load/pallas_call | solution.py:114
  13.0 0.0 copy-start
  13.0 3.3 %copy-done = bf16[1,4096,1024]{2,1,0:T(8,128)(2,1)} copy-done((bf16[1,4096,1024]{2,1,0:T(8,128)(2,1)}, bf16[1,4096,1024]{2,1,0:T(8,128)(2,1)S(1)}, u32[]{:S(2)}) %copy-start) | copy-done | bytes 8388632
  16.3 0.0 collective-permute-done.refs_1_
  16.3 1.8 %collective-permute-start.1 = (bf16[64,4096]{1,0:T(8,128)(2,1)S(1)}, bf16[64,4096]{1,0:T(8,128)(2,1)S(1)}, u32[]{:S(2)}, u32[]{:S(2)}) collective-permute-start(bf16[64,4096]{1,0:T(8,128)(2,1)S(1)} %join.3.refs_0_), channel_id=1, source_target_pairs={{0,2},{2,0},{4,6},{6,4},{8,10},{10,8},{12,14},{14,12},{1,3},{3,1},... | collective-permute-start | bytes 1572872 | tf_op jit(solution)/shard_map/ppermute | solution.py:372
  18.1 0.0 collective-permute-done.2.refs_0_
  18.1 3.0 %collective-permute-done.3.refs_1_ = bf16[16,4096]{1,0:T(8,128)(2,1)S(1)} collective-permute-done((bf16[16,4096]{1,0:T(8,128)(2,1)S(1)}, bf16[16,4096]{1,0:T(8,128)(2,1)S(1)}, u32[]{:S(2)}, u32[]{:S(2)}) %collective-permute-start.3) | collective-permute-done | bytes 131104 | tf_op jit(solution)/shard_map/ppermute | solution.py:372
  21.2 1.7 %collective-permute-start.4 = (bf16[16,4096]{1,0:T(8,128)(2,1)S(1)}, bf16[16,4096]{1,0:T(8,128)(2,1)S(1)}, u32[]{:S(2)}, u32[]{:S(2)}) collective-permute-start(bf16[16,4096]{1,0:T(8,128)(2,1)S(1)} %get-tuple-element.42), channel_id=1, source_target_pairs={{0,8},{2,10},{4,12},{6,14},{8,0},{10,2},{12,4},{14,6},{1,9},{3,11}... | collective-permute-start | bytes 393224 | tf_op jit(solution)/shard_map/ppermute | solution.py:372
  22.9 1.5 %collective-permute-start.5 = (bf16[16,4096]{1,0:T(8,128)(2,1)S(1)}, bf16[16,4096]{1,0:T(8,128)(2,1)S(1)}, u32[]{:S(2)}, u32[]{:S(2)}) collective-permute-start(bf16[16,4096]{1,0:T(8,128)(2,1)S(1)} %get-tuple-element.43), channel_id=1, source_target_pairs={{0,12},{2,14},{4,8},{6,10},{8,4},{10,6},{12,0},{14,2},{1,13},{3,15... | collective-permute-start | bytes 393224 | tf_op jit(solution)/shard_map/ppermute | solution.py:372
  24.4 3.5 %load.4 = (bf16[1,4096,1024]{2,1,0:T(8,128)(2,1)S(1)}, bf16[32,4096]{1,0:T(8,128)(2,1)S(1)}) custom-call(bf16[1,4096,1024]{2,1,0:T(8,128)(2,1)} %src.4, bf16[32,4096]{1,0:T(8,128)(2,1)S(1)} %get-tuple-element.44.refs_0_), custom_call_target="tpu_custom_call", output_to_operand_aliasing={{1}: (1, {})} | custom-call | bytes 1024 | tf_op jit(solution)/shard_map/load/pallas_call | solution.py:114
  27.9 0.0 copy-start.2
  27.9 3.2 %copy-done.2 = bf16[1,4096,1024]{2,1,0:T(8,128)(2,1)} copy-done((bf16[1,4096,1024]{2,1,0:T(8,128)(2,1)}, bf16[1,4096,1024]{2,1,0:T(8,128)(2,1)S(1)}, u32[]{:S(2)}) %copy-start.2) | copy-done | bytes 8388632
  31.1 1.4 %collective-permute-start.7 = (bf16[32,4096]{1,0:T(8,128)(2,1)S(1)}, bf16[32,4096]{1,0:T(8,128)(2,1)S(1)}, u32[]{:S(2)}, u32[]{:S(2)}) collective-permute-start(bf16[32,4096]{1,0:T(8,128)(2,1)S(1)} %get-tuple-element.45.refs_2_), channel_id=1, source_target_pairs={{0,2},{2,0},{4,6},{6,4},{8,10},{10,8},{12,14},{14,12},{1,3},{3,1},... | collective-permute-start | bytes 786440 | tf_op jit(solution)/shard_map/ppermute | solution.py:372
  32.5 0.0 collective-permute-done.4.refs_0_
  32.5 0.0 collective-permute-done.5.refs_1_
  32.5 0.9 %collective-permute-start.6 = (bf16[32,4096]{1,0:T(8,128)(2,1)S(1)}, bf16[32,4096]{1,0:T(8,128)(2,1)S(1)}, u32[]{:S(2)}, u32[]{:S(2)}) collective-permute-start(bf16[32,4096]{1,0:T(8,128)(2,1)S(1)} %join.5.refs_0_.refs_2_), channel_id=1, source_target_pairs={{0,2},{2,0},{4,6},{6,4},{8,10},{10,8},{12,14},{14,12},{1,3},{3,1},... | collective-permute-start | bytes 786440 | tf_op jit(solution)/shard_map/ppermute | solution.py:372
  33.4 0.0 copy-start.3
  33.4 3.6 %load.5.refs_7_ = bf16[1,1024,4096]{2,1,0:T(8,128)(2,1)S(1)} custom-call(bf16[1,1024,4096]{2,1,0:T(8,128)(2,1)} %src.5, bf16[32,4096]{1,0:T(8,128)(2,1)S(1)} %join.5.refs_0_.refs_2_), custom_call_target="tpu_custom_call" | custom-call | bytes 1024 | tf_op jit(solution)/shard_map/load/pallas_call | solution.py:114
  37.0 2.0 %collective-permute-done.7.refs_3_ = bf16[32,4096]{1,0:T(8,128)(2,1)S(1)} collective-permute-done((bf16[32,4096]{1,0:T(8,128)(2,1)S(1)}, bf16[32,4096]{1,0:T(8,128)(2,1)S(1)}, u32[]{:S(2)}, u32[]{:S(2)}) %collective-permute-start.7) | collective-permute-done | bytes 262176 | tf_op jit(solution)/shard_map/ppermute | solution.py:372
  39.0 0.0 collective-permute-done.1.refs_1_
  39.0 0.2 copy-done.3
  39.2 0.0 copy-start.1
  39.2 3.4 %copy-done.1 = bf16[1,4096,1024]{2,1,0:T(8,128)(2,1)S(1)} copy-done((bf16[1,4096,1024]{2,1,0:T(8,128)(2,1)S(1)}, bf16[1,4096,1024]{2,1,0:T(8,128)(2,1)}, u32[]{:S(2)}) %copy-start.1) | copy-done | bytes 8388632
  42.6 2.6 %pre_activations.1 = (f32[128,1024]{1,0:T(8,128)S(1)}, f32[128,1024]{1,0:T(8,128)S(1)}, f32[128,1024]{1,0:T(8,128)S(1)}) custom-call(bf16[64,4096]{1,0:T(8,128)(2,1)S(1)} %join.3.refs_0_, bf16[64,4096]{1,0:T(8,128)(2,1)S(1)} %collective-permute-done.1.refs_1_, bf16[32,4096]{1,0:T(8,128)(2,1)S(1)} %get-tuple-element.45.refs_2_, ...), custom_call_target="tpu_custom_call" | custom-call | flops 1024 | bytes 1024 | tf_op jit(solution)/shard_map/pre_activations/pallas_call | solution.py:192
  45.3 0.0 collective-permute-done.6.refs_3_
  45.3 5.7 %hidden_grads.1 = (bf16[64,2176]{1,0:T(8,128)(2,1)S(1)}, bf16[64,2176]{1,0:T(8,128)(2,1)S(1)}, bf16[128,1024]{1,0:T(8,128)(2,1)S(1)}, bf16[128,1024]{1,0:T(8,128)(2,1)S(1)}, bf16[128,128]{1,0:T(8,128)(2,1)S(1)}) custom-call(s32[1]{0:T(128)} %bitcast.5.half_ref, bf16[64,4096]{1,0:T(8,128)(2,1)S(1)} %join.3.refs_0_, ...), custom_call_target="tpu_custom_call" | custom-call | flops 2147483648 | bytes 16777216 | tf_op jit(solution)/shard_map/hidden_grads/pallas_call | solution.py:244
  51.0 0.0 copy-start.4
  51.0 0.0 copy-start.5
  51.0 0.0 copy-start.6
  51.0 2.9 %back_half.1 = (bf16[64,2176]{1,0:T(8,128)(2,1)S(1)}, bf16[64,2176]{1,0:T(8,128)(2,1)S(1)}) custom-call(s32[1]{0:T(128)} %bitcast.1.half_ref, bf16[128,1024]{1,0:T(8,128)(2,1)S(1)} %get-tuple-element.51.dgate_ref, bf16[128,1024]{1,0:T(8,128)(2,1)S(1)} %get-tuple-element.52.dup_ref, bf16[128,128]{1,0:T(8,128)(2,1)S(1)} %get-tuple-element.53.part_ref, ...), custom_call_target="tpu_custom_call" | custom-call | flops 1073741824 | bytes 8388608 | tf_op jit(solution)/shard_map/back_half/pallas_call | solution.py:269
  53.9 1.3 %collective-permute-start.8 = (bf16[64,2176]{1,0:T(8,128)(2,1)S(1)}, bf16[64,2176]{1,0:T(8,128)(2,1)S(1)}, u32[]{:S(2)}, u32[]{:S(2)}) collective-permute-start(bf16[64,2176]{1,0:T(8,128)(2,1)S(1)} %get-tuple-element.55), channel_id=1, source_target_pairs={{0,2},{2,0},{4,6},{6,4},{8,10},{10,8},{12,14},{14,12},{1,3},{3,1},... | collective-permute-start | bytes 835592 | tf_op jit(solution)/shard_map/ppermute | solution.py:372
  55.3 0.7 collective-permute-start.12
  56.0 5.9 %collective-permute-done.8.refs_1_ = bf16[64,2176]{1,0:T(8,128)(2,1)S(1)} collective-permute-done((bf16[64,2176]{1,0:T(8,128)(2,1)S(1)}, bf16[64,2176]{1,0:T(8,128)(2,1)S(1)}, u32[]{:S(2)}, u32[]{:S(2)}) %collective-permute-start.8) | collective-permute-done | bytes 278560 | tf_op jit(solution)/shard_map/ppermute | solution.py:372
  61.9 0.1 sum_pieces.2
  62.0 4.1 %collective-permute-start.9 = (bf16[16,2176]{1,0:T(8,128)(2,1)S(1)}, bf16[16,2176]{1,0:T(8,128)(2,1)S(1)}, u32[]{:S(2)}, u32[]{:S(2)}) collective-permute-start(bf16[16,2176]{1,0:T(8,128)(2,1)S(1)} %get-tuple-element.57), channel_id=1, source_target_pairs={{0,4},{1,5},{2,6},{3,7},{4,0},{5,1},{6,2},{7,3},{8,12},{9,13},{10,... | collective-permute-start | bytes 208904 | tf_op jit(solution)/shard_map/ppermute | solution.py:386
  66.1 1.1 %collective-permute-start.10 = (bf16[16,2176]{1,0:T(8,128)(2,1)S(1)}, bf16[16,2176]{1,0:T(8,128)(2,1)S(1)}, u32[]{:S(2)}, u32[]{:S(2)}) collective-permute-start(bf16[16,2176]{1,0:T(8,128)(2,1)S(1)} %get-tuple-element.58), channel_id=1, source_target_pairs={{0,8},{1,9},{2,10},{3,11},{4,12},{5,13},{6,14},{7,15},{8,0},{9,1},... | collective-permute-start | bytes 208904 | tf_op jit(solution)/shard_map/ppermute | solution.py:386
  67.1 1.4 %collective-permute-start.11 = (bf16[16,2176]{1,0:T(8,128)(2,1)S(1)}, bf16[16,2176]{1,0:T(8,128)(2,1)S(1)}, u32[]{:S(2)}, u32[]{:S(2)}) collective-permute-start(bf16[16,2176]{1,0:T(8,128)(2,1)S(1)} %get-tuple-element.59), channel_id=1, source_target_pairs={{0,12},{1,13},{2,14},{3,15},{4,8},{5,9},{6,10},{7,11},{8,4},{9,5},... | collective-permute-start | bytes 208904 | tf_op jit(solution)/shard_map/ppermute | solution.py:386
  68.5 0.0 collective-permute-done.12.refs_1_
  68.5 0.1 sum_pieces.3
  68.6 0.1 collective-permute-start.13
  68.7 1.2 %collective-permute-start.14 = (bf16[16,2176]{1,0:T(8,128)(2,1)S(1)}, bf16[16,2176]{1,0:T(8,128)(2,1)S(1)}, u32[]{:S(2)}, u32[]{:S(2)}) collective-permute-start(bf16[16,2176]{1,0:T(8,128)(2,1)S(1)} %get-tuple-element.63), channel_id=1, source_target_pairs={{0,5},{1,4},{2,7},{3,6},{4,1},{5,0},{6,3},{7,2},{8,13},{9,12},{10,... | collective-permute-start | bytes 208904 | tf_op jit(solution)/shard_map/ppermute | solution.py:386
  70.0 0.0 collective-permute-done.9.refs_1_
  70.0 1.9 %collective-permute-start.15 = (bf16[16,2176]{1,0:T(8,128)(2,1)S(1)}, bf16[16,2176]{1,0:T(8,128)(2,1)S(1)}, u32[]{:S(2)}, u32[]{:S(2)}) collective-permute-start(bf16[16,2176]{1,0:T(8,128)(2,1)S(1)} %get-tuple-element.64), channel_id=1, source_target_pairs={{0,9},{1,8},{2,11},{3,10},{4,13},{5,12},{6,15},{7,14},{8,1},{9,0},... | collective-permute-start | bytes 208904 | tf_op jit(solution)/shard_map/ppermute | solution.py:386
  71.8 0.2 collective-permute-done.10.refs_2_
  72.1 1.0 %collective-permute-start.16 = (bf16[16,2176]{1,0:T(8,128)(2,1)S(1)}, bf16[16,2176]{1,0:T(8,128)(2,1)S(1)}, u32[]{:S(2)}, u32[]{:S(2)}) collective-permute-start(bf16[16,2176]{1,0:T(8,128)(2,1)S(1)} %get-tuple-element.65), channel_id=1, source_target_pairs={{0,13},{1,12},{2,15},{3,14},{4,9},{5,8},{6,11},{7,10},{8,5},{9,4},... | collective-permute-start | bytes 208904 | tf_op jit(solution)/shard_map/ppermute | solution.py:386
  73.0 0.4 collective-permute-done.11.refs_3_
  73.4 0.0 collective-permute-done.13.refs_4_
  73.4 2.0 %collective-permute-done.14.refs_5_ = bf16[16,2176]{1,0:T(8,128)(2,1)S(1)} collective-permute-done((bf16[16,2176]{1,0:T(8,128)(2,1)S(1)}, bf16[16,2176]{1,0:T(8,128)(2,1)S(1)}, u32[]{:S(2)}, u32[]{:S(2)}) %collective-permute-start.14) | collective-permute-done | bytes 69664 | tf_op jit(solution)/shard_map/ppermute | solution.py:386
  75.4 0.0 collective-permute-done.15.refs_6_
  75.4 3.1 %collective-permute-done.16.refs_7_ = bf16[16,2176]{1,0:T(8,128)(2,1)S(1)} collective-permute-done((bf16[16,2176]{1,0:T(8,128)(2,1)S(1)}, bf16[16,2176]{1,0:T(8,128)(2,1)S(1)}, u32[]{:S(2)}, u32[]{:S(2)}) %collective-permute-start.16) | collective-permute-done | bytes 69664 | tf_op jit(solution)/shard_map/ppermute | solution.py:386
  78.5 0.0 copy-done.4
  78.5 0.0 copy-done.5
  78.5 0.0 copy-done.6
  78.5 2.0 %combine.1 = (bf16[128,2048]{1,0:T(8,128)(2,1)}, f32[1,128]{1,0:T(1,128)}) custom-call(s32[2]{0:T(128)S(1)} %pad_add_fusion.ids_ref, s32[1,128]{1,0:T(1,128)S(1)} %bitcast.10, s32[2,128]{1,0:T(2,128)S(1)} %bitcast.8, f32[2,128]{1,0:T(2,128)S(1)} %bitcast.11, bf16[16,2176]{1,0:T(8,128)(2,1)S(1)} %get-tuple-element.56.refs_0_, ...), custom_call_target="tpu_custom_call" | custom-call | flops 134217728 | bytes 1048576 | tf_op jit(solution)/shard_map/combine/pallas_call | solution.py:346
  (3 shorter events, 0.1 us)
Async XLA Ops:
  3.8 12.4 %collective-permute-start = (bf16[32,4096]{1,0:T(8,128)(2,1)S(1)}, bf16[32,4096]{1,0:T(8,128)(2,1)S(1)}, u32[]{:S(2)}, u32[]{:S(2)}) collective-permute-start(bf16[32,4096]{1,0:T(8,128)(2,1)S(1)} %get-tuple-element.37), channel_id=1, source_target_pairs={{0,4},{2,6},{4,0},{6,2},{8,12},{10,14},{12,8},{14,10},{1,5},{3,7},... | collective-permute-start | bytes 786440 | tf_op jit(solution)/shard_map/ppermute | solution.py:372
  6.9 11.2 %collective-permute-start.2 = (bf16[16,4096]{1,0:T(8,128)(2,1)S(1)}, bf16[16,4096]{1,0:T(8,128)(2,1)S(1)}, u32[]{:S(2)}, u32[]{:S(2)}) collective-permute-start(bf16[16,4096]{1,0:T(8,128)(2,1)S(1)} %get-tuple-element.38), channel_id=1, source_target_pairs={{0,8},{2,10},{4,12},{6,14},{8,0},{10,2},{12,4},{14,6},{1,9},{3,11}... | collective-permute-start | bytes 393224 | tf_op jit(solution)/shard_map/ppermute | solution.py:372
  9.5 11.6 %collective-permute-start.3 = (bf16[16,4096]{1,0:T(8,128)(2,1)S(1)}, bf16[16,4096]{1,0:T(8,128)(2,1)S(1)}, u32[]{:S(2)}, u32[]{:S(2)}) collective-permute-start(bf16[16,4096]{1,0:T(8,128)(2,1)S(1)} %get-tuple-element.39), channel_id=1, source_target_pairs={{0,12},{2,14},{4,8},{6,10},{8,4},{10,6},{12,0},{14,2},{1,13},{3,15... | collective-permute-start | bytes 393224 | tf_op jit(solution)/shard_map/ppermute | solution.py:372
  13.0 3.3 %copy-start = (bf16[1,4096,1024]{2,1,0:T(8,128)(2,1)}, bf16[1,4096,1024]{2,1,0:T(8,128)(2,1)S(1)}, u32[]{:S(2)}) copy-start(bf16[1,4096,1024]{2,1,0:T(8,128)(2,1)S(1)} %get-tuple-element.46.refs_4_.refs_8_.gate_ref) | copy-start | bytes 25165828
  16.3 22.7 %collective-permute-start.1 = (bf16[64,4096]{1,0:T(8,128)(2,1)S(1)}, bf16[64,4096]{1,0:T(8,128)(2,1)S(1)}, u32[]{:S(2)}, u32[]{:S(2)}) collective-permute-start(bf16[64,4096]{1,0:T(8,128)(2,1)S(1)} %join.3.refs_0_), channel_id=1, source_target_pairs={{0,2},{2,0},{4,6},{6,4},{8,10},{10,8},{12,14},{14,12},{1,3},{3,1},... | collective-permute-start | bytes 1572872 | tf_op jit(solution)/shard_map/ppermute | solution.py:372
  21.2 11.3 %collective-permute-start.4 = (bf16[16,4096]{1,0:T(8,128)(2,1)S(1)}, bf16[16,4096]{1,0:T(8,128)(2,1)S(1)}, u32[]{:S(2)}, u32[]{:S(2)}) collective-permute-start(bf16[16,4096]{1,0:T(8,128)(2,1)S(1)} %get-tuple-element.42), channel_id=1, source_target_pairs={{0,8},{2,10},{4,12},{6,14},{8,0},{10,2},{12,4},{14,6},{1,9},{3,11}... | collective-permute-start | bytes 393224 | tf_op jit(solution)/shard_map/ppermute | solution.py:372
  22.9 9.6 %collective-permute-start.5 = (bf16[16,4096]{1,0:T(8,128)(2,1)S(1)}, bf16[16,4096]{1,0:T(8,128)(2,1)S(1)}, u32[]{:S(2)}, u32[]{:S(2)}) collective-permute-start(bf16[16,4096]{1,0:T(8,128)(2,1)S(1)} %get-tuple-element.43), channel_id=1, source_target_pairs={{0,12},{2,14},{4,8},{6,10},{8,4},{10,6},{12,0},{14,2},{1,13},{3,15... | collective-permute-start | bytes 393224 | tf_op jit(solution)/shard_map/ppermute | solution.py:372
  27.9 3.2 %copy-start.2 = (bf16[1,4096,1024]{2,1,0:T(8,128)(2,1)}, bf16[1,4096,1024]{2,1,0:T(8,128)(2,1)S(1)}, u32[]{:S(2)}) copy-start(bf16[1,4096,1024]{2,1,0:T(8,128)(2,1)S(1)} %get-tuple-element.47.refs_5_.refs_9_.up_ref) | copy-start | bytes 25165828
  31.1 7.9 %collective-permute-start.7 = (bf16[32,4096]{1,0:T(8,128)(2,1)S(1)}, bf16[32,4096]{1,0:T(8,128)(2,1)S(1)}, u32[]{:S(2)}, u32[]{:S(2)}) collective-permute-start(bf16[32,4096]{1,0:T(8,128)(2,1)S(1)} %get-tuple-element.45.refs_2_), channel_id=1, source_target_pairs={{0,2},{2,0},{4,6},{6,4},{8,10},{10,8},{12,14},{14,12},{1,3},{3,1},... | collective-permute-start | bytes 786440 | tf_op jit(solution)/shard_map/ppermute | solution.py:372
  32.5 12.7 %collective-permute-start.6 = (bf16[32,4096]{1,0:T(8,128)(2,1)S(1)}, bf16[32,4096]{1,0:T(8,128)(2,1)S(1)}, u32[]{:S(2)}, u32[]{:S(2)}) collective-permute-start(bf16[32,4096]{1,0:T(8,128)(2,1)S(1)} %join.5.refs_0_.refs_2_), channel_id=1, source_target_pairs={{0,2},{2,0},{4,6},{6,4},{8,10},{10,8},{12,14},{14,12},{1,3},{3,1},... | collective-permute-start | bytes 786440 | tf_op jit(solution)/shard_map/ppermute | solution.py:372
  33.4 5.9 %copy-start.3 = (bf16[1,4096,1024]{2,1,0:T(8,128)(2,1)S(1)}, bf16[1,4096,1024]{2,1,0:T(8,128)(2,1)}, u32[]{:S(2)}) copy-start(bf16[1,4096,1024]{2,1,0:T(8,128)(2,1)} %copy-done.2) | copy-start | bytes 25165828
  39.2 3.4 %copy-start.1 = (bf16[1,4096,1024]{2,1,0:T(8,128)(2,1)S(1)}, bf16[1,4096,1024]{2,1,0:T(8,128)(2,1)}, u32[]{:S(2)}) copy-start(bf16[1,4096,1024]{2,1,0:T(8,128)(2,1)} %copy-done) | copy-start | bytes 25165828
  51.0 27.5 %copy-start.4 = (s32[128,2]{0,1:T(2,128)S(1)}, s32[128,2]{0,1:T(2,128)}, u32[]{:S(2)}) copy-start(s32[128,2]{0,1:T(2,128)} %param.11) | copy-start | bytes 3076
  51.0 27.5 %copy-start.5 = (s32[128]{0:T(128)S(1)}, s32[128]{0:T(128)}, u32[]{:S(2)}) copy-start(s32[128]{0:T(128)} %param.10) | copy-start | bytes 1540
  51.0 27.5 %copy-start.6 = (f32[128,2]{0,1:T(2,128)S(1)}, f32[128,2]{0,1:T(2,128)}, u32[]{:S(2)}) copy-start(f32[128,2]{0,1:T(2,128)} %param.12) | copy-start | bytes 3076
  53.9 8.0 %collective-permute-start.8 = (bf16[64,2176]{1,0:T(8,128)(2,1)S(1)}, bf16[64,2176]{1,0:T(8,128)(2,1)S(1)}, u32[]{:S(2)}, u32[]{:S(2)}) collective-permute-start(bf16[64,2176]{1,0:T(8,128)(2,1)S(1)} %get-tuple-element.55), channel_id=1, source_target_pairs={{0,2},{2,0},{4,6},{6,4},{8,10},{10,8},{12,14},{14,12},{1,3},{3,1},... | collective-permute-start | bytes 835592 | tf_op jit(solution)/shard_map/ppermute | solution.py:372
  55.3 13.3 %collective-permute-start.12 = (bf16[64,2176]{1,0:T(8,128)(2,1)S(1)}, bf16[64,2176]{1,0:T(8,128)(2,1)S(1)}, u32[]{:S(2)}, u32[]{:S(2)}) collective-permute-start(bf16[64,2176]{1,0:T(8,128)(2,1)S(1)} %get-tuple-element.61), channel_id=1, source_target_pairs={{0,2},{2,0},{4,6},{6,4},{8,10},{10,8},{12,14},{14,12},{1,3},{3,1},... | collective-permute-start | bytes 835592 | tf_op jit(solution)/shard_map/ppermute | solution.py:372
  62.0 7.9 %collective-permute-start.9 = (bf16[16,2176]{1,0:T(8,128)(2,1)S(1)}, bf16[16,2176]{1,0:T(8,128)(2,1)S(1)}, u32[]{:S(2)}, u32[]{:S(2)}) collective-permute-start(bf16[16,2176]{1,0:T(8,128)(2,1)S(1)} %get-tuple-element.57), channel_id=1, source_target_pairs={{0,4},{1,5},{2,6},{3,7},{4,0},{5,1},{6,2},{7,3},{8,12},{9,13},{10,... | collective-permute-start | bytes 208904 | tf_op jit(solution)/shard_map/ppermute | solution.py:386
  66.1 6.0 %collective-permute-start.10 = (bf16[16,2176]{1,0:T(8,128)(2,1)S(1)}, bf16[16,2176]{1,0:T(8,128)(2,1)S(1)}, u32[]{:S(2)}, u32[]{:S(2)}) collective-permute-start(bf16[16,2176]{1,0:T(8,128)(2,1)S(1)} %get-tuple-element.58), channel_id=1, source_target_pairs={{0,8},{1,9},{2,10},{3,11},{4,12},{5,13},{6,14},{7,15},{8,0},{9,1},... | collective-permute-start | bytes 208904 | tf_op jit(solution)/shard_map/ppermute | solution.py:386
  67.1 6.3 %collective-permute-start.11 = (bf16[16,2176]{1,0:T(8,128)(2,1)S(1)}, bf16[16,2176]{1,0:T(8,128)(2,1)S(1)}, u32[]{:S(2)}, u32[]{:S(2)}) collective-permute-start(bf16[16,2176]{1,0:T(8,128)(2,1)S(1)} %get-tuple-element.59), channel_id=1, source_target_pairs={{0,12},{1,13},{2,14},{3,15},{4,8},{5,9},{6,10},{7,11},{8,4},{9,5},... | collective-permute-start | bytes 208904 | tf_op jit(solution)/shard_map/ppermute | solution.py:386
  68.6 4.8 %collective-permute-start.13 = (bf16[16,2176]{1,0:T(8,128)(2,1)S(1)}, bf16[16,2176]{1,0:T(8,128)(2,1)S(1)}, u32[]{:S(2)}, u32[]{:S(2)}) collective-permute-start(bf16[16,2176]{1,0:T(8,128)(2,1)S(1)} %get-tuple-element.62), channel_id=1, source_target_pairs={{0,1},{1,0},{2,3},{3,2},{4,5},{5,4},{6,7},{7,6},{8,9},{9,8},{10,11... | collective-permute-start | bytes 208904 | tf_op jit(solution)/shard_map/ppermute | solution.py:386
  68.7 6.7 %collective-permute-start.14 = (bf16[16,2176]{1,0:T(8,128)(2,1)S(1)}, bf16[16,2176]{1,0:T(8,128)(2,1)S(1)}, u32[]{:S(2)}, u32[]{:S(2)}) collective-permute-start(bf16[16,2176]{1,0:T(8,128)(2,1)S(1)} %get-tuple-element.63), channel_id=1, source_target_pairs={{0,5},{1,4},{2,7},{3,6},{4,1},{5,0},{6,3},{7,2},{8,13},{9,12},{10,... | collective-permute-start | bytes 208904 | tf_op jit(solution)/shard_map/ppermute | solution.py:386
  70.0 5.4 %collective-permute-start.15 = (bf16[16,2176]{1,0:T(8,128)(2,1)S(1)}, bf16[16,2176]{1,0:T(8,128)(2,1)S(1)}, u32[]{:S(2)}, u32[]{:S(2)}) collective-permute-start(bf16[16,2176]{1,0:T(8,128)(2,1)S(1)} %get-tuple-element.64), channel_id=1, source_target_pairs={{0,9},{1,8},{2,11},{3,10},{4,13},{5,12},{6,15},{7,14},{8,1},{9,0},... | collective-permute-start | bytes 208904 | tf_op jit(solution)/shard_map/ppermute | solution.py:386
  72.1 6.4 %collective-permute-start.16 = (bf16[16,2176]{1,0:T(8,128)(2,1)S(1)}, bf16[16,2176]{1,0:T(8,128)(2,1)S(1)}, u32[]{:S(2)}, u32[]{:S(2)}) collective-permute-start(bf16[16,2176]{1,0:T(8,128)(2,1)S(1)} %get-tuple-element.65), channel_id=1, source_target_pairs={{0,13},{1,12},{2,15},{3,14},{4,9},{5,8},{6,11},{7,10},{8,5},{9,4},... | collective-permute-start | bytes 208904 | tf_op jit(solution)/shard_map/ppermute | solution.py:386

commit v5 on v4

--- a/solution.py
+++ b/solution.py
@@ -92,8 +92,8 @@
     )(ids, in_hbm(modality), in_hbm(picks), in_hbm(rows), in_hbm(grads))
 
 
-def load_kernel(parts, ties, src, *refs):
-    dst, sems = refs[ties], refs[-1]
+def load_kernel(parts, src, *refs):
+    dst, sems = refs[-2:]
     rows = src.shape[1] // parts
     copies = [
         pltpu.make_async_copy(
@@ -107,22 +107,72 @@
         copy.wait()
 
 
-def load(weight, after, through=()):
+def load(weight, after):
     parts = 8
-    place = pl.BlockSpec(memory_space=pl.ANY)
-    ties = len(after) + len(through)
-    return pl.pallas_call(
-        functools.partial(load_kernel, parts, ties),
-        in_specs=[place] * (1 + ties),
-        out_specs=[pl.BlockSpec(memory_space=pltpu.VMEM)] + [place] * len(through),
-        out_shape=[pltpu.VMEM(weight.shape, weight.dtype)]
-        + [jax.ShapeDtypeStruct(tie.shape, tie.dtype) for tie in through],
-        input_output_aliases={1 + len(after) + i: 1 + i for i in range(len(through))},
+    return pl.pallas_call(
+        functools.partial(load_kernel, parts),
+        in_specs=[pl.BlockSpec(memory_space=pl.ANY)] * (1 + len(after)),
+        out_specs=pl.BlockSpec(memory_space=pltpu.VMEM),
+        out_shape=pltpu.VMEM(weight.shape, weight.dtype),
         scratch_shapes=[pltpu.SemaphoreType.DMA((parts,))],
         compiler_params=pltpu.CompilerParams(vmem_limit_bytes=SCOPED),
         cost_estimate=cost(0, 1024),
         name="load",
-    )(in_hbm(weight), *after, *through)
+    )(in_hbm(weight), *after)
+
+
+def load_turned_kernel(parts, src, *refs):
+    dst, stage, sems = refs[-3:]
+    rows, width = stage.shape[1:]
+    copies = [
+        pltpu.make_async_copy(src.at[0, pl.ds(i * rows, rows), :], stage.at[i], sems.at[i])
+        for i in range(parts)
+    ]
+    for copy in copies:
+        copy.start()
+    chunk = 512
+    for i in range(parts):
+        copies[i].wait()
+        for start in range(0, width, chunk):
+            block = stage[i, :, start : start + chunk]
+            dst[start : start + chunk, i * rows : (i + 1) * rows] = block.T
+
+
+def load_turned(weight, after):
+    _, height, width = weight.shape
+    rows = 128
+    parts = height // rows
+    return pl.pallas_call(
+        functools.partial(load_turned_kernel, parts),
+        in_specs=[pl.BlockSpec(memory_space=pl.ANY)] * (1 + len(after)),
+        out_specs=pl.BlockSpec(memory_space=pltpu.VMEM),
+        out_shape=pltpu.VMEM((width, height), weight.dtype),
+        scratch_shapes=[
+            pltpu.VMEM((parts, rows, width), weight.dtype),
+            pltpu.SemaphoreType.DMA((parts,)),
+        ],
+        compiler_params=pltpu.CompilerParams(vmem_limit_bytes=SCOPED),
+        cost_estimate=cost(0, 1024),
+        name="load_turned",
+    )(in_hbm(weight), *after)
+
+
+def pass_kernel(*refs):
+    pass
+
+
+def pass_after(block, need):
+    place = pl.BlockSpec(memory_space=pl.ANY)
+    return pl.pallas_call(
+        pass_kernel,
+        in_specs=[place] * 2,
+        out_specs=place,
+        out_shape=jax.ShapeDtypeStruct(block.shape, block.dtype),
+        input_output_aliases={0: 0},
+        compiler_params=pltpu.CompilerParams(vmem_limit_bytes=SCOPED),
+        cost_estimate=cost(0, 1024),
+        name="pass_after",
+    )(block, in_vmem(need))
 
 
 def join_kernel(count, *refs):
@@ -226,7 +276,7 @@
     part = jnp.zeros((rows.shape[0], 1), F32)
     for start in range(0, hidden, chunk):
         cols = slice(start, start + chunk)
-        grad = nt_dot(rows[...], down_ref[0, cols, :])
+        grad = jnp.dot(rows[...], down_ref[:, cols], preferred_element_type=F32)
         part = part + jnp.sum(grad * both_ref[:, cols], axis=1, keepdims=True)
         dgate[:, cols] = (grad * slope_ref[:, cols]).astype(BF16)
         dup[:, cols] = (grad * act_ref[:, cols]).astype(BF16)
@@ -397,15 +447,16 @@
     sent = gather_slots(ids, modality, picks, tokens, cotangent)
     far = [[to_expert(sent[2 * s - 2], s) for s in range(2, E_MOD)]]
     near = to_expert(sent[1], 1)
-    gate_piece, own = load(gate_proj, [], sent[:1])
-    (near,) = join([own, near])
+    gate_piece = load(gate_proj, sent[:1])
+    (near,) = join([pass_after(sent[0], gate_piece), near])
     near = [near] + [to_piece(near, t) for t in range(1, groups)]
     far[0], *later = join(far[0], [sent[2 * s - 1] for s in range(2, E_MOD)])
     far.append([to_expert(x, s) for x, s in zip(later, range(2, E_MOD))])
-    up_piece, far[0] = load(up_proj, [], [far[0]])
+    up_piece = load(up_proj, [far[0]])
+    far[0] = pass_after(far[0], up_piece)
     far[0] = [far[0]] + [to_piece(far[0], t) for t in range(1, groups)]
     (far[1],) = join(far[1])
-    (down_piece,) = load(down_proj, [far[1]])
+    down_piece = load_turned(down_proj, [far[1]])
     far[1] = [far[1]] + [to_piece(far[1], t) for t in range(1, groups)]
     blocks = [near + far[a] for a in range(2)]
     places = [

time: 80.7 us -> 79.1 us (0.980)
    pallas_call x1, Pallas kernels: 5.69 us -> 4.09 us  [hidden_grads(): pl.pallas_call(functools.partial(hidden_kernel, count, places, groups), i...]
    ppermute x10, waiting for transfers between devices: 10.9 us -> 10.1 us  [to_expert(): lax.ppermute(x, 'ep', [(e * groups + j, (e ^ s) * groups + (j + t) % grou...]
    pallas_call x3 -> x5, Pallas kernels: 10.6 us -> 11.4 us  [the longest x2 6.94 us: load(): pl.pallas_call(functools.partial(load_kernel, parts), in_specs=[pl.BlockS...]
  transfers between devices with their start and end apart: 17 -> 17, of which waited for: 7 -> 7; matrix products, arithmetic and copies ran while one was open for 0% -> 0% of each run, Pallas kernels for 17% -> 18%
where the time goes in v5:
time: 79.1 us; the launch traced here: 78.9 us
  Pallas kernels  26.3 us (33%)
  starting transfers between devices  25.7 us (32%)
  waiting for transfers between devices  15.8 us (20%)
  local copies, waits for them, and re-layouts  10.1 us (13%)
  between operations  0.81 us (1%)
    ppermute x10, starting transfers between devices, to_expert(): lax.ppermute(x, 'ep', [(e * groups + j, (e ^ s) * groups + (j + t) % grou...  15.1 us
    ppermute x7, starting transfers between devices, to_source(): lax.ppermute(x, ('ep', 'mod'), [((e * groups + j) * 2 + m, ((e ^ s) * gro...  10.7 us
    unnamed x14, local copies, waits for them, and re-layouts  10.1 us
    ppermute x10, waiting for transfers between devices, to_expert(): lax.ppermute(x, 'ep', [(e * groups + j, (e ^ s) * groups + (j + t) % grou...  10.1 us
    pallas_call x2, Pallas kernels, load(): pl.pallas_call(functools.partial(load_kernel, parts), in_specs=[pl.BlockS...  6.94 us
    ppermute x7, waiting for transfers between devices, to_source(): lax.ppermute(x, ('ep', 'mod'), [((e * groups + j) * 2 + m, ((e ^ s) * gro...  5.74 us
    pallas_call x1, Pallas kernels, load_turned(): pl.pallas_call(functools.partial(load_turned_kernel, parts), in_specs=[pl...  4.44 us
    pallas_call x1, Pallas kernels, hidden_grads(): pl.pallas_call(functools.partial(hidden_kernel, count, places, groups), i...  4.09 us
  transfers between devices with their start and end apart: 17, of which 7 were waited for; matrix products, arithmetic and copies ran while one was open for 0% of the time, Pallas kernels for 18%

profile of v5, /device:TPU:0, one launch (start us, length us, event | category | flops | bytes accessed | tf_op | source)
XLA Modules:
  0.0 78.9 jit_solution(812228412460502822)
XLA Ops:
  0.6 0.1 pad_add_fusion.ids_ref
  0.7 3.1 %gather_slots.1 = (bf16[32,4096]{1,0:T(8,128)(2,1)S(1)}, bf16[32,4096]{1,0:T(8,128)(2,1)S(1)}, bf16[16,4096]{1,0:T(8,128)(2,1)S(1)}, bf16[16,4096]{1,0:T(8,128)(...) custom-call(s32[2]{0:T(128)S(1)} %pad_add_fusion.ids_ref, s32[1,128]{1,0:T(1,128)} %bitcast.9, ...), custom_call_target="tpu_custom_call" | custom-call | flops 134217728 | bytes 3145728 | tf_op jit(solution)/shard_map/gather_slots/pallas_call | solution.py:76
  3.8 3.1 %collective-permute-start = (bf16[32,4096]{1,0:T(8,128)(2,1)S(1)}, bf16[32,4096]{1,0:T(8,128)(2,1)S(1)}, u32[]{:S(2)}, u32[]{:S(2)}) collective-permute-start(bf16[32,4096]{1,0:T(8,128)(2,1)S(1)} %get-tuple-element.32), channel_id=1, source_target_pairs={{0,4},{2,6},{4,0},{6,2},{8,12},{10,14},{12,8},{14,10},{1,5},{3,7},... | collective-permute-start | bytes 786440 | tf_op jit(solution)/shard_map/ppermute | solution.py:422
  6.9 2.6 %collective-permute-start.2 = (bf16[16,4096]{1,0:T(8,128)(2,1)S(1)}, bf16[16,4096]{1,0:T(8,128)(2,1)S(1)}, u32[]{:S(2)}, u32[]{:S(2)}) collective-permute-start(bf16[16,4096]{1,0:T(8,128)(2,1)S(1)} %get-tuple-element.33), channel_id=1, source_target_pairs={{0,8},{2,10},{4,12},{6,14},{8,0},{10,2},{12,4},{14,6},{1,9},{3,11}... | collective-permute-start | bytes 393224 | tf_op jit(solution)/shard_map/ppermute | solution.py:422
  9.5 0.0 collective-permute-start.3
  9.5 3.5 %load.2.refs_1_.refs_4_.refs_8_.gate_ref = bf16[1,4096,1024]{2,1,0:T(8,128)(2,1)S(1)} custom-call(bf16[1,4096,1024]{2,1,0:T(8,128)(2,1)} %src.3, bf16[32,4096]{1,0:T(8,128)(2,1)S(1)} %get-tuple-element.31.refs_0_), custom_call_target="tpu_custom_call" | custom-call | bytes 1024 | tf_op jit(solution)/shard_map/load/pallas_call | solution.py:112
  13.0 0.0 copy-start
  13.0 3.3 %copy-done = bf16[1,4096,1024]{2,1,0:T(8,128)(2,1)} copy-done((bf16[1,4096,1024]{2,1,0:T(8,128)(2,1)}, bf16[1,4096,1024]{2,1,0:T(8,128)(2,1)S(1)}, u32[]{:S(2)}) %copy-start) | copy-done | bytes 8388632
  16.3 0.0 collective-permute-done.refs_1_
  16.3 1.8 %collective-permute-start.1 = (bf16[64,4096]{1,0:T(8,128)(2,1)S(1)}, bf16[64,4096]{1,0:T(8,128)(2,1)S(1)}, u32[]{:S(2)}, u32[]{:S(2)}) collective-permute-start(bf16[64,4096]{1,0:T(8,128)(2,1)S(1)} %join.3.refs_0_), channel_id=1, source_target_pairs={{0,2},{2,0},{4,6},{6,4},{8,10},{10,8},{12,14},{14,12},{1,3},{3,1},... | collective-permute-start | bytes 1572872 | tf_op jit(solution)/shard_map/ppermute | solution.py:422
  18.1 0.0 collective-permute-done.2.refs_0_
  18.1 3.0 %collective-permute-done.3.refs_1_ = bf16[16,4096]{1,0:T(8,128)(2,1)S(1)} collective-permute-done((bf16[16,4096]{1,0:T(8,128)(2,1)S(1)}, bf16[16,4096]{1,0:T(8,128)(2,1)S(1)}, u32[]{:S(2)}, u32[]{:S(2)}) %collective-permute-start.3) | collective-permute-done | bytes 131104 | tf_op jit(solution)/shard_map/ppermute | solution.py:422
  21.2 1.7 %collective-permute-start.4 = (bf16[16,4096]{1,0:T(8,128)(2,1)S(1)}, bf16[16,4096]{1,0:T(8,128)(2,1)S(1)}, u32[]{:S(2)}, u32[]{:S(2)}) collective-permute-start(bf16[16,4096]{1,0:T(8,128)(2,1)S(1)} %get-tuple-element.37), channel_id=1, source_target_pairs={{0,8},{2,10},{4,12},{6,14},{8,0},{10,2},{12,4},{14,6},{1,9},{3,11}... | collective-permute-start | bytes 393224 | tf_op jit(solution)/shard_map/ppermute | solution.py:422
  22.9 1.5 %collective-permute-start.5 = (bf16[16,4096]{1,0:T(8,128)(2,1)S(1)}, bf16[16,4096]{1,0:T(8,128)(2,1)S(1)}, u32[]{:S(2)}, u32[]{:S(2)}) collective-permute-start(bf16[16,4096]{1,0:T(8,128)(2,1)S(1)} %get-tuple-element.38), channel_id=1, source_target_pairs={{0,12},{2,14},{4,8},{6,10},{8,4},{10,6},{12,0},{14,2},{1,13},{3,15... | collective-permute-start | bytes 393224 | tf_op jit(solution)/shard_map/ppermute | solution.py:422
  24.4 3.5 %load.3.refs_1_.refs_5_.refs_9_.up_ref = bf16[1,4096,1024]{2,1,0:T(8,128)(2,1)S(1)} custom-call(bf16[1,4096,1024]{2,1,0:T(8,128)(2,1)} %src.4, bf16[32,4096]{1,0:T(8,128)(2,1)S(1)} %get-tuple-element.39.refs_0_), custom_call_target="tpu_custom_call" | custom-call | bytes 1024 | tf_op jit(solution)/shard_map/load/pallas_call | solution.py:112
  27.9 0.0 copy-start.2
  27.9 3.2 %copy-done.2 = bf16[1,4096,1024]{2,1,0:T(8,128)(2,1)} copy-done((bf16[1,4096,1024]{2,1,0:T(8,128)(2,1)}, bf16[1,4096,1024]{2,1,0:T(8,128)(2,1)S(1)}, u32[]{:S(2)}) %copy-start.2) | copy-done | bytes 8388632
  31.1 1.4 %collective-permute-start.7 = (bf16[32,4096]{1,0:T(8,128)(2,1)S(1)}, bf16[32,4096]{1,0:T(8,128)(2,1)S(1)}, u32[]{:S(2)}, u32[]{:S(2)}) collective-permute-start(bf16[32,4096]{1,0:T(8,128)(2,1)S(1)} %pass_after.3.refs_2_), channel_id=1, source_target_pairs={{0,2},{2,0},{4,6},{6,4},{8,10},{10,8},{12,14},{14,12},{1,3},{3,1},... | collective-permute-start | bytes 786440 | tf_op jit(solution)/shard_map/ppermute | solution.py:422
  32.5 0.0 collective-permute-done.4.refs_0_
  32.5 0.0 collective-permute-done.5.refs_1_
  32.5 0.9 %collective-permute-start.6 = (bf16[32,4096]{1,0:T(8,128)(2,1)S(1)}, bf16[32,4096]{1,0:T(8,128)(2,1)S(1)}, u32[]{:S(2)}, u32[]{:S(2)}) collective-permute-start(bf16[32,4096]{1,0:T(8,128)(2,1)S(1)} %join.5.refs_0_.refs_2_), channel_id=1, source_target_pairs={{0,2},{2,0},{4,6},{6,4},{8,10},{10,8},{12,14},{14,12},{1,3},{3,1},... | collective-permute-start | bytes 786440 | tf_op jit(solution)/shard_map/ppermute | solution.py:422
  33.4 0.0 copy-start.3
  33.4 4.4 %load_turned.1.refs_7_ = bf16[4096,1024]{1,0:T(8,128)(2,1)S(1)} custom-call(bf16[1,1024,4096]{2,1,0:T(8,128)(2,1)} %src.5, bf16[32,4096]{1,0:T(8,128)(2,1)S(1)} %join.5.refs_0_.refs_2_), custom_call_target="tpu_custom_call" | custom-call | bytes 1024 | tf_op jit(solution)/shard_map/load_turned/pallas_call | solution.py:145
  37.8 1.2 %collective-permute-done.7.refs_3_ = bf16[32,4096]{1,0:T(8,128)(2,1)S(1)} collective-permute-done((bf16[32,4096]{1,0:T(8,128)(2,1)S(1)}, bf16[32,4096]{1,0:T(8,128)(2,1)S(1)}, u32[]{:S(2)}, u32[]{:S(2)}) %collective-permute-start.7) | collective-permute-done | bytes 262176 | tf_op jit(solution)/shard_map/ppermute | solution.py:422
  39.0 0.0 collective-permute-done.1.refs_1_
  39.0 0.2 copy-done.3
  39.2 0.0 copy-start.1
  39.2 3.4 %copy-done.1 = bf16[1,4096,1024]{2,1,0:T(8,128)(2,1)S(1)} copy-done((bf16[1,4096,1024]{2,1,0:T(8,128)(2,1)S(1)}, bf16[1,4096,1024]{2,1,0:T(8,128)(2,1)}, u32[]{:S(2)}) %copy-start.1) | copy-done | bytes 8388632
  42.6 2.6 %pre_activations.1 = (f32[128,1024]{1,0:T(8,128)S(1)}, f32[128,1024]{1,0:T(8,128)S(1)}, f32[128,1024]{1,0:T(8,128)S(1)}) custom-call(bf16[64,4096]{1,0:T(8,128)(2,1)S(1)} %join.3.refs_0_, bf16[64,4096]{1,0:T(8,128)(2,1)S(1)} %collective-permute-done.1.refs_1_, bf16[32,4096]{1,0:T(8,128)(2,1)S(1)} %pass_after.3.refs_2_, ...), custom_call_target="tpu_custom_call" | custom-call | flops 1024 | bytes 1024 | tf_op jit(solution)/shard_map/pre_activations/pallas_call | solution.py:242
  45.3 0.0 collective-permute-done.6.refs_3_
  45.3 4.1 %hidden_grads.1 = (bf16[64,2176]{1,0:T(8,128)(2,1)S(1)}, bf16[64,2176]{1,0:T(8,128)(2,1)S(1)}, bf16[128,1024]{1,0:T(8,128)(2,1)S(1)}, bf16[128,1024]{1,0:T(8,128)(2,1)S(1)}, bf16[128,128]{1,0:T(8,128)(2,1)S(1)}) custom-call(s32[1]{0:T(128)} %bitcast.5.half_ref, bf16[64,4096]{1,0:T(8,128)(2,1)S(1)} %join.3.refs_0_, ...), custom_call_target="tpu_custom_call" | custom-call | flops 2147483648 | bytes 16777216 | tf_op jit(solution)/shard_map/hidden_grads/pallas_call | solution.py:294
  49.4 0.0 copy-start.4
  49.4 0.0 copy-start.5
  49.4 0.0 copy-start.6
  49.4 2.9 %back_half.1 = (bf16[64,2176]{1,0:T(8,128)(2,1)S(1)}, bf16[64,2176]{1,0:T(8,128)(2,1)S(1)}) custom-call(s32[1]{0:T(128)} %bitcast.1.half_ref, bf16[128,1024]{1,0:T(8,128)(2,1)S(1)} %get-tuple-element.43.dgate_ref, bf16[128,1024]{1,0:T(8,128)(2,1)S(1)} %get-tuple-element.44.dup_ref, bf16[128,128]{1,0:T(8,128)(2,1)S(1)} %get-tuple-element.45.part_ref, ...), custom_call_target="tpu_custom_call" | custom-call | flops 1073741824 | bytes 8388608 | tf_op jit(solution)/shard_map/back_half/pallas_call | solution.py:319
  52.3 1.4 %collective-permute-start.8 = (bf16[64,2176]{1,0:T(8,128)(2,1)S(1)}, bf16[64,2176]{1,0:T(8,128)(2,1)S(1)}, u32[]{:S(2)}, u32[]{:S(2)}) collective-permute-start(bf16[64,2176]{1,0:T(8,128)(2,1)S(1)} %get-tuple-element.47), channel_id=1, source_target_pairs={{0,2},{2,0},{4,6},{6,4},{8,10},{10,8},{12,14},{14,12},{1,3},{3,1},... | collective-permute-start | bytes 835592 | tf_op jit(solution)/shard_map/ppermute | solution.py:422
  53.7 0.7 collective-permute-start.12
  54.4 5.9 %collective-permute-done.8.refs_1_ = bf16[64,2176]{1,0:T(8,128)(2,1)S(1)} collective-permute-done((bf16[64,2176]{1,0:T(8,128)(2,1)S(1)}, bf16[64,2176]{1,0:T(8,128)(2,1)S(1)}, u32[]{:S(2)}, u32[]{:S(2)}) %collective-permute-start.8) | collective-permute-done | bytes 278560 | tf_op jit(solution)/shard_map/ppermute | solution.py:422
  60.3 0.1 sum_pieces.2
  60.4 4.1 %collective-permute-start.9 = (bf16[16,2176]{1,0:T(8,128)(2,1)S(1)}, bf16[16,2176]{1,0:T(8,128)(2,1)S(1)}, u32[]{:S(2)}, u32[]{:S(2)}) collective-permute-start(bf16[16,2176]{1,0:T(8,128)(2,1)S(1)} %get-tuple-element.49), channel_id=1, source_target_pairs={{0,4},{1,5},{2,6},{3,7},{4,0},{5,1},{6,2},{7,3},{8,12},{9,13},{10,... | collective-permute-start | bytes 208904 | tf_op jit(solution)/shard_map/ppermute | solution.py:436
  64.5 1.1 %collective-permute-start.10 = (bf16[16,2176]{1,0:T(8,128)(2,1)S(1)}, bf16[16,2176]{1,0:T(8,128)(2,1)S(1)}, u32[]{:S(2)}, u32[]{:S(2)}) collective-permute-start(bf16[16,2176]{1,0:T(8,128)(2,1)S(1)} %get-tuple-element.50), channel_id=1, source_target_pairs={{0,8},{1,9},{2,10},{3,11},{4,12},{5,13},{6,14},{7,15},{8,0},{9,1},... | collective-permute-start | bytes 208904 | tf_op jit(solution)/shard_map/ppermute | solution.py:436
  65.5 1.4 %collective-permute-start.11 = (bf16[16,2176]{1,0:T(8,128)(2,1)S(1)}, bf16[16,2176]{1,0:T(8,128)(2,1)S(1)}, u32[]{:S(2)}, u32[]{:S(2)}) collective-permute-start(bf16[16,2176]{1,0:T(8,128)(2,1)S(1)} %get-tuple-element.51), channel_id=1, source_target_pairs={{0,12},{1,13},{2,14},{3,15},{4,8},{5,9},{6,10},{7,11},{8,4},{9,5},... | collective-permute-start | bytes 208904 | tf_op jit(solution)/shard_map/ppermute | solution.py:436
  66.9 0.0 collective-permute-done.12.refs_1_
  66.9 0.1 sum_pieces.3
  67.0 0.1 collective-permute-start.13
  67.1 1.2 %collective-permute-start.14 = (bf16[16,2176]{1,0:T(8,128)(2,1)S(1)}, bf16[16,2176]{1,0:T(8,128)(2,1)S(1)}, u32[]{:S(2)}, u32[]{:S(2)}) collective-permute-start(bf16[16,2176]{1,0:T(8,128)(2,1)S(1)} %get-tuple-element.55), channel_id=1, source_target_pairs={{0,5},{1,4},{2,7},{3,6},{4,1},{5,0},{6,3},{7,2},{8,13},{9,12},{10,... | collective-permute-start | bytes 208904 | tf_op jit(solution)/shard_map/ppermute | solution.py:436
  68.3 0.0 collective-permute-done.9.refs_1_
  68.3 1.9 %collective-permute-start.15 = (bf16[16,2176]{1,0:T(8,128)(2,1)S(1)}, bf16[16,2176]{1,0:T(8,128)(2,1)S(1)}, u32[]{:S(2)}, u32[]{:S(2)}) collective-permute-start(bf16[16,2176]{1,0:T(8,128)(2,1)S(1)} %get-tuple-element.56), channel_id=1, source_target_pairs={{0,9},{1,8},{2,11},{3,10},{4,13},{5,12},{6,15},{7,14},{8,1},{9,0},... | collective-permute-start | bytes 208904 | tf_op jit(solution)/shard_map/ppermute | solution.py:436
  70.2 0.3 collective-permute-done.10.refs_2_
  70.5 1.0 %collective-permute-start.16 = (bf16[16,2176]{1,0:T(8,128)(2,1)S(1)}, bf16[16,2176]{1,0:T(8,128)(2,1)S(1)}, u32[]{:S(2)}, u32[]{:S(2)}) collective-permute-start(bf16[16,2176]{1,0:T(8,128)(2,1)S(1)} %get-tuple-element.57), channel_id=1, source_target_pairs={{0,13},{1,12},{2,15},{3,14},{4,9},{5,8},{6,11},{7,10},{8,5},{9,4},... | collective-permute-start | bytes 208904 | tf_op jit(solution)/shard_map/ppermute | solution.py:436
  71.4 0.4 collective-permute-done.11.refs_3_
  71.8 0.0 collective-permute-done.13.refs_4_
  71.8 2.0 %collective-permute-done.14.refs_5_ = bf16[16,2176]{1,0:T(8,128)(2,1)S(1)} collective-permute-done((bf16[16,2176]{1,0:T(8,128)(2,1)S(1)}, bf16[16,2176]{1,0:T(8,128)(2,1)S(1)}, u32[]{:S(2)}, u32[]{:S(2)}) %collective-permute-start.14) | collective-permute-done | bytes 69664 | tf_op jit(solution)/shard_map/ppermute | solution.py:436
  73.8 0.0 collective-permute-done.15.refs_6_
  73.8 3.1 %collective-permute-done.16.refs_7_ = bf16[16,2176]{1,0:T(8,128)(2,1)S(1)} collective-permute-done((bf16[16,2176]{1,0:T(8,128)(2,1)S(1)}, bf16[16,2176]{1,0:T(8,128)(2,1)S(1)}, u32[]{:S(2)}, u32[]{:S(2)}) %collective-permute-start.16) | collective-permute-done | bytes 69664 | tf_op jit(solution)/shard_map/ppermute | solution.py:436
  76.9 0.0 copy-done.4
  76.9 0.0 copy-done.5
  76.9 0.0 copy-done.6
  76.9 2.0 %combine.1 = (bf16[128,2048]{1,0:T(8,128)(2,1)}, f32[1,128]{1,0:T(1,128)}) custom-call(s32[2]{0:T(128)S(1)} %pad_add_fusion.ids_ref, s32[1,128]{1,0:T(1,128)S(1)} %bitcast.10, s32[2,128]{1,0:T(2,128)S(1)} %bitcast.8, f32[2,128]{1,0:T(2,128)S(1)} %bitcast.11, bf16[16,2176]{1,0:T(8,128)(2,1)S(1)} %get-tuple-element.48.refs_0_, ...), custom_call_target="tpu_custom_call" | custom-call | flops 134217728 | bytes 1048576 | tf_op jit(solution)/shard_map/combine/pallas_call | solution.py:396
  (5 shorter events, 0.1 us)
Async XLA Ops:
  3.8 12.4 %collective-permute-start = (bf16[32,4096]{1,0:T(8,128)(2,1)S(1)}, bf16[32,4096]{1,0:T(8,128)(2,1)S(1)}, u32[]{:S(2)}, u32[]{:S(2)}) collective-permute-start(bf16[32,4096]{1,0:T(8,128)(2,1)S(1)} %get-tuple-element.32), channel_id=1, source_target_pairs={{0,4},{2,6},{4,0},{6,2},{8,12},{10,14},{12,8},{14,10},{1,5},{3,7},... | collective-permute-start | bytes 786440 | tf_op jit(solution)/shard_map/ppermute | solution.py:422
  6.9 11.2 %collective-permute-start.2 = (bf16[16,4096]{1,0:T(8,128)(2,1)S(1)}, bf16[16,4096]{1,0:T(8,128)(2,1)S(1)}, u32[]{:S(2)}, u32[]{:S(2)}) collective-permute-start(bf16[16,4096]{1,0:T(8,128)(2,1)S(1)} %get-tuple-element.33), channel_id=1, source_target_pairs={{0,8},{2,10},{4,12},{6,14},{8,0},{10,2},{12,4},{14,6},{1,9},{3,11}... | collective-permute-start | bytes 393224 | tf_op jit(solution)/shard_map/ppermute | solution.py:422
  9.5 11.6 %collective-permute-start.3 = (bf16[16,4096]{1,0:T(8,128)(2,1)S(1)}, bf16[16,4096]{1,0:T(8,128)(2,1)S(1)}, u32[]{:S(2)}, u32[]{:S(2)}) collective-permute-start(bf16[16,4096]{1,0:T(8,128)(2,1)S(1)} %get-tuple-element.34), channel_id=1, source_target_pairs={{0,12},{2,14},{4,8},{6,10},{8,4},{10,6},{12,0},{14,2},{1,13},{3,15... | collective-permute-start | bytes 393224 | tf_op jit(solution)/shard_map/ppermute | solution.py:422
  13.0 3.3 %copy-start = (bf16[1,4096,1024]{2,1,0:T(8,128)(2,1)}, bf16[1,4096,1024]{2,1,0:T(8,128)(2,1)S(1)}, u32[]{:S(2)}) copy-start(bf16[1,4096,1024]{2,1,0:T(8,128)(2,1)S(1)} %load.2.refs_1_.refs_4_.refs_8_.gate_ref) | copy-start | bytes 25165828
  16.3 22.7 %collective-permute-start.1 = (bf16[64,4096]{1,0:T(8,128)(2,1)S(1)}, bf16[64,4096]{1,0:T(8,128)(2,1)S(1)}, u32[]{:S(2)}, u32[]{:S(2)}) collective-permute-start(bf16[64,4096]{1,0:T(8,128)(2,1)S(1)} %join.3.refs_0_), channel_id=1, source_target_pairs={{0,2},{2,0},{4,6},{6,4},{8,10},{10,8},{12,14},{14,12},{1,3},{3,1},... | collective-permute-start | bytes 1572872 | tf_op jit(solution)/shard_map/ppermute | solution.py:422
  21.2 11.3 %collective-permute-start.4 = (bf16[16,4096]{1,0:T(8,128)(2,1)S(1)}, bf16[16,4096]{1,0:T(8,128)(2,1)S(1)}, u32[]{:S(2)}, u32[]{:S(2)}) collective-permute-start(bf16[16,4096]{1,0:T(8,128)(2,1)S(1)} %get-tuple-element.37), channel_id=1, source_target_pairs={{0,8},{2,10},{4,12},{6,14},{8,0},{10,2},{12,4},{14,6},{1,9},{3,11}... | collective-permute-start | bytes 393224 | tf_op jit(solution)/shard_map/ppermute | solution.py:422
  22.9 9.6 %collective-permute-start.5 = (bf16[16,4096]{1,0:T(8,128)(2,1)S(1)}, bf16[16,4096]{1,0:T(8,128)(2,1)S(1)}, u32[]{:S(2)}, u32[]{:S(2)}) collective-permute-start(bf16[16,4096]{1,0:T(8,128)(2,1)S(1)} %get-tuple-element.38), channel_id=1, source_target_pairs={{0,12},{2,14},{4,8},{6,10},{8,4},{10,6},{12,0},{14,2},{1,13},{3,15... | collective-permute-start | bytes 393224 | tf_op jit(solution)/shard_map/ppermute | solution.py:422
  27.9 3.2 %copy-start.2 = (bf16[1,4096,1024]{2,1,0:T(8,128)(2,1)}, bf16[1,4096,1024]{2,1,0:T(8,128)(2,1)S(1)}, u32[]{:S(2)}) copy-start(bf16[1,4096,1024]{2,1,0:T(8,128)(2,1)S(1)} %load.3.refs_1_.refs_5_.refs_9_.up_ref) | copy-start | bytes 25165828
  31.1 7.9 %collective-permute-start.7 = (bf16[32,4096]{1,0:T(8,128)(2,1)S(1)}, bf16[32,4096]{1,0:T(8,128)(2,1)S(1)}, u32[]{:S(2)}, u32[]{:S(2)}) collective-permute-start(bf16[32,4096]{1,0:T(8,128)(2,1)S(1)} %pass_after.3.refs_2_), channel_id=1, source_target_pairs={{0,2},{2,0},{4,6},{6,4},{8,10},{10,8},{12,14},{14,12},{1,3},{3,1},... | collective-permute-start | bytes 786440 | tf_op jit(solution)/shard_map/ppermute | solution.py:422
  32.5 12.7 %collective-permute-start.6 = (bf16[32,4096]{1,0:T(8,128)(2,1)S(1)}, bf16[32,4096]{1,0:T(8,128)(2,1)S(1)}, u32[]{:S(2)}, u32[]{:S(2)}) collective-permute-start(bf16[32,4096]{1,0:T(8,128)(2,1)S(1)} %join.5.refs_0_.refs_2_), channel_id=1, source_target_pairs={{0,2},{2,0},{4,6},{6,4},{8,10},{10,8},{12,14},{14,12},{1,3},{3,1},... | collective-permute-start | bytes 786440 | tf_op jit(solution)/shard_map/ppermute | solution.py:422
  33.4 5.9 %copy-start.3 = (bf16[1,4096,1024]{2,1,0:T(8,128)(2,1)S(1)}, bf16[1,4096,1024]{2,1,0:T(8,128)(2,1)}, u32[]{:S(2)}) copy-start(bf16[1,4096,1024]{2,1,0:T(8,128)(2,1)} %copy-done.2) | copy-start | bytes 25165828
  39.2 3.4 %copy-start.1 = (bf16[1,4096,1024]{2,1,0:T(8,128)(2,1)S(1)}, bf16[1,4096,1024]{2,1,0:T(8,128)(2,1)}, u32[]{:S(2)}) copy-start(bf16[1,4096,1024]{2,1,0:T(8,128)(2,1)} %copy-done) | copy-start | bytes 25165828
  49.4 27.5 %copy-start.4 = (s32[128,2]{0,1:T(2,128)S(1)}, s32[128,2]{0,1:T(2,128)}, u32[]{:S(2)}) copy-start(s32[128,2]{0,1:T(2,128)} %param.11) | copy-start | bytes 3076
  49.4 27.5 %copy-start.5 = (s32[128]{0:T(128)S(1)}, s32[128]{0:T(128)}, u32[]{:S(2)}) copy-start(s32[128]{0:T(128)} %param.10) | copy-start | bytes 1540
  49.4 27.5 %copy-start.6 = (f32[128,2]{0,1:T(2,128)S(1)}, f32[128,2]{0,1:T(2,128)}, u32[]{:S(2)}) copy-start(f32[128,2]{0,1:T(2,128)} %param.12) | copy-start | bytes 3076
  52.3 8.0 %collective-permute-start.8 = (bf16[64,2176]{1,0:T(8,128)(2,1)S(1)}, bf16[64,2176]{1,0:T(8,128)(2,1)S(1)}, u32[]{:S(2)}, u32[]{:S(2)}) collective-permute-start(bf16[64,2176]{1,0:T(8,128)(2,1)S(1)} %get-tuple-element.47), channel_id=1, source_target_pairs={{0,2},{2,0},{4,6},{6,4},{8,10},{10,8},{12,14},{14,12},{1,3},{3,1},... | collective-permute-start | bytes 835592 | tf_op jit(solution)/shard_map/ppermute | solution.py:422
  53.7 13.3 %collective-permute-start.12 = (bf16[64,2176]{1,0:T(8,128)(2,1)S(1)}, bf16[64,2176]{1,0:T(8,128)(2,1)S(1)}, u32[]{:S(2)}, u32[]{:S(2)}) collective-permute-start(bf16[64,2176]{1,0:T(8,128)(2,1)S(1)} %get-tuple-element.53), channel_id=1, source_target_pairs={{0,2},{2,0},{4,6},{6,4},{8,10},{10,8},{12,14},{14,12},{1,3},{3,1},... | collective-permute-start | bytes 835592 | tf_op jit(solution)/shard_map/ppermute | solution.py:422
  60.4 7.9 %collective-permute-start.9 = (bf16[16,2176]{1,0:T(8,128)(2,1)S(1)}, bf16[16,2176]{1,0:T(8,128)(2,1)S(1)}, u32[]{:S(2)}, u32[]{:S(2)}) collective-permute-start(bf16[16,2176]{1,0:T(8,128)(2,1)S(1)} %get-tuple-element.49), channel_id=1, source_target_pairs={{0,4},{1,5},{2,6},{3,7},{4,0},{5,1},{6,2},{7,3},{8,12},{9,13},{10,... | collective-permute-start | bytes 208904 | tf_op jit(solution)/shard_map/ppermute | solution.py:436
  64.5 6.0 %collective-permute-start.10 = (bf16[16,2176]{1,0:T(8,128)(2,1)S(1)}, bf16[16,2176]{1,0:T(8,128)(2,1)S(1)}, u32[]{:S(2)}, u32[]{:S(2)}) collective-permute-start(bf16[16,2176]{1,0:T(8,128)(2,1)S(1)} %get-tuple-element.50), channel_id=1, source_target_pairs={{0,8},{1,9},{2,10},{3,11},{4,12},{5,13},{6,14},{7,15},{8,0},{9,1},... | collective-permute-start | bytes 208904 | tf_op jit(solution)/shard_map/ppermute | solution.py:436
  65.5 6.3 %collective-permute-start.11 = (bf16[16,2176]{1,0:T(8,128)(2,1)S(1)}, bf16[16,2176]{1,0:T(8,128)(2,1)S(1)}, u32[]{:S(2)}, u32[]{:S(2)}) collective-permute-start(bf16[16,2176]{1,0:T(8,128)(2,1)S(1)} %get-tuple-element.51), channel_id=1, source_target_pairs={{0,12},{1,13},{2,14},{3,15},{4,8},{5,9},{6,10},{7,11},{8,4},{9,5},... | collective-permute-start | bytes 208904 | tf_op jit(solution)/shard_map/ppermute | solution.py:436
  67.0 4.8 %collective-permute-start.13 = (bf16[16,2176]{1,0:T(8,128)(2,1)S(1)}, bf16[16,2176]{1,0:T(8,128)(2,1)S(1)}, u32[]{:S(2)}, u32[]{:S(2)}) collective-permute-start(bf16[16,2176]{1,0:T(8,128)(2,1)S(1)} %get-tuple-element.54), channel_id=1, source_target_pairs={{0,1},{1,0},{2,3},{3,2},{4,5},{5,4},{6,7},{7,6},{8,9},{9,8},{10,11... | collective-permute-start | bytes 208904 | tf_op jit(solution)/shard_map/ppermute | solution.py:436
  67.1 6.7 %collective-permute-start.14 = (bf16[16,2176]{1,0:T(8,128)(2,1)S(1)}, bf16[16,2176]{1,0:T(8,128)(2,1)S(1)}, u32[]{:S(2)}, u32[]{:S(2)}) collective-permute-start(bf16[16,2176]{1,0:T(8,128)(2,1)S(1)} %get-tuple-element.55), channel_id=1, source_target_pairs={{0,5},{1,4},{2,7},{3,6},{4,1},{5,0},{6,3},{7,2},{8,13},{9,12},{10,... | collective-permute-start | bytes 208904 | tf_op jit(solution)/shard_map/ppermute | solution.py:436
  68.3 5.5 %collective-permute-start.15 = (bf16[16,2176]{1,0:T(8,128)(2,1)S(1)}, bf16[16,2176]{1,0:T(8,128)(2,1)S(1)}, u32[]{:S(2)}, u32[]{:S(2)}) collective-permute-start(bf16[16,2176]{1,0:T(8,128)(2,1)S(1)} %get-tuple-element.56), channel_id=1, source_target_pairs={{0,9},{1,8},{2,11},{3,10},{4,13},{5,12},{6,15},{7,14},{8,1},{9,0},... | collective-permute-start | bytes 208904 | tf_op jit(solution)/shard_map/ppermute | solution.py:436
  70.5 6.4 %collective-permute-start.16 = (bf16[16,2176]{1,0:T(8,128)(2,1)S(1)}, bf16[16,2176]{1,0:T(8,128)(2,1)S(1)}, u32[]{:S(2)}, u32[]{:S(2)}) collective-permute-start(bf16[16,2176]{1,0:T(8,128)(2,1)S(1)} %get-tuple-element.57), channel_id=1, source_target_pairs={{0,13},{1,12},{2,15},{3,14},{4,9},{5,8},{6,11},{7,10},{8,5},{9,4},... | collective-permute-start | bytes 208904 | tf_op jit(solution)/shard_map/ppermute | solution.py:436

commit v6 on v5

--- a/solution.py
+++ b/solution.py
@@ -28,11 +28,16 @@
     return lax.dot_general(lhs, rhs, (((1,), (1,)), ((), ())), preferred_element_type=F32)
 
 
-def slot_of_labels(ids_ref, modality_ref, picks_ref):
+def position(groups):
+    return lax.axis_index("ep") // groups, lax.axis_index("mod")
+
+
+def slot_of_labels(groups, modality_ref, picks_ref):
     tok_rows = modality_ref.shape[1]
     label = lax.broadcasted_iota(jnp.int32, (2 * E_MOD, tok_rows), 0)
-    expert = jnp.bitwise_xor(label % E_MOD, ids_ref[0])
-    modal = jnp.bitwise_xor(label // E_MOD, ids_ref[1])
+    own_expert, core = position(groups)
+    expert = jnp.bitwise_xor(label % E_MOD, own_expert)
+    modal = jnp.bitwise_xor(label // E_MOD, core)
     mine = modality_ref[...] == modal
     first = mine & (picks_ref[0:1, :] == expert)
     second = mine & (picks_ref[1:2, :] == expert)
@@ -44,52 +49,67 @@
     return count, first, second, member
 
 
-def gather_kernel(ids_ref, modality_ref, picks_ref, rows_ref, grads_ref, *refs):
-    outs, chosen = refs[:-1], refs[-1]
-
-    @pl.when(pl.program_id(0) == 0)
-    def _():
-        count, _, _, member = slot_of_labels(ids_ref, modality_ref, picks_ref)
-        slot = jnp.where(member, count, -1)
-        want = lax.broadcasted_iota(jnp.int32, (CAP, slot.shape[1]), 0)
-        for s in range(E_MOD):
-            hit = (slot[s : s + 1, :] == want).astype(F32)
-            chosen[s * CAP : (s + 1) * CAP, :] = hit.astype(BF16)
-
-    both = [
-        jnp.dot(chosen[...], ref[...], preferred_element_type=F32).astype(BF16)
-        for ref in (rows_ref, grads_ref)
+def gather_kernel(groups, parts, modality_hbm, picks_hbm, rows_hbm, grads_hbm, *refs):
+    outs, (modality, picks, rows, chosen, sems) = refs[:-5], refs[-5:]
+    chunk = rows.shape[2] // parts
+    small = [
+        pltpu.make_async_copy(src, dst, sems.at[i])
+        for i, (src, dst) in enumerate([(modality_hbm, modality), (picks_hbm, picks)])
     ]
-    for s in range(2):
+    large = [
+        [
+            pltpu.make_async_copy(
+                src.at[:, pl.ds(i * chunk, chunk)],
+                rows.at[a, :, pl.ds(i * chunk, chunk)],
+                sems.at[2 + 2 * i + a],
+            )
+            for a, src in enumerate([rows_hbm, grads_hbm])
+        ]
+        for i in range(parts)
+    ]
+    for copy in small + sum(large, []):
+        copy.start()
+    for copy in small:
+        copy.wait()
+    count, _, _, member = slot_of_labels(groups, modality, picks)
+    slot = jnp.where(member, count, -1)
+    want = lax.broadcasted_iota(jnp.int32, (CAP, slot.shape[1]), 0)
+    for s in range(E_MOD):
+        hit = (slot[s : s + 1, :] == want).astype(F32)
+        chosen[s * CAP : (s + 1) * CAP, :] = hit.astype(BF16)
+    for i in range(parts):
+        cols = slice(i * chunk, (i + 1) * chunk)
         for a in range(2):
-            outs[s][a * CAP : (a + 1) * CAP, :] = both[a][s * CAP : (s + 1) * CAP, :]
-    for s in range(2, E_MOD):
-        for a in range(2):
-            outs[2 * s - 2 + a][...] = both[a][s * CAP : (s + 1) * CAP, :]
-
-
-def gather_slots(ids, modality, picks, rows, grads):
+            large[i][a].wait()
+            picked = jnp.dot(chosen[...], rows[a, :, cols], preferred_element_type=F32).astype(BF16)
+            for s in range(E_MOD):
+                block = picked[s * CAP : (s + 1) * CAP, :]
+                if s < 2:
+                    outs[s][a * CAP : (a + 1) * CAP, cols] = block
+                else:
+                    outs[2 * s - 2 + a][:, cols] = block
+
+
+def gather_slots(groups, modality, picks, rows, grads):
     tok_rows, width = rows.shape
-    chunk = width // 4
+    parts = 4
     heights = [2 * CAP] * 2 + [CAP] * (2 * E_MOD - 4)
-    source = pl.BlockSpec((tok_rows, chunk), lambda i: (0, i))
-    return pl.pallas_call(
-        gather_kernel,
-        grid=(width // chunk,),
-        in_specs=[
-            pl.BlockSpec(memory_space=pltpu.SMEM),
-            whole(modality.shape),
-            whole(picks.shape),
-            source,
-            source,
+    return pl.pallas_call(
+        functools.partial(gather_kernel, groups, parts),
+        in_specs=[pl.BlockSpec(memory_space=pl.ANY)] * 4,
+        out_specs=[pl.BlockSpec(memory_space=pltpu.VMEM)] * len(heights),
+        out_shape=[jax.ShapeDtypeStruct((h, width), BF16) for h in heights],
+        scratch_shapes=[
+            pltpu.VMEM(modality.shape, jnp.int32),
+            pltpu.VMEM(picks.shape, jnp.int32),
+            pltpu.VMEM((2, tok_rows, width), BF16),
+            pltpu.VMEM((E_MOD * CAP, tok_rows), BF16),
+            pltpu.SemaphoreType.DMA((2 + 2 * parts,)),
         ],
-        out_specs=[pl.BlockSpec((h, chunk), lambda i: (0, i)) for h in heights],
-        out_shape=[jax.ShapeDtypeStruct((h, width), BF16) for h in heights],
-        scratch_shapes=[pltpu.VMEM((E_MOD * CAP, tok_rows), BF16)],
         compiler_params=pltpu.CompilerParams(vmem_limit_bytes=SCOPED),
         cost_estimate=cost(4 * E_MOD * CAP * tok_rows * width, 6 * tok_rows * width),
         name="gather_slots",
-    )(ids, in_hbm(modality), in_hbm(picks), in_hbm(rows), in_hbm(grads))
+    )(in_hbm(modality), in_hbm(picks), in_hbm(rows), in_hbm(grads))
 
 
 def load_kernel(parts, src, *refs):
@@ -161,18 +181,18 @@
     pass
 
 
-def pass_after(block, need):
+def pass_after(block, *need):
     place = pl.BlockSpec(memory_space=pl.ANY)
     return pl.pallas_call(
         pass_kernel,
-        in_specs=[place] * 2,
+        in_specs=[place] * (1 + len(need)),
         out_specs=place,
         out_shape=jax.ShapeDtypeStruct(block.shape, block.dtype),
         input_output_aliases={0: 0},
         compiler_params=pltpu.CompilerParams(vmem_limit_bytes=SCOPED),
         cost_estimate=cost(0, 1024),
         name="pass_after",
-    )(block, in_vmem(need))
+    )(block, *[in_vmem(x) for x in need])
 
 
 def join_kernel(count, *refs):
@@ -183,26 +203,19 @@
         start += block.shape[0]
 
 
-def join_and_pass_kernel(count, through, *refs):
-    join_kernel(count, *refs[:count], refs[count + through])
-
-
-def join(blocks, through=()):
+def join(blocks, *need):
     count = len(blocks)
     total = sum(block.shape[0] for block in blocks)
     vmem = pl.BlockSpec(memory_space=pltpu.VMEM)
-    ties = [pl.BlockSpec(memory_space=pl.ANY)] * len(through)
-    return pl.pallas_call(
-        functools.partial(join_and_pass_kernel, count, len(through)),
-        in_specs=[vmem] * count + ties,
-        out_specs=[vmem] + ties,
-        out_shape=[jax.ShapeDtypeStruct((total, blocks[0].shape[1]), BF16)]
-        + [jax.ShapeDtypeStruct(tie.shape, tie.dtype) for tie in through],
-        input_output_aliases={count + i: 1 + i for i in range(len(through))},
-        compiler_params=pltpu.CompilerParams(vmem_limit_bytes=SCOPED),
-        cost_estimate=cost(0, 1024),
+    return pl.pallas_call(
+        functools.partial(join_kernel, count),
+        in_specs=[vmem] * count + [pl.BlockSpec(memory_space=pl.ANY)] * len(need),
+        out_specs=vmem,
+        out_shape=jax.ShapeDtypeStruct((total, blocks[0].shape[1]), BF16),
+        compiler_params=pltpu.CompilerParams(vmem_limit_bytes=SCOPED),
+        cost_estimate=cost(2 * 10**9, 1024),
         name="join",
-    )(*blocks, *through)
+    )(*blocks, *[in_vmem(x) for x in need])
 
 
 def in_hbm(x):
@@ -246,12 +259,13 @@
         out_shape=[jax.ShapeDtypeStruct((total, hidden), F32)] * 3,
         scratch_shapes=[pltpu.VMEM((total, width), BF16)],
         compiler_params=pltpu.CompilerParams(vmem_limit_bytes=SCOPED),
-        cost_estimate=cost(1024, 1024),
+        cost_estimate=cost(5 * 10**9, 1024),
         name="pre_activations",
     )(*blocks, in_vmem(gate_piece), in_vmem(up_piece))
 
 
-def back_columns(groups, half, dgate_ref, dup_ref, part, gate_ref, up_ref, outs):
+def back_columns(groups, flip, dgate_ref, dup_ref, part, gate_ref, up_ref, outs):
+    half = jnp.bitwise_xor(position(groups)[1], flip)
     wide = outs[0].shape[1] - EXT
     own_rows = outs[0].shape[0]
     chunk = 512
@@ -265,7 +279,7 @@
         outs[t][:, wide:] = part[t * own_rows : (t + 1) * own_rows, :]
 
 
-def hidden_kernel(count, places, groups, half_ref, *refs):
+def hidden_kernel(count, places, groups, *refs):
     blocks = refs[:count]
     act_ref, slope_ref, both_ref, down_ref, gate_ref, up_ref = refs[count : count + 6]
     outs = refs[count + 6 : count + 6 + groups]
@@ -281,19 +295,18 @@
         dgate[:, cols] = (grad * slope_ref[:, cols]).astype(BF16)
         dup[:, cols] = (grad * act_ref[:, cols]).astype(BF16)
     part_out[...] = two_terms(part)
-    back_columns(groups, half_ref[0], dgate, dup, part_out[...], gate_ref, up_ref, outs)
-
-
-def hidden_grads(blocks, places, groups, half, factors, down_piece, gate_piece, up_piece):
+    back_columns(groups, 1, dgate, dup, part_out[...], gate_ref, up_ref, outs)
+
+
+def hidden_grads(blocks, places, groups, factors, down_piece, gate_piece, up_piece):
     count = len(blocks)
     _, width, hidden = gate_piece.shape
     total = len(places) * CAP
     shape = (total // groups, width // 2 + EXT)
     vmem = pl.BlockSpec(memory_space=pltpu.VMEM)
-    smem = pl.BlockSpec(memory_space=pltpu.SMEM)
     out = pl.pallas_call(
         functools.partial(hidden_kernel, count, places, groups),
-        in_specs=[smem] + [vmem] * (count + 6),
+        in_specs=[vmem] * (count + 6),
         out_specs=[vmem] * (groups + 3),
         out_shape=[jax.ShapeDtypeStruct(shape, BF16)] * groups
         + [jax.ShapeDtypeStruct((total, hidden), BF16)] * 2
@@ -302,29 +315,28 @@
         compiler_params=pltpu.CompilerParams(vmem_limit_bytes=SCOPED),
         cost_estimate=cost(4 * total * width * hidden, 4 * width * hidden),
         name="hidden_grads",
-    )(half, *blocks, *factors, in_vmem(down_piece), in_vmem(gate_piece), in_vmem(up_piece))
+    )(*blocks, *factors, in_vmem(down_piece), in_vmem(gate_piece), in_vmem(up_piece))
     return out[:groups], out[groups:]
 
 
-def back_kernel(groups, half_ref, dgate_ref, dup_ref, part_ref, gate_ref, up_ref, *outs):
-    back_columns(groups, half_ref[0], dgate_ref, dup_ref, part_ref[...], gate_ref, up_ref, outs)
-
-
-def back_half(groups, half, dgate, dup, part, gate_piece, up_piece):
+def back_kernel(groups, dgate_ref, dup_ref, part_ref, gate_ref, up_ref, *outs):
+    back_columns(groups, 0, dgate_ref, dup_ref, part_ref[...], gate_ref, up_ref, outs)
+
+
+def back_half(groups, dgate, dup, part, gate_piece, up_piece):
     _, width, hidden = gate_piece.shape
     total = dgate.shape[0]
     shape = (total // groups, width // 2 + EXT)
     vmem = pl.BlockSpec(memory_space=pltpu.VMEM)
-    smem = pl.BlockSpec(memory_space=pltpu.SMEM)
     return pl.pallas_call(
         functools.partial(back_kernel, groups),
-        in_specs=[smem] + [vmem] * 5,
+        in_specs=[vmem] * 5,
         out_specs=[vmem] * groups,
         out_shape=[jax.ShapeDtypeStruct(shape, BF16)] * groups,
         compiler_params=pltpu.CompilerParams(vmem_limit_bytes=SCOPED),
         cost_estimate=cost(2 * total * width * hidden, 2 * width * hidden),
         name="back_half",
-    )(half, dgate, dup, part, in_vmem(gate_piece), in_vmem(up_piece))
+    )(dgate, dup, part, in_vmem(gate_piece), in_vmem(up_piece))
 
 
 def two_terms(value):
@@ -358,15 +370,15 @@
     )(*partials)
 
 
-def combine_kernel(ids_ref, modality_ref, picks_ref, weights_ref, *refs):
+def combine_kernel(groups, modality_ref, picks_ref, weights_ref, *refs):
     blocks, (grad_out, gate_out, table) = refs[: 2 * E_MOD], refs[2 * E_MOD :]
     wide = grad_out.shape[1]
     for i in range(2 * E_MOD):
         table[i * CAP : (i + 1) * CAP, :] = blocks[i][...]
-    count, first, second, member = slot_of_labels(ids_ref, modality_ref, picks_ref)
+    count, first, second, member = slot_of_labels(groups, modality_ref, picks_ref)
     slot = jnp.where(member, count, -1)
     scale = jnp.where(first, weights_ref[0:1, :], jnp.where(second, weights_ref[1:2, :], 0.0))
-    own = jnp.where(ids_ref[1] == 0, first.astype(F32), second.astype(F32))
+    own = jnp.where(position(groups)[1] == 0, first.astype(F32), second.astype(F32))
     tok_rows = slot.shape[1]
     want = lax.broadcasted_iota(jnp.int32, (CAP, tok_rows), 0)
     mix = []
@@ -388,14 +400,14 @@
     grad_out[...] = total.astype(BF16)
 
 
-def combine(ids, modality, picks, weights, blocks):
+def combine(groups, modality, picks, weights, blocks):
     tok_rows = modality.shape[1]
     wide = blocks[0].shape[1] - EXT
     count = len(blocks)
     vmem = pl.BlockSpec(memory_space=pltpu.VMEM)
     return pl.pallas_call(
-        combine_kernel,
-        in_specs=[pl.BlockSpec(memory_space=pltpu.SMEM)] + [vmem] * (3 + count),
+        functools.partial(combine_kernel, groups),
+        in_specs=[vmem] * (3 + count),
         out_specs=[vmem] * 2,
         out_shape=[
             jax.ShapeDtypeStruct((tok_rows, wide), BF16),
@@ -405,15 +417,12 @@
         cost_estimate=cost(4 * count * CAP * tok_rows * wide, 4 * tok_rows * wide),
         compiler_params=pltpu.CompilerParams(vmem_limit_bytes=SCOPED),
         name="combine",
-    )(ids, modality, picks, weights, *blocks)
+    )(modality, picks, weights, *blocks)
 
 
 def local(tokens, cotangent, modality, picks, gate_weights, gate_proj, up_proj, down_proj):
     device_count = lax.axis_size("ep")
     groups = device_count // E_MOD
-    core = lax.axis_index("mod")
-    expert = lax.axis_index("ep") // groups
-    ids = jnp.stack([expert, core]).astype(jnp.int32)
     modality = modality.reshape(1, -1)
     picks = picks.T
     weights = gate_weights.T
@@ -444,19 +453,18 @@
             ],
         )
 
-    sent = gather_slots(ids, modality, picks, tokens, cotangent)
-    far = [[to_expert(sent[2 * s - 2], s) for s in range(2, E_MOD)]]
+    sent = gather_slots(groups, modality, picks, tokens, cotangent)
+    far = [[to_expert(sent[2 * s - 2 + a], s) for s in range(2, E_MOD)] for a in range(2)]
     near = to_expert(sent[1], 1)
     gate_piece = load(gate_proj, sent[:1])
-    (near,) = join([pass_after(sent[0], gate_piece), near])
+    near = join([pass_after(sent[0], gate_piece), near])
     near = [near] + [to_piece(near, t) for t in range(1, groups)]
-    far[0], *later = join(far[0], [sent[2 * s - 1] for s in range(2, E_MOD)])
-    far.append([to_expert(x, s) for x, s in zip(later, range(2, E_MOD))])
+    far[0] = join(far[0], gate_piece)
     up_piece = load(up_proj, [far[0]])
-    far[0] = pass_after(far[0], up_piece)
+    far[0] = pass_after(far[0], gate_piece, up_piece)
     far[0] = [far[0]] + [to_piece(far[0], t) for t in range(1, groups)]
-    (far[1],) = join(far[1])
-    down_piece = load_turned(down_proj, [far[1]])
+    down_piece = load_turned(down_proj, [far[0][0], in_vmem(gate_piece), in_vmem(up_piece)])
+    far[1] = join(far[1], gate_piece, up_piece, down_piece)
     far[1] = [far[1]] + [to_piece(far[1], t) for t in range(1, groups)]
     blocks = [near + far[a] for a in range(2)]
     places = [
@@ -469,22 +477,21 @@
         for a in range(2)
     ]
     factors = pre_activations(blocks[0], places[0], gate_piece, up_piece)
-    halves = [(core ^ flip).astype(jnp.int32).reshape(1) for flip in range(2)]
     first, (dgate, dup, part) = hidden_grads(
-        blocks[1], places[1], groups, halves[1], factors, down_piece, gate_piece, up_piece
+        blocks[1], places[1], groups, factors, down_piece, gate_piece, up_piece
     )
     arrived = []
     for flip in (1, 0):
         if flip:
             partials = first
         else:
-            partials = back_half(groups, halves[0], dgate, dup, part, gate_piece, up_piece)
+            partials = back_half(groups, dgate, dup, part, gate_piece, up_piece)
         partials = [partials[0]] + [to_piece(partials[t], groups - t) for t in range(1, groups)]
         sums = sum_pieces(partials)
         arrived.append(
             [sums[s] if s + flip == 0 else to_source(sums[s], s, flip) for s in range(E_MOD)]
         )
-    token_grad, gate_grad = combine(ids, modality, picks, weights, arrived[1] + arrived[0])
+    token_grad, gate_grad = combine(groups, modality, picks, weights, arrived[1] + arrived[0])
     return token_grad, gate_grad.reshape(-1, 1)
 
 

time: 79.1 us -> 72.9 us (0.922)
  local copies, waits for them, and re-layouts: 10.1 us -> 0.02 us
  waiting for transfers between devices: 15.8 us -> 21.9 us
  Pallas kernels: 26.3 us -> 24.9 us
    unnamed x14 -> x6, local copies, waits for them, and re-layouts: 10.1 us -> 0.02 us
    ppermute x10, waiting for transfers between devices: 10.1 us -> 14.9 us  [to_expert(): lax.ppermute(x, 'ep', [(e * groups + j, (e ^ s) * groups + (j + t) % grou...]
    ppermute x7, starting transfers between devices: 10.7 us -> 7.67 us  [to_source(): lax.ppermute(x, ('ep', 'mod'), [((e * groups + j) * 2 + m, ((e ^ s) * gro...]
    ppermute x10, starting transfers between devices: 15.1 us -> 17.4 us  [to_expert(): lax.ppermute(x, 'ep', [(e * groups + j, (e ^ s) * groups + (j + t) % grou...]
    ppermute x7, waiting for transfers between devices: 5.74 us -> 6.98 us  [to_source(): lax.ppermute(x, ('ep', 'mod'), [((e * groups + j) * 2 + m, ((e ^ s) * gro...]
    pallas_call x8, Pallas kernels: 8.05 us -> 6.9 us  [the longest x1 2.9 us: back_half(): pl.pallas_call(functools.partial(back_kernel, groups), in_specs=[vmem] *...]
  transfers between devices with their start and end apart: 17 -> 17, of which waited for: 7 -> 8; matrix products, arithmetic and copies ran while one was open for 0% -> 0% of each run, Pallas kernels for 18% -> 19%
where the time goes in v6:
time: 72.9 us; the launch traced here: 72.7 us
  starting transfers between devices  25.1 us (34%)
  Pallas kernels  24.9 us (34%)
  waiting for transfers between devices  21.9 us (30%)
  between operations  0.79 us (1%)
    ppermute x10, starting transfers between devices, to_expert(): lax.ppermute(x, 'ep', [(e * groups + j, (e ^ s) * groups + (j + t) % grou...  17.4 us
    ppermute x10, waiting for transfers between devices, to_expert(): lax.ppermute(x, 'ep', [(e * groups + j, (e ^ s) * groups + (j + t) % grou...  14.9 us
    ppermute x7, starting transfers between devices, to_source(): lax.ppermute(x, ('ep', 'mod'), [((e * groups + j) * 2 + m, ((e ^ s) * gro...  7.67 us
    ppermute x7, waiting for transfers between devices, to_source(): lax.ppermute(x, ('ep', 'mod'), [((e * groups + j) * 2 + m, ((e ^ s) * gro...  6.98 us
    pallas_call x2, Pallas kernels, load(): pl.pallas_call(functools.partial(load_kernel, parts), in_specs=[pl.BlockS...  6.95 us
    pallas_call x1, Pallas kernels, load_turned(): pl.pallas_call(functools.partial(load_turned_kernel, parts), in_specs=[pl...  4.29 us
    pallas_call x1, Pallas kernels, hidden_grads(): pl.pallas_call(functools.partial(hidden_kernel, count, places, groups), i...  4.04 us
    pallas_call x1, Pallas kernels, back_half(): pl.pallas_call(functools.partial(back_kernel, groups), in_specs=[vmem] *...  2.9 us
  transfers between devices with their start and end apart: 17, of which 8 were waited for; matrix products, arithmetic and copies ran while one was open for 0% of the time, Pallas kernels for 19%

profile of v6, /device:TPU:0, one launch (start us, length us, event | category | flops | bytes accessed | tf_op | source)
XLA Modules:
  0.0 72.7 jit_solution(7989272782514507598)
XLA Ops:
  0.6 2.5 %gather_slots.1 = (bf16[32,4096]{1,0:T(8,128)(2,1)S(1)}, bf16[32,4096]{1,0:T(8,128)(2,1)S(1)}, bf16[16,4096]{1,0:T(8,128)(2,1)S(1)}, bf16[16,4096]{1,0:T(8,128)(...) custom-call(s32[1,128]{1,0:T(1,128)} %bitcast.6, s32[2,128]{1,0:T(2,128)} %bitcast.4, ...), custom_call_target="tpu_custom_call" | custom-call | flops 134217728 | bytes 3145728 | tf_op jit(solution)/shard_map/gather_slots/pallas_call | solution.py:97
  3.1 3.1 %collective-permute-start = (bf16[32,4096]{1,0:T(8,128)(2,1)S(1)}, bf16[32,4096]{1,0:T(8,128)(2,1)S(1)}, u32[]{:S(2)}, u32[]{:S(2)}) collective-permute-start(bf16[32,4096]{1,0:T(8,128)(2,1)S(1)} %get-tuple-element.29), channel_id=1, source_target_pairs={{0,4},{2,6},{4,0},{6,2},{8,12},{10,14},{12,8},{14,10},{1,5},{3,7},... | collective-permute-start | bytes 786440 | tf_op jit(solution)/shard_map/ppermute | solution.py:431
  6.2 2.6 %collective-permute-start.4 = (bf16[16,4096]{1,0:T(8,128)(2,1)S(1)}, bf16[16,4096]{1,0:T(8,128)(2,1)S(1)}, u32[]{:S(2)}, u32[]{:S(2)}) collective-permute-start(bf16[16,4096]{1,0:T(8,128)(2,1)S(1)} %get-tuple-element.32), channel_id=1, source_target_pairs={{0,8},{2,10},{4,12},{6,14},{8,0},{10,2},{12,4},{14,6},{1,9},{3,11}... | collective-permute-start | bytes 393224 | tf_op jit(solution)/shard_map/ppermute | solution.py:431
  8.8 0.0 collective-permute-start.5
  8.8 3.5 %load.2.refs_1_.refs_2_.refs_4_.refs_8_.gate_ref = bf16[1,4096,1024]{2,1,0:T(8,128)(2,1)S(1)} custom-call(bf16[1,4096,1024]{2,1,0:T(8,128)(2,1)} %src.3, bf16[32,4096]{1,0:T(8,128)(2,1)S(1)} %get-tuple-element.28.refs_0_), custom_call_target="tpu_custom_call" | custom-call | bytes 1024 | tf_op jit(solution)/shard_map/load/pallas_call | solution.py:132
  12.3 3.0 %collective-permute-done.refs_1_ = bf16[32,4096]{1,0:T(8,128)(2,1)S(1)} collective-permute-done((bf16[32,4096]{1,0:T(8,128)(2,1)S(1)}, bf16[32,4096]{1,0:T(8,128)(2,1)S(1)}, u32[]{:S(2)}, u32[]{:S(2)}) %collective-permute-start) | collective-permute-done | bytes 262176 | tf_op jit(solution)/shard_map/ppermute | solution.py:431
  15.4 1.7 %collective-permute-start.1 = (bf16[64,4096]{1,0:T(8,128)(2,1)S(1)}, bf16[64,4096]{1,0:T(8,128)(2,1)S(1)}, u32[]{:S(2)}, u32[]{:S(2)}) collective-permute-start(bf16[64,4096]{1,0:T(8,128)(2,1)S(1)} %join.3.refs_0_), channel_id=1, source_target_pairs={{0,2},{2,0},{4,6},{6,4},{8,10},{10,8},{12,14},{14,12},{1,3},{3,1},... | collective-permute-start | bytes 1572872 | tf_op jit(solution)/shard_map/ppermute | solution.py:431
  17.1 2.8 %collective-permute-start.2 = (bf16[16,4096]{1,0:T(8,128)(2,1)S(1)}, bf16[16,4096]{1,0:T(8,128)(2,1)S(1)}, u32[]{:S(2)}, u32[]{:S(2)}) collective-permute-start(bf16[16,4096]{1,0:T(8,128)(2,1)S(1)} %get-tuple-element.30), channel_id=1, source_target_pairs={{0,8},{2,10},{4,12},{6,14},{8,0},{10,2},{12,4},{14,6},{1,9},{3,11}... | collective-permute-start | bytes 393224 | tf_op jit(solution)/shard_map/ppermute | solution.py:431
  19.9 2.9 %collective-permute-start.3 = (bf16[16,4096]{1,0:T(8,128)(2,1)S(1)}, bf16[16,4096]{1,0:T(8,128)(2,1)S(1)}, u32[]{:S(2)}, u32[]{:S(2)}) collective-permute-start(bf16[16,4096]{1,0:T(8,128)(2,1)S(1)} %get-tuple-element.31), channel_id=1, source_target_pairs={{0,12},{2,14},{4,8},{6,10},{8,4},{10,6},{12,0},{14,2},{1,13},{3,15... | collective-permute-start | bytes 393224 | tf_op jit(solution)/shard_map/ppermute | solution.py:431
  22.9 0.0 collective-permute-done.4.refs_0_
  22.9 0.0 collective-permute-done.5.refs_1_
  22.9 3.5 %load.3.refs_2_.refs_3_.refs_5_.refs_9_.up_ref = bf16[1,4096,1024]{2,1,0:T(8,128)(2,1)S(1)} custom-call(bf16[1,4096,1024]{2,1,0:T(8,128)(2,1)} %src.4, bf16[32,4096]{1,0:T(8,128)(2,1)S(1)} %join.4.refs_0_), custom_call_target="tpu_custom_call" | custom-call | bytes 1024 | tf_op jit(solution)/shard_map/load/pallas_call | solution.py:132
  26.4 1.2 %collective-permute-start.7 = (bf16[32,4096]{1,0:T(8,128)(2,1)S(1)}, bf16[32,4096]{1,0:T(8,128)(2,1)S(1)}, u32[]{:S(2)}, u32[]{:S(2)}) collective-permute-start(bf16[32,4096]{1,0:T(8,128)(2,1)S(1)} %pass_after.3.refs_0_.refs_2_), channel_id=1, source_target_pairs={{0,2},{2,0},{4,6},{6,4},{8,10},{10,8},{12,14},{14,12},{1,3},{3,1},... | collective-permute-start | bytes 786440 | tf_op jit(solution)/shard_map/ppermute | solution.py:431
  27.6 4.3 %load_turned.1.refs_4_.refs_7_ = bf16[4096,1024]{1,0:T(8,128)(2,1)S(1)} custom-call(bf16[1,1024,4096]{2,1,0:T(8,128)(2,1)} %src.5, bf16[32,4096]{1,0:T(8,128)(2,1)S(1)} %pass_after.3.refs_0_.refs_2_, bf16[1,4096,1024]{2,1,0:T(8,128)(2,1)S(1)} %load.2.refs_1_.refs_2_.refs_4_.refs_8_.gate_ref, bf16[1,4096,1024]{2,1,0:T(8,128)(2,1)S(1)} %load.3.refs_2_.refs_3_.refs_5_.refs_9_.up_ref), custom_call_target="tpu_custom_call" | custom-call | bytes 1024 | tf_op jit(solution)/shard_map/load_turned/pallas_call | solution.py:165
  31.9 0.0 collective-permute-done.2.refs_0_
  32.0 0.0 collective-permute-done.3.refs_1_
  32.0 0.9 %collective-permute-start.6 = (bf16[32,4096]{1,0:T(8,128)(2,1)S(1)}, bf16[32,4096]{1,0:T(8,128)(2,1)S(1)}, u32[]{:S(2)}, u32[]{:S(2)}) collective-permute-start(bf16[32,4096]{1,0:T(8,128)(2,1)S(1)} %join.5.refs_2_), channel_id=1, source_target_pairs={{0,2},{2,0},{4,6},{6,4},{8,10},{10,8},{12,14},{14,12},{1,3},{3,1},... | collective-permute-start | bytes 786440 | tf_op jit(solution)/shard_map/ppermute | solution.py:431
  32.9 3.0 %collective-permute-done.7.refs_3_ = bf16[32,4096]{1,0:T(8,128)(2,1)S(1)} collective-permute-done((bf16[32,4096]{1,0:T(8,128)(2,1)S(1)}, bf16[32,4096]{1,0:T(8,128)(2,1)S(1)}, u32[]{:S(2)}, u32[]{:S(2)}) %collective-permute-start.7) | collective-permute-done | bytes 262176 | tf_op jit(solution)/shard_map/ppermute | solution.py:431
  35.9 0.0 collective-permute-done.1.refs_1_
  35.9 2.6 %pre_activations.1 = (f32[128,1024]{1,0:T(8,128)S(1)}, f32[128,1024]{1,0:T(8,128)S(1)}, f32[128,1024]{1,0:T(8,128)S(1)}) custom-call(bf16[64,4096]{1,0:T(8,128)(2,1)S(1)} %join.3.refs_0_, bf16[64,4096]{1,0:T(8,128)(2,1)S(1)} %collective-permute-done.1.refs_1_, bf16[32,4096]{1,0:T(8,128)(2,1)S(1)} %pass_after.3.refs_0_.refs_2_, ...), custom_call_target="tpu_custom_call" | custom-call | flops 5000000000 | bytes 1024 | tf_op jit(solution)/shard_map/pre_activations/pallas_call | solution.py:255
  38.5 1.3 %collective-permute-done.6.refs_3_ = bf16[32,4096]{1,0:T(8,128)(2,1)S(1)} collective-permute-done((bf16[32,4096]{1,0:T(8,128)(2,1)S(1)}, bf16[32,4096]{1,0:T(8,128)(2,1)S(1)}, u32[]{:S(2)}, u32[]{:S(2)}) %collective-permute-start.6) | collective-permute-done | bytes 262176 | tf_op jit(solution)/shard_map/ppermute | solution.py:431
  39.8 4.0 %hidden_grads.1 = (bf16[64,2176]{1,0:T(8,128)(2,1)S(1)}, bf16[64,2176]{1,0:T(8,128)(2,1)S(1)}, bf16[128,1024]{1,0:T(8,128)(2,1)S(1)}, bf16[128,1024]{1,0:T(8,128)(2,1)S(1)}, bf16[128,128]{1,0:T(8,128)(2,1)S(1)}) custom-call(bf16[64,4096]{1,0:T(8,128)(2,1)S(1)} %join.3.refs_0_, bf16[64,4096]{1,0:T(8,128)(2,1)S(1)} %collective-permute-done.1.refs_1_, ...), custom_call_target="tpu_custom_call" | custom-call | flops 2147483648 | bytes 16777216 | tf_op jit(solution)/shard_map/hidden_grads/pallas_call | solution.py:307
  43.8 0.0 copy-start
  43.8 0.0 copy-start.1
  43.9 0.0 copy-start.2
  43.9 2.9 %back_half.1 = (bf16[64,2176]{1,0:T(8,128)(2,1)S(1)}, bf16[64,2176]{1,0:T(8,128)(2,1)S(1)}) custom-call(bf16[128,1024]{1,0:T(8,128)(2,1)S(1)} %get-tuple-element.37.dgate_ref, bf16[128,1024]{1,0:T(8,128)(2,1)S(1)} %get-tuple-element.38.dup_ref, bf16[128,128]{1,0:T(8,128)(2,1)S(1)} %get-tuple-element.39.part_ref, ...), custom_call_target="tpu_custom_call" | custom-call | flops 1073741824 | bytes 8388608 | tf_op jit(solution)/shard_map/back_half/pallas_call | solution.py:331
  46.8 1.4 %collective-permute-start.8 = (bf16[64,2176]{1,0:T(8,128)(2,1)S(1)}, bf16[64,2176]{1,0:T(8,128)(2,1)S(1)}, u32[]{:S(2)}, u32[]{:S(2)}) collective-permute-start(bf16[64,2176]{1,0:T(8,128)(2,1)S(1)} %get-tuple-element.41), channel_id=1, source_target_pairs={{0,2},{2,0},{4,6},{6,4},{8,10},{10,8},{12,14},{14,12},{1,3},{3,1},... | collective-permute-start | bytes 835592 | tf_op jit(solution)/shard_map/ppermute | solution.py:431
  48.2 0.7 collective-permute-start.12
  48.9 7.6 %collective-permute-done.8.refs_1_ = bf16[64,2176]{1,0:T(8,128)(2,1)S(1)} collective-permute-done((bf16[64,2176]{1,0:T(8,128)(2,1)S(1)}, bf16[64,2176]{1,0:T(8,128)(2,1)S(1)}, u32[]{:S(2)}, u32[]{:S(2)}) %collective-permute-start.8) | collective-permute-done | bytes 278560 | tf_op jit(solution)/shard_map/ppermute | solution.py:431
  56.4 0.1 sum_pieces.2
  56.5 2.8 %collective-permute-start.9 = (bf16[16,2176]{1,0:T(8,128)(2,1)S(1)}, bf16[16,2176]{1,0:T(8,128)(2,1)S(1)}, u32[]{:S(2)}, u32[]{:S(2)}) collective-permute-start(bf16[16,2176]{1,0:T(8,128)(2,1)S(1)} %get-tuple-element.43), channel_id=1, source_target_pairs={{0,4},{1,5},{2,6},{3,7},{4,0},{5,1},{6,2},{7,3},{8,12},{9,13},{10,... | collective-permute-start | bytes 208904 | tf_op jit(solution)/shard_map/ppermute | solution.py:445
  59.4 0.0 collective-permute-start.10
  59.4 2.4 %collective-permute-start.11 = (bf16[16,2176]{1,0:T(8,128)(2,1)S(1)}, bf16[16,2176]{1,0:T(8,128)(2,1)S(1)}, u32[]{:S(2)}, u32[]{:S(2)}) collective-permute-start(bf16[16,2176]{1,0:T(8,128)(2,1)S(1)} %get-tuple-element.45), channel_id=1, source_target_pairs={{0,12},{1,13},{2,14},{3,15},{4,8},{5,9},{6,10},{7,11},{8,4},{9,5},... | collective-permute-start | bytes 208904 | tf_op jit(solution)/shard_map/ppermute | solution.py:445
  61.8 0.0 collective-permute-done.12.refs_1_
  61.8 0.1 sum_pieces.3
  61.9 0.1 collective-permute-start.13
  62.0 1.2 %collective-permute-start.14 = (bf16[16,2176]{1,0:T(8,128)(2,1)S(1)}, bf16[16,2176]{1,0:T(8,128)(2,1)S(1)}, u32[]{:S(2)}, u32[]{:S(2)}) collective-permute-start(bf16[16,2176]{1,0:T(8,128)(2,1)S(1)} %get-tuple-element.49), channel_id=1, source_target_pairs={{0,5},{1,4},{2,7},{3,6},{4,1},{5,0},{6,3},{7,2},{8,13},{9,12},{10,... | collective-permute-start | bytes 208904 | tf_op jit(solution)/shard_map/ppermute | solution.py:445
  63.2 0.0 collective-permute-done.9.refs_1_
  63.2 0.6 collective-permute-start.15
  63.7 1.9 %collective-permute-done.10.refs_2_ = bf16[16,2176]{1,0:T(8,128)(2,1)S(1)} collective-permute-done((bf16[16,2176]{1,0:T(8,128)(2,1)S(1)}, bf16[16,2176]{1,0:T(8,128)(2,1)S(1)}, u32[]{:S(2)}, u32[]{:S(2)}) %collective-permute-start.10) | collective-permute-done | bytes 69664 | tf_op jit(solution)/shard_map/ppermute | solution.py:445
  65.6 0.6 collective-permute-start.16
  66.2 0.0 collective-permute-done.11.refs_3_
  66.2 0.0 collective-permute-done.13.refs_4_
  66.2 0.8 %collective-permute-done.14.refs_5_ = bf16[16,2176]{1,0:T(8,128)(2,1)S(1)} collective-permute-done((bf16[16,2176]{1,0:T(8,128)(2,1)S(1)}, bf16[16,2176]{1,0:T(8,128)(2,1)S(1)}, u32[]{:S(2)}, u32[]{:S(2)}) %collective-permute-start.14) | collective-permute-done | bytes 69664 | tf_op jit(solution)/shard_map/ppermute | solution.py:445
  67.0 3.5 %collective-permute-done.15.refs_6_ = bf16[16,2176]{1,0:T(8,128)(2,1)S(1)} collective-permute-done((bf16[16,2176]{1,0:T(8,128)(2,1)S(1)}, bf16[16,2176]{1,0:T(8,128)(2,1)S(1)}, u32[]{:S(2)}, u32[]{:S(2)}) %collective-permute-start.15) | collective-permute-done | bytes 69664 | tf_op jit(solution)/shard_map/ppermute | solution.py:445
  70.5 0.7 %collective-permute-done.16.refs_7_ = bf16[16,2176]{1,0:T(8,128)(2,1)S(1)} collective-permute-done((bf16[16,2176]{1,0:T(8,128)(2,1)S(1)}, bf16[16,2176]{1,0:T(8,128)(2,1)S(1)}, u32[]{:S(2)}, u32[]{:S(2)}) %collective-permute-start.16) | collective-permute-done | bytes 69664 | tf_op jit(solution)/shard_map/ppermute | solution.py:445
  71.3 0.0 copy-done
  71.3 0.0 copy-done.1
  71.3 0.0 copy-done.2
  71.3 1.4 %combine.1 = (bf16[128,2048]{1,0:T(8,128)(2,1)}, f32[1,128]{1,0:T(1,128)}) custom-call(s32[1,128]{1,0:T(1,128)S(1)} %bitcast.7, s32[2,128]{1,0:T(2,128)S(1)} %bitcast.5, f32[2,128]{1,0:T(2,128)S(1)} %bitcast.8, bf16[16,2176]{1,0:T(8,128)(2,1)S(1)} %get-tuple-element.42.refs_0_, bf16[16,2176]{1,0:T(8,128)(2,1)S(1)} %collective-permute-done.9.refs_1_, ...), custom_call_target="tpu_custom_call" | custom-call | flops 134217728 | bytes 1048576 | tf_op jit(solution)/shard_map/combine/pallas_call | solution.py:408
  (5 shorter events, 0.1 us)
Async XLA Ops:
  3.1 12.2 %collective-permute-start = (bf16[32,4096]{1,0:T(8,128)(2,1)S(1)}, bf16[32,4096]{1,0:T(8,128)(2,1)S(1)}, u32[]{:S(2)}, u32[]{:S(2)}) collective-permute-start(bf16[32,4096]{1,0:T(8,128)(2,1)S(1)} %get-tuple-element.29), channel_id=1, source_target_pairs={{0,4},{2,6},{4,0},{6,2},{8,12},{10,14},{12,8},{14,10},{1,5},{3,7},... | collective-permute-start | bytes 786440 | tf_op jit(solution)/shard_map/ppermute | solution.py:431
  6.2 16.7 %collective-permute-start.4 = (bf16[16,4096]{1,0:T(8,128)(2,1)S(1)}, bf16[16,4096]{1,0:T(8,128)(2,1)S(1)}, u32[]{:S(2)}, u32[]{:S(2)}) collective-permute-start(bf16[16,4096]{1,0:T(8,128)(2,1)S(1)} %get-tuple-element.32), channel_id=1, source_target_pairs={{0,8},{2,10},{4,12},{6,14},{8,0},{10,2},{12,4},{14,6},{1,9},{3,11}... | collective-permute-start | bytes 393224 | tf_op jit(solution)/shard_map/ppermute | solution.py:431
  8.8 14.1 %collective-permute-start.5 = (bf16[16,4096]{1,0:T(8,128)(2,1)S(1)}, bf16[16,4096]{1,0:T(8,128)(2,1)S(1)}, u32[]{:S(2)}, u32[]{:S(2)}) collective-permute-start(bf16[16,4096]{1,0:T(8,128)(2,1)S(1)} %get-tuple-element.33), channel_id=1, source_target_pairs={{0,12},{2,14},{4,8},{6,10},{8,4},{10,6},{12,0},{14,2},{1,13},{3,15... | collective-permute-start | bytes 393224 | tf_op jit(solution)/shard_map/ppermute | solution.py:431
  15.4 20.5 %collective-permute-start.1 = (bf16[64,4096]{1,0:T(8,128)(2,1)S(1)}, bf16[64,4096]{1,0:T(8,128)(2,1)S(1)}, u32[]{:S(2)}, u32[]{:S(2)}) collective-permute-start(bf16[64,4096]{1,0:T(8,128)(2,1)S(1)} %join.3.refs_0_), channel_id=1, source_target_pairs={{0,2},{2,0},{4,6},{6,4},{8,10},{10,8},{12,14},{14,12},{1,3},{3,1},... | collective-permute-start | bytes 1572872 | tf_op jit(solution)/shard_map/ppermute | solution.py:431
  17.1 14.8 %collective-permute-start.2 = (bf16[16,4096]{1,0:T(8,128)(2,1)S(1)}, bf16[16,4096]{1,0:T(8,128)(2,1)S(1)}, u32[]{:S(2)}, u32[]{:S(2)}) collective-permute-start(bf16[16,4096]{1,0:T(8,128)(2,1)S(1)} %get-tuple-element.30), channel_id=1, source_target_pairs={{0,8},{2,10},{4,12},{6,14},{8,0},{10,2},{12,4},{14,6},{1,9},{3,11}... | collective-permute-start | bytes 393224 | tf_op jit(solution)/shard_map/ppermute | solution.py:431
  19.9 12.0 %collective-permute-start.3 = (bf16[16,4096]{1,0:T(8,128)(2,1)S(1)}, bf16[16,4096]{1,0:T(8,128)(2,1)S(1)}, u32[]{:S(2)}, u32[]{:S(2)}) collective-permute-start(bf16[16,4096]{1,0:T(8,128)(2,1)S(1)} %get-tuple-element.31), channel_id=1, source_target_pairs={{0,12},{2,14},{4,8},{6,10},{8,4},{10,6},{12,0},{14,2},{1,13},{3,15... | collective-permute-start | bytes 393224 | tf_op jit(solution)/shard_map/ppermute | solution.py:431
  26.4 9.5 %collective-permute-start.7 = (bf16[32,4096]{1,0:T(8,128)(2,1)S(1)}, bf16[32,4096]{1,0:T(8,128)(2,1)S(1)}, u32[]{:S(2)}, u32[]{:S(2)}) collective-permute-start(bf16[32,4096]{1,0:T(8,128)(2,1)S(1)} %pass_after.3.refs_0_.refs_2_), channel_id=1, source_target_pairs={{0,2},{2,0},{4,6},{6,4},{8,10},{10,8},{12,14},{14,12},{1,3},{3,1},... | collective-permute-start | bytes 786440 | tf_op jit(solution)/shard_map/ppermute | solution.py:431
  32.0 7.8 %collective-permute-start.6 = (bf16[32,4096]{1,0:T(8,128)(2,1)S(1)}, bf16[32,4096]{1,0:T(8,128)(2,1)S(1)}, u32[]{:S(2)}, u32[]{:S(2)}) collective-permute-start(bf16[32,4096]{1,0:T(8,128)(2,1)S(1)} %join.5.refs_2_), channel_id=1, source_target_pairs={{0,2},{2,0},{4,6},{6,4},{8,10},{10,8},{12,14},{14,12},{1,3},{3,1},... | collective-permute-start | bytes 786440 | tf_op jit(solution)/shard_map/ppermute | solution.py:431
  43.8 27.4 %copy-start = (s32[128,2]{0,1:T(2,128)S(1)}, s32[128,2]{0,1:T(2,128)}, u32[]{:S(2)}) copy-start(s32[128,2]{0,1:T(2,128)} %param.11) | copy-start | bytes 3076
  43.8 27.4 %copy-start.1 = (s32[128]{0:T(128)S(1)}, s32[128]{0:T(128)}, u32[]{:S(2)}) copy-start(s32[128]{0:T(128)} %param.10) | copy-start | bytes 1540
  43.9 27.4 %copy-start.2 = (f32[128,2]{0,1:T(2,128)S(1)}, f32[128,2]{0,1:T(2,128)}, u32[]{:S(2)}) copy-start(f32[128,2]{0,1:T(2,128)} %param.12) | copy-start | bytes 3076
  46.8 9.7 %collective-permute-start.8 = (bf16[64,2176]{1,0:T(8,128)(2,1)S(1)}, bf16[64,2176]{1,0:T(8,128)(2,1)S(1)}, u32[]{:S(2)}, u32[]{:S(2)}) collective-permute-start(bf16[64,2176]{1,0:T(8,128)(2,1)S(1)} %get-tuple-element.41), channel_id=1, source_target_pairs={{0,2},{2,0},{4,6},{6,4},{8,10},{10,8},{12,14},{14,12},{1,3},{3,1},... | collective-permute-start | bytes 835592 | tf_op jit(solution)/shard_map/ppermute | solution.py:431
  48.2 13.6 %collective-permute-start.12 = (bf16[64,2176]{1,0:T(8,128)(2,1)S(1)}, bf16[64,2176]{1,0:T(8,128)(2,1)S(1)}, u32[]{:S(2)}, u32[]{:S(2)}) collective-permute-start(bf16[64,2176]{1,0:T(8,128)(2,1)S(1)} %get-tuple-element.47), channel_id=1, source_target_pairs={{0,2},{2,0},{4,6},{6,4},{8,10},{10,8},{12,14},{14,12},{1,3},{3,1},... | collective-permute-start | bytes 835592 | tf_op jit(solution)/shard_map/ppermute | solution.py:431
  56.5 6.6 %collective-permute-start.9 = (bf16[16,2176]{1,0:T(8,128)(2,1)S(1)}, bf16[16,2176]{1,0:T(8,128)(2,1)S(1)}, u32[]{:S(2)}, u32[]{:S(2)}) collective-permute-start(bf16[16,2176]{1,0:T(8,128)(2,1)S(1)} %get-tuple-element.43), channel_id=1, source_target_pairs={{0,4},{1,5},{2,6},{3,7},{4,0},{5,1},{6,2},{7,3},{8,12},{9,13},{10,... | collective-permute-start | bytes 208904 | tf_op jit(solution)/shard_map/ppermute | solution.py:445
  59.4 6.3 %collective-permute-start.10 = (bf16[16,2176]{1,0:T(8,128)(2,1)S(1)}, bf16[16,2176]{1,0:T(8,128)(2,1)S(1)}, u32[]{:S(2)}, u32[]{:S(2)}) collective-permute-start(bf16[16,2176]{1,0:T(8,128)(2,1)S(1)} %get-tuple-element.44), channel_id=1, source_target_pairs={{0,8},{1,9},{2,10},{3,11},{4,12},{5,13},{6,14},{7,15},{8,0},{9,1},... | collective-permute-start | bytes 208904 | tf_op jit(solution)/shard_map/ppermute | solution.py:445
  59.4 6.8 %collective-permute-start.11 = (bf16[16,2176]{1,0:T(8,128)(2,1)S(1)}, bf16[16,2176]{1,0:T(8,128)(2,1)S(1)}, u32[]{:S(2)}, u32[]{:S(2)}) collective-permute-start(bf16[16,2176]{1,0:T(8,128)(2,1)S(1)} %get-tuple-element.45), channel_id=1, source_target_pairs={{0,12},{1,13},{2,14},{3,15},{4,8},{5,9},{6,10},{7,11},{8,4},{9,5},... | collective-permute-start | bytes 208904 | tf_op jit(solution)/shard_map/ppermute | solution.py:445
  61.9 4.3 %collective-permute-start.13 = (bf16[16,2176]{1,0:T(8,128)(2,1)S(1)}, bf16[16,2176]{1,0:T(8,128)(2,1)S(1)}, u32[]{:S(2)}, u32[]{:S(2)}) collective-permute-start(bf16[16,2176]{1,0:T(8,128)(2,1)S(1)} %get-tuple-element.48), channel_id=1, source_target_pairs={{0,1},{1,0},{2,3},{3,2},{4,5},{5,4},{6,7},{7,6},{8,9},{9,8},{10,11... | collective-permute-start | bytes 208904 | tf_op jit(solution)/shard_map/ppermute | solution.py:445
  62.0 5.0 %collective-permute-start.14 = (bf16[16,2176]{1,0:T(8,128)(2,1)S(1)}, bf16[16,2176]{1,0:T(8,128)(2,1)S(1)}, u32[]{:S(2)}, u32[]{:S(2)}) collective-permute-start(bf16[16,2176]{1,0:T(8,128)(2,1)S(1)} %get-tuple-element.49), channel_id=1, source_target_pairs={{0,5},{1,4},{2,7},{3,6},{4,1},{5,0},{6,3},{7,2},{8,13},{9,12},{10,... | collective-permute-start | bytes 208904 | tf_op jit(solution)/shard_map/ppermute | solution.py:445
  63.2 7.4 %collective-permute-start.15 = (bf16[16,2176]{1,0:T(8,128)(2,1)S(1)}, bf16[16,2176]{1,0:T(8,128)(2,1)S(1)}, u32[]{:S(2)}, u32[]{:S(2)}) collective-permute-start(bf16[16,2176]{1,0:T(8,128)(2,1)S(1)} %get-tuple-element.50), channel_id=1, source_target_pairs={{0,9},{1,8},{2,11},{3,10},{4,13},{5,12},{6,15},{7,14},{8,1},{9,0},... | collective-permute-start | bytes 208904 | tf_op jit(solution)/shard_map/ppermute | solution.py:445
  65.6 5.6 %collective-permute-start.16 = (bf16[16,2176]{1,0:T(8,128)(2,1)S(1)}, bf16[16,2176]{1,0:T(8,128)(2,1)S(1)}, u32[]{:S(2)}, u32[]{:S(2)}) collective-permute-start(bf16[16,2176]{1,0:T(8,128)(2,1)S(1)} %get-tuple-element.51), channel_id=1, source_target_pairs={{0,13},{1,12},{2,15},{3,14},{4,9},{5,8},{6,11},{7,10},{8,5},{9,4},... | collective-permute-start | bytes 208904 | tf_op jit(solution)/shard_map/ppermute | solution.py:445

commit v7 on v6

--- a/solution.py
+++ b/solution.py
@@ -13,7 +13,7 @@
 BF16 = jnp.bfloat16
 F32 = jnp.float32
 MIB = 1024 * 1024
-SCOPED = 16 * MIB
+SCOPED = 12 * MIB
 
 
 def cost(flops, nbytes):
@@ -181,18 +181,18 @@
     pass
 
 
-def pass_after(block, *need):
+def pass_after(blocks, *need):
     place = pl.BlockSpec(memory_space=pl.ANY)
     return pl.pallas_call(
         pass_kernel,
-        in_specs=[place] * (1 + len(need)),
-        out_specs=place,
-        out_shape=jax.ShapeDtypeStruct(block.shape, block.dtype),
-        input_output_aliases={0: 0},
+        in_specs=[place] * (len(blocks) + len(need)),
+        out_specs=[place] * len(blocks),
+        out_shape=[jax.ShapeDtypeStruct(block.shape, block.dtype) for block in blocks],
+        input_output_aliases={i: i for i in range(len(blocks))},
         compiler_params=pltpu.CompilerParams(vmem_limit_bytes=SCOPED),
         cost_estimate=cost(0, 1024),
         name="pass_after",
-    )(block, *[in_vmem(x) for x in need])
+    )(*blocks, *need)
 
 
 def join_kernel(count, *refs):
@@ -215,7 +215,7 @@
         compiler_params=pltpu.CompilerParams(vmem_limit_bytes=SCOPED),
         cost_estimate=cost(2 * 10**9, 1024),
         name="join",
-    )(*blocks, *[in_vmem(x) for x in need])
+    )(*blocks, *need)
 
 
 def in_hbm(x):
@@ -232,7 +232,7 @@
 
 
 def pre_kernel(count, places, *refs):
-    blocks, (gate_ref, up_ref, act_out, slope_out, both_out, rows) = refs[:count], refs[count:]
+    blocks, (gate_ref, up_ref, _, act_out, slope_out, both_out, rows) = refs[:count], refs[count:]
     fill(rows, blocks, places)
     hidden = gate_ref.shape[2]
     chunk = min(256, hidden)
@@ -247,21 +247,21 @@
         both_out[:, cols] = act * up_pre
 
 
-def pre_activations(blocks, places, gate_piece, up_piece):
+def pre_activations(blocks, places, gate_piece, up_piece, need):
     count = len(blocks)
     _, width, hidden = gate_piece.shape
     total = len(places) * CAP
     vmem = pl.BlockSpec(memory_space=pltpu.VMEM)
     return pl.pallas_call(
         functools.partial(pre_kernel, count, places),
-        in_specs=[vmem] * (count + 2),
+        in_specs=[vmem] * (count + 2) + [pl.BlockSpec(memory_space=pl.ANY)],
         out_specs=[vmem] * 3,
         out_shape=[jax.ShapeDtypeStruct((total, hidden), F32)] * 3,
         scratch_shapes=[pltpu.VMEM((total, width), BF16)],
         compiler_params=pltpu.CompilerParams(vmem_limit_bytes=SCOPED),
         cost_estimate=cost(5 * 10**9, 1024),
         name="pre_activations",
-    )(*blocks, in_vmem(gate_piece), in_vmem(up_piece))
+    )(*blocks, in_vmem(gate_piece), in_vmem(up_piece), in_vmem(need))
 
 
 def back_columns(groups, flip, dgate_ref, dup_ref, part, gate_ref, up_ref, outs):
@@ -454,29 +454,31 @@
         )
 
     sent = gather_slots(groups, modality, picks, tokens, cotangent)
-    far = [[to_expert(sent[2 * s - 2 + a], s) for s in range(2, E_MOD)] for a in range(2)]
-    near = to_expert(sent[1], 1)
+    far = [[to_expert(sent[2 * s - 2], s) for s in range(2, E_MOD)]]
+    near = [sent[0], to_expert(sent[1], 1)]
+    near_pieces = [[to_piece(sent[0], t), to_expert(sent[1], 1, t)] for t in range(1, groups)]
     gate_piece = load(gate_proj, sent[:1])
-    near = join([pass_after(sent[0], gate_piece), near])
-    near = [near] + [to_piece(near, t) for t in range(1, groups)]
-    far[0] = join(far[0], gate_piece)
+    later = [sent[2 * s - 1] for s in range(2, E_MOD)]
+    later = pass_after(later, in_vmem(gate_piece), near[1], *sum(near_pieces, []))
+    far.append([to_expert(x, s) for x, s in zip(later, range(2, E_MOD))])
+    far[0] = join(far[0], in_vmem(gate_piece))
     up_piece = load(up_proj, [far[0]])
-    far[0] = pass_after(far[0], gate_piece, up_piece)
     far[0] = [far[0]] + [to_piece(far[0], t) for t in range(1, groups)]
     down_piece = load_turned(down_proj, [far[0][0], in_vmem(gate_piece), in_vmem(up_piece)])
-    far[1] = join(far[1], gate_piece, up_piece, down_piece)
+    far[1] = join(far[1], in_vmem(gate_piece), in_vmem(up_piece), in_vmem(down_piece))
     far[1] = [far[1]] + [to_piece(far[1], t) for t in range(1, groups)]
+    near = near + sum(near_pieces, [])
     blocks = [near + far[a] for a in range(2)]
     places = [
         tuple(
             place
             for t in range(groups)
-            for place in [(t, a * CAP), (t, (2 + a) * CAP)]
-            + [(groups + t, i * CAP) for i in range(E_MOD - 2)]
+            for place in [(2 * t, a * CAP), (2 * t + 1, a * CAP)]
+            + [(2 * groups + t, i * CAP) for i in range(E_MOD - 2)]
         )
         for a in range(2)
     ]
-    factors = pre_activations(blocks[0], places[0], gate_piece, up_piece)
+    factors = pre_activations(blocks[0], places[0], gate_piece, up_piece, down_piece)
     first, (dgate, dup, part) = hidden_grads(
         blocks[1], places[1], groups, factors, down_piece, gate_piece, up_piece
     )

time: 72.9 us -> 78 us (1.070)
  waiting for transfers between devices: 21.9 us -> 24.9 us
  starting transfers between devices: 25.1 us -> 27.2 us
    ppermute x10 -> x11, waiting for transfers between devices: 14.9 us -> 17.3 us  [to_expert(): lax.ppermute(x, 'ep', [(e * groups + j, (e ^ s) * groups + (j + t) % grou...]
    ppermute x10 -> x11, starting transfers between devices: 17.4 us -> 18.8 us  [to_expert(): lax.ppermute(x, 'ep', [(e * groups + j, (e ^ s) * groups + (j + t) % grou...]
  transfers between devices with their start and end apart: 17 -> 18, of which waited for: 8 -> 8; matrix products, arithmetic and copies ran while one was open for 0% -> 0% of each run, Pallas kernels for 19% -> 18%
where the time goes in v7:
time: 78 us; the launch traced here: 77.9 us
  starting transfers between devices  27.2 us (35%)
  Pallas kernels  24.9 us (32%)
  waiting for transfers between devices  24.9 us (32%)
  between operations  0.78 us (1%)
    ppermute x11, starting transfers between devices, to_expert(): lax.ppermute(x, 'ep', [(e * groups + j, (e ^ s) * groups + (j + t) % grou...  18.8 us
    ppermute x11, waiting for transfers between devices, to_expert(): lax.ppermute(x, 'ep', [(e * groups + j, (e ^ s) * groups + (j + t) % grou...  17.3 us
    ppermute x7, starting transfers between devices, to_source(): lax.ppermute(x, ('ep', 'mod'), [((e * groups + j) * 2 + m, ((e ^ s) * gro...  8.43 us
    ppermute x7, waiting for transfers between devices, to_source(): lax.ppermute(x, ('ep', 'mod'), [((e * groups + j) * 2 + m, ((e ^ s) * gro...  7.61 us
    pallas_call x2, Pallas kernels, load(): pl.pallas_call(functools.partial(load_kernel, parts), in_specs=[pl.BlockS...  6.94 us
    pallas_call x1, Pallas kernels, load_turned(): pl.pallas_call(functools.partial(load_turned_kernel, parts), in_specs=[pl...  4.3 us
    pallas_call x1, Pallas kernels, hidden_grads(): pl.pallas_call(functools.partial(hidden_kernel, count, places, groups), i...  4.04 us
    pallas_call x1, Pallas kernels, back_half(): pl.pallas_call(functools.partial(back_kernel, groups), in_specs=[vmem] *...  2.9 us
  transfers between devices with their start and end apart: 18, of which 8 were waited for; matrix products, arithmetic and copies ran while one was open for 0% of the time, Pallas kernels for 18%

profile of v7, /device:TPU:0, one launch (start us, length us, event | category | flops | bytes accessed | tf_op | source)
XLA Modules:
  0.0 77.9 jit_solution(7924457897742431765)
XLA Ops:
  0.6 2.5 %gather_slots.1 = (bf16[32,4096]{1,0:T(8,128)(2,1)S(1)}, bf16[32,4096]{1,0:T(8,128)(2,1)S(1)}, bf16[16,4096]{1,0:T(8,128)(2,1)S(1)}, bf16[16,4096]{1,0:T(8,128)(...) custom-call(s32[1,128]{1,0:T(1,128)} %bitcast.6, s32[2,128]{1,0:T(2,128)} %bitcast.4, ...), custom_call_target="tpu_custom_call" | custom-call | flops 134217728 | bytes 3145728 | tf_op jit(solution)/shard_map/gather_slots/pallas_call | solution.py:97
  3.1 4.0 %collective-permute-start.2 = (bf16[32,4096]{1,0:T(8,128)(2,1)S(1)}, bf16[32,4096]{1,0:T(8,128)(2,1)S(1)}, u32[]{:S(2)}, u32[]{:S(2)}) collective-permute-start(bf16[32,4096]{1,0:T(8,128)(2,1)S(1)} %get-tuple-element.31), channel_id=1, source_target_pairs={{0,6},{2,4},{4,2},{6,0},{8,14},{10,12},{12,10},{14,8},{1,7},{3,5},... | collective-permute-start | bytes 786440 | tf_op jit(solution)/shard_map/ppermute | solution.py:431
  7.2 0.4 collective-permute-start
  7.6 0.2 collective-permute-start.1
  7.8 2.9 %collective-permute-start.5 = (bf16[16,4096]{1,0:T(8,128)(2,1)S(1)}, bf16[16,4096]{1,0:T(8,128)(2,1)S(1)}, u32[]{:S(2)}, u32[]{:S(2)}) collective-permute-start(bf16[16,4096]{1,0:T(8,128)(2,1)S(1)} %get-tuple-element.36), channel_id=1, source_target_pairs={{0,8},{2,10},{4,12},{6,14},{8,0},{10,2},{12,4},{14,6},{1,9},{3,11}... | collective-permute-start | bytes 393224 | tf_op jit(solution)/shard_map/ppermute | solution.py:431
  10.7 1.3 %collective-permute-start.6 = (bf16[16,4096]{1,0:T(8,128)(2,1)S(1)}, bf16[16,4096]{1,0:T(8,128)(2,1)S(1)}, u32[]{:S(2)}, u32[]{:S(2)}) collective-permute-start(bf16[16,4096]{1,0:T(8,128)(2,1)S(1)} %get-tuple-element.37), channel_id=1, source_target_pairs={{0,12},{2,14},{4,8},{6,10},{8,4},{10,6},{12,0},{14,2},{1,13},{3,15... | collective-permute-start | bytes 393224 | tf_op jit(solution)/shard_map/ppermute | solution.py:431
  12.1 3.5 %load.2.refs_2_.refs_1_.refs_6_.refs_10_.gate_ref = bf16[1,4096,1024]{2,1,0:T(8,128)(2,1)S(1)} custom-call(bf16[1,4096,1024]{2,1,0:T(8,128)(2,1)} %src.3, bf16[32,4096]{1,0:T(8,128)(2,1)S(1)} %get-tuple-element.30.refs_0_), custom_call_target="tpu_custom_call" | custom-call | bytes 1024 | tf_op jit(solution)/shard_map/load/pallas_call | solution.py:132
  15.6 1.6 %collective-permute-done.2.refs_5_.refs_3_ = bf16[32,4096]{1,0:T(8,128)(2,1)S(1)} collective-permute-done((bf16[32,4096]{1,0:T(8,128)(2,1)S(1)}, bf16[32,4096]{1,0:T(8,128)(2,1)S(1)}, u32[]{:S(2)}, u32[]{:S(2)}) %collective-permute-start.2) | collective-permute-done | bytes 262176 | tf_op jit(solution)/shard_map/ppermute | solution.py:431
  17.2 5.0 %collective-permute-done.refs_3_.refs_1_ = bf16[32,4096]{1,0:T(8,128)(2,1)S(1)} collective-permute-done((bf16[32,4096]{1,0:T(8,128)(2,1)S(1)}, bf16[32,4096]{1,0:T(8,128)(2,1)S(1)}, u32[]{:S(2)}, u32[]{:S(2)}) %collective-permute-start) | collective-permute-done | bytes 262176 | tf_op jit(solution)/shard_map/ppermute | solution.py:431
  22.1 0.0 collective-permute-done.1.refs_4_.refs_2_
  22.1 2.9 %collective-permute-start.3 = (bf16[16,4096]{1,0:T(8,128)(2,1)S(1)}, bf16[16,4096]{1,0:T(8,128)(2,1)S(1)}, u32[]{:S(2)}, u32[]{:S(2)}) collective-permute-start(bf16[16,4096]{1,0:T(8,128)(2,1)S(1)} %get-tuple-element.34), channel_id=1, source_target_pairs={{0,8},{2,10},{4,12},{6,14},{8,0},{10,2},{12,4},{14,6},{1,9},{3,11}... | collective-permute-start | bytes 393224 | tf_op jit(solution)/shard_map/ppermute | solution.py:431
  25.0 2.7 %collective-permute-start.4 = (bf16[16,4096]{1,0:T(8,128)(2,1)S(1)}, bf16[16,4096]{1,0:T(8,128)(2,1)S(1)}, u32[]{:S(2)}, u32[]{:S(2)}) collective-permute-start(bf16[16,4096]{1,0:T(8,128)(2,1)S(1)} %get-tuple-element.35), channel_id=1, source_target_pairs={{0,12},{2,14},{4,8},{6,10},{8,4},{10,6},{12,0},{14,2},{1,13},{3,15... | collective-permute-start | bytes 393224 | tf_op jit(solution)/shard_map/ppermute | solution.py:431
  27.7 0.0 collective-permute-done.5.refs_0_
  27.7 0.5 collective-permute-done.6.refs_1_
  28.2 0.6 collective-permute-start.8
  28.8 3.5 %load.3.refs_2_.refs_3_.refs_7_.refs_11_.up_ref = bf16[1,4096,1024]{2,1,0:T(8,128)(2,1)S(1)} custom-call(bf16[1,4096,1024]{2,1,0:T(8,128)(2,1)} %src.4, bf16[32,4096]{1,0:T(8,128)(2,1)S(1)} %join.2.refs_0_.refs_4_), custom_call_target="tpu_custom_call" | custom-call | bytes 1024 | tf_op jit(solution)/shard_map/load/pallas_call | solution.py:132
  32.3 4.3 %load_turned.1.refs_4_.refs_8_.refs_9_ = bf16[4096,1024]{1,0:T(8,128)(2,1)S(1)} custom-call(bf16[1,1024,4096]{2,1,0:T(8,128)(2,1)} %src.5, bf16[32,4096]{1,0:T(8,128)(2,1)S(1)} %join.2.refs_0_.refs_4_, bf16[1,4096,1024]{2,1,0:T(8,128)(2,1)S(1)} %load.2.refs_2_.refs_1_.refs_6_.refs_10_.gate_ref, ...), custom_call_target="tpu_custom_call" | custom-call | bytes 1024 | tf_op jit(solution)/shard_map/load_turned/pallas_call | solution.py:165
  36.6 0.0 collective-permute-done.3.refs_0_
  36.6 0.0 collective-permute-done.4.refs_1_
  36.6 1.6 %collective-permute-start.7 = (bf16[32,4096]{1,0:T(8,128)(2,1)S(1)}, bf16[32,4096]{1,0:T(8,128)(2,1)S(1)}, u32[]{:S(2)}, u32[]{:S(2)}) collective-permute-start(bf16[32,4096]{1,0:T(8,128)(2,1)S(1)} %join.3.refs_4_), channel_id=1, source_target_pairs={{0,2},{2,0},{4,6},{6,4},{8,10},{10,8},{12,14},{14,12},{1,3},{3,1},... | collective-permute-start | bytes 786440 | tf_op jit(solution)/shard_map/ppermute | solution.py:431
  38.2 0.0 collective-permute-done.8.refs_5_
  38.2 2.6 %pre_activations.1 = (f32[128,1024]{1,0:T(8,128)S(1)}, f32[128,1024]{1,0:T(8,128)S(1)}, f32[128,1024]{1,0:T(8,128)S(1)}) custom-call(bf16[32,4096]{1,0:T(8,128)(2,1)S(1)} %get-tuple-element.30.refs_0_, bf16[32,4096]{1,0:T(8,128)(2,1)S(1)} %collective-permute-done.refs_3_.refs_1_, bf16[32,4096]{1,0:T(8,128)(2,1)S(1)} %collective-permute-done.1.refs_4_.refs_2_, ...), custom_call_target="tpu_custom_call" | custom-call | flops 5000000000 | bytes 1024 | tf_op jit(solution)/shard_map/pre_activations/pallas_call | solution.py:255
  40.8 2.9 %collective-permute-done.7.refs_5_ = bf16[32,4096]{1,0:T(8,128)(2,1)S(1)} collective-permute-done((bf16[32,4096]{1,0:T(8,128)(2,1)S(1)}, bf16[32,4096]{1,0:T(8,128)(2,1)S(1)}, u32[]{:S(2)}, u32[]{:S(2)}) %collective-permute-start.7) | collective-permute-done | bytes 262176 | tf_op jit(solution)/shard_map/ppermute | solution.py:431
  43.7 4.0 %hidden_grads.1 = (bf16[64,2176]{1,0:T(8,128)(2,1)S(1)}, bf16[64,2176]{1,0:T(8,128)(2,1)S(1)}, bf16[128,1024]{1,0:T(8,128)(2,1)S(1)}, bf16[128,1024]{1,0:T(8,128)(2,1)S(1)}, bf16[128,128]{1,0:T(8,128)(2,1)S(1)}) custom-call(bf16[32,4096]{1,0:T(8,128)(2,1)S(1)} %get-tuple-element.30.refs_0_, bf16[32,4096]{1,0:T(8,128)(2,1)S(1)} %collective-permute-done.refs_3_.refs_1_, ...), custom_call_target="tpu_custom_call" | custom-call | flops 2147483648 | bytes 16777216 | tf_op jit(solution)/shard_map/hidden_grads/pallas_call | solution.py:307
  47.8 0.0 copy-start
  47.8 0.0 copy-start.1
  47.8 0.0 copy-start.2
  47.8 2.9 %back_half.1 = (bf16[64,2176]{1,0:T(8,128)(2,1)S(1)}, bf16[64,2176]{1,0:T(8,128)(2,1)S(1)}) custom-call(bf16[128,1024]{1,0:T(8,128)(2,1)S(1)} %get-tuple-element.41.dgate_ref, bf16[128,1024]{1,0:T(8,128)(2,1)S(1)} %get-tuple-element.42.dup_ref, bf16[128,128]{1,0:T(8,128)(2,1)S(1)} %get-tuple-element.43.part_ref, ...), custom_call_target="tpu_custom_call" | custom-call | flops 1073741824 | bytes 8388608 | tf_op jit(solution)/shard_map/back_half/pallas_call | solution.py:331
  50.7 1.0 %collective-permute-start.9 = (bf16[64,2176]{1,0:T(8,128)(2,1)S(1)}, bf16[64,2176]{1,0:T(8,128)(2,1)S(1)}, u32[]{:S(2)}, u32[]{:S(2)}) collective-permute-start(bf16[64,2176]{1,0:T(8,128)(2,1)S(1)} %get-tuple-element.45), channel_id=1, source_target_pairs={{0,2},{2,0},{4,6},{6,4},{8,10},{10,8},{12,14},{14,12},{1,3},{3,1},... | collective-permute-start | bytes 835592 | tf_op jit(solution)/shard_map/ppermute | solution.py:431
  51.6 1.1 %collective-permute-start.13 = (bf16[64,2176]{1,0:T(8,128)(2,1)S(1)}, bf16[64,2176]{1,0:T(8,128)(2,1)S(1)}, u32[]{:S(2)}, u32[]{:S(2)}) collective-permute-start(bf16[64,2176]{1,0:T(8,128)(2,1)S(1)} %get-tuple-element.51), channel_id=1, source_target_pairs={{0,2},{2,0},{4,6},{6,4},{8,10},{10,8},{12,14},{14,12},{1,3},{3,1},... | collective-permute-start | bytes 835592 | tf_op jit(solution)/shard_map/ppermute | solution.py:431
  52.8 7.4 %collective-permute-done.9.refs_1_ = bf16[64,2176]{1,0:T(8,128)(2,1)S(1)} collective-permute-done((bf16[64,2176]{1,0:T(8,128)(2,1)S(1)}, bf16[64,2176]{1,0:T(8,128)(2,1)S(1)}, u32[]{:S(2)}, u32[]{:S(2)}) %collective-permute-start.9) | collective-permute-done | bytes 278560 | tf_op jit(solution)/shard_map/ppermute | solution.py:431
  60.2 0.1 sum_pieces.2
  60.3 3.6 %collective-permute-start.10 = (bf16[16,2176]{1,0:T(8,128)(2,1)S(1)}, bf16[16,2176]{1,0:T(8,128)(2,1)S(1)}, u32[]{:S(2)}, u32[]{:S(2)}) collective-permute-start(bf16[16,2176]{1,0:T(8,128)(2,1)S(1)} %get-tuple-element.47), channel_id=1, source_target_pairs={{0,4},{1,5},{2,6},{3,7},{4,0},{5,1},{6,2},{7,3},{8,12},{9,13},{10,... | collective-permute-start | bytes 208904 | tf_op jit(solution)/shard_map/ppermute | solution.py:445
  63.9 0.0 collective-permute-start.11
  63.9 2.4 %collective-permute-start.12 = (bf16[16,2176]{1,0:T(8,128)(2,1)S(1)}, bf16[16,2176]{1,0:T(8,128)(2,1)S(1)}, u32[]{:S(2)}, u32[]{:S(2)}) collective-permute-start(bf16[16,2176]{1,0:T(8,128)(2,1)S(1)} %get-tuple-element.49), channel_id=1, source_target_pairs={{0,12},{1,13},{2,14},{3,15},{4,8},{5,9},{6,10},{7,11},{8,4},{9,5},... | collective-permute-start | bytes 208904 | tf_op jit(solution)/shard_map/ppermute | solution.py:445
  66.3 0.0 collective-permute-done.13.refs_1_
  66.3 0.1 sum_pieces.3
  66.4 0.1 collective-permute-start.14
  66.5 1.6 %collective-permute-start.15 = (bf16[16,2176]{1,0:T(8,128)(2,1)S(1)}, bf16[16,2176]{1,0:T(8,128)(2,1)S(1)}, u32[]{:S(2)}, u32[]{:S(2)}) collective-permute-start(bf16[16,2176]{1,0:T(8,128)(2,1)S(1)} %get-tuple-element.53), channel_id=1, source_target_pairs={{0,5},{1,4},{2,7},{3,6},{4,1},{5,0},{6,3},{7,2},{8,13},{9,12},{10,... | collective-permute-start | bytes 208904 | tf_op jit(solution)/shard_map/ppermute | solution.py:445
  68.1 0.0 collective-permute-done.10.refs_1_
  68.1 0.1 collective-permute-start.16
  68.2 1.9 %collective-permute-done.11.refs_2_ = bf16[16,2176]{1,0:T(8,128)(2,1)S(1)} collective-permute-done((bf16[16,2176]{1,0:T(8,128)(2,1)S(1)}, bf16[16,2176]{1,0:T(8,128)(2,1)S(1)}, u32[]{:S(2)}, u32[]{:S(2)}) %collective-permute-start.11) | collective-permute-done | bytes 69664 | tf_op jit(solution)/shard_map/ppermute | solution.py:445
  70.1 0.6 collective-permute-start.17
  70.7 0.0 collective-permute-done.12.refs_3_
  70.7 0.0 collective-permute-done.14.refs_4_
  70.7 0.8 collective-permute-done.15.refs_5_
  71.5 4.9 %collective-permute-done.16.refs_6_ = bf16[16,2176]{1,0:T(8,128)(2,1)S(1)} collective-permute-done((bf16[16,2176]{1,0:T(8,128)(2,1)S(1)}, bf16[16,2176]{1,0:T(8,128)(2,1)S(1)}, u32[]{:S(2)}, u32[]{:S(2)}) %collective-permute-start.16) | collective-permute-done | bytes 69664 | tf_op jit(solution)/shard_map/ppermute | solution.py:445
  76.4 0.0 collective-permute-done.17.refs_7_
  76.4 0.0 copy-done
  76.4 0.0 copy-done.1
  76.4 0.0 copy-done.2
  76.4 1.4 %combine.1 = (bf16[128,2048]{1,0:T(8,128)(2,1)}, f32[1,128]{1,0:T(1,128)}) custom-call(s32[1,128]{1,0:T(1,128)S(1)} %bitcast.7, s32[2,128]{1,0:T(2,128)S(1)} %bitcast.5, f32[2,128]{1,0:T(2,128)S(1)} %bitcast.8, bf16[16,2176]{1,0:T(8,128)(2,1)S(1)} %get-tuple-element.46.refs_0_, bf16[16,2176]{1,0:T(8,128)(2,1)S(1)} %collective-permute-done.10.refs_1_, ...), custom_call_target="tpu_custom_call" | custom-call | flops 134217728 | bytes 1048576 | tf_op jit(solution)/shard_map/combine/pallas_call | solution.py:408
  (3 shorter events, 0.0 us)
Async XLA Ops:
  3.1 14.0 %collective-permute-start.2 = (bf16[32,4096]{1,0:T(8,128)(2,1)S(1)}, bf16[32,4096]{1,0:T(8,128)(2,1)S(1)}, u32[]{:S(2)}, u32[]{:S(2)}) collective-permute-start(bf16[32,4096]{1,0:T(8,128)(2,1)S(1)} %get-tuple-element.31), channel_id=1, source_target_pairs={{0,6},{2,4},{4,2},{6,0},{8,14},{10,12},{12,10},{14,8},{1,7},{3,5},... | collective-permute-start | bytes 786440 | tf_op jit(solution)/shard_map/ppermute | solution.py:431
  7.2 14.9 %collective-permute-start = (bf16[32,4096]{1,0:T(8,128)(2,1)S(1)}, bf16[32,4096]{1,0:T(8,128)(2,1)S(1)}, u32[]{:S(2)}, u32[]{:S(2)}) collective-permute-start(bf16[32,4096]{1,0:T(8,128)(2,1)S(1)} %get-tuple-element.31), channel_id=1, source_target_pairs={{0,4},{2,6},{4,0},{6,2},{8,12},{10,14},{12,8},{14,10},{1,5},{3,7},... | collective-permute-start | bytes 786440 | tf_op jit(solution)/shard_map/ppermute | solution.py:431
  7.6 14.5 %collective-permute-start.1 = (bf16[32,4096]{1,0:T(8,128)(2,1)S(1)}, bf16[32,4096]{1,0:T(8,128)(2,1)S(1)}, u32[]{:S(2)}, u32[]{:S(2)}) collective-permute-start(bf16[32,4096]{1,0:T(8,128)(2,1)S(1)} %get-tuple-element.30.refs_0_), channel_id=1, source_target_pairs={{0,2},{2,0},{4,6},{6,4},{8,10},{10,8},{12,14},{14,12},{1,3},{3,1},... | collective-permute-start | bytes 786440 | tf_op jit(solution)/shard_map/ppermute | solution.py:431
  7.8 19.9 %collective-permute-start.5 = (bf16[16,4096]{1,0:T(8,128)(2,1)S(1)}, bf16[16,4096]{1,0:T(8,128)(2,1)S(1)}, u32[]{:S(2)}, u32[]{:S(2)}) collective-permute-start(bf16[16,4096]{1,0:T(8,128)(2,1)S(1)} %get-tuple-element.36), channel_id=1, source_target_pairs={{0,8},{2,10},{4,12},{6,14},{8,0},{10,2},{12,4},{14,6},{1,9},{3,11}... | collective-permute-start | bytes 393224 | tf_op jit(solution)/shard_map/ppermute | solution.py:431
  10.7 17.5 %collective-permute-start.6 = (bf16[16,4096]{1,0:T(8,128)(2,1)S(1)}, bf16[16,4096]{1,0:T(8,128)(2,1)S(1)}, u32[]{:S(2)}, u32[]{:S(2)}) collective-permute-start(bf16[16,4096]{1,0:T(8,128)(2,1)S(1)} %get-tuple-element.37), channel_id=1, source_target_pairs={{0,12},{2,14},{4,8},{6,10},{8,4},{10,6},{12,0},{14,2},{1,13},{3,15... | collective-permute-start | bytes 393224 | tf_op jit(solution)/shard_map/ppermute | solution.py:431
  22.1 14.5 %collective-permute-start.3 = (bf16[16,4096]{1,0:T(8,128)(2,1)S(1)}, bf16[16,4096]{1,0:T(8,128)(2,1)S(1)}, u32[]{:S(2)}, u32[]{:S(2)}) collective-permute-start(bf16[16,4096]{1,0:T(8,128)(2,1)S(1)} %get-tuple-element.34), channel_id=1, source_target_pairs={{0,8},{2,10},{4,12},{6,14},{8,0},{10,2},{12,4},{14,6},{1,9},{3,11}... | collective-permute-start | bytes 393224 | tf_op jit(solution)/shard_map/ppermute | solution.py:431
  25.0 11.6 %collective-permute-start.4 = (bf16[16,4096]{1,0:T(8,128)(2,1)S(1)}, bf16[16,4096]{1,0:T(8,128)(2,1)S(1)}, u32[]{:S(2)}, u32[]{:S(2)}) collective-permute-start(bf16[16,4096]{1,0:T(8,128)(2,1)S(1)} %get-tuple-element.35), channel_id=1, source_target_pairs={{0,12},{2,14},{4,8},{6,10},{8,4},{10,6},{12,0},{14,2},{1,13},{3,15... | collective-permute-start | bytes 393224 | tf_op jit(solution)/shard_map/ppermute | solution.py:431
  28.2 10.0 %collective-permute-start.8 = (bf16[32,4096]{1,0:T(8,128)(2,1)S(1)}, bf16[32,4096]{1,0:T(8,128)(2,1)S(1)}, u32[]{:S(2)}, u32[]{:S(2)}) collective-permute-start(bf16[32,4096]{1,0:T(8,128)(2,1)S(1)} %join.2.refs_0_.refs_4_), channel_id=1, source_target_pairs={{0,2},{2,0},{4,6},{6,4},{8,10},{10,8},{12,14},{14,12},{1,3},{3,1},... | collective-permute-start | bytes 786440 | tf_op jit(solution)/shard_map/ppermute | solution.py:431
  36.6 7.1 %collective-permute-start.7 = (bf16[32,4096]{1,0:T(8,128)(2,1)S(1)}, bf16[32,4096]{1,0:T(8,128)(2,1)S(1)}, u32[]{:S(2)}, u32[]{:S(2)}) collective-permute-start(bf16[32,4096]{1,0:T(8,128)(2,1)S(1)} %join.3.refs_4_), channel_id=1, source_target_pairs={{0,2},{2,0},{4,6},{6,4},{8,10},{10,8},{12,14},{14,12},{1,3},{3,1},... | collective-permute-start | bytes 786440 | tf_op jit(solution)/shard_map/ppermute | solution.py:431
  47.8 28.7 %copy-start = (s32[128,2]{0,1:T(2,128)S(1)}, s32[128,2]{0,1:T(2,128)}, u32[]{:S(2)}) copy-start(s32[128,2]{0,1:T(2,128)} %param.11) | copy-start | bytes 3076
  47.8 28.7 %copy-start.1 = (s32[128]{0:T(128)S(1)}, s32[128]{0:T(128)}, u32[]{:S(2)}) copy-start(s32[128]{0:T(128)} %param.10) | copy-start | bytes 1540
  47.8 28.6 %copy-start.2 = (f32[128,2]{0,1:T(2,128)S(1)}, f32[128,2]{0,1:T(2,128)}, u32[]{:S(2)}) copy-start(f32[128,2]{0,1:T(2,128)} %param.12) | copy-start | bytes 3076
  50.7 9.5 %collective-permute-start.9 = (bf16[64,2176]{1,0:T(8,128)(2,1)S(1)}, bf16[64,2176]{1,0:T(8,128)(2,1)S(1)}, u32[]{:S(2)}, u32[]{:S(2)}) collective-permute-start(bf16[64,2176]{1,0:T(8,128)(2,1)S(1)} %get-tuple-element.45), channel_id=1, source_target_pairs={{0,2},{2,0},{4,6},{6,4},{8,10},{10,8},{12,14},{14,12},{1,3},{3,1},... | collective-permute-start | bytes 835592 | tf_op jit(solution)/shard_map/ppermute | solution.py:431
  51.6 14.7 %collective-permute-start.13 = (bf16[64,2176]{1,0:T(8,128)(2,1)S(1)}, bf16[64,2176]{1,0:T(8,128)(2,1)S(1)}, u32[]{:S(2)}, u32[]{:S(2)}) collective-permute-start(bf16[64,2176]{1,0:T(8,128)(2,1)S(1)} %get-tuple-element.51), channel_id=1, source_target_pairs={{0,2},{2,0},{4,6},{6,4},{8,10},{10,8},{12,14},{14,12},{1,3},{3,1},... | collective-permute-start | bytes 835592 | tf_op jit(solution)/shard_map/ppermute | solution.py:431
  60.3 7.8 %collective-permute-start.10 = (bf16[16,2176]{1,0:T(8,128)(2,1)S(1)}, bf16[16,2176]{1,0:T(8,128)(2,1)S(1)}, u32[]{:S(2)}, u32[]{:S(2)}) collective-permute-start(bf16[16,2176]{1,0:T(8,128)(2,1)S(1)} %get-tuple-element.47), channel_id=1, source_target_pairs={{0,4},{1,5},{2,6},{3,7},{4,0},{5,1},{6,2},{7,3},{8,12},{9,13},{10,... | collective-permute-start | bytes 208904 | tf_op jit(solution)/shard_map/ppermute | solution.py:445
  63.9 6.3 %collective-permute-start.11 = (bf16[16,2176]{1,0:T(8,128)(2,1)S(1)}, bf16[16,2176]{1,0:T(8,128)(2,1)S(1)}, u32[]{:S(2)}, u32[]{:S(2)}) collective-permute-start(bf16[16,2176]{1,0:T(8,128)(2,1)S(1)} %get-tuple-element.48), channel_id=1, source_target_pairs={{0,8},{1,9},{2,10},{3,11},{4,12},{5,13},{6,14},{7,15},{8,0},{9,1},... | collective-permute-start | bytes 208904 | tf_op jit(solution)/shard_map/ppermute | solution.py:445
  63.9 6.8 %collective-permute-start.12 = (bf16[16,2176]{1,0:T(8,128)(2,1)S(1)}, bf16[16,2176]{1,0:T(8,128)(2,1)S(1)}, u32[]{:S(2)}, u32[]{:S(2)}) collective-permute-start(bf16[16,2176]{1,0:T(8,128)(2,1)S(1)} %get-tuple-element.49), channel_id=1, source_target_pairs={{0,12},{1,13},{2,14},{3,15},{4,8},{5,9},{6,10},{7,11},{8,4},{9,5},... | collective-permute-start | bytes 208904 | tf_op jit(solution)/shard_map/ppermute | solution.py:445
  66.4 4.3 %collective-permute-start.14 = (bf16[16,2176]{1,0:T(8,128)(2,1)S(1)}, bf16[16,2176]{1,0:T(8,128)(2,1)S(1)}, u32[]{:S(2)}, u32[]{:S(2)}) collective-permute-start(bf16[16,2176]{1,0:T(8,128)(2,1)S(1)} %get-tuple-element.52), channel_id=1, source_target_pairs={{0,1},{1,0},{2,3},{3,2},{4,5},{5,4},{6,7},{7,6},{8,9},{9,8},{10,11... | collective-permute-start | bytes 208904 | tf_op jit(solution)/shard_map/ppermute | solution.py:445
  66.5 5.0 %collective-permute-start.15 = (bf16[16,2176]{1,0:T(8,128)(2,1)S(1)}, bf16[16,2176]{1,0:T(8,128)(2,1)S(1)}, u32[]{:S(2)}, u32[]{:S(2)}) collective-permute-start(bf16[16,2176]{1,0:T(8,128)(2,1)S(1)} %get-tuple-element.53), channel_id=1, source_target_pairs={{0,5},{1,4},{2,7},{3,6},{4,1},{5,0},{6,3},{7,2},{8,13},{9,12},{10,... | collective-permute-start | bytes 208904 | tf_op jit(solution)/shard_map/ppermute | solution.py:445
  68.1 8.3 %collective-permute-start.16 = (bf16[16,2176]{1,0:T(8,128)(2,1)S(1)}, bf16[16,2176]{1,0:T(8,128)(2,1)S(1)}, u32[]{:S(2)}, u32[]{:S(2)}) collective-permute-start(bf16[16,2176]{1,0:T(8,128)(2,1)S(1)} %get-tuple-element.54), channel_id=1, source_target_pairs={{0,9},{1,8},{2,11},{3,10},{4,13},{5,12},{6,15},{7,14},{8,1},{9,0},... | collective-permute-start | bytes 208904 | tf_op jit(solution)/shard_map/ppermute | solution.py:445
  70.1 6.3 %collective-permute-start.17 = (bf16[16,2176]{1,0:T(8,128)(2,1)S(1)}, bf16[16,2176]{1,0:T(8,128)(2,1)S(1)}, u32[]{:S(2)}, u32[]{:S(2)}) collective-permute-start(bf16[16,2176]{1,0:T(8,128)(2,1)S(1)} %get-tuple-element.55), channel_id=1, source_target_pairs={{0,13},{1,12},{2,15},{3,14},{4,9},{5,8},{6,11},{7,10},{8,5},{9,4},... | collective-permute-start | bytes 208904 | tf_op jit(solution)/shard_map/ppermute | solution.py:445

commit v8 on v7

--- a/solution.py
+++ b/solution.py
@@ -456,16 +456,17 @@
     sent = gather_slots(groups, modality, picks, tokens, cotangent)
     far = [[to_expert(sent[2 * s - 2], s) for s in range(2, E_MOD)]]
     near = [sent[0], to_expert(sent[1], 1)]
-    near_pieces = [[to_piece(sent[0], t), to_expert(sent[1], 1, t)] for t in range(1, groups)]
+    own_pieces = [to_piece(sent[0], t) for t in range(1, groups)]
     gate_piece = load(gate_proj, sent[:1])
     later = [sent[2 * s - 1] for s in range(2, E_MOD)]
-    later = pass_after(later, in_vmem(gate_piece), near[1], *sum(near_pieces, []))
+    later = pass_after(later, in_vmem(gate_piece), *own_pieces)
     far.append([to_expert(x, s) for x, s in zip(later, range(2, E_MOD))])
-    far[0] = join(far[0], in_vmem(gate_piece))
+    near_pieces = [[x, to_piece(near[1], t)] for t, x in enumerate(own_pieces, 1)]
+    far[0] = join(far[0], in_vmem(gate_piece), near[1])
     up_piece = load(up_proj, [far[0]])
     far[0] = [far[0]] + [to_piece(far[0], t) for t in range(1, groups)]
-    down_piece = load_turned(down_proj, [far[0][0], in_vmem(gate_piece), in_vmem(up_piece)])
-    far[1] = join(far[1], in_vmem(gate_piece), in_vmem(up_piece), in_vmem(down_piece))
+    far[1] = join(far[1], in_vmem(gate_piece), in_vmem(up_piece))
+    down_piece = load_turned(down_proj, [far[1], in_vmem(gate_piece), in_vmem(up_piece)])
     far[1] = [far[1]] + [to_piece(far[1], t) for t in range(1, groups)]
     near = near + sum(near_pieces, [])
     blocks = [near + far[a] for a in range(2)]
@@ -482,13 +483,12 @@
     first, (dgate, dup, part) = hidden_grads(
         blocks[1], places[1], groups, factors, down_piece, gate_piece, up_piece
     )
+    second = back_half(groups, dgate, dup, part, gate_piece, up_piece)
+    first = [first[0]] + [to_piece(first[t], groups - t) for t in range(1, groups)]
+    waiting = pass_after(second[1:], *first[1:])
+    second = [second[0]] + [to_piece(x, groups - t) for t, x in enumerate(waiting, 1)]
     arrived = []
-    for flip in (1, 0):
-        if flip:
-            partials = first
-        else:
-            partials = back_half(groups, dgate, dup, part, gate_piece, up_piece)
-        partials = [partials[0]] + [to_piece(partials[t], groups - t) for t in range(1, groups)]
+    for flip, partials in ((1, first), (0, second)):
         sums = sum_pieces(partials)
         arrived.append(
             [sums[s] if s + flip == 0 else to_source(sums[s], s, flip) for s in range(E_MOD)]

time: 78 us -> 70.8 us (0.908)
  waiting for transfers between devices: 24.9 us -> 18.2 us
    ppermute x11, waiting for transfers between devices: 17.3 us -> 11.1 us  [to_expert(): lax.ppermute(x, 'ep', [(e * groups + j, (e ^ s) * groups + (j + t) % grou...]
    ppermute x11, starting transfers between devices: 18.8 us -> 15.9 us  [to_expert(): lax.ppermute(x, 'ep', [(e * groups + j, (e ^ s) * groups + (j + t) % grou...]
    ppermute x7, starting transfers between devices: 8.43 us -> 10.8 us  [to_source(): lax.ppermute(x, ('ep', 'mod'), [((e * groups + j) * 2 + m, ((e ^ s) * gro...]
  transfers between devices with their start and end apart: 18 -> 18, of which waited for: 8 -> 6; matrix products, arithmetic and copies ran while one was open for 0% -> 0% of each run, Pallas kernels for 18% -> 24%
where the time goes in v8:
time: 70.8 us; the launch traced here: 70.6 us
  starting transfers between devices  26.8 us (38%)
  Pallas kernels  24.9 us (35%)
  waiting for transfers between devices  18.2 us (26%)
  between operations  0.77 us (1%)
    ppermute x11, starting transfers between devices, to_expert(): lax.ppermute(x, 'ep', [(e * groups + j, (e ^ s) * groups + (j + t) % grou...  15.9 us
    ppermute x11, waiting for transfers between devices, to_expert(): lax.ppermute(x, 'ep', [(e * groups + j, (e ^ s) * groups + (j + t) % grou...  11.1 us
    ppermute x7, starting transfers between devices, to_source(): lax.ppermute(x, ('ep', 'mod'), [((e * groups + j) * 2 + m, ((e ^ s) * gro...  10.8 us
    ppermute x7, waiting for transfers between devices, to_source(): lax.ppermute(x, ('ep', 'mod'), [((e * groups + j) * 2 + m, ((e ^ s) * gro...  7.05 us
    pallas_call x2, Pallas kernels, load(): pl.pallas_call(functools.partial(load_kernel, parts), in_specs=[pl.BlockS...  6.94 us
    pallas_call x1, Pallas kernels, load_turned(): pl.pallas_call(functools.partial(load_turned_kernel, parts), in_specs=[pl...  4.29 us
    pallas_call x1, Pallas kernels, hidden_grads(): pl.pallas_call(functools.partial(hidden_kernel, count, places, groups), i...  4.05 us
    pallas_call x1, Pallas kernels, back_half(): pl.pallas_call(functools.partial(back_kernel, groups), in_specs=[vmem] *...  2.9 us
  transfers between devices with their start and end apart: 18, of which 6 were waited for; matrix products, arithmetic and copies ran while one was open for 0% of the time, Pallas kernels for 24%

profile of v8, /device:TPU:0, one launch (start us, length us, event | category | flops | bytes accessed | tf_op | source)
XLA Modules:
  0.0 70.6 jit_solution(7768749780364930540)
XLA Ops:
  0.6 2.5 %gather_slots.1 = (bf16[32,4096]{1,0:T(8,128)(2,1)S(1)}, bf16[32,4096]{1,0:T(8,128)(2,1)S(1)}, bf16[16,4096]{1,0:T(8,128)(2,1)S(1)}, bf16[16,4096]{1,0:T(8,128)(...) custom-call(s32[1,128]{1,0:T(1,128)} %bitcast.6, s32[2,128]{1,0:T(2,128)} %bitcast.4, ...), custom_call_target="tpu_custom_call" | custom-call | flops 134217728 | bytes 3145728 | tf_op jit(solution)/shard_map/gather_slots/pallas_call | solution.py:97
  3.1 3.0 %collective-permute-start.1 = (bf16[32,4096]{1,0:T(8,128)(2,1)S(1)}, bf16[32,4096]{1,0:T(8,128)(2,1)S(1)}, u32[]{:S(2)}, u32[]{:S(2)}) collective-permute-start(bf16[32,4096]{1,0:T(8,128)(2,1)S(1)} %get-tuple-element.30.refs_0_), channel_id=1, source_target_pairs={{0,2},{2,0},{4,6},{6,4},{8,10},{10,8},{12,14},{14,12},{1,3},{3,1},... | collective-permute-start | bytes 786440 | tf_op jit(solution)/shard_map/ppermute | solution.py:431
  6.2 1.6 %collective-permute-start = (bf16[32,4096]{1,0:T(8,128)(2,1)S(1)}, bf16[32,4096]{1,0:T(8,128)(2,1)S(1)}, u32[]{:S(2)}, u32[]{:S(2)}) collective-permute-start(bf16[32,4096]{1,0:T(8,128)(2,1)S(1)} %get-tuple-element.31), channel_id=1, source_target_pairs={{0,4},{2,6},{4,0},{6,2},{8,12},{10,14},{12,8},{14,10},{1,5},{3,7},... | collective-permute-start | bytes 786440 | tf_op jit(solution)/shard_map/ppermute | solution.py:431
  7.7 2.6 %collective-permute-start.5 = (bf16[16,4096]{1,0:T(8,128)(2,1)S(1)}, bf16[16,4096]{1,0:T(8,128)(2,1)S(1)}, u32[]{:S(2)}, u32[]{:S(2)}) collective-permute-start(bf16[16,4096]{1,0:T(8,128)(2,1)S(1)} %get-tuple-element.36), channel_id=1, source_target_pairs={{0,8},{2,10},{4,12},{6,14},{8,0},{10,2},{12,4},{14,6},{1,9},{3,11}... | collective-permute-start | bytes 393224 | tf_op jit(solution)/shard_map/ppermute | solution.py:431
  10.3 0.2 collective-permute-start.6
  10.6 3.5 %load.2.refs_2_.refs_1_.refs_6_.refs_10_.gate_ref = bf16[1,4096,1024]{2,1,0:T(8,128)(2,1)S(1)} custom-call(bf16[1,4096,1024]{2,1,0:T(8,128)(2,1)} %src.3, bf16[32,4096]{1,0:T(8,128)(2,1)S(1)} %get-tuple-element.30.refs_0_), custom_call_target="tpu_custom_call" | custom-call | bytes 1024 | tf_op jit(solution)/shard_map/load/pallas_call | solution.py:132
  14.0 0.0 collective-permute-done.1.refs_3_.refs_2_
  14.1 1.8 %collective-permute-start.3 = (bf16[16,4096]{1,0:T(8,128)(2,1)S(1)}, bf16[16,4096]{1,0:T(8,128)(2,1)S(1)}, u32[]{:S(2)}, u32[]{:S(2)}) collective-permute-start(bf16[16,4096]{1,0:T(8,128)(2,1)S(1)} %get-tuple-element.34), channel_id=1, source_target_pairs={{0,8},{2,10},{4,12},{6,14},{8,0},{10,2},{12,4},{14,6},{1,9},{3,11}... | collective-permute-start | bytes 393224 | tf_op jit(solution)/shard_map/ppermute | solution.py:431
  15.8 2.0 %collective-permute-start.4 = (bf16[16,4096]{1,0:T(8,128)(2,1)S(1)}, bf16[16,4096]{1,0:T(8,128)(2,1)S(1)}, u32[]{:S(2)}, u32[]{:S(2)}) collective-permute-start(bf16[16,4096]{1,0:T(8,128)(2,1)S(1)} %get-tuple-element.35), channel_id=1, source_target_pairs={{0,12},{2,14},{4,8},{6,10},{8,4},{10,6},{12,0},{14,2},{1,13},{3,15... | collective-permute-start | bytes 393224 | tf_op jit(solution)/shard_map/ppermute | solution.py:431
  17.8 0.0 collective-permute-done.refs_3_.refs_1_
  17.8 0.5 collective-permute-start.2
  18.3 0.0 collective-permute-done.5.refs_0_
  18.3 4.8 %collective-permute-done.6.refs_1_ = bf16[16,4096]{1,0:T(8,128)(2,1)S(1)} collective-permute-done((bf16[16,4096]{1,0:T(8,128)(2,1)S(1)}, bf16[16,4096]{1,0:T(8,128)(2,1)S(1)}, u32[]{:S(2)}, u32[]{:S(2)}) %collective-permute-start.6) | collective-permute-done | bytes 131104 | tf_op jit(solution)/shard_map/ppermute | solution.py:431
  23.2 0.6 collective-permute-start.8
  23.7 3.5 %load.3.refs_3_.refs_2_.refs_7_.refs_11_.up_ref = bf16[1,4096,1024]{2,1,0:T(8,128)(2,1)S(1)} custom-call(bf16[1,4096,1024]{2,1,0:T(8,128)(2,1)} %src.4, bf16[32,4096]{1,0:T(8,128)(2,1)S(1)} %join.2.refs_0_.refs_4_), custom_call_target="tpu_custom_call" | custom-call | bytes 1024 | tf_op jit(solution)/shard_map/load/pallas_call | solution.py:132
  27.2 3.7 %collective-permute-done.3.refs_0_ = bf16[16,4096]{1,0:T(8,128)(2,1)S(1)} collective-permute-done((bf16[16,4096]{1,0:T(8,128)(2,1)S(1)}, bf16[16,4096]{1,0:T(8,128)(2,1)S(1)}, u32[]{:S(2)}, u32[]{:S(2)}) %collective-permute-start.3) | collective-permute-done | bytes 131104 | tf_op jit(solution)/shard_map/ppermute | solution.py:431
  30.9 0.0 collective-permute-done.4.refs_1_
  30.9 0.6 collective-permute-start.7
  31.5 4.3 %load_turned.1.refs_8_.refs_9_ = bf16[4096,1024]{1,0:T(8,128)(2,1)S(1)} custom-call(bf16[1,1024,4096]{2,1,0:T(8,128)(2,1)} %src.5, bf16[32,4096]{1,0:T(8,128)(2,1)S(1)} %join.3.refs_0_.refs_4_, bf16[1,4096,1024]{2,1,0:T(8,128)(2,1)S(1)} %load.2.refs_2_.refs_1_.refs_6_.refs_10_.gate_ref, bf16[1,4096,1024]{2,1,0:T(8,128)(2,1)S(1)} %load.3.refs_3_.refs_2_.refs_7_.refs_11_.up_ref), custom_call_target="tpu_custom_call" | custom-call | bytes 1024 | tf_op jit(solution)/shard_map/load_turned/pallas_call | solution.py:165
  35.8 0.0 collective-permute-done.2.refs_3_
  35.8 0.0 collective-permute-done.8.refs_5_
  35.8 2.6 %pre_activations.1 = (f32[128,1024]{1,0:T(8,128)S(1)}, f32[128,1024]{1,0:T(8,128)S(1)}, f32[128,1024]{1,0:T(8,128)S(1)}) custom-call(bf16[32,4096]{1,0:T(8,128)(2,1)S(1)} %get-tuple-element.30.refs_0_, bf16[32,4096]{1,0:T(8,128)(2,1)S(1)} %collective-permute-done.refs_3_.refs_1_, bf16[32,4096]{1,0:T(8,128)(2,1)S(1)} %collective-permute-done.1.refs_3_.refs_2_, ...), custom_call_target="tpu_custom_call" | custom-call | flops 5000000000 | bytes 1024 | tf_op jit(solution)/shard_map/pre_activations/pallas_call | solution.py:255
  38.4 0.0 collective-permute-done.7.refs_5_
  38.4 4.0 %hidden_grads.1 = (bf16[64,2176]{1,0:T(8,128)(2,1)S(1)}, bf16[64,2176]{1,0:T(8,128)(2,1)S(1)}, bf16[128,1024]{1,0:T(8,128)(2,1)S(1)}, bf16[128,1024]{1,0:T(8,128)(2,1)S(1)}, bf16[128,128]{1,0:T(8,128)(2,1)S(1)}) custom-call(bf16[32,4096]{1,0:T(8,128)(2,1)S(1)} %get-tuple-element.30.refs_0_, bf16[32,4096]{1,0:T(8,128)(2,1)S(1)} %collective-permute-done.refs_3_.refs_1_, ...), custom_call_target="tpu_custom_call" | custom-call | flops 2147483648 | bytes 16777216 | tf_op jit(solution)/shard_map/hidden_grads/pallas_call | solution.py:307
  42.5 1.6 %collective-permute-start.9 = (bf16[64,2176]{1,0:T(8,128)(2,1)S(1)}, bf16[64,2176]{1,0:T(8,128)(2,1)S(1)}, u32[]{:S(2)}, u32[]{:S(2)}) collective-permute-start(bf16[64,2176]{1,0:T(8,128)(2,1)S(1)} %get-tuple-element.46), channel_id=1, source_target_pairs={{0,2},{2,0},{4,6},{6,4},{8,10},{10,8},{12,14},{14,12},{1,3},{3,1},... | collective-permute-start | bytes 835592 | tf_op jit(solution)/shard_map/ppermute | solution.py:431
  44.0 0.0 copy-start
  44.0 0.0 copy-start.1
  44.0 0.0 copy-start.2
  44.0 2.9 %back_half.1 = (bf16[64,2176]{1,0:T(8,128)(2,1)S(1)}, bf16[64,2176]{1,0:T(8,128)(2,1)S(1)}) custom-call(bf16[128,1024]{1,0:T(8,128)(2,1)S(1)} %get-tuple-element.41.dgate_ref, bf16[128,1024]{1,0:T(8,128)(2,1)S(1)} %get-tuple-element.42.dup_ref, bf16[128,128]{1,0:T(8,128)(2,1)S(1)} %get-tuple-element.43.part_ref, ...), custom_call_target="tpu_custom_call" | custom-call | flops 1073741824 | bytes 8388608 | tf_op jit(solution)/shard_map/back_half/pallas_call | solution.py:331
  47.0 2.6 %collective-permute-done.9.refs_1_ = bf16[64,2176]{1,0:T(8,128)(2,1)S(1)} collective-permute-done((bf16[64,2176]{1,0:T(8,128)(2,1)S(1)}, bf16[64,2176]{1,0:T(8,128)(2,1)S(1)}, u32[]{:S(2)}, u32[]{:S(2)}) %collective-permute-start.9) | collective-permute-done | bytes 278560 | tf_op jit(solution)/shard_map/ppermute | solution.py:431
  49.6 1.5 %collective-permute-start.10 = (bf16[64,2176]{1,0:T(8,128)(2,1)S(1)}, bf16[64,2176]{1,0:T(8,128)(2,1)S(1)}, u32[]{:S(2)}, u32[]{:S(2)}) collective-permute-start(bf16[64,2176]{1,0:T(8,128)(2,1)S(1)} %pass_after.3), channel_id=1, source_target_pairs={{0,2},{2,0},{4,6},{6,4},{8,10},{10,8},{12,14},{14,12},{1,3},{3,1},... | collective-permute-start | bytes 835592 | tf_op jit(solution)/shard_map/ppermute | solution.py:431
  51.1 0.1 sum_pieces.3
  51.2 0.1 collective-permute-start.14
  51.3 3.5 %collective-permute-start.15 = (bf16[16,2176]{1,0:T(8,128)(2,1)S(1)}, bf16[16,2176]{1,0:T(8,128)(2,1)S(1)}, u32[]{:S(2)}, u32[]{:S(2)}) collective-permute-start(bf16[16,2176]{1,0:T(8,128)(2,1)S(1)} %get-tuple-element.53), channel_id=1, source_target_pairs={{0,5},{1,4},{2,7},{3,6},{4,1},{5,0},{6,3},{7,2},{8,13},{9,12},{10,... | collective-permute-start | bytes 208904 | tf_op jit(solution)/shard_map/ppermute | solution.py:445
  54.8 0.5 collective-permute-start.16
  55.2 1.6 %collective-permute-start.17 = (bf16[16,2176]{1,0:T(8,128)(2,1)S(1)}, bf16[16,2176]{1,0:T(8,128)(2,1)S(1)}, u32[]{:S(2)}, u32[]{:S(2)}) collective-permute-start(bf16[16,2176]{1,0:T(8,128)(2,1)S(1)} %get-tuple-element.55), channel_id=1, source_target_pairs={{0,13},{1,12},{2,15},{3,14},{4,9},{5,8},{6,11},{7,10},{8,5},{9,4},... | collective-permute-start | bytes 208904 | tf_op jit(solution)/shard_map/ppermute | solution.py:445
  56.9 0.0 collective-permute-done.10.refs_1_
  56.9 0.1 sum_pieces.2
  57.0 2.7 %collective-permute-start.11 = (bf16[16,2176]{1,0:T(8,128)(2,1)S(1)}, bf16[16,2176]{1,0:T(8,128)(2,1)S(1)}, u32[]{:S(2)}, u32[]{:S(2)}) collective-permute-start(bf16[16,2176]{1,0:T(8,128)(2,1)S(1)} %get-tuple-element.48), channel_id=1, source_target_pairs={{0,4},{1,5},{2,6},{3,7},{4,0},{5,1},{6,2},{7,3},{8,12},{9,13},{10,... | collective-permute-start | bytes 208904 | tf_op jit(solution)/shard_map/ppermute | solution.py:445
  59.7 0.0 collective-permute-done.14.refs_4_
  59.7 0.6 collective-permute-start.12
  60.3 0.0 collective-permute-done.15.refs_5_
  60.3 1.8 %collective-permute-start.13 = (bf16[16,2176]{1,0:T(8,128)(2,1)S(1)}, bf16[16,2176]{1,0:T(8,128)(2,1)S(1)}, u32[]{:S(2)}, u32[]{:S(2)}) collective-permute-start(bf16[16,2176]{1,0:T(8,128)(2,1)S(1)} %get-tuple-element.50), channel_id=1, source_target_pairs={{0,12},{1,13},{2,14},{3,15},{4,8},{5,9},{6,10},{7,11},{8,4},{9,5},... | collective-permute-start | bytes 208904 | tf_op jit(solution)/shard_map/ppermute | solution.py:445
  62.1 1.2 %collective-permute-done.16.refs_6_ = bf16[16,2176]{1,0:T(8,128)(2,1)S(1)} collective-permute-done((bf16[16,2176]{1,0:T(8,128)(2,1)S(1)}, bf16[16,2176]{1,0:T(8,128)(2,1)S(1)}, u32[]{:S(2)}, u32[]{:S(2)}) %collective-permute-start.16) | collective-permute-done | bytes 69664 | tf_op jit(solution)/shard_map/ppermute | solution.py:445
  63.4 0.0 collective-permute-done.17.refs_7_
  63.4 0.5 collective-permute-done.11.refs_1_
  63.8 5.4 %collective-permute-done.12.refs_2_ = bf16[16,2176]{1,0:T(8,128)(2,1)S(1)} collective-permute-done((bf16[16,2176]{1,0:T(8,128)(2,1)S(1)}, bf16[16,2176]{1,0:T(8,128)(2,1)S(1)}, u32[]{:S(2)}, u32[]{:S(2)}) %collective-permute-start.12) | collective-permute-done | bytes 69664 | tf_op jit(solution)/shard_map/ppermute | solution.py:445
  69.2 0.0 collective-permute-done.13.refs_3_
  69.2 0.0 copy-done
  69.2 0.0 copy-done.1
  69.2 0.0 copy-done.2
  69.2 1.4 %combine.1 = (bf16[128,2048]{1,0:T(8,128)(2,1)}, f32[1,128]{1,0:T(1,128)}) custom-call(s32[1,128]{1,0:T(1,128)S(1)} %bitcast.7, s32[2,128]{1,0:T(2,128)S(1)} %bitcast.5, f32[2,128]{1,0:T(2,128)S(1)} %bitcast.8, bf16[16,2176]{1,0:T(8,128)(2,1)S(1)} %get-tuple-element.47.refs_0_, bf16[16,2176]{1,0:T(8,128)(2,1)S(1)} %collective-permute-done.11.refs_1_, ...), custom_call_target="tpu_custom_call" | custom-call | flops 134217728 | bytes 1048576 | tf_op jit(solution)/shard_map/combine/pallas_call | solution.py:408
  (4 shorter events, 0.0 us)
Async XLA Ops:
  3.1 10.9 %collective-permute-start.1 = (bf16[32,4096]{1,0:T(8,128)(2,1)S(1)}, bf16[32,4096]{1,0:T(8,128)(2,1)S(1)}, u32[]{:S(2)}, u32[]{:S(2)}) collective-permute-start(bf16[32,4096]{1,0:T(8,128)(2,1)S(1)} %get-tuple-element.30.refs_0_), channel_id=1, source_target_pairs={{0,2},{2,0},{4,6},{6,4},{8,10},{10,8},{12,14},{14,12},{1,3},{3,1},... | collective-permute-start | bytes 786440 | tf_op jit(solution)/shard_map/ppermute | solution.py:431
  6.2 11.6 %collective-permute-start = (bf16[32,4096]{1,0:T(8,128)(2,1)S(1)}, bf16[32,4096]{1,0:T(8,128)(2,1)S(1)}, u32[]{:S(2)}, u32[]{:S(2)}) collective-permute-start(bf16[32,4096]{1,0:T(8,128)(2,1)S(1)} %get-tuple-element.31), channel_id=1, source_target_pairs={{0,4},{2,6},{4,0},{6,2},{8,12},{10,14},{12,8},{14,10},{1,5},{3,7},... | collective-permute-start | bytes 786440 | tf_op jit(solution)/shard_map/ppermute | solution.py:431
  7.7 10.6 %collective-permute-start.5 = (bf16[16,4096]{1,0:T(8,128)(2,1)S(1)}, bf16[16,4096]{1,0:T(8,128)(2,1)S(1)}, u32[]{:S(2)}, u32[]{:S(2)}) collective-permute-start(bf16[16,4096]{1,0:T(8,128)(2,1)S(1)} %get-tuple-element.36), channel_id=1, source_target_pairs={{0,8},{2,10},{4,12},{6,14},{8,0},{10,2},{12,4},{14,6},{1,9},{3,11}... | collective-permute-start | bytes 393224 | tf_op jit(solution)/shard_map/ppermute | solution.py:431
  10.3 12.8 %collective-permute-start.6 = (bf16[16,4096]{1,0:T(8,128)(2,1)S(1)}, bf16[16,4096]{1,0:T(8,128)(2,1)S(1)}, u32[]{:S(2)}, u32[]{:S(2)}) collective-permute-start(bf16[16,4096]{1,0:T(8,128)(2,1)S(1)} %get-tuple-element.37), channel_id=1, source_target_pairs={{0,12},{2,14},{4,8},{6,10},{8,4},{10,6},{12,0},{14,2},{1,13},{3,15... | collective-permute-start | bytes 393224 | tf_op jit(solution)/shard_map/ppermute | solution.py:431
  14.1 16.8 %collective-permute-start.3 = (bf16[16,4096]{1,0:T(8,128)(2,1)S(1)}, bf16[16,4096]{1,0:T(8,128)(2,1)S(1)}, u32[]{:S(2)}, u32[]{:S(2)}) collective-permute-start(bf16[16,4096]{1,0:T(8,128)(2,1)S(1)} %get-tuple-element.34), channel_id=1, source_target_pairs={{0,8},{2,10},{4,12},{6,14},{8,0},{10,2},{12,4},{14,6},{1,9},{3,11}... | collective-permute-start | bytes 393224 | tf_op jit(solution)/shard_map/ppermute | solution.py:431
  15.8 15.1 %collective-permute-start.4 = (bf16[16,4096]{1,0:T(8,128)(2,1)S(1)}, bf16[16,4096]{1,0:T(8,128)(2,1)S(1)}, u32[]{:S(2)}, u32[]{:S(2)}) collective-permute-start(bf16[16,4096]{1,0:T(8,128)(2,1)S(1)} %get-tuple-element.35), channel_id=1, source_target_pairs={{0,12},{2,14},{4,8},{6,10},{8,4},{10,6},{12,0},{14,2},{1,13},{3,15... | collective-permute-start | bytes 393224 | tf_op jit(solution)/shard_map/ppermute | solution.py:431
  17.8 18.0 %collective-permute-start.2 = (bf16[32,4096]{1,0:T(8,128)(2,1)S(1)}, bf16[32,4096]{1,0:T(8,128)(2,1)S(1)}, u32[]{:S(2)}, u32[]{:S(2)}) collective-permute-start(bf16[32,4096]{1,0:T(8,128)(2,1)S(1)} %collective-permute-done.refs_3_.refs_1_), channel_id=1, source_target_pairs={{0,2},{2,0},{4,6},{6,4},{8,10},{10,8},{12,14},{14,12},{1,3},{3,1},... | collective-permute-start | bytes 786440 | tf_op jit(solution)/shard_map/ppermute | solution.py:431
  23.2 12.6 %collective-permute-start.8 = (bf16[32,4096]{1,0:T(8,128)(2,1)S(1)}, bf16[32,4096]{1,0:T(8,128)(2,1)S(1)}, u32[]{:S(2)}, u32[]{:S(2)}) collective-permute-start(bf16[32,4096]{1,0:T(8,128)(2,1)S(1)} %join.2.refs_0_.refs_4_), channel_id=1, source_target_pairs={{0,2},{2,0},{4,6},{6,4},{8,10},{10,8},{12,14},{14,12},{1,3},{3,1},... | collective-permute-start | bytes 786440 | tf_op jit(solution)/shard_map/ppermute | solution.py:431
  30.9 7.5 %collective-permute-start.7 = (bf16[32,4096]{1,0:T(8,128)(2,1)S(1)}, bf16[32,4096]{1,0:T(8,128)(2,1)S(1)}, u32[]{:S(2)}, u32[]{:S(2)}) collective-permute-start(bf16[32,4096]{1,0:T(8,128)(2,1)S(1)} %join.3.refs_0_.refs_4_), channel_id=1, source_target_pairs={{0,2},{2,0},{4,6},{6,4},{8,10},{10,8},{12,14},{14,12},{1,3},{3,1},... | collective-permute-start | bytes 786440 | tf_op jit(solution)/shard_map/ppermute | solution.py:431
  42.5 7.1 %collective-permute-start.9 = (bf16[64,2176]{1,0:T(8,128)(2,1)S(1)}, bf16[64,2176]{1,0:T(8,128)(2,1)S(1)}, u32[]{:S(2)}, u32[]{:S(2)}) collective-permute-start(bf16[64,2176]{1,0:T(8,128)(2,1)S(1)} %get-tuple-element.46), channel_id=1, source_target_pairs={{0,2},{2,0},{4,6},{6,4},{8,10},{10,8},{12,14},{14,12},{1,3},{3,1},... | collective-permute-start | bytes 835592 | tf_op jit(solution)/shard_map/ppermute | solution.py:431
  44.0 25.1 %copy-start = (s32[128,2]{0,1:T(2,128)S(1)}, s32[128,2]{0,1:T(2,128)}, u32[]{:S(2)}) copy-start(s32[128,2]{0,1:T(2,128)} %param.11) | copy-start | bytes 3076
  44.0 25.2 %copy-start.1 = (s32[128]{0:T(128)S(1)}, s32[128]{0:T(128)}, u32[]{:S(2)}) copy-start(s32[128]{0:T(128)} %param.10) | copy-start | bytes 1540
  44.0 25.2 %copy-start.2 = (f32[128,2]{0,1:T(2,128)S(1)}, f32[128,2]{0,1:T(2,128)}, u32[]{:S(2)}) copy-start(f32[128,2]{0,1:T(2,128)} %param.12) | copy-start | bytes 3076
  49.6 7.3 %collective-permute-start.10 = (bf16[64,2176]{1,0:T(8,128)(2,1)S(1)}, bf16[64,2176]{1,0:T(8,128)(2,1)S(1)}, u32[]{:S(2)}, u32[]{:S(2)}) collective-permute-start(bf16[64,2176]{1,0:T(8,128)(2,1)S(1)} %pass_after.3), channel_id=1, source_target_pairs={{0,2},{2,0},{4,6},{6,4},{8,10},{10,8},{12,14},{14,12},{1,3},{3,1},... | collective-permute-start | bytes 835592 | tf_op jit(solution)/shard_map/ppermute | solution.py:431
  51.2 8.5 %collective-permute-start.14 = (bf16[16,2176]{1,0:T(8,128)(2,1)S(1)}, bf16[16,2176]{1,0:T(8,128)(2,1)S(1)}, u32[]{:S(2)}, u32[]{:S(2)}) collective-permute-start(bf16[16,2176]{1,0:T(8,128)(2,1)S(1)} %get-tuple-element.52), channel_id=1, source_target_pairs={{0,1},{1,0},{2,3},{3,2},{4,5},{5,4},{6,7},{7,6},{8,9},{9,8},{10,11... | collective-permute-start | bytes 208904 | tf_op jit(solution)/shard_map/ppermute | solution.py:445
  51.3 9.1 %collective-permute-start.15 = (bf16[16,2176]{1,0:T(8,128)(2,1)S(1)}, bf16[16,2176]{1,0:T(8,128)(2,1)S(1)}, u32[]{:S(2)}, u32[]{:S(2)}) collective-permute-start(bf16[16,2176]{1,0:T(8,128)(2,1)S(1)} %get-tuple-element.53), channel_id=1, source_target_pairs={{0,5},{1,4},{2,7},{3,6},{4,1},{5,0},{6,3},{7,2},{8,13},{9,12},{10,... | collective-permute-start | bytes 208904 | tf_op jit(solution)/shard_map/ppermute | solution.py:445
  54.8 8.6 %collective-permute-start.16 = (bf16[16,2176]{1,0:T(8,128)(2,1)S(1)}, bf16[16,2176]{1,0:T(8,128)(2,1)S(1)}, u32[]{:S(2)}, u32[]{:S(2)}) collective-permute-start(bf16[16,2176]{1,0:T(8,128)(2,1)S(1)} %get-tuple-element.54), channel_id=1, source_target_pairs={{0,9},{1,8},{2,11},{3,10},{4,13},{5,12},{6,15},{7,14},{8,1},{9,0},... | collective-permute-start | bytes 208904 | tf_op jit(solution)/shard_map/ppermute | solution.py:445
  55.2 8.1 %collective-permute-start.17 = (bf16[16,2176]{1,0:T(8,128)(2,1)S(1)}, bf16[16,2176]{1,0:T(8,128)(2,1)S(1)}, u32[]{:S(2)}, u32[]{:S(2)}) collective-permute-start(bf16[16,2176]{1,0:T(8,128)(2,1)S(1)} %get-tuple-element.55), channel_id=1, source_target_pairs={{0,13},{1,12},{2,15},{3,14},{4,9},{5,8},{6,11},{7,10},{8,5},{9,4},... | collective-permute-start | bytes 208904 | tf_op jit(solution)/shard_map/ppermute | solution.py:445
  57.0 6.9 %collective-permute-start.11 = (bf16[16,2176]{1,0:T(8,128)(2,1)S(1)}, bf16[16,2176]{1,0:T(8,128)(2,1)S(1)}, u32[]{:S(2)}, u32[]{:S(2)}) collective-permute-start(bf16[16,2176]{1,0:T(8,128)(2,1)S(1)} %get-tuple-element.48), channel_id=1, source_target_pairs={{0,4},{1,5},{2,6},{3,7},{4,0},{5,1},{6,2},{7,3},{8,12},{9,13},{10,... | collective-permute-start | bytes 208904 | tf_op jit(solution)/shard_map/ppermute | solution.py:445
  59.7 9.5 %collective-permute-start.12 = (bf16[16,2176]{1,0:T(8,128)(2,1)S(1)}, bf16[16,2176]{1,0:T(8,128)(2,1)S(1)}, u32[]{:S(2)}, u32[]{:S(2)}) collective-permute-start(bf16[16,2176]{1,0:T(8,128)(2,1)S(1)} %get-tuple-element.49), channel_id=1, source_target_pairs={{0,8},{1,9},{2,10},{3,11},{4,12},{5,13},{6,14},{7,15},{8,0},{9,1},... | collective-permute-start | bytes 208904 | tf_op jit(solution)/shard_map/ppermute | solution.py:445
  60.3 8.8 %collective-permute-start.13 = (bf16[16,2176]{1,0:T(8,128)(2,1)S(1)}, bf16[16,2176]{1,0:T(8,128)(2,1)S(1)}, u32[]{:S(2)}, u32[]{:S(2)}) collective-permute-start(bf16[16,2176]{1,0:T(8,128)(2,1)S(1)} %get-tuple-element.50), channel_id=1, source_target_pairs={{0,12},{1,13},{2,14},{3,15},{4,8},{5,9},{6,10},{7,11},{8,4},{9,5},... | collective-permute-start | bytes 208904 | tf_op jit(solution)/shard_map/ppermute | solution.py:445

commit v9 on v8

--- a/solution.py
+++ b/solution.py
@@ -13,7 +13,7 @@
 BF16 = jnp.bfloat16
 F32 = jnp.float32
 MIB = 1024 * 1024
-SCOPED = 12 * MIB
+SCOPED = 10 * MIB
 
 
 def cost(flops, nbytes):
@@ -136,7 +136,7 @@
         out_shape=pltpu.VMEM(weight.shape, weight.dtype),
         scratch_shapes=[pltpu.SemaphoreType.DMA((parts,))],
         compiler_params=pltpu.CompilerParams(vmem_limit_bytes=SCOPED),
-        cost_estimate=cost(0, 1024),
+        cost_estimate=cost(2 * 10**9, 1024),
         name="load",
     )(in_hbm(weight), *after)
 
@@ -172,7 +172,7 @@
             pltpu.SemaphoreType.DMA((parts,)),
         ],
         compiler_params=pltpu.CompilerParams(vmem_limit_bytes=SCOPED),
-        cost_estimate=cost(0, 1024),
+        cost_estimate=cost(10 * 10**9, 1024),
         name="load_turned",
     )(in_hbm(weight), *after)
 
@@ -190,7 +190,7 @@
         out_shape=[jax.ShapeDtypeStruct(block.shape, block.dtype) for block in blocks],
         input_output_aliases={i: i for i in range(len(blocks))},
         compiler_params=pltpu.CompilerParams(vmem_limit_bytes=SCOPED),
-        cost_estimate=cost(0, 1024),
+        cost_estimate=cost(2 * 10**9, 1024),
         name="pass_after",
     )(*blocks, *need)
 
@@ -370,11 +370,11 @@
     )(*partials)
 
 
-def combine_kernel(groups, modality_ref, picks_ref, weights_ref, *refs):
+def combine_kernel(groups, order, modality_ref, picks_ref, weights_ref, *refs):
     blocks, (grad_out, gate_out, table) = refs[: 2 * E_MOD], refs[2 * E_MOD :]
     wide = grad_out.shape[1]
-    for i in range(2 * E_MOD):
-        table[i * CAP : (i + 1) * CAP, :] = blocks[i][...]
+    for i, block in zip(order, blocks):
+        table[i * CAP : (i + 1) * CAP, :] = block[...]
     count, first, second, member = slot_of_labels(groups, modality_ref, picks_ref)
     slot = jnp.where(member, count, -1)
     scale = jnp.where(first, weights_ref[0:1, :], jnp.where(second, weights_ref[1:2, :], 0.0))
@@ -400,13 +400,13 @@
     grad_out[...] = total.astype(BF16)
 
 
-def combine(groups, modality, picks, weights, blocks):
+def combine(groups, order, modality, picks, weights, blocks):
     tok_rows = modality.shape[1]
     wide = blocks[0].shape[1] - EXT
     count = len(blocks)
     vmem = pl.BlockSpec(memory_space=pltpu.VMEM)
     return pl.pallas_call(
-        functools.partial(combine_kernel, groups),
+        functools.partial(combine_kernel, groups, order),
         in_specs=[vmem] * (3 + count),
         out_specs=[vmem] * 2,
         out_shape=[
@@ -459,14 +459,14 @@
     own_pieces = [to_piece(sent[0], t) for t in range(1, groups)]
     gate_piece = load(gate_proj, sent[:1])
     later = [sent[2 * s - 1] for s in range(2, E_MOD)]
-    later = pass_after(later, in_vmem(gate_piece), *own_pieces)
+    later = pass_after(later, in_vmem(gate_piece))
     far.append([to_expert(x, s) for x, s in zip(later, range(2, E_MOD))])
     near_pieces = [[x, to_piece(near[1], t)] for t, x in enumerate(own_pieces, 1)]
-    far[0] = join(far[0], in_vmem(gate_piece), near[1])
-    up_piece = load(up_proj, [far[0]])
+    up_piece = load(up_proj, [near[1], *own_pieces, in_vmem(gate_piece)])
+    far[0] = join(far[0], in_vmem(gate_piece), in_vmem(up_piece))
     far[0] = [far[0]] + [to_piece(far[0], t) for t in range(1, groups)]
-    far[1] = join(far[1], in_vmem(gate_piece), in_vmem(up_piece))
-    down_piece = load_turned(down_proj, [far[1], in_vmem(gate_piece), in_vmem(up_piece)])
+    down_piece = load_turned(down_proj, [far[0][0], *sum(near_pieces, []), in_vmem(gate_piece), in_vmem(up_piece)])
+    far[1] = join(far[1], in_vmem(gate_piece), in_vmem(up_piece), in_vmem(down_piece))
     far[1] = [far[1]] + [to_piece(far[1], t) for t in range(1, groups)]
     near = near + sum(near_pieces, [])
     blocks = [near + far[a] for a in range(2)]
@@ -487,13 +487,16 @@
     first = [first[0]] + [to_piece(first[t], groups - t) for t in range(1, groups)]
     waiting = pass_after(second[1:], *first[1:])
     second = [second[0]] + [to_piece(x, groups - t) for t, x in enumerate(waiting, 1)]
-    arrived = []
-    for flip, partials in ((1, first), (0, second)):
-        sums = sum_pieces(partials)
-        arrived.append(
-            [sums[s] if s + flip == 0 else to_source(sums[s], s, flip) for s in range(E_MOD)]
-        )
-    token_grad, gate_grad = combine(groups, modality, picks, weights, arrived[1] + arrived[0])
+    crossed, kept = sum_pieces(first), sum_pieces(second)
+    arrived = {0: kept[0]}
+    for s in range(1, E_MOD):
+        arrived[s] = to_source(kept[s], s, 0)
+    for s in range(E_MOD):
+        arrived[E_MOD + s] = to_source(crossed[s], s, 1)
+    order = tuple(reversed(arrived))
+    token_grad, gate_grad = combine(
+        groups, order, modality, picks, weights, [arrived[i] for i in order]
+    )
     return token_grad, gate_grad.reshape(-1, 1)
 
 

time: 70.8 us -> 74.1 us (1.047)
  starting transfers between devices: 26.8 us -> 29.4 us
    ppermute x11, starting transfers between devices: 15.9 us -> 21.7 us  [to_expert(): lax.ppermute(x, 'ep', [(e * groups + j, (e ^ s) * groups + (j + t) % grou...]
    ppermute x7, starting transfers between devices: 10.8 us -> 7.71 us  [to_source(): lax.ppermute(x, ('ep', 'mod'), [((e * groups + j) * 2 + m, ((e ^ s) * gro...]
    ppermute x11, waiting for transfers between devices: 11.1 us -> 12.9 us  [to_expert(): lax.ppermute(x, 'ep', [(e * groups + j, (e ^ s) * groups + (j + t) % grou...]
    ppermute x7, waiting for transfers between devices: 7.05 us -> 5.91 us  [to_source(): lax.ppermute(x, ('ep', 'mod'), [((e * groups + j) * 2 + m, ((e ^ s) * gro...]
  transfers between devices with their start and end apart: 18 -> 18, of which waited for: 6 -> 9; matrix products, arithmetic and copies ran while one was open for 0% -> 0% of each run, Pallas kernels for 24% -> 23%
where the time goes in v9:
time: 74.1 us; the launch traced here: 74 us
  starting transfers between devices  29.4 us (40%)
  Pallas kernels  24.9 us (34%)
  waiting for transfers between devices  18.8 us (25%)
  between operations  0.8 us (1%)
    ppermute x11, starting transfers between devices, to_expert(): lax.ppermute(x, 'ep', [(e * groups + j, (e ^ s) * groups + (j + t) % grou...  21.7 us
    ppermute x11, waiting for transfers between devices, to_expert(): lax.ppermute(x, 'ep', [(e * groups + j, (e ^ s) * groups + (j + t) % grou...  12.9 us
    ppermute x7, starting transfers between devices, to_source(): lax.ppermute(x, ('ep', 'mod'), [((e * groups + j) * 2 + m, ((e ^ s) * gro...  7.71 us
    pallas_call x2, Pallas kernels, load(): pl.pallas_call(functools.partial(load_kernel, parts), in_specs=[pl.BlockS...  6.94 us
    ppermute x7, waiting for transfers between devices, to_source(): lax.ppermute(x, ('ep', 'mod'), [((e * groups + j) * 2 + m, ((e ^ s) * gro...  5.91 us
    pallas_call x1, Pallas kernels, load_turned(): pl.pallas_call(functools.partial(load_turned_kernel, parts), in_specs=[pl...  4.29 us
    pallas_call x1, Pallas kernels, hidden_grads(): pl.pallas_call(functools.partial(hidden_kernel, count, places, groups), i...  4.04 us
    pallas_call x1, Pallas kernels, back_half(): pl.pallas_call(functools.partial(back_kernel, groups), in_specs=[vmem] *...  2.9 us
  transfers between devices with their start and end apart: 18, of which 9 were waited for; matrix products, arithmetic and copies ran while one was open for 0% of the time, Pallas kernels for 23%

profile of v9, /device:TPU:0, one launch (start us, length us, event | category | flops | bytes accessed | tf_op | source)
XLA Modules:
  0.0 74.0 jit_solution(11057860087978045538)
XLA Ops:
  0.6 2.5 %gather_slots.1 = (bf16[32,4096]{1,0:T(8,128)(2,1)S(1)}, bf16[32,4096]{1,0:T(8,128)(2,1)S(1)}, bf16[16,4096]{1,0:T(8,128)(2,1)S(1)}, bf16[16,4096]{1,0:T(8,128)(...) custom-call(s32[1,128]{1,0:T(1,128)} %bitcast.6, s32[2,128]{1,0:T(2,128)} %bitcast.4, ...), custom_call_target="tpu_custom_call" | custom-call | flops 134217728 | bytes 3145728 | tf_op jit(solution)/shard_map/gather_slots/pallas_call | solution.py:97
  3.1 4.1 %collective-permute-start.5 = (bf16[16,4096]{1,0:T(8,128)(2,1)S(1)}, bf16[16,4096]{1,0:T(8,128)(2,1)S(1)}, u32[]{:S(2)}, u32[]{:S(2)}) collective-permute-start(bf16[16,4096]{1,0:T(8,128)(2,1)S(1)} %get-tuple-element.36), channel_id=1, source_target_pairs={{0,8},{2,10},{4,12},{6,14},{8,0},{10,2},{12,4},{14,6},{1,9},{3,11}... | collective-permute-start | bytes 393224 | tf_op jit(solution)/shard_map/ppermute | solution.py:431
  7.2 1.3 %collective-permute-start.6 = (bf16[16,4096]{1,0:T(8,128)(2,1)S(1)}, bf16[16,4096]{1,0:T(8,128)(2,1)S(1)}, u32[]{:S(2)}, u32[]{:S(2)}) collective-permute-start(bf16[16,4096]{1,0:T(8,128)(2,1)S(1)} %get-tuple-element.37), channel_id=1, source_target_pairs={{0,12},{2,14},{4,8},{6,10},{8,4},{10,6},{12,0},{14,2},{1,13},{3,15... | collective-permute-start | bytes 393224 | tf_op jit(solution)/shard_map/ppermute | solution.py:431
  8.6 0.2 collective-permute-start
  8.8 1.5 %collective-permute-start.1 = (bf16[32,4096]{1,0:T(8,128)(2,1)S(1)}, bf16[32,4096]{1,0:T(8,128)(2,1)S(1)}, u32[]{:S(2)}, u32[]{:S(2)}) collective-permute-start(bf16[32,4096]{1,0:T(8,128)(2,1)S(1)} %get-tuple-element.30.refs_0_), channel_id=1, source_target_pairs={{0,2},{2,0},{4,6},{6,4},{8,10},{10,8},{12,14},{14,12},{1,3},{3,1},... | collective-permute-start | bytes 786440 | tf_op jit(solution)/shard_map/ppermute | solution.py:431
  10.3 3.5 %load.2.refs_2_.refs_3_.refs_6_.refs_10_.gate_ref = bf16[1,4096,1024]{2,1,0:T(8,128)(2,1)S(1)} custom-call(bf16[1,4096,1024]{2,1,0:T(8,128)(2,1)} %src.3, bf16[32,4096]{1,0:T(8,128)(2,1)S(1)} %get-tuple-element.30.refs_0_), custom_call_target="tpu_custom_call" | custom-call | flops 2000000000 | bytes 1024 | tf_op jit(solution)/shard_map/load/pallas_call | solution.py:132
  13.8 2.9 %collective-permute-start.3 = (bf16[16,4096]{1,0:T(8,128)(2,1)S(1)}, bf16[16,4096]{1,0:T(8,128)(2,1)S(1)}, u32[]{:S(2)}, u32[]{:S(2)}) collective-permute-start(bf16[16,4096]{1,0:T(8,128)(2,1)S(1)} %get-tuple-element.34), channel_id=1, source_target_pairs={{0,8},{2,10},{4,12},{6,14},{8,0},{10,2},{12,4},{14,6},{1,9},{3,11}... | collective-permute-start | bytes 393224 | tf_op jit(solution)/shard_map/ppermute | solution.py:431
  16.7 5.0 %collective-permute-done.refs_0_.refs_1_ = bf16[32,4096]{1,0:T(8,128)(2,1)S(1)} collective-permute-done((bf16[32,4096]{1,0:T(8,128)(2,1)S(1)}, bf16[32,4096]{1,0:T(8,128)(2,1)S(1)}, u32[]{:S(2)}, u32[]{:S(2)}) %collective-permute-start) | collective-permute-done | bytes 262176 | tf_op jit(solution)/shard_map/ppermute | solution.py:431
  21.7 2.5 %collective-permute-start.4 = (bf16[16,4096]{1,0:T(8,128)(2,1)S(1)}, bf16[16,4096]{1,0:T(8,128)(2,1)S(1)}, u32[]{:S(2)}, u32[]{:S(2)}) collective-permute-start(bf16[16,4096]{1,0:T(8,128)(2,1)S(1)} %get-tuple-element.35), channel_id=1, source_target_pairs={{0,12},{2,14},{4,8},{6,10},{8,4},{10,6},{12,0},{14,2},{1,13},{3,15... | collective-permute-start | bytes 393224 | tf_op jit(solution)/shard_map/ppermute | solution.py:431
  24.2 0.0 collective-permute-done.1.refs_1_.refs_2_
  24.2 1.5 %collective-permute-start.2 = (bf16[32,4096]{1,0:T(8,128)(2,1)S(1)}, bf16[32,4096]{1,0:T(8,128)(2,1)S(1)}, u32[]{:S(2)}, u32[]{:S(2)}) collective-permute-start(bf16[32,4096]{1,0:T(8,128)(2,1)S(1)} %collective-permute-done.refs_0_.refs_1_), channel_id=1, source_target_pairs={{0,2},{2,0},{4,6},{6,4},{8,10},{10,8},{12,14},{14,12},{1,3},{3,1},... | collective-permute-start | bytes 786440 | tf_op jit(solution)/shard_map/ppermute | solution.py:431
  25.7 3.5 %load.3.refs_3_.refs_4_.refs_7_.refs_11_.up_ref = bf16[1,4096,1024]{2,1,0:T(8,128)(2,1)S(1)} custom-call(bf16[1,4096,1024]{2,1,0:T(8,128)(2,1)} %src.4, bf16[32,4096]{1,0:T(8,128)(2,1)S(1)} %collective-permute-done.refs_0_.refs_1_, bf16[32,4096]{1,0:T(8,128)(2,1)S(1)} %collective-permute-done.1.refs_1_.refs_2_, ...), custom_call_target="tpu_custom_call" | custom-call | flops 2000000000 | bytes 1024 | tf_op jit(solution)/shard_map/load/pallas_call | solution.py:132
  29.2 0.0 collective-permute-done.5.refs_0_
  29.2 0.0 collective-permute-done.6.refs_1_
  29.2 0.6 collective-permute-start.8
  29.8 2.0 %collective-permute-done.2.refs_2_.refs_3_ = bf16[32,4096]{1,0:T(8,128)(2,1)S(1)} collective-permute-done((bf16[32,4096]{1,0:T(8,128)(2,1)S(1)}, bf16[32,4096]{1,0:T(8,128)(2,1)S(1)}, u32[]{:S(2)}, u32[]{:S(2)}) %collective-permute-start.2) | collective-permute-done | bytes 262176 | tf_op jit(solution)/shard_map/ppermute | solution.py:431
  31.8 4.3 %load_turned.1.refs_4_.refs_8_.refs_9_ = bf16[4096,1024]{1,0:T(8,128)(2,1)S(1)} custom-call(bf16[1,1024,4096]{2,1,0:T(8,128)(2,1)} %src.5, bf16[32,4096]{1,0:T(8,128)(2,1)S(1)} %join.2.refs_0_.refs_4_, bf16[32,4096]{1,0:T(8,128)(2,1)S(1)} %collective-permute-done.1.refs_1_.refs_2_, bf16[32,4096]{1,0:T(8,128)(2,1)S(1)} %collective-permute-done.2.refs_2_.refs_3_, ...), custom_call_target="tpu_custom_call" | custom-call | flops 10000000000 | bytes 1024 | tf_op jit(solution)/shard_map/load_turned/pallas_call | solution.py:165
  36.1 0.0 collective-permute-done.3.refs_0_
  36.1 0.0 collective-permute-done.4.refs_1_
  36.2 2.5 %collective-permute-start.7 = (bf16[32,4096]{1,0:T(8,128)(2,1)S(1)}, bf16[32,4096]{1,0:T(8,128)(2,1)S(1)}, u32[]{:S(2)}, u32[]{:S(2)}) collective-permute-start(bf16[32,4096]{1,0:T(8,128)(2,1)S(1)} %join.3.refs_4_), channel_id=1, source_target_pairs={{0,2},{2,0},{4,6},{6,4},{8,10},{10,8},{12,14},{14,12},{1,3},{3,1},... | collective-permute-start | bytes 786440 | tf_op jit(solution)/shard_map/ppermute | solution.py:431
  38.7 0.0 collective-permute-done.8.refs_5_
  38.7 2.6 %pre_activations.1 = (f32[128,1024]{1,0:T(8,128)S(1)}, f32[128,1024]{1,0:T(8,128)S(1)}, f32[128,1024]{1,0:T(8,128)S(1)}) custom-call(bf16[32,4096]{1,0:T(8,128)(2,1)S(1)} %get-tuple-element.30.refs_0_, bf16[32,4096]{1,0:T(8,128)(2,1)S(1)} %collective-permute-done.refs_0_.refs_1_, bf16[32,4096]{1,0:T(8,128)(2,1)S(1)} %collective-permute-done.1.refs_1_.refs_2_, ...), custom_call_target="tpu_custom_call" | custom-call | flops 5000000000 | bytes 1024 | tf_op jit(solution)/shard_map/pre_activations/pallas_call | solution.py:255
  41.3 1.7 %collective-permute-done.7.refs_5_ = bf16[32,4096]{1,0:T(8,128)(2,1)S(1)} collective-permute-done((bf16[32,4096]{1,0:T(8,128)(2,1)S(1)}, bf16[32,4096]{1,0:T(8,128)(2,1)S(1)}, u32[]{:S(2)}, u32[]{:S(2)}) %collective-permute-start.7) | collective-permute-done | bytes 262176 | tf_op jit(solution)/shard_map/ppermute | solution.py:431
  43.1 4.0 %hidden_grads.1 = (bf16[64,2176]{1,0:T(8,128)(2,1)S(1)}, bf16[64,2176]{1,0:T(8,128)(2,1)S(1)}, bf16[128,1024]{1,0:T(8,128)(2,1)S(1)}, bf16[128,1024]{1,0:T(8,128)(2,1)S(1)}, bf16[128,128]{1,0:T(8,128)(2,1)S(1)}) custom-call(bf16[32,4096]{1,0:T(8,128)(2,1)S(1)} %get-tuple-element.30.refs_0_, bf16[32,4096]{1,0:T(8,128)(2,1)S(1)} %collective-permute-done.refs_0_.refs_1_, ...), custom_call_target="tpu_custom_call" | custom-call | flops 2147483648 | bytes 16777216 | tf_op jit(solution)/shard_map/hidden_grads/pallas_call | solution.py:307
  47.1 2.1 %collective-permute-start.9 = (bf16[64,2176]{1,0:T(8,128)(2,1)S(1)}, bf16[64,2176]{1,0:T(8,128)(2,1)S(1)}, u32[]{:S(2)}, u32[]{:S(2)}) collective-permute-start(bf16[64,2176]{1,0:T(8,128)(2,1)S(1)} %get-tuple-element.42), channel_id=1, source_target_pairs={{0,2},{2,0},{4,6},{6,4},{8,10},{10,8},{12,14},{14,12},{1,3},{3,1},... | collective-permute-start | bytes 835592 | tf_op jit(solution)/shard_map/ppermute | solution.py:431
  49.2 2.9 %back_half.1 = (bf16[64,2176]{1,0:T(8,128)(2,1)S(1)}, bf16[64,2176]{1,0:T(8,128)(2,1)S(1)}) custom-call(bf16[128,1024]{1,0:T(8,128)(2,1)S(1)} %get-tuple-element.47.dgate_ref, bf16[128,1024]{1,0:T(8,128)(2,1)S(1)} %get-tuple-element.48.dup_ref, bf16[128,128]{1,0:T(8,128)(2,1)S(1)} %get-tuple-element.49.part_ref, ...), custom_call_target="tpu_custom_call" | custom-call | flops 1073741824 | bytes 8388608 | tf_op jit(solution)/shard_map/back_half/pallas_call | solution.py:331
  52.1 0.0 copy-start
  52.1 0.0 copy-start.1
  52.1 0.0 copy-start.2
  52.1 3.9 %collective-permute-done.9.refs_1_ = bf16[64,2176]{1,0:T(8,128)(2,1)S(1)} collective-permute-done((bf16[64,2176]{1,0:T(8,128)(2,1)S(1)}, bf16[64,2176]{1,0:T(8,128)(2,1)S(1)}, u32[]{:S(2)}, u32[]{:S(2)}) %collective-permute-start.9) | collective-permute-done | bytes 278560 | tf_op jit(solution)/shard_map/ppermute | solution.py:431
  56.1 2.5 %collective-permute-start.14 = (bf16[64,2176]{1,0:T(8,128)(2,1)S(1)}, bf16[64,2176]{1,0:T(8,128)(2,1)S(1)}, u32[]{:S(2)}, u32[]{:S(2)}) collective-permute-start(bf16[64,2176]{1,0:T(8,128)(2,1)S(1)} %pass_after.3), channel_id=1, source_target_pairs={{0,2},{2,0},{4,6},{6,4},{8,10},{10,8},{12,14},{14,12},{1,3},{3,1},... | collective-permute-start | bytes 835592 | tf_op jit(solution)/shard_map/ppermute | solution.py:431
  58.6 0.1 sum_pieces.2
  58.7 0.1 collective-permute-start.10
  58.7 0.1 collective-permute-start.11
  58.8 1.6 %collective-permute-start.12 = (bf16[16,2176]{1,0:T(8,128)(2,1)S(1)}, bf16[16,2176]{1,0:T(8,128)(2,1)S(1)}, u32[]{:S(2)}, u32[]{:S(2)}) collective-permute-start(bf16[16,2176]{1,0:T(8,128)(2,1)S(1)} %get-tuple-element.45), channel_id=1, source_target_pairs={{0,5},{1,4},{2,7},{3,6},{4,1},{5,0},{6,3},{7,2},{8,13},{9,12},{10,... | collective-permute-start | bytes 208904 | tf_op jit(solution)/shard_map/ppermute | solution.py:445
  60.4 2.5 %collective-permute-start.13 = (bf16[16,2176]{1,0:T(8,128)(2,1)S(1)}, bf16[16,2176]{1,0:T(8,128)(2,1)S(1)}, u32[]{:S(2)}, u32[]{:S(2)}) collective-permute-start(bf16[16,2176]{1,0:T(8,128)(2,1)S(1)} %get-tuple-element.46), channel_id=1, source_target_pairs={{0,1},{1,0},{2,3},{3,2},{4,5},{5,4},{6,7},{7,6},{8,9},{9,8},{10,11... | collective-permute-start | bytes 208904 | tf_op jit(solution)/shard_map/ppermute | solution.py:445
  62.9 0.1 collective-permute-done.14.refs_1_
  63.1 0.1 sum_pieces.3
  63.2 1.4 %collective-permute-start.15 = (bf16[16,2176]{1,0:T(8,128)(2,1)S(1)}, bf16[16,2176]{1,0:T(8,128)(2,1)S(1)}, u32[]{:S(2)}, u32[]{:S(2)}) collective-permute-start(bf16[16,2176]{1,0:T(8,128)(2,1)S(1)} %get-tuple-element.52), channel_id=1, source_target_pairs={{0,12},{1,13},{2,14},{3,15},{4,8},{5,9},{6,10},{7,11},{8,4},{9,5},... | collective-permute-start | bytes 208904 | tf_op jit(solution)/shard_map/ppermute | solution.py:445
  64.6 0.0 collective-permute-done.10.refs_0_
  64.6 0.0 collective-permute-start.16
  64.6 1.0 %collective-permute-done.11.refs_1_ = bf16[16,2176]{1,0:T(8,128)(2,1)S(1)} collective-permute-done((bf16[16,2176]{1,0:T(8,128)(2,1)S(1)}, bf16[16,2176]{1,0:T(8,128)(2,1)S(1)}, u32[]{:S(2)}, u32[]{:S(2)}) %collective-permute-start.11) | collective-permute-done | bytes 69664 | tf_op jit(solution)/shard_map/ppermute | solution.py:445
  65.6 2.1 %collective-permute-start.17 = (bf16[16,2176]{1,0:T(8,128)(2,1)S(1)}, bf16[16,2176]{1,0:T(8,128)(2,1)S(1)}, u32[]{:S(2)}, u32[]{:S(2)}) collective-permute-start(bf16[16,2176]{1,0:T(8,128)(2,1)S(1)} %get-tuple-element.54), channel_id=1, source_target_pairs={{0,4},{1,5},{2,6},{3,7},{4,0},{5,1},{6,2},{7,3},{8,12},{9,13},{10,... | collective-permute-start | bytes 208904 | tf_op jit(solution)/shard_map/ppermute | solution.py:445
  67.6 0.0 collective-permute-done.12.refs_2_
  67.6 0.0 collective-permute-done.13.refs_3_
  67.6 2.6 %collective-permute-done.15.refs_4_ = bf16[16,2176]{1,0:T(8,128)(2,1)S(1)} collective-permute-done((bf16[16,2176]{1,0:T(8,128)(2,1)S(1)}, bf16[16,2176]{1,0:T(8,128)(2,1)S(1)}, u32[]{:S(2)}, u32[]{:S(2)}) %collective-permute-start.15) | collective-permute-done | bytes 69664 | tf_op jit(solution)/shard_map/ppermute | solution.py:445
  70.3 1.8 %collective-permute-done.16.refs_5_ = bf16[16,2176]{1,0:T(8,128)(2,1)S(1)} collective-permute-done((bf16[16,2176]{1,0:T(8,128)(2,1)S(1)}, bf16[16,2176]{1,0:T(8,128)(2,1)S(1)}, u32[]{:S(2)}, u32[]{:S(2)}) %collective-permute-start.16) | collective-permute-done | bytes 69664 | tf_op jit(solution)/shard_map/ppermute | solution.py:445
  72.1 0.4 collective-permute-done.17.refs_6_
  72.5 0.0 copy-done
  72.5 0.0 copy-done.1
  72.5 0.0 copy-done.2
  72.5 1.4 %combine.1 = (bf16[128,2048]{1,0:T(8,128)(2,1)}, f32[1,128]{1,0:T(1,128)}) custom-call(s32[1,128]{1,0:T(1,128)S(1)} %bitcast.7, s32[2,128]{1,0:T(2,128)S(1)} %bitcast.5, f32[2,128]{1,0:T(2,128)S(1)} %bitcast.8, bf16[16,2176]{1,0:T(8,128)(2,1)S(1)} %collective-permute-done.10.refs_0_, bf16[16,2176]{1,0:T(8,128)(2,1)S(1)} %collective-permute-done.11.refs_1_, ...), custom_call_target="tpu_custom_call" | custom-call | flops 134217728 | bytes 1048576 | tf_op jit(solution)/shard_map/combine/pallas_call | solution.py:408
  (4 shorter events, 0.0 us)
Async XLA Ops:
  3.1 26.0 %collective-permute-start.5 = (bf16[16,4096]{1,0:T(8,128)(2,1)S(1)}, bf16[16,4096]{1,0:T(8,128)(2,1)S(1)}, u32[]{:S(2)}, u32[]{:S(2)}) collective-permute-start(bf16[16,4096]{1,0:T(8,128)(2,1)S(1)} %get-tuple-element.36), channel_id=1, source_target_pairs={{0,8},{2,10},{4,12},{6,14},{8,0},{10,2},{12,4},{14,6},{1,9},{3,11}... | collective-permute-start | bytes 393224 | tf_op jit(solution)/shard_map/ppermute | solution.py:431
  7.2 21.9 %collective-permute-start.6 = (bf16[16,4096]{1,0:T(8,128)(2,1)S(1)}, bf16[16,4096]{1,0:T(8,128)(2,1)S(1)}, u32[]{:S(2)}, u32[]{:S(2)}) collective-permute-start(bf16[16,4096]{1,0:T(8,128)(2,1)S(1)} %get-tuple-element.37), channel_id=1, source_target_pairs={{0,12},{2,14},{4,8},{6,10},{8,4},{10,6},{12,0},{14,2},{1,13},{3,15... | collective-permute-start | bytes 393224 | tf_op jit(solution)/shard_map/ppermute | solution.py:431
  8.6 13.1 %collective-permute-start = (bf16[32,4096]{1,0:T(8,128)(2,1)S(1)}, bf16[32,4096]{1,0:T(8,128)(2,1)S(1)}, u32[]{:S(2)}, u32[]{:S(2)}) collective-permute-start(bf16[32,4096]{1,0:T(8,128)(2,1)S(1)} %get-tuple-element.31), channel_id=1, source_target_pairs={{0,4},{2,6},{4,0},{6,2},{8,12},{10,14},{12,8},{14,10},{1,5},{3,7},... | collective-permute-start | bytes 786440 | tf_op jit(solution)/shard_map/ppermute | solution.py:431
  8.8 15.4 %collective-permute-start.1 = (bf16[32,4096]{1,0:T(8,128)(2,1)S(1)}, bf16[32,4096]{1,0:T(8,128)(2,1)S(1)}, u32[]{:S(2)}, u32[]{:S(2)}) collective-permute-start(bf16[32,4096]{1,0:T(8,128)(2,1)S(1)} %get-tuple-element.30.refs_0_), channel_id=1, source_target_pairs={{0,2},{2,0},{4,6},{6,4},{8,10},{10,8},{12,14},{14,12},{1,3},{3,1},... | collective-permute-start | bytes 786440 | tf_op jit(solution)/shard_map/ppermute | solution.py:431
  13.8 22.3 %collective-permute-start.3 = (bf16[16,4096]{1,0:T(8,128)(2,1)S(1)}, bf16[16,4096]{1,0:T(8,128)(2,1)S(1)}, u32[]{:S(2)}, u32[]{:S(2)}) collective-permute-start(bf16[16,4096]{1,0:T(8,128)(2,1)S(1)} %get-tuple-element.34), channel_id=1, source_target_pairs={{0,8},{2,10},{4,12},{6,14},{8,0},{10,2},{12,4},{14,6},{1,9},{3,11}... | collective-permute-start | bytes 393224 | tf_op jit(solution)/shard_map/ppermute | solution.py:431
  21.7 14.4 %collective-permute-start.4 = (bf16[16,4096]{1,0:T(8,128)(2,1)S(1)}, bf16[16,4096]{1,0:T(8,128)(2,1)S(1)}, u32[]{:S(2)}, u32[]{:S(2)}) collective-permute-start(bf16[16,4096]{1,0:T(8,128)(2,1)S(1)} %get-tuple-element.35), channel_id=1, source_target_pairs={{0,12},{2,14},{4,8},{6,10},{8,4},{10,6},{12,0},{14,2},{1,13},{3,15... | collective-permute-start | bytes 393224 | tf_op jit(solution)/shard_map/ppermute | solution.py:431
  24.2 7.6 %collective-permute-start.2 = (bf16[32,4096]{1,0:T(8,128)(2,1)S(1)}, bf16[32,4096]{1,0:T(8,128)(2,1)S(1)}, u32[]{:S(2)}, u32[]{:S(2)}) collective-permute-start(bf16[32,4096]{1,0:T(8,128)(2,1)S(1)} %collective-permute-done.refs_0_.refs_1_), channel_id=1, source_target_pairs={{0,2},{2,0},{4,6},{6,4},{8,10},{10,8},{12,14},{14,12},{1,3},{3,1},... | collective-permute-start | bytes 786440 | tf_op jit(solution)/shard_map/ppermute | solution.py:431
  29.2 9.5 %collective-permute-start.8 = (bf16[32,4096]{1,0:T(8,128)(2,1)S(1)}, bf16[32,4096]{1,0:T(8,128)(2,1)S(1)}, u32[]{:S(2)}, u32[]{:S(2)}) collective-permute-start(bf16[32,4096]{1,0:T(8,128)(2,1)S(1)} %join.2.refs_0_.refs_4_), channel_id=1, source_target_pairs={{0,2},{2,0},{4,6},{6,4},{8,10},{10,8},{12,14},{14,12},{1,3},{3,1},... | collective-permute-start | bytes 786440 | tf_op jit(solution)/shard_map/ppermute | solution.py:431
  36.2 6.9 %collective-permute-start.7 = (bf16[32,4096]{1,0:T(8,128)(2,1)S(1)}, bf16[32,4096]{1,0:T(8,128)(2,1)S(1)}, u32[]{:S(2)}, u32[]{:S(2)}) collective-permute-start(bf16[32,4096]{1,0:T(8,128)(2,1)S(1)} %join.3.refs_4_), channel_id=1, source_target_pairs={{0,2},{2,0},{4,6},{6,4},{8,10},{10,8},{12,14},{14,12},{1,3},{3,1},... | collective-permute-start | bytes 786440 | tf_op jit(solution)/shard_map/ppermute | solution.py:431
  47.1 9.0 %collective-permute-start.9 = (bf16[64,2176]{1,0:T(8,128)(2,1)S(1)}, bf16[64,2176]{1,0:T(8,128)(2,1)S(1)}, u32[]{:S(2)}, u32[]{:S(2)}) collective-permute-start(bf16[64,2176]{1,0:T(8,128)(2,1)S(1)} %get-tuple-element.42), channel_id=1, source_target_pairs={{0,2},{2,0},{4,6},{6,4},{8,10},{10,8},{12,14},{14,12},{1,3},{3,1},... | collective-permute-start | bytes 835592 | tf_op jit(solution)/shard_map/ppermute | solution.py:431
  52.1 20.4 %copy-start = (s32[128,2]{0,1:T(2,128)S(1)}, s32[128,2]{0,1:T(2,128)}, u32[]{:S(2)}) copy-start(s32[128,2]{0,1:T(2,128)} %param.11) | copy-start | bytes 3076
  52.1 20.4 %copy-start.1 = (s32[128]{0:T(128)S(1)}, s32[128]{0:T(128)}, u32[]{:S(2)}) copy-start(s32[128]{0:T(128)} %param.10) | copy-start | bytes 1540
  52.1 20.4 %copy-start.2 = (f32[128,2]{0,1:T(2,128)S(1)}, f32[128,2]{0,1:T(2,128)}, u32[]{:S(2)}) copy-start(f32[128,2]{0,1:T(2,128)} %param.12) | copy-start | bytes 3076
  56.1 7.0 %collective-permute-start.14 = (bf16[64,2176]{1,0:T(8,128)(2,1)S(1)}, bf16[64,2176]{1,0:T(8,128)(2,1)S(1)}, u32[]{:S(2)}, u32[]{:S(2)}) collective-permute-start(bf16[64,2176]{1,0:T(8,128)(2,1)S(1)} %pass_after.3), channel_id=1, source_target_pairs={{0,2},{2,0},{4,6},{6,4},{8,10},{10,8},{12,14},{14,12},{1,3},{3,1},... | collective-permute-start | bytes 835592 | tf_op jit(solution)/shard_map/ppermute | solution.py:431
  58.7 5.9 %collective-permute-start.10 = (bf16[16,2176]{1,0:T(8,128)(2,1)S(1)}, bf16[16,2176]{1,0:T(8,128)(2,1)S(1)}, u32[]{:S(2)}, u32[]{:S(2)}) collective-permute-start(bf16[16,2176]{1,0:T(8,128)(2,1)S(1)} %get-tuple-element.43), channel_id=1, source_target_pairs={{0,13},{1,12},{2,15},{3,14},{4,9},{5,8},{6,11},{7,10},{8,5},{9,4},... | collective-permute-start | bytes 208904 | tf_op jit(solution)/shard_map/ppermute | solution.py:445
  58.7 6.9 %collective-permute-start.11 = (bf16[16,2176]{1,0:T(8,128)(2,1)S(1)}, bf16[16,2176]{1,0:T(8,128)(2,1)S(1)}, u32[]{:S(2)}, u32[]{:S(2)}) collective-permute-start(bf16[16,2176]{1,0:T(8,128)(2,1)S(1)} %get-tuple-element.44), channel_id=1, source_target_pairs={{0,9},{1,8},{2,11},{3,10},{4,13},{5,12},{6,15},{7,14},{8,1},{9,0},... | collective-permute-start | bytes 208904 | tf_op jit(solution)/shard_map/ppermute | solution.py:445
  58.8 8.8 %collective-permute-start.12 = (bf16[16,2176]{1,0:T(8,128)(2,1)S(1)}, bf16[16,2176]{1,0:T(8,128)(2,1)S(1)}, u32[]{:S(2)}, u32[]{:S(2)}) collective-permute-start(bf16[16,2176]{1,0:T(8,128)(2,1)S(1)} %get-tuple-element.45), channel_id=1, source_target_pairs={{0,5},{1,4},{2,7},{3,6},{4,1},{5,0},{6,3},{7,2},{8,13},{9,12},{10,... | collective-permute-start | bytes 208904 | tf_op jit(solution)/shard_map/ppermute | solution.py:445
  60.4 7.3 %collective-permute-start.13 = (bf16[16,2176]{1,0:T(8,128)(2,1)S(1)}, bf16[16,2176]{1,0:T(8,128)(2,1)S(1)}, u32[]{:S(2)}, u32[]{:S(2)}) collective-permute-start(bf16[16,2176]{1,0:T(8,128)(2,1)S(1)} %get-tuple-element.46), channel_id=1, source_target_pairs={{0,1},{1,0},{2,3},{3,2},{4,5},{5,4},{6,7},{7,6},{8,9},{9,8},{10,11... | collective-permute-start | bytes 208904 | tf_op jit(solution)/shard_map/ppermute | solution.py:445
  63.2 7.1 %collective-permute-start.15 = (bf16[16,2176]{1,0:T(8,128)(2,1)S(1)}, bf16[16,2176]{1,0:T(8,128)(2,1)S(1)}, u32[]{:S(2)}, u32[]{:S(2)}) collective-permute-start(bf16[16,2176]{1,0:T(8,128)(2,1)S(1)} %get-tuple-element.52), channel_id=1, source_target_pairs={{0,12},{1,13},{2,14},{3,15},{4,8},{5,9},{6,10},{7,11},{8,4},{9,5},... | collective-permute-start | bytes 208904 | tf_op jit(solution)/shard_map/ppermute | solution.py:445
  64.6 7.5 %collective-permute-start.16 = (bf16[16,2176]{1,0:T(8,128)(2,1)S(1)}, bf16[16,2176]{1,0:T(8,128)(2,1)S(1)}, u32[]{:S(2)}, u32[]{:S(2)}) collective-permute-start(bf16[16,2176]{1,0:T(8,128)(2,1)S(1)} %get-tuple-element.53), channel_id=1, source_target_pairs={{0,8},{1,9},{2,10},{3,11},{4,12},{5,13},{6,14},{7,15},{8,0},{9,1},... | collective-permute-start | bytes 208904 | tf_op jit(solution)/shard_map/ppermute | solution.py:445
  65.6 6.9 %collective-permute-start.17 = (bf16[16,2176]{1,0:T(8,128)(2,1)S(1)}, bf16[16,2176]{1,0:T(8,128)(2,1)S(1)}, u32[]{:S(2)}, u32[]{:S(2)}) collective-permute-start(bf16[16,2176]{1,0:T(8,128)(2,1)S(1)} %get-tuple-element.54), channel_id=1, source_target_pairs={{0,4},{1,5},{2,6},{3,7},{4,0},{5,1},{6,2},{7,3},{8,12},{9,13},{10,... | collective-permute-start | bytes 208904 | tf_op jit(solution)/shard_map/ppermute | solution.py:445

commit v10 on v9

--- a/solution.py
+++ b/solution.py
@@ -136,7 +136,7 @@
         out_shape=pltpu.VMEM(weight.shape, weight.dtype),
         scratch_shapes=[pltpu.SemaphoreType.DMA((parts,))],
         compiler_params=pltpu.CompilerParams(vmem_limit_bytes=SCOPED),
-        cost_estimate=cost(2 * 10**9, 1024),
+        cost_estimate=cost(0, 1024),
         name="load",
     )(in_hbm(weight), *after)
 
@@ -172,7 +172,7 @@
             pltpu.SemaphoreType.DMA((parts,)),
         ],
         compiler_params=pltpu.CompilerParams(vmem_limit_bytes=SCOPED),
-        cost_estimate=cost(10 * 10**9, 1024),
+        cost_estimate=cost(0, 1024),
         name="load_turned",
     )(in_hbm(weight), *after)
 
@@ -190,7 +190,7 @@
         out_shape=[jax.ShapeDtypeStruct(block.shape, block.dtype) for block in blocks],
         input_output_aliases={i: i for i in range(len(blocks))},
         compiler_params=pltpu.CompilerParams(vmem_limit_bytes=SCOPED),
-        cost_estimate=cost(2 * 10**9, 1024),
+        cost_estimate=cost(0, 1024),
         name="pass_after",
     )(*blocks, *need)
 
@@ -213,7 +213,7 @@
         out_specs=vmem,
         out_shape=jax.ShapeDtypeStruct((total, blocks[0].shape[1]), BF16),
         compiler_params=pltpu.CompilerParams(vmem_limit_bytes=SCOPED),
-        cost_estimate=cost(2 * 10**9, 1024),
+        cost_estimate=cost(3 * 10**9, 1024),
         name="join",
     )(*blocks, *need)
 
@@ -370,54 +370,71 @@
     )(*partials)
 
 
-def combine_kernel(groups, order, modality_ref, picks_ref, weights_ref, *refs):
-    blocks, (grad_out, gate_out, table) = refs[: 2 * E_MOD], refs[2 * E_MOD :]
-    wide = grad_out.shape[1]
-    for i, block in zip(order, blocks):
-        table[i * CAP : (i + 1) * CAP, :] = block[...]
+def mix_kernel(groups, modality_ref, picks_ref, weights_ref, mix_out, gate_out):
     count, first, second, member = slot_of_labels(groups, modality_ref, picks_ref)
     slot = jnp.where(member, count, -1)
     scale = jnp.where(first, weights_ref[0:1, :], jnp.where(second, weights_ref[1:2, :], 0.0))
     own = jnp.where(position(groups)[1] == 0, first.astype(F32), second.astype(F32))
-    tok_rows = slot.shape[1]
-    want = lax.broadcasted_iota(jnp.int32, (CAP, tok_rows), 0)
+    want = lax.broadcasted_iota(jnp.int32, (CAP, slot.shape[1]), 0)
     mix = []
-    gate = jnp.zeros((1, tok_rows), F32)
     for i in range(2 * E_MOD):
         hit = slot[i : i + 1, :] == want
         mix.append(jnp.where(hit, scale[i : i + 1, :], 0.0))
-        part = jnp.sum(table[i * CAP : (i + 1) * CAP, wide:].astype(F32), axis=1, keepdims=True)
-        gate = gate + jnp.sum(
-            jnp.where(hit, own[i : i + 1, :] * part, 0.0), axis=0, keepdims=True
-        )
-    gate_out[...] = gate
+        gate_out[i * CAP : (i + 1) * CAP, :] = jnp.where(hit, own[i : i + 1, :], 0.0)
     mix = jnp.concatenate(mix, axis=0).T
     high = mix.astype(BF16)
-    low = (mix - high.astype(F32)).astype(BF16)
-    values = table[:, :wide]
-    total = jnp.dot(high, values, preferred_element_type=F32)
-    total = total + jnp.dot(low, values, preferred_element_type=F32)
+    mix_out[0] = high
+    mix_out[1] = (mix - high.astype(F32)).astype(BF16)
+
+
+def mixing(groups, modality, picks, weights):
+    tok_rows = modality.shape[1]
+    slots = 2 * E_MOD * CAP
+    vmem = pl.BlockSpec(memory_space=pltpu.VMEM)
+    return pl.pallas_call(
+        functools.partial(mix_kernel, groups),
+        in_specs=[vmem] * 3,
+        out_specs=[vmem] * 2,
+        out_shape=[
+            jax.ShapeDtypeStruct((2, tok_rows, slots), BF16),
+            jax.ShapeDtypeStruct((slots, tok_rows), F32),
+        ],
+        compiler_params=pltpu.CompilerParams(vmem_limit_bytes=SCOPED),
+        cost_estimate=cost(MIB, 1024),
+        name="mixing",
+    )(modality, picks, weights)
+
+
+def combine_kernel(order, mix_ref, hit_ref, *refs):
+    blocks, (grad_out, gate_out, table) = refs[: len(order)], refs[len(order) :]
+    wide = grad_out.shape[1]
+    for i, block in zip(order, blocks):
+        table[i * CAP : (i + 1) * CAP, :] = block[...]
+    part = jnp.sum(table[:, wide:].astype(F32), axis=1, keepdims=True)
+    gate_out[...] = jnp.sum(hit_ref[...] * part, axis=0, keepdims=True)
+    total = jnp.dot(mix_ref[0], table[:, :wide], preferred_element_type=F32)
+    total = total + jnp.dot(mix_ref[1], table[:, :wide], preferred_element_type=F32)
     grad_out[...] = total.astype(BF16)
 
 
-def combine(groups, order, modality, picks, weights, blocks):
-    tok_rows = modality.shape[1]
+def combine(order, mix, hits, blocks):
+    tok_rows = hits.shape[1]
     wide = blocks[0].shape[1] - EXT
     count = len(blocks)
     vmem = pl.BlockSpec(memory_space=pltpu.VMEM)
     return pl.pallas_call(
-        functools.partial(combine_kernel, groups, order),
-        in_specs=[vmem] * (3 + count),
+        functools.partial(combine_kernel, order),
+        in_specs=[vmem] * (2 + count),
         out_specs=[vmem] * 2,
         out_shape=[
             jax.ShapeDtypeStruct((tok_rows, wide), BF16),
             jax.ShapeDtypeStruct((1, tok_rows), F32),
         ],
         scratch_shapes=[pltpu.VMEM((count * CAP, wide + EXT), BF16)],
+        compiler_params=pltpu.CompilerParams(vmem_limit_bytes=SCOPED),
         cost_estimate=cost(4 * count * CAP * tok_rows * wide, 4 * tok_rows * wide),
-        compiler_params=pltpu.CompilerParams(vmem_limit_bytes=SCOPED),
         name="combine",
-    )(modality, picks, weights, *blocks)
+    )(mix, hits, *blocks)
 
 
 def local(tokens, cotangent, modality, picks, gate_weights, gate_proj, up_proj, down_proj):
@@ -453,16 +470,17 @@
             ],
         )
 
+    mix, hits = mixing(groups, modality, picks, weights)
     sent = gather_slots(groups, modality, picks, tokens, cotangent)
     far = [[to_expert(sent[2 * s - 2], s) for s in range(2, E_MOD)]]
     near = [sent[0], to_expert(sent[1], 1)]
     own_pieces = [to_piece(sent[0], t) for t in range(1, groups)]
     gate_piece = load(gate_proj, sent[:1])
     later = [sent[2 * s - 1] for s in range(2, E_MOD)]
-    later = pass_after(later, in_vmem(gate_piece))
+    later = pass_after(later, in_vmem(gate_piece), *own_pieces)
     far.append([to_expert(x, s) for x, s in zip(later, range(2, E_MOD))])
     near_pieces = [[x, to_piece(near[1], t)] for t, x in enumerate(own_pieces, 1)]
-    up_piece = load(up_proj, [near[1], *own_pieces, in_vmem(gate_piece)])
+    up_piece = load(up_proj, [near[1], in_vmem(gate_piece)])
     far[0] = join(far[0], in_vmem(gate_piece), in_vmem(up_piece))
     far[0] = [far[0]] + [to_piece(far[0], t) for t in range(1, groups)]
     down_piece = load_turned(down_proj, [far[0][0], *sum(near_pieces, []), in_vmem(gate_piece), in_vmem(up_piece)])
@@ -494,9 +512,7 @@
     for s in range(E_MOD):
         arrived[E_MOD + s] = to_source(crossed[s], s, 1)
     order = tuple(reversed(arrived))
-    token_grad, gate_grad = combine(
-        groups, order, modality, picks, weights, [arrived[i] for i in order]
-    )
+    token_grad, gate_grad = combine(order, mix, hits, [arrived[i] for i in order])
     return token_grad, gate_grad.reshape(-1, 1)
 
 

time: 74.1 us -> 68.3 us (0.922)
  starting transfers between devices: 29.4 us -> 25.4 us
  waiting for transfers between devices: 18.8 us -> 17 us
    ppermute x11, starting transfers between devices: 21.7 us -> 13.9 us  [to_expert(): lax.ppermute(x, 'ep', [(e * groups + j, (e ^ s) * groups + (j + t) % grou...]
    ppermute x7, starting transfers between devices: 7.71 us -> 11.5 us  [to_source(): lax.ppermute(x, ('ep', 'mod'), [((e * groups + j) * 2 + m, ((e ^ s) * gro...]
    ppermute x7, waiting for transfers between devices: 5.91 us -> 4.66 us  [to_source(): lax.ppermute(x, ('ep', 'mod'), [((e * groups + j) * 2 + m, ((e ^ s) * gro...]
  transfers between devices with their start and end apart: 18 -> 18, of which waited for: 9 -> 9; matrix products, arithmetic and copies ran while one was open for 0% -> 0% of each run, Pallas kernels for 23% -> 25%
where the time goes in v10:
time: 68.3 us; the launch traced here: 68.2 us
  starting transfers between devices  25.4 us (37%)
  Pallas kernels  25 us (37%)
  waiting for transfers between devices  17 us (25%)
  between operations  0.77 us (1%)
    ppermute x11, starting transfers between devices, to_expert(): lax.ppermute(x, 'ep', [(e * groups + j, (e ^ s) * groups + (j + t) % grou...  13.9 us
    ppermute x11, waiting for transfers between devices, to_expert(): lax.ppermute(x, 'ep', [(e * groups + j, (e ^ s) * groups + (j + t) % grou...  12.3 us
    ppermute x7, starting transfers between devices, to_source(): lax.ppermute(x, ('ep', 'mod'), [((e * groups + j) * 2 + m, ((e ^ s) * gro...  11.5 us
    pallas_call x2, Pallas kernels, load(): pl.pallas_call(functools.partial(load_kernel, parts), in_specs=[pl.BlockS...  6.94 us
    ppermute x7, waiting for transfers between devices, to_source(): lax.ppermute(x, ('ep', 'mod'), [((e * groups + j) * 2 + m, ((e ^ s) * gro...  4.66 us
    pallas_call x1, Pallas kernels, load_turned(): pl.pallas_call(functools.partial(load_turned_kernel, parts), in_specs=[pl...  4.29 us
    pallas_call x1, Pallas kernels, hidden_grads(): pl.pallas_call(functools.partial(hidden_kernel, count, places, groups), i...  4.04 us
    pallas_call x1, Pallas kernels, back_half(): pl.pallas_call(functools.partial(back_kernel, groups), in_specs=[vmem] *...  2.9 us
  transfers between devices with their start and end apart: 18, of which 9 were waited for; matrix products, arithmetic and copies ran while one was open for 0% of the time, Pallas kernels for 25%

profile of v10, /device:TPU:0, one launch (start us, length us, event | category | flops | bytes accessed | tf_op | source)
XLA Modules:
  0.0 68.2 jit_solution(14573384294829093214)
XLA Ops:
  0.6 2.5 %gather_slots.1 = (bf16[32,4096]{1,0:T(8,128)(2,1)S(1)}, bf16[32,4096]{1,0:T(8,128)(2,1)S(1)}, bf16[16,4096]{1,0:T(8,128)(2,1)S(1)}, bf16[16,4096]{1,0:T(8,128)(...) custom-call(s32[1,128]{1,0:T(1,128)} %bitcast.6, s32[2,128]{1,0:T(2,128)} %bitcast.4, ...), custom_call_target="tpu_custom_call" | custom-call | flops 134217728 | bytes 3145728 | tf_op jit(solution)/shard_map/gather_slots/pallas_call | solution.py:97
  3.1 3.0 %collective-permute-start.1 = (bf16[32,4096]{1,0:T(8,128)(2,1)S(1)}, bf16[32,4096]{1,0:T(8,128)(2,1)S(1)}, u32[]{:S(2)}, u32[]{:S(2)}) collective-permute-start(bf16[32,4096]{1,0:T(8,128)(2,1)S(1)} %get-tuple-element.34.refs_0_), channel_id=1, source_target_pairs={{0,2},{2,0},{4,6},{6,4},{8,10},{10,8},{12,14},{14,12},{1,3},{3,1},... | collective-permute-start | bytes 786440 | tf_op jit(solution)/shard_map/ppermute | solution.py:448
  6.2 1.6 %collective-permute-start = (bf16[32,4096]{1,0:T(8,128)(2,1)S(1)}, bf16[32,4096]{1,0:T(8,128)(2,1)S(1)}, u32[]{:S(2)}, u32[]{:S(2)}) collective-permute-start(bf16[32,4096]{1,0:T(8,128)(2,1)S(1)} %get-tuple-element.35), channel_id=1, source_target_pairs={{0,4},{2,6},{4,0},{6,2},{8,12},{10,14},{12,8},{14,10},{1,5},{3,7},... | collective-permute-start | bytes 786440 | tf_op jit(solution)/shard_map/ppermute | solution.py:448
  7.7 2.6 %collective-permute-start.5 = (bf16[16,4096]{1,0:T(8,128)(2,1)S(1)}, bf16[16,4096]{1,0:T(8,128)(2,1)S(1)}, u32[]{:S(2)}, u32[]{:S(2)}) collective-permute-start(bf16[16,4096]{1,0:T(8,128)(2,1)S(1)} %get-tuple-element.40), channel_id=1, source_target_pairs={{0,8},{2,10},{4,12},{6,14},{8,0},{10,2},{12,4},{14,6},{1,9},{3,11}... | collective-permute-start | bytes 393224 | tf_op jit(solution)/shard_map/ppermute | solution.py:448
  10.3 0.2 collective-permute-start.6
  10.6 3.5 %load.2.refs_2_.refs_1_.refs_3_.refs_6_.refs_10_.gate_ref = bf16[1,4096,1024]{2,1,0:T(8,128)(2,1)S(1)} custom-call(bf16[1,4096,1024]{2,1,0:T(8,128)(2,1)} %src.3, bf16[32,4096]{1,0:T(8,128)(2,1)S(1)} %get-tuple-element.34.refs_0_), custom_call_target="tpu_custom_call" | custom-call | bytes 1024 | tf_op jit(solution)/shard_map/load/pallas_call | solution.py:132
  14.0 0.0 collective-permute-done.1.refs_3_.refs_1_.refs_2_
  14.1 1.8 %collective-permute-start.3 = (bf16[16,4096]{1,0:T(8,128)(2,1)S(1)}, bf16[16,4096]{1,0:T(8,128)(2,1)S(1)}, u32[]{:S(2)}, u32[]{:S(2)}) collective-permute-start(bf16[16,4096]{1,0:T(8,128)(2,1)S(1)} %get-tuple-element.38), channel_id=1, source_target_pairs={{0,8},{2,10},{4,12},{6,14},{8,0},{10,2},{12,4},{14,6},{1,9},{3,11}... | collective-permute-start | bytes 393224 | tf_op jit(solution)/shard_map/ppermute | solution.py:448
  15.8 2.0 %collective-permute-start.4 = (bf16[16,4096]{1,0:T(8,128)(2,1)S(1)}, bf16[16,4096]{1,0:T(8,128)(2,1)S(1)}, u32[]{:S(2)}, u32[]{:S(2)}) collective-permute-start(bf16[16,4096]{1,0:T(8,128)(2,1)S(1)} %get-tuple-element.39), channel_id=1, source_target_pairs={{0,12},{2,14},{4,8},{6,10},{8,4},{10,6},{12,0},{14,2},{1,13},{3,15... | collective-permute-start | bytes 393224 | tf_op jit(solution)/shard_map/ppermute | solution.py:448
  17.8 0.0 collective-permute-done.refs_0_.refs_1_
  17.8 0.5 collective-permute-start.2
  18.3 3.5 %load.3.refs_3_.refs_4_.refs_7_.refs_11_.up_ref = bf16[1,4096,1024]{2,1,0:T(8,128)(2,1)S(1)} custom-call(bf16[1,4096,1024]{2,1,0:T(8,128)(2,1)} %src.4, bf16[32,4096]{1,0:T(8,128)(2,1)S(1)} %collective-permute-done.refs_0_.refs_1_, bf16[1,4096,1024]{2,1,0:T(8,128)(2,1)S(1)} %load.2.refs_2_.refs_1_.refs_3_.refs_6_.refs_10_.gate_ref), custom_call_target="tpu_custom_call" | custom-call | bytes 1024 | tf_op jit(solution)/shard_map/load/pallas_call | solution.py:132
  21.8 0.0 collective-permute-done.5.refs_0_
  21.8 1.3 %collective-permute-done.6.refs_1_ = bf16[16,4096]{1,0:T(8,128)(2,1)S(1)} collective-permute-done((bf16[16,4096]{1,0:T(8,128)(2,1)S(1)}, bf16[16,4096]{1,0:T(8,128)(2,1)S(1)}, u32[]{:S(2)}, u32[]{:S(2)}) %collective-permute-start.6) | collective-permute-done | bytes 131104 | tf_op jit(solution)/shard_map/ppermute | solution.py:448
  23.2 0.6 collective-permute-start.8
  23.7 2.4 %collective-permute-done.2.refs_2_.refs_3_ = bf16[32,4096]{1,0:T(8,128)(2,1)S(1)} collective-permute-done((bf16[32,4096]{1,0:T(8,128)(2,1)S(1)}, bf16[32,4096]{1,0:T(8,128)(2,1)S(1)}, u32[]{:S(2)}, u32[]{:S(2)}) %collective-permute-start.2) | collective-permute-done | bytes 262176 | tf_op jit(solution)/shard_map/ppermute | solution.py:448
  26.2 4.3 %load_turned.1.refs_4_.refs_8_.refs_9_ = bf16[4096,1024]{1,0:T(8,128)(2,1)S(1)} custom-call(bf16[1,1024,4096]{2,1,0:T(8,128)(2,1)} %src.5, bf16[32,4096]{1,0:T(8,128)(2,1)S(1)} %join.2.refs_0_.refs_4_, bf16[32,4096]{1,0:T(8,128)(2,1)S(1)} %collective-permute-done.1.refs_3_.refs_1_.refs_2_, bf16[32,4096]{1,0:T(8,128)(2,1)S(1)} %collective-permute-done.2.refs_2_.refs_3_, ...), custom_call_target="tpu_custom_call" | custom-call | bytes 1024 | tf_op jit(solution)/shard_map/load_turned/pallas_call | solution.py:165
  30.5 0.4 collective-permute-done.3.refs_0_
  30.9 0.0 collective-permute-done.4.refs_1_
  30.9 0.6 collective-permute-start.7
  31.5 0.0 collective-permute-done.8.refs_5_
  31.5 2.6 %pre_activations.1 = (f32[128,1024]{1,0:T(8,128)S(1)}, f32[128,1024]{1,0:T(8,128)S(1)}, f32[128,1024]{1,0:T(8,128)S(1)}) custom-call(bf16[32,4096]{1,0:T(8,128)(2,1)S(1)} %get-tuple-element.34.refs_0_, bf16[32,4096]{1,0:T(8,128)(2,1)S(1)} %collective-permute-done.refs_0_.refs_1_, bf16[32,4096]{1,0:T(8,128)(2,1)S(1)} %collective-permute-done.1.refs_3_.refs_1_.refs_2_, ...), custom_call_target="tpu_custom_call" | custom-call | flops 5000000000 | bytes 1024 | tf_op jit(solution)/shard_map/pre_activations/pallas_call | solution.py:255
  34.1 3.9 %collective-permute-done.7.refs_5_ = bf16[32,4096]{1,0:T(8,128)(2,1)S(1)} collective-permute-done((bf16[32,4096]{1,0:T(8,128)(2,1)S(1)}, bf16[32,4096]{1,0:T(8,128)(2,1)S(1)}, u32[]{:S(2)}, u32[]{:S(2)}) %collective-permute-start.7) | collective-permute-done | bytes 262176 | tf_op jit(solution)/shard_map/ppermute | solution.py:448
  38.0 4.0 %hidden_grads.1 = (bf16[64,2176]{1,0:T(8,128)(2,1)S(1)}, bf16[64,2176]{1,0:T(8,128)(2,1)S(1)}, bf16[128,1024]{1,0:T(8,128)(2,1)S(1)}, bf16[128,1024]{1,0:T(8,128)(2,1)S(1)}, bf16[128,128]{1,0:T(8,128)(2,1)S(1)}) custom-call(bf16[32,4096]{1,0:T(8,128)(2,1)S(1)} %get-tuple-element.34.refs_0_, bf16[32,4096]{1,0:T(8,128)(2,1)S(1)} %collective-permute-done.refs_0_.refs_1_, ...), custom_call_target="tpu_custom_call" | custom-call | flops 2147483648 | bytes 16777216 | tf_op jit(solution)/shard_map/hidden_grads/pallas_call | solution.py:307
  42.0 0.6 collective-permute-start.9
  42.6 0.0 copy-start
  42.6 0.0 copy-start.1
  42.6 0.0 copy-start.2
  42.6 2.9 %back_half.1 = (bf16[64,2176]{1,0:T(8,128)(2,1)S(1)}, bf16[64,2176]{1,0:T(8,128)(2,1)S(1)}) custom-call(bf16[128,1024]{1,0:T(8,128)(2,1)S(1)} %get-tuple-element.51.dgate_ref, bf16[128,1024]{1,0:T(8,128)(2,1)S(1)} %get-tuple-element.52.dup_ref, bf16[128,128]{1,0:T(8,128)(2,1)S(1)} %get-tuple-element.53.part_ref, ...), custom_call_target="tpu_custom_call" | custom-call | flops 1073741824 | bytes 8388608 | tf_op jit(solution)/shard_map/back_half/pallas_call | solution.py:331
  45.5 3.7 %collective-permute-done.9.refs_1_ = bf16[64,2176]{1,0:T(8,128)(2,1)S(1)} collective-permute-done((bf16[64,2176]{1,0:T(8,128)(2,1)S(1)}, bf16[64,2176]{1,0:T(8,128)(2,1)S(1)}, u32[]{:S(2)}, u32[]{:S(2)}) %collective-permute-start.9) | collective-permute-done | bytes 278560 | tf_op jit(solution)/shard_map/ppermute | solution.py:448
  49.3 0.5 collective-permute-start.14
  49.8 0.1 sum_pieces.2
  49.9 0.1 collective-permute-start.10
  49.9 4.2 %collective-permute-start.11 = (bf16[16,2176]{1,0:T(8,128)(2,1)S(1)}, bf16[16,2176]{1,0:T(8,128)(2,1)S(1)}, u32[]{:S(2)}, u32[]{:S(2)}) collective-permute-start(bf16[16,2176]{1,0:T(8,128)(2,1)S(1)} %get-tuple-element.48), channel_id=1, source_target_pairs={{0,9},{1,8},{2,11},{3,10},{4,13},{5,12},{6,15},{7,14},{8,1},{9,0},... | collective-permute-start | bytes 208904 | tf_op jit(solution)/shard_map/ppermute | solution.py:462
  54.2 1.1 %collective-permute-start.12 = (bf16[16,2176]{1,0:T(8,128)(2,1)S(1)}, bf16[16,2176]{1,0:T(8,128)(2,1)S(1)}, u32[]{:S(2)}, u32[]{:S(2)}) collective-permute-start(bf16[16,2176]{1,0:T(8,128)(2,1)S(1)} %get-tuple-element.49), channel_id=1, source_target_pairs={{0,5},{1,4},{2,7},{3,6},{4,1},{5,0},{6,3},{7,2},{8,13},{9,12},{10,... | collective-permute-start | bytes 208904 | tf_op jit(solution)/shard_map/ppermute | solution.py:462
  55.3 0.0 collective-permute-start.13
  55.3 0.5 collective-permute-done.14.refs_1_
  55.8 0.1 sum_pieces.3
  55.9 5.5 %collective-permute-start.15 = (bf16[16,2176]{1,0:T(8,128)(2,1)S(1)}, bf16[16,2176]{1,0:T(8,128)(2,1)S(1)}, u32[]{:S(2)}, u32[]{:S(2)}) collective-permute-start(bf16[16,2176]{1,0:T(8,128)(2,1)S(1)} %get-tuple-element.56), channel_id=1, source_target_pairs={{0,12},{1,13},{2,14},{3,15},{4,8},{5,9},{6,10},{7,11},{8,4},{9,5},... | collective-permute-start | bytes 208904 | tf_op jit(solution)/shard_map/ppermute | solution.py:462
  61.3 0.0 collective-permute-done.10.refs_0_
  61.4 0.0 collective-permute-start.16
  61.4 0.0 collective-permute-done.11.refs_1_
  61.4 0.6 collective-permute-start.17
  62.0 0.0 copy-done
  62.0 0.0 copy-done.1
  62.0 0.0 copy-done.2
  62.0 0.2 mixing.1
  62.3 0.0 collective-permute-done.12.refs_2_
  62.3 0.0 collective-permute-done.13.refs_3_
  62.3 2.1 %collective-permute-done.15.refs_4_ = bf16[16,2176]{1,0:T(8,128)(2,1)S(1)} collective-permute-done((bf16[16,2176]{1,0:T(8,128)(2,1)S(1)}, bf16[16,2176]{1,0:T(8,128)(2,1)S(1)}, u32[]{:S(2)}, u32[]{:S(2)}) %collective-permute-start.15) | collective-permute-done | bytes 69664 | tf_op jit(solution)/shard_map/ppermute | solution.py:462
  64.3 2.5 %collective-permute-done.16.refs_5_ = bf16[16,2176]{1,0:T(8,128)(2,1)S(1)} collective-permute-done((bf16[16,2176]{1,0:T(8,128)(2,1)S(1)}, bf16[16,2176]{1,0:T(8,128)(2,1)S(1)}, u32[]{:S(2)}, u32[]{:S(2)}) %collective-permute-start.16) | collective-permute-done | bytes 69664 | tf_op jit(solution)/shard_map/ppermute | solution.py:462
  66.8 0.1 collective-permute-done.17.refs_6_
  66.9 1.2 %combine.1 = (bf16[128,2048]{1,0:T(8,128)(2,1)}, f32[1,128]{1,0:T(1,128)}) custom-call(bf16[2,128,128]{2,1,0:T(8,128)(2,1)S(1)} %get-tuple-element.32.mix_ref, f32[128,128]{1,0:T(8,128)S(1)} %get-tuple-element.33.hit_ref, bf16[16,2176]{1,0:T(8,128)(2,1)S(1)} %collective-permute-done.10.refs_0_, bf16[16,2176]{1,0:T(8,128)(2,1)S(1)} %collective-permute-done.11.refs_1_, ...), custom_call_target="tpu_custom_call" | custom-call | flops 134217728 | bytes 1048576 | tf_op jit(solution)/shard_map/combine/pallas_call | solution.py:425
  (4 shorter events, 0.0 us)
Async XLA Ops:
  3.1 10.9 %collective-permute-start.1 = (bf16[32,4096]{1,0:T(8,128)(2,1)S(1)}, bf16[32,4096]{1,0:T(8,128)(2,1)S(1)}, u32[]{:S(2)}, u32[]{:S(2)}) collective-permute-start(bf16[32,4096]{1,0:T(8,128)(2,1)S(1)} %get-tuple-element.34.refs_0_), channel_id=1, source_target_pairs={{0,2},{2,0},{4,6},{6,4},{8,10},{10,8},{12,14},{14,12},{1,3},{3,1},... | collective-permute-start | bytes 786440 | tf_op jit(solution)/shard_map/ppermute | solution.py:448
  6.2 11.6 %collective-permute-start = (bf16[32,4096]{1,0:T(8,128)(2,1)S(1)}, bf16[32,4096]{1,0:T(8,128)(2,1)S(1)}, u32[]{:S(2)}, u32[]{:S(2)}) collective-permute-start(bf16[32,4096]{1,0:T(8,128)(2,1)S(1)} %get-tuple-element.35), channel_id=1, source_target_pairs={{0,4},{2,6},{4,0},{6,2},{8,12},{10,14},{12,8},{14,10},{1,5},{3,7},... | collective-permute-start | bytes 786440 | tf_op jit(solution)/shard_map/ppermute | solution.py:448
  7.7 14.1 %collective-permute-start.5 = (bf16[16,4096]{1,0:T(8,128)(2,1)S(1)}, bf16[16,4096]{1,0:T(8,128)(2,1)S(1)}, u32[]{:S(2)}, u32[]{:S(2)}) collective-permute-start(bf16[16,4096]{1,0:T(8,128)(2,1)S(1)} %get-tuple-element.40), channel_id=1, source_target_pairs={{0,8},{2,10},{4,12},{6,14},{8,0},{10,2},{12,4},{14,6},{1,9},{3,11}... | collective-permute-start | bytes 393224 | tf_op jit(solution)/shard_map/ppermute | solution.py:448
  10.3 12.8 %collective-permute-start.6 = (bf16[16,4096]{1,0:T(8,128)(2,1)S(1)}, bf16[16,4096]{1,0:T(8,128)(2,1)S(1)}, u32[]{:S(2)}, u32[]{:S(2)}) collective-permute-start(bf16[16,4096]{1,0:T(8,128)(2,1)S(1)} %get-tuple-element.41), channel_id=1, source_target_pairs={{0,12},{2,14},{4,8},{6,10},{8,4},{10,6},{12,0},{14,2},{1,13},{3,15... | collective-permute-start | bytes 393224 | tf_op jit(solution)/shard_map/ppermute | solution.py:448
  14.1 16.8 %collective-permute-start.3 = (bf16[16,4096]{1,0:T(8,128)(2,1)S(1)}, bf16[16,4096]{1,0:T(8,128)(2,1)S(1)}, u32[]{:S(2)}, u32[]{:S(2)}) collective-permute-start(bf16[16,4096]{1,0:T(8,128)(2,1)S(1)} %get-tuple-element.38), channel_id=1, source_target_pairs={{0,8},{2,10},{4,12},{6,14},{8,0},{10,2},{12,4},{14,6},{1,9},{3,11}... | collective-permute-start | bytes 393224 | tf_op jit(solution)/shard_map/ppermute | solution.py:448
  15.8 15.1 %collective-permute-start.4 = (bf16[16,4096]{1,0:T(8,128)(2,1)S(1)}, bf16[16,4096]{1,0:T(8,128)(2,1)S(1)}, u32[]{:S(2)}, u32[]{:S(2)}) collective-permute-start(bf16[16,4096]{1,0:T(8,128)(2,1)S(1)} %get-tuple-element.39), channel_id=1, source_target_pairs={{0,12},{2,14},{4,8},{6,10},{8,4},{10,6},{12,0},{14,2},{1,13},{3,15... | collective-permute-start | bytes 393224 | tf_op jit(solution)/shard_map/ppermute | solution.py:448
  17.8 8.3 %collective-permute-start.2 = (bf16[32,4096]{1,0:T(8,128)(2,1)S(1)}, bf16[32,4096]{1,0:T(8,128)(2,1)S(1)}, u32[]{:S(2)}, u32[]{:S(2)}) collective-permute-start(bf16[32,4096]{1,0:T(8,128)(2,1)S(1)} %collective-permute-done.refs_0_.refs_1_), channel_id=1, source_target_pairs={{0,2},{2,0},{4,6},{6,4},{8,10},{10,8},{12,14},{14,12},{1,3},{3,1},... | collective-permute-start | bytes 786440 | tf_op jit(solution)/shard_map/ppermute | solution.py:448
  23.2 8.3 %collective-permute-start.8 = (bf16[32,4096]{1,0:T(8,128)(2,1)S(1)}, bf16[32,4096]{1,0:T(8,128)(2,1)S(1)}, u32[]{:S(2)}, u32[]{:S(2)}) collective-permute-start(bf16[32,4096]{1,0:T(8,128)(2,1)S(1)} %join.2.refs_0_.refs_4_), channel_id=1, source_target_pairs={{0,2},{2,0},{4,6},{6,4},{8,10},{10,8},{12,14},{14,12},{1,3},{3,1},... | collective-permute-start | bytes 786440 | tf_op jit(solution)/shard_map/ppermute | solution.py:448
  30.9 7.1 %collective-permute-start.7 = (bf16[32,4096]{1,0:T(8,128)(2,1)S(1)}, bf16[32,4096]{1,0:T(8,128)(2,1)S(1)}, u32[]{:S(2)}, u32[]{:S(2)}) collective-permute-start(bf16[32,4096]{1,0:T(8,128)(2,1)S(1)} %join.3.refs_4_), channel_id=1, source_target_pairs={{0,2},{2,0},{4,6},{6,4},{8,10},{10,8},{12,14},{14,12},{1,3},{3,1},... | collective-permute-start | bytes 786440 | tf_op jit(solution)/shard_map/ppermute | solution.py:448
  42.0 7.2 %collective-permute-start.9 = (bf16[64,2176]{1,0:T(8,128)(2,1)S(1)}, bf16[64,2176]{1,0:T(8,128)(2,1)S(1)}, u32[]{:S(2)}, u32[]{:S(2)}) collective-permute-start(bf16[64,2176]{1,0:T(8,128)(2,1)S(1)} %get-tuple-element.46), channel_id=1, source_target_pairs={{0,2},{2,0},{4,6},{6,4},{8,10},{10,8},{12,14},{14,12},{1,3},{3,1},... | collective-permute-start | bytes 835592 | tf_op jit(solution)/shard_map/ppermute | solution.py:448
  42.6 19.4 %copy-start = (s32[128,2]{0,1:T(2,128)S(1)}, s32[128,2]{0,1:T(2,128)}, u32[]{:S(2)}) copy-start(s32[128,2]{0,1:T(2,128)} %param.11) | copy-start | bytes 3076
  42.6 19.4 %copy-start.1 = (s32[128]{0:T(128)S(1)}, s32[128]{0:T(128)}, u32[]{:S(2)}) copy-start(s32[128]{0:T(128)} %param.10) | copy-start | bytes 1540
  42.6 19.4 %copy-start.2 = (f32[128,2]{0,1:T(2,128)S(1)}, f32[128,2]{0,1:T(2,128)}, u32[]{:S(2)}) copy-start(f32[128,2]{0,1:T(2,128)} %param.12) | copy-start | bytes 3076
  49.3 6.5 %collective-permute-start.14 = (bf16[64,2176]{1,0:T(8,128)(2,1)S(1)}, bf16[64,2176]{1,0:T(8,128)(2,1)S(1)}, u32[]{:S(2)}, u32[]{:S(2)}) collective-permute-start(bf16[64,2176]{1,0:T(8,128)(2,1)S(1)} %pass_after.3), channel_id=1, source_target_pairs={{0,2},{2,0},{4,6},{6,4},{8,10},{10,8},{12,14},{14,12},{1,3},{3,1},... | collective-permute-start | bytes 835592 | tf_op jit(solution)/shard_map/ppermute | solution.py:448
  49.9 11.5 %collective-permute-start.10 = (bf16[16,2176]{1,0:T(8,128)(2,1)S(1)}, bf16[16,2176]{1,0:T(8,128)(2,1)S(1)}, u32[]{:S(2)}, u32[]{:S(2)}) collective-permute-start(bf16[16,2176]{1,0:T(8,128)(2,1)S(1)} %get-tuple-element.47), channel_id=1, source_target_pairs={{0,13},{1,12},{2,15},{3,14},{4,9},{5,8},{6,11},{7,10},{8,5},{9,4},... | collective-permute-start | bytes 208904 | tf_op jit(solution)/shard_map/ppermute | solution.py:462
  49.9 11.4 %collective-permute-start.11 = (bf16[16,2176]{1,0:T(8,128)(2,1)S(1)}, bf16[16,2176]{1,0:T(8,128)(2,1)S(1)}, u32[]{:S(2)}, u32[]{:S(2)}) collective-permute-start(bf16[16,2176]{1,0:T(8,128)(2,1)S(1)} %get-tuple-element.48), channel_id=1, source_target_pairs={{0,9},{1,8},{2,11},{3,10},{4,13},{5,12},{6,15},{7,14},{8,1},{9,0},... | collective-permute-start | bytes 208904 | tf_op jit(solution)/shard_map/ppermute | solution.py:462
  54.2 8.1 %collective-permute-start.12 = (bf16[16,2176]{1,0:T(8,128)(2,1)S(1)}, bf16[16,2176]{1,0:T(8,128)(2,1)S(1)}, u32[]{:S(2)}, u32[]{:S(2)}) collective-permute-start(bf16[16,2176]{1,0:T(8,128)(2,1)S(1)} %get-tuple-element.49), channel_id=1, source_target_pairs={{0,5},{1,4},{2,7},{3,6},{4,1},{5,0},{6,3},{7,2},{8,13},{9,12},{10,... | collective-permute-start | bytes 208904 | tf_op jit(solution)/shard_map/ppermute | solution.py:462
  55.3 7.0 %collective-permute-start.13 = (bf16[16,2176]{1,0:T(8,128)(2,1)S(1)}, bf16[16,2176]{1,0:T(8,128)(2,1)S(1)}, u32[]{:S(2)}, u32[]{:S(2)}) collective-permute-start(bf16[16,2176]{1,0:T(8,128)(2,1)S(1)} %get-tuple-element.50), channel_id=1, source_target_pairs={{0,1},{1,0},{2,3},{3,2},{4,5},{5,4},{6,7},{7,6},{8,9},{9,8},{10,11... | collective-permute-start | bytes 208904 | tf_op jit(solution)/shard_map/ppermute | solution.py:462
  55.9 8.4 %collective-permute-start.15 = (bf16[16,2176]{1,0:T(8,128)(2,1)S(1)}, bf16[16,2176]{1,0:T(8,128)(2,1)S(1)}, u32[]{:S(2)}, u32[]{:S(2)}) collective-permute-start(bf16[16,2176]{1,0:T(8,128)(2,1)S(1)} %get-tuple-element.56), channel_id=1, source_target_pairs={{0,12},{1,13},{2,14},{3,15},{4,8},{5,9},{6,10},{7,11},{8,4},{9,5},... | collective-permute-start | bytes 208904 | tf_op jit(solution)/shard_map/ppermute | solution.py:462
  61.4 5.5 %collective-permute-start.16 = (bf16[16,2176]{1,0:T(8,128)(2,1)S(1)}, bf16[16,2176]{1,0:T(8,128)(2,1)S(1)}, u32[]{:S(2)}, u32[]{:S(2)}) collective-permute-start(bf16[16,2176]{1,0:T(8,128)(2,1)S(1)} %get-tuple-element.57), channel_id=1, source_target_pairs={{0,8},{1,9},{2,10},{3,11},{4,12},{5,13},{6,14},{7,15},{8,0},{9,1},... | collective-permute-start | bytes 208904 | tf_op jit(solution)/shard_map/ppermute | solution.py:462
  61.4 5.6 %collective-permute-start.17 = (bf16[16,2176]{1,0:T(8,128)(2,1)S(1)}, bf16[16,2176]{1,0:T(8,128)(2,1)S(1)}, u32[]{:S(2)}, u32[]{:S(2)}) collective-permute-start(bf16[16,2176]{1,0:T(8,128)(2,1)S(1)} %get-tuple-element.58), channel_id=1, source_target_pairs={{0,4},{1,5},{2,6},{3,7},{4,0},{5,1},{6,2},{7,3},{8,12},{9,13},{10,... | collective-permute-start | bytes 208904 | tf_op jit(solution)/shard_map/ppermute | solution.py:462

commit v11 on v10

--- a/solution.py
+++ b/solution.py
@@ -267,46 +267,48 @@
 def back_columns(groups, flip, dgate_ref, dup_ref, part, gate_ref, up_ref, outs):
     half = jnp.bitwise_xor(position(groups)[1], flip)
     wide = outs[0].shape[1] - EXT
-    own_rows = outs[0].shape[0]
     chunk = 512
+    places = [slice(i * 2 * CAP, (i + 1) * 2 * CAP) for i in range(len(outs))]
     for step in range(wide // chunk):
         rows = pl.ds(pl.multiple_of(half * wide + step * chunk, chunk), chunk)
         grad = nt_dot(dgate_ref[...], gate_ref[0, rows, :]) + nt_dot(dup_ref[...], up_ref[0, rows, :])
         grad = grad.astype(BF16)
-        for t in range(groups):
-            outs[t][:, step * chunk : (step + 1) * chunk] = grad[t * own_rows : (t + 1) * own_rows, :]
-    for t in range(groups):
-        outs[t][:, wide:] = part[t * own_rows : (t + 1) * own_rows, :]
-
-
-def hidden_kernel(count, places, groups, *refs):
+        for out, place in zip(outs, places):
+            out[:, step * chunk : (step + 1) * chunk] = grad[place, :]
+    for out, place in zip(outs, places):
+        out[:, wide:] = part[place, :]
+
+
+def hidden_kernel(count, places, first_row, groups, *refs):
     blocks = refs[:count]
     act_ref, slope_ref, both_ref, down_ref, gate_ref, up_ref = refs[count : count + 6]
-    outs = refs[count + 6 : count + 6 + groups]
-    dgate, dup, part_out, rows = refs[count + 6 + groups :]
+    outs = refs[-4 - groups : -4]
+    dgate, dup, part_out, rows = refs[-4:]
     fill(rows, blocks, places)
     hidden = gate_ref.shape[2]
     chunk = min(256, hidden)
+    used = slice(first_row, first_row + rows.shape[0])
     part = jnp.zeros((rows.shape[0], 1), F32)
     for start in range(0, hidden, chunk):
         cols = slice(start, start + chunk)
         grad = jnp.dot(rows[...], down_ref[:, cols], preferred_element_type=F32)
-        part = part + jnp.sum(grad * both_ref[:, cols], axis=1, keepdims=True)
-        dgate[:, cols] = (grad * slope_ref[:, cols]).astype(BF16)
-        dup[:, cols] = (grad * act_ref[:, cols]).astype(BF16)
+        part = part + jnp.sum(grad * both_ref[used, cols], axis=1, keepdims=True)
+        dgate[:, cols] = (grad * slope_ref[used, cols]).astype(BF16)
+        dup[:, cols] = (grad * act_ref[used, cols]).astype(BF16)
     part_out[...] = two_terms(part)
     back_columns(groups, 1, dgate, dup, part_out[...], gate_ref, up_ref, outs)
 
 
-def hidden_grads(blocks, places, groups, factors, down_piece, gate_piece, up_piece):
+def hidden_grads(blocks, places, first_row, groups, factors, pieces, after):
     count = len(blocks)
+    gate_piece, up_piece, down_piece = pieces
     _, width, hidden = gate_piece.shape
     total = len(places) * CAP
-    shape = (total // groups, width // 2 + EXT)
+    shape = (2 * CAP, width // 2 + EXT)
     vmem = pl.BlockSpec(memory_space=pltpu.VMEM)
     out = pl.pallas_call(
-        functools.partial(hidden_kernel, count, places, groups),
-        in_specs=[vmem] * (count + 6),
+        functools.partial(hidden_kernel, count, places, first_row, groups),
+        in_specs=[vmem] * (count + 6) + [pl.BlockSpec(memory_space=pl.ANY)] * len(after),
         out_specs=[vmem] * (groups + 3),
         out_shape=[jax.ShapeDtypeStruct(shape, BF16)] * groups
         + [jax.ShapeDtypeStruct((total, hidden), BF16)] * 2
@@ -315,28 +317,38 @@
         compiler_params=pltpu.CompilerParams(vmem_limit_bytes=SCOPED),
         cost_estimate=cost(4 * total * width * hidden, 4 * width * hidden),
         name="hidden_grads",
-    )(*blocks, *factors, in_vmem(down_piece), in_vmem(gate_piece), in_vmem(up_piece))
-    return out[:groups], out[groups:]
-
-
-def back_kernel(groups, dgate_ref, dup_ref, part_ref, gate_ref, up_ref, *outs):
-    back_columns(groups, 0, dgate_ref, dup_ref, part_ref[...], gate_ref, up_ref, outs)
-
-
-def back_half(groups, dgate, dup, part, gate_piece, up_piece):
+    )(*blocks, *factors, in_vmem(down_piece), in_vmem(gate_piece), in_vmem(up_piece), *after)
+    return list(out[:groups]), list(out[groups:])
+
+
+def back_kernel(groups, *refs):
+    parts, (gate_ref, up_ref) = (refs[:3], refs[3:6]), refs[6:8]
+    outs, (dgate, dup) = refs[-2 - 2 * groups : -2], refs[-2:]
+    half = dgate.shape[0] // 2
+    for i, (dgate_ref, dup_ref, _) in enumerate(parts):
+        dgate[i * half : (i + 1) * half, :] = dgate_ref[...]
+        dup[i * half : (i + 1) * half, :] = dup_ref[...]
+    part = jnp.concatenate([refs[2][...], refs[5][...]], axis=0)
+    back_columns(groups, 0, dgate, dup, part, gate_ref, up_ref, outs)
+
+
+def back_half(groups, near, far, pieces, after):
+    gate_piece, up_piece, _ = pieces
     _, width, hidden = gate_piece.shape
-    total = dgate.shape[0]
-    shape = (total // groups, width // 2 + EXT)
+    total = 2 * near[0].shape[0]
+    shape = (2 * CAP, width // 2 + EXT)
     vmem = pl.BlockSpec(memory_space=pltpu.VMEM)
-    return pl.pallas_call(
+    out = pl.pallas_call(
         functools.partial(back_kernel, groups),
-        in_specs=[vmem] * 5,
-        out_specs=[vmem] * groups,
-        out_shape=[jax.ShapeDtypeStruct(shape, BF16)] * groups,
+        in_specs=[vmem] * 8 + [pl.BlockSpec(memory_space=pl.ANY)] * len(after),
+        out_specs=[vmem] * (2 * groups),
+        out_shape=[jax.ShapeDtypeStruct(shape, BF16)] * (2 * groups),
+        scratch_shapes=[pltpu.VMEM((total, hidden), BF16)] * 2,
         compiler_params=pltpu.CompilerParams(vmem_limit_bytes=SCOPED),
         cost_estimate=cost(2 * total * width * hidden, 2 * width * hidden),
         name="back_half",
-    )(dgate, dup, part, in_vmem(gate_piece), in_vmem(up_piece))
+    )(*near, *far, in_vmem(gate_piece), in_vmem(up_piece), *after)
+    return list(out[:groups]), list(out[groups:])
 
 
 def two_terms(value):
@@ -349,7 +361,7 @@
 def sum_kernel(groups, *refs):
     ins, outs = refs[:groups], refs[groups:]
     wide = ins[0].shape[1] - EXT
-    for s in range(E_MOD):
+    for s in range(2):
         rows = slice(s * CAP, (s + 1) * CAP)
         total = ins[0][rows, :].astype(F32)
         for t in range(1, groups):
@@ -363,7 +375,7 @@
     own_rows, wide = partials[0].shape
     return pl.pallas_call(
         functools.partial(sum_kernel, groups),
-        out_shape=[jax.ShapeDtypeStruct((CAP, wide), BF16)] * E_MOD,
+        out_shape=[jax.ShapeDtypeStruct((CAP, wide), BF16)] * 2,
         cost_estimate=cost(own_rows * wide, 4 * groups * own_rows * wide),
         compiler_params=pltpu.CompilerParams(vmem_limit_bytes=SCOPED),
         name="sum_pieces",
@@ -487,31 +499,39 @@
     far[1] = join(far[1], in_vmem(gate_piece), in_vmem(up_piece), in_vmem(down_piece))
     far[1] = [far[1]] + [to_piece(far[1], t) for t in range(1, groups)]
     near = near + sum(near_pieces, [])
-    blocks = [near + far[a] for a in range(2)]
-    places = [
-        tuple(
-            place
-            for t in range(groups)
-            for place in [(2 * t, a * CAP), (2 * t + 1, a * CAP)]
-            + [(2 * groups + t, i * CAP) for i in range(E_MOD - 2)]
-        )
-        for a in range(2)
+    pieces = (gate_piece, up_piece, down_piece)
+    near_places, far_places = [
+        [(i, start) for i in range(count) for start in starts]
+        for count, starts in ((2 * groups, [0]), (groups, [0, CAP]))
     ]
-    factors = pre_activations(blocks[0], places[0], gate_piece, up_piece, down_piece)
-    first, (dgate, dup, part) = hidden_grads(
-        blocks[1], places[1], groups, factors, down_piece, gate_piece, up_piece
+    pre_places = near_places + [(2 * groups + i, start) for i, start in far_places]
+    factors = pre_activations(near + far[0], pre_places, gate_piece, up_piece, down_piece)
+
+    def exchange(parts):
+        return [parts[0]] + [to_piece(parts[t], groups - t) for t in range(1, groups)]
+
+    near_places = [(i, CAP) for i, _ in near_places]
+    near_rows = len(near_places) * CAP
+    near_first, near_back = hidden_grads(near, near_places, 0, groups, factors, pieces, [])
+    near_first = exchange(near_first)
+    far_first, far_back = hidden_grads(
+        far[1], far_places, near_rows, groups, factors, pieces, near_back[2:]
     )
-    second = back_half(groups, dgate, dup, part, gate_piece, up_piece)
-    first = [first[0]] + [to_piece(first[t], groups - t) for t in range(1, groups)]
-    waiting = pass_after(second[1:], *first[1:])
-    second = [second[0]] + [to_piece(x, groups - t) for t, x in enumerate(waiting, 1)]
-    crossed, kept = sum_pieces(first), sum_pieces(second)
+    far_first = exchange(far_first)
+    near_second, far_second = back_half(groups, near_back, far_back, pieces, near_first[1:])
+    near_second = exchange(near_second)
+    far_second[1:] = pass_after(far_second[1:], *far_first[1:])
+    far_second = exchange(far_second)
+    crossed = sum_pieces(far_first)
+    kept = sum_pieces(far_second)
+    crossed = [*pass_after(sum_pieces(near_first), kept[0]), *crossed]
+    kept = [*sum_pieces(near_second), *kept]
     arrived = {0: kept[0]}
     for s in range(1, E_MOD):
         arrived[s] = to_source(kept[s], s, 0)
     for s in range(E_MOD):
         arrived[E_MOD + s] = to_source(crossed[s], s, 1)
-    order = tuple(reversed(arrived))
+    order = (5, 4, 7, 6, 1, 3, 2, 0)
     token_grad, gate_grad = combine(order, mix, hits, [arrived[i] for i in order])
     return token_grad, gate_grad.reshape(-1, 1)
 

time: 68.3 us -> 69.6 us (1.019)
  waiting for transfers between devices: 17 us -> 11.3 us
  Pallas kernels: 25 us -> 29.5 us
  starting transfers between devices: 25.4 us -> 27.9 us
    ppermute x11 -> x13, waiting for transfers between devices: 12.3 us -> 5.09 us  [to_expert(): lax.ppermute(x, 'ep', [(e * groups + j, (e ^ s) * groups + (j + t) % grou...]
    pallas_call x1 -> x2, Pallas kernels: 4.04 us -> 8.24 us  [hidden_grads(): pl.pallas_call(functools.partial(hidden_kernel, count, places, first_row,...]
    ppermute x11 -> x13, starting transfers between devices: 13.9 us -> 16.6 us  [to_expert(): lax.ppermute(x, 'ep', [(e * groups + j, (e ^ s) * groups + (j + t) % grou...]
    ppermute x7, waiting for transfers between devices: 4.66 us -> 6.21 us  [to_source(): lax.ppermute(x, ('ep', 'mod'), [((e * groups + j) * 2 + m, ((e ^ s) * gro...]
  transfers between devices with their start and end apart: 18 -> 20, of which waited for: 9 -> 7; matrix products, arithmetic and copies ran while one was open for 0% -> 0% of each run, Pallas kernels for 25% -> 37%
where the time goes in v11:
time: 69.6 us; the launch traced here: 69.5 us
  Pallas kernels  29.5 us (42%)
  starting transfers between devices  27.9 us (40%)
  waiting for transfers between devices  11.3 us (16%)
  between operations  0.77 us (1%)
    ppermute x13, starting transfers between devices, to_expert(): lax.ppermute(x, 'ep', [(e * groups + j, (e ^ s) * groups + (j + t) % grou...  16.6 us
    ppermute x7, starting transfers between devices, to_source(): lax.ppermute(x, ('ep', 'mod'), [((e * groups + j) * 2 + m, ((e ^ s) * gro...  11.4 us
    pallas_call x2, Pallas kernels, hidden_grads(): pl.pallas_call(functools.partial(hidden_kernel, count, places, first_row,...  8.24 us
    pallas_call x2, Pallas kernels, load(): pl.pallas_call(functools.partial(load_kernel, parts), in_specs=[pl.BlockS...  6.94 us
    ppermute x7, waiting for transfers between devices, to_source(): lax.ppermute(x, ('ep', 'mod'), [((e * groups + j) * 2 + m, ((e ^ s) * gro...  6.21 us
    ppermute x13, waiting for transfers between devices, to_expert(): lax.ppermute(x, 'ep', [(e * groups + j, (e ^ s) * groups + (j + t) % grou...  5.09 us
    pallas_call x1, Pallas kernels, load_turned(): pl.pallas_call(functools.partial(load_turned_kernel, parts), in_specs=[pl...  4.29 us
    pallas_call x1, Pallas kernels, back_half(): pl.pallas_call(functools.partial(back_kernel, groups), in_specs=[vmem] *...  3.03 us
  transfers between devices with their start and end apart: 20, of which 7 were waited for; matrix products, arithmetic and copies ran while one was open for 0% of the time, Pallas kernels for 37%

profile of v11, /device:TPU:0, one launch (start us, length us, event | category | flops | bytes accessed | tf_op | source)
XLA Modules:
  0.0 69.5 jit_solution(16147131799210881918)
XLA Ops:
  0.6 2.5 %gather_slots.1 = (bf16[32,4096]{1,0:T(8,128)(2,1)S(1)}, bf16[32,4096]{1,0:T(8,128)(2,1)S(1)}, bf16[16,4096]{1,0:T(8,128)(2,1)S(1)}, bf16[16,4096]{1,0:T(8,128)(...) custom-call(s32[1,128]{1,0:T(1,128)} %bitcast.6, s32[2,128]{1,0:T(2,128)} %bitcast.4, ...), custom_call_target="tpu_custom_call" | custom-call | flops 134217728 | bytes 3145728 | tf_op jit(solution)/shard_map/gather_slots/pallas_call | solution.py:97
  3.1 3.0 %collective-permute-start.1 = (bf16[32,4096]{1,0:T(8,128)(2,1)S(1)}, bf16[32,4096]{1,0:T(8,128)(2,1)S(1)}, u32[]{:S(2)}, u32[]{:S(2)}) collective-permute-start(bf16[32,4096]{1,0:T(8,128)(2,1)S(1)} %get-tuple-element.43.refs_0_), channel_id=1, source_target_pairs={{0,2},{2,0},{4,6},{6,4},{8,10},{10,8},{12,14},{14,12},{1,3},{3,1},... | collective-permute-start | bytes 786440 | tf_op jit(solution)/shard_map/ppermute | solution.py:460
  6.2 1.6 %collective-permute-start = (bf16[32,4096]{1,0:T(8,128)(2,1)S(1)}, bf16[32,4096]{1,0:T(8,128)(2,1)S(1)}, u32[]{:S(2)}, u32[]{:S(2)}) collective-permute-start(bf16[32,4096]{1,0:T(8,128)(2,1)S(1)} %get-tuple-element.44), channel_id=1, source_target_pairs={{0,4},{2,6},{4,0},{6,2},{8,12},{10,14},{12,8},{14,10},{1,5},{3,7},... | collective-permute-start | bytes 786440 | tf_op jit(solution)/shard_map/ppermute | solution.py:460
  7.7 2.6 %collective-permute-start.3 = (bf16[16,4096]{1,0:T(8,128)(2,1)S(1)}, bf16[16,4096]{1,0:T(8,128)(2,1)S(1)}, u32[]{:S(2)}, u32[]{:S(2)}) collective-permute-start(bf16[16,4096]{1,0:T(8,128)(2,1)S(1)} %get-tuple-element.45), channel_id=1, source_target_pairs={{0,8},{2,10},{4,12},{6,14},{8,0},{10,2},{12,4},{14,6},{1,9},{3,11}... | collective-permute-start | bytes 393224 | tf_op jit(solution)/shard_map/ppermute | solution.py:460
  10.3 0.2 collective-permute-start.4
  10.6 3.5 %load.2.refs_1_.refs_2_.refs_3_.refs_6_.refs_8_ = bf16[1,4096,1024]{2,1,0:T(8,128)(2,1)S(1)} custom-call(bf16[1,4096,1024]{2,1,0:T(8,128)(2,1)} %src.3, bf16[32,4096]{1,0:T(8,128)(2,1)S(1)} %get-tuple-element.43.refs_0_), custom_call_target="tpu_custom_call" | custom-call | bytes 1024 | tf_op jit(solution)/shard_map/load/pallas_call | solution.py:132
  14.0 0.0 collective-permute-done.1.refs_1_.refs_2_.refs_3_
  14.1 1.8 %collective-permute-start.7 = (bf16[16,4096]{1,0:T(8,128)(2,1)S(1)}, bf16[16,4096]{1,0:T(8,128)(2,1)S(1)}, u32[]{:S(2)}, u32[]{:S(2)}) collective-permute-start(bf16[16,4096]{1,0:T(8,128)(2,1)S(1)} %get-tuple-element.59), channel_id=1, source_target_pairs={{0,8},{2,10},{4,12},{6,14},{8,0},{10,2},{12,4},{14,6},{1,9},{3,11}... | collective-permute-start | bytes 393224 | tf_op jit(solution)/shard_map/ppermute | solution.py:460
  15.8 2.0 %collective-permute-start.8 = (bf16[16,4096]{1,0:T(8,128)(2,1)S(1)}, bf16[16,4096]{1,0:T(8,128)(2,1)S(1)}, u32[]{:S(2)}, u32[]{:S(2)}) collective-permute-start(bf16[16,4096]{1,0:T(8,128)(2,1)S(1)} %get-tuple-element.60), channel_id=1, source_target_pairs={{0,12},{2,14},{4,8},{6,10},{8,4},{10,6},{12,0},{14,2},{1,13},{3,15... | collective-permute-start | bytes 393224 | tf_op jit(solution)/shard_map/ppermute | solution.py:460
  17.8 0.0 collective-permute-done.refs_0_.refs_1_
  17.8 0.5 collective-permute-start.2
  18.3 3.5 %load.3.refs_3_.refs_4_.refs_7_.refs_9_ = bf16[1,4096,1024]{2,1,0:T(8,128)(2,1)S(1)} custom-call(bf16[1,4096,1024]{2,1,0:T(8,128)(2,1)} %src.4, bf16[32,4096]{1,0:T(8,128)(2,1)S(1)} %collective-permute-done.refs_0_.refs_1_, bf16[1,4096,1024]{2,1,0:T(8,128)(2,1)S(1)} %load.2.refs_1_.refs_2_.refs_3_.refs_6_.refs_8_), custom_call_target="tpu_custom_call" | custom-call | bytes 1024 | tf_op jit(solution)/shard_map/load/pallas_call | solution.py:132
  21.8 0.0 collective-permute-done.3.refs_0_
  21.8 1.3 %collective-permute-done.4.refs_1_ = bf16[16,4096]{1,0:T(8,128)(2,1)S(1)} collective-permute-done((bf16[16,4096]{1,0:T(8,128)(2,1)S(1)}, bf16[16,4096]{1,0:T(8,128)(2,1)S(1)}, u32[]{:S(2)}, u32[]{:S(2)}) %collective-permute-start.4) | collective-permute-done | bytes 131104 | tf_op jit(solution)/shard_map/ppermute | solution.py:460
  23.2 0.6 collective-permute-start.5
  23.7 2.4 %collective-permute-done.2.refs_2_.refs_3_ = bf16[32,4096]{1,0:T(8,128)(2,1)S(1)} collective-permute-done((bf16[32,4096]{1,0:T(8,128)(2,1)S(1)}, bf16[32,4096]{1,0:T(8,128)(2,1)S(1)}, u32[]{:S(2)}, u32[]{:S(2)}) %collective-permute-start.2) | collective-permute-done | bytes 262176 | tf_op jit(solution)/shard_map/ppermute | solution.py:460
  26.2 4.3 %load_turned.1.refs_8_.refs_7_.refs_4_.refs_5_ = bf16[4096,1024]{1,0:T(8,128)(2,1)S(1)} custom-call(bf16[1,1024,4096]{2,1,0:T(8,128)(2,1)} %src.5, bf16[32,4096]{1,0:T(8,128)(2,1)S(1)} %join.2.refs_0_.refs_4_, bf16[32,4096]{1,0:T(8,128)(2,1)S(1)} %collective-permute-done.1.refs_1_.refs_2_.refs_3_, ...), custom_call_target="tpu_custom_call" | custom-call | bytes 1024 | tf_op jit(solution)/shard_map/load_turned/pallas_call | solution.py:165
  30.5 0.4 collective-permute-done.7.refs_0_
  30.9 0.0 collective-permute-done.8.refs_1_
  30.9 0.6 collective-permute-start.9
  31.5 0.0 collective-permute-done.5.refs_5_
  31.5 2.6 %pre_activations.1 = (f32[128,1024]{1,0:T(8,128)S(1)}, f32[128,1024]{1,0:T(8,128)S(1)}, f32[128,1024]{1,0:T(8,128)S(1)}) custom-call(bf16[32,4096]{1,0:T(8,128)(2,1)S(1)} %get-tuple-element.43.refs_0_, bf16[32,4096]{1,0:T(8,128)(2,1)S(1)} %collective-permute-done.refs_0_.refs_1_, bf16[32,4096]{1,0:T(8,128)(2,1)S(1)} %collective-permute-done.1.refs_1_.refs_2_.refs_3_, ...), custom_call_target="tpu_custom_call" | custom-call | flops 5000000000 | bytes 1024 | tf_op jit(solution)/shard_map/pre_activations/pallas_call | solution.py:255
  34.1 4.1 %hidden_grads.2 = (bf16[32,2176]{1,0:T(8,128)(2,1)S(1)}, bf16[32,2176]{1,0:T(8,128)(2,1)S(1)}, bf16[64,1024]{1,0:T(8,128)(2,1)S(1)}, bf16[64,1024]{1,0:T(8,128)(2,1)S(1)}, bf16[64,128]{1,0:T(8,128)(2,1)S(1)}) custom-call(bf16[32,4096]{1,0:T(8,128)(2,1)S(1)} %get-tuple-element.43.refs_0_, bf16[32,4096]{1,0:T(8,128)(2,1)S(1)} %collective-permute-done.refs_0_.refs_1_, ...), custom_call_target="tpu_custom_call" | custom-call | flops 1073741824 | bytes 16777216 | tf_op jit(solution)/shard_map/hidden_grads/pallas_call | solution.py:309
  38.2 1.6 %collective-permute-start.6 = (bf16[32,2176]{1,0:T(8,128)(2,1)S(1)}, bf16[32,2176]{1,0:T(8,128)(2,1)S(1)}, u32[]{:S(2)}, u32[]{:S(2)}) collective-permute-start(bf16[32,2176]{1,0:T(8,128)(2,1)S(1)} %get-tuple-element.51), channel_id=1, source_target_pairs={{0,2},{2,0},{4,6},{6,4},{8,10},{10,8},{12,14},{14,12},{1,3},{3,1},... | collective-permute-start | bytes 417800 | tf_op jit(solution)/shard_map/ppermute | solution.py:460
  39.8 0.0 collective-permute-done.9.refs_1_
  39.8 4.1 %hidden_grads.3 = (bf16[32,2176]{1,0:T(8,128)(2,1)S(1)}, bf16[32,2176]{1,0:T(8,128)(2,1)S(1)}, bf16[64,1024]{1,0:T(8,128)(2,1)S(1)}, bf16[64,1024]{1,0:T(8,128)(2,1)S(1)}, bf16[64,128]{1,0:T(8,128)(2,1)S(1)}) custom-call(bf16[32,4096]{1,0:T(8,128)(2,1)S(1)} %join.3.refs_0_, bf16[32,4096]{1,0:T(8,128)(2,1)S(1)} %collective-permute-done.9.refs_1_, ...), custom_call_target="tpu_custom_call" | custom-call | flops 1073741824 | bytes 16777216 | tf_op jit(solution)/shard_map/hidden_grads/pallas_call | solution.py:309
  43.9 0.6 collective-permute-start.10
  44.5 0.0 collective-permute-done.6.refs_1_.refs_8_
  44.5 0.0 copy-start
  44.5 0.0 copy-start.1
  44.5 0.0 copy-start.2
  44.5 3.0 %back_half.1 = (bf16[32,2176]{1,0:T(8,128)(2,1)S(1)}, bf16[32,2176]{1,0:T(8,128)(2,1)S(1)}, bf16[32,2176]{1,0:T(8,128)(2,1)S(1)}, bf16[32,2176]{1,0:T(8,128)(2,1)S(1)}) custom-call(bf16[64,1024]{1,0:T(8,128)(2,1)S(1)} %get-tuple-element.54.refs_0_, bf16[64,1024]{1,0:T(8,128)(2,1)S(1)} %get-tuple-element.55.refs_1_, ...), custom_call_target="tpu_custom_call" | custom-call | flops 1073741824 | bytes 8388608 | tf_op jit(solution)/shard_map/back_half/pallas_call | solution.py:341
  47.5 1.6 %collective-permute-start.16 = (bf16[32,2176]{1,0:T(8,128)(2,1)S(1)}, bf16[32,2176]{1,0:T(8,128)(2,1)S(1)}, u32[]{:S(2)}, u32[]{:S(2)}) collective-permute-start(bf16[32,2176]{1,0:T(8,128)(2,1)S(1)} %get-tuple-element.74), channel_id=1, source_target_pairs={{0,2},{2,0},{4,6},{6,4},{8,10},{10,8},{12,14},{14,12},{1,3},{3,1},... | collective-permute-start | bytes 417800 | tf_op jit(solution)/shard_map/ppermute | solution.py:460
  49.1 0.9 %collective-permute-done.10.refs_1_ = bf16[32,2176]{1,0:T(8,128)(2,1)S(1)} collective-permute-done((bf16[32,2176]{1,0:T(8,128)(2,1)S(1)}, bf16[32,2176]{1,0:T(8,128)(2,1)S(1)}, u32[]{:S(2)}, u32[]{:S(2)}) %collective-permute-start.10) | collective-permute-done | bytes 139296 | tf_op jit(solution)/shard_map/ppermute | solution.py:460
  50.0 0.0 collective-permute-start.11
  50.0 0.1 sum_pieces.6
  50.1 0.0 collective-permute-start.14
  50.1 4.5 %collective-permute-start.15 = (bf16[16,2176]{1,0:T(8,128)(2,1)S(1)}, bf16[16,2176]{1,0:T(8,128)(2,1)S(1)}, u32[]{:S(2)}, u32[]{:S(2)}) collective-permute-start(bf16[16,2176]{1,0:T(8,128)(2,1)S(1)} %get-tuple-element.72), channel_id=1, source_target_pairs={{0,9},{1,8},{2,11},{3,10},{4,13},{5,12},{6,15},{7,14},{8,1},{9,0},... | collective-permute-start | bytes 208904 | tf_op jit(solution)/shard_map/ppermute | solution.py:474
  54.7 0.1 sum_pieces.4
  54.8 0.0 collective-permute-done.16.refs_1_
  54.8 0.1 sum_pieces.7
  54.9 1.6 %collective-permute-start.17 = (bf16[16,2176]{1,0:T(8,128)(2,1)S(1)}, bf16[16,2176]{1,0:T(8,128)(2,1)S(1)}, u32[]{:S(2)}, u32[]{:S(2)}) collective-permute-start(bf16[16,2176]{1,0:T(8,128)(2,1)S(1)} %get-tuple-element.75), channel_id=1, source_target_pairs={{0,4},{1,5},{2,6},{3,7},{4,0},{5,1},{6,2},{7,3},{8,12},{9,13},{10,... | collective-permute-start | bytes 208904 | tf_op jit(solution)/shard_map/ppermute | solution.py:474
  56.5 0.0 collective-permute-done.11.refs_1_
  56.5 0.1 sum_pieces.5
  56.6 1.9 %collective-permute-start.12 = (bf16[16,2176]{1,0:T(8,128)(2,1)S(1)}, bf16[16,2176]{1,0:T(8,128)(2,1)S(1)}, u32[]{:S(2)}, u32[]{:S(2)}) collective-permute-start(bf16[16,2176]{1,0:T(8,128)(2,1)S(1)} %get-tuple-element.68), channel_id=1, source_target_pairs={{0,5},{1,4},{2,7},{3,6},{4,1},{5,0},{6,3},{7,2},{8,13},{9,12},{10,... | collective-permute-start | bytes 208904 | tf_op jit(solution)/shard_map/ppermute | solution.py:474
  58.5 0.0 collective-permute-start.13
  58.5 0.0 collective-permute-done.14.refs_2_
  58.5 3.3 %collective-permute-start.18 = (bf16[16,2176]{1,0:T(8,128)(2,1)S(1)}, bf16[16,2176]{1,0:T(8,128)(2,1)S(1)}, u32[]{:S(2)}, u32[]{:S(2)}) collective-permute-start(bf16[16,2176]{1,0:T(8,128)(2,1)S(1)} %get-tuple-element.76), channel_id=1, source_target_pairs={{0,12},{1,13},{2,14},{3,15},{4,8},{5,9},{6,10},{7,11},{8,4},{9,5},... | collective-permute-start | bytes 208904 | tf_op jit(solution)/shard_map/ppermute | solution.py:474
  61.7 0.0 collective-permute-done.15.refs_3_
  61.7 0.0 collective-permute-start.19
  61.8 0.0 copy-done
  61.8 0.0 copy-done.1
  61.8 0.0 copy-done.2
  61.8 0.2 mixing.1
  62.0 0.0 collective-permute-done.17.refs_4_
  62.0 0.7 %collective-permute-done.12.refs_0_ = bf16[16,2176]{1,0:T(8,128)(2,1)S(1)} collective-permute-done((bf16[16,2176]{1,0:T(8,128)(2,1)S(1)}, bf16[16,2176]{1,0:T(8,128)(2,1)S(1)}, u32[]{:S(2)}, u32[]{:S(2)}) %collective-permute-start.12) | collective-permute-done | bytes 69664 | tf_op jit(solution)/shard_map/ppermute | solution.py:474
  62.8 0.0 collective-permute-done.13.refs_1_
  62.8 2.6 %collective-permute-done.18.refs_5_ = bf16[16,2176]{1,0:T(8,128)(2,1)S(1)} collective-permute-done((bf16[16,2176]{1,0:T(8,128)(2,1)S(1)}, bf16[16,2176]{1,0:T(8,128)(2,1)S(1)}, u32[]{:S(2)}, u32[]{:S(2)}) %collective-permute-start.18) | collective-permute-done | bytes 69664 | tf_op jit(solution)/shard_map/ppermute | solution.py:474
  65.4 2.8 %collective-permute-done.19.refs_6_ = bf16[16,2176]{1,0:T(8,128)(2,1)S(1)} collective-permute-done((bf16[16,2176]{1,0:T(8,128)(2,1)S(1)}, bf16[16,2176]{1,0:T(8,128)(2,1)S(1)}, u32[]{:S(2)}, u32[]{:S(2)}) %collective-permute-start.19) | collective-permute-done | bytes 69664 | tf_op jit(solution)/shard_map/ppermute | solution.py:474
  68.2 1.2 %combine.1 = (bf16[128,2048]{1,0:T(8,128)(2,1)}, f32[1,128]{1,0:T(1,128)}) custom-call(bf16[2,128,128]{2,1,0:T(8,128)(2,1)S(1)} %get-tuple-element.41.mix_ref, f32[128,128]{1,0:T(8,128)S(1)} %get-tuple-element.42.hit_ref, bf16[16,2176]{1,0:T(8,128)(2,1)S(1)} %collective-permute-done.12.refs_0_, bf16[16,2176]{1,0:T(8,128)(2,1)S(1)} %collective-permute-done.13.refs_1_, ...), custom_call_target="tpu_custom_call" | custom-call | flops 134217728 | bytes 1048576 | tf_op jit(solution)/shard_map/combine/pallas_call | solution.py:437
  (5 shorter events, 0.0 us)
Async XLA Ops:
  3.1 10.9 %collective-permute-start.1 = (bf16[32,4096]{1,0:T(8,128)(2,1)S(1)}, bf16[32,4096]{1,0:T(8,128)(2,1)S(1)}, u32[]{:S(2)}, u32[]{:S(2)}) collective-permute-start(bf16[32,4096]{1,0:T(8,128)(2,1)S(1)} %get-tuple-element.43.refs_0_), channel_id=1, source_target_pairs={{0,2},{2,0},{4,6},{6,4},{8,10},{10,8},{12,14},{14,12},{1,3},{3,1},... | collective-permute-start | bytes 786440 | tf_op jit(solution)/shard_map/ppermute | solution.py:460
  6.2 11.6 %collective-permute-start = (bf16[32,4096]{1,0:T(8,128)(2,1)S(1)}, bf16[32,4096]{1,0:T(8,128)(2,1)S(1)}, u32[]{:S(2)}, u32[]{:S(2)}) collective-permute-start(bf16[32,4096]{1,0:T(8,128)(2,1)S(1)} %get-tuple-element.44), channel_id=1, source_target_pairs={{0,4},{2,6},{4,0},{6,2},{8,12},{10,14},{12,8},{14,10},{1,5},{3,7},... | collective-permute-start | bytes 786440 | tf_op jit(solution)/shard_map/ppermute | solution.py:460
  7.7 14.0 %collective-permute-start.3 = (bf16[16,4096]{1,0:T(8,128)(2,1)S(1)}, bf16[16,4096]{1,0:T(8,128)(2,1)S(1)}, u32[]{:S(2)}, u32[]{:S(2)}) collective-permute-start(bf16[16,4096]{1,0:T(8,128)(2,1)S(1)} %get-tuple-element.45), channel_id=1, source_target_pairs={{0,8},{2,10},{4,12},{6,14},{8,0},{10,2},{12,4},{14,6},{1,9},{3,11}... | collective-permute-start | bytes 393224 | tf_op jit(solution)/shard_map/ppermute | solution.py:460
  10.3 12.8 %collective-permute-start.4 = (bf16[16,4096]{1,0:T(8,128)(2,1)S(1)}, bf16[16,4096]{1,0:T(8,128)(2,1)S(1)}, u32[]{:S(2)}, u32[]{:S(2)}) collective-permute-start(bf16[16,4096]{1,0:T(8,128)(2,1)S(1)} %get-tuple-element.46), channel_id=1, source_target_pairs={{0,12},{2,14},{4,8},{6,10},{8,4},{10,6},{12,0},{14,2},{1,13},{3,15... | collective-permute-start | bytes 393224 | tf_op jit(solution)/shard_map/ppermute | solution.py:460
  14.1 16.8 %collective-permute-start.7 = (bf16[16,4096]{1,0:T(8,128)(2,1)S(1)}, bf16[16,4096]{1,0:T(8,128)(2,1)S(1)}, u32[]{:S(2)}, u32[]{:S(2)}) collective-permute-start(bf16[16,4096]{1,0:T(8,128)(2,1)S(1)} %get-tuple-element.59), channel_id=1, source_target_pairs={{0,8},{2,10},{4,12},{6,14},{8,0},{10,2},{12,4},{14,6},{1,9},{3,11}... | collective-permute-start | bytes 393224 | tf_op jit(solution)/shard_map/ppermute | solution.py:460
  15.8 15.1 %collective-permute-start.8 = (bf16[16,4096]{1,0:T(8,128)(2,1)S(1)}, bf16[16,4096]{1,0:T(8,128)(2,1)S(1)}, u32[]{:S(2)}, u32[]{:S(2)}) collective-permute-start(bf16[16,4096]{1,0:T(8,128)(2,1)S(1)} %get-tuple-element.60), channel_id=1, source_target_pairs={{0,12},{2,14},{4,8},{6,10},{8,4},{10,6},{12,0},{14,2},{1,13},{3,15... | collective-permute-start | bytes 393224 | tf_op jit(solution)/shard_map/ppermute | solution.py:460
  17.8 8.4 %collective-permute-start.2 = (bf16[32,4096]{1,0:T(8,128)(2,1)S(1)}, bf16[32,4096]{1,0:T(8,128)(2,1)S(1)}, u32[]{:S(2)}, u32[]{:S(2)}) collective-permute-start(bf16[32,4096]{1,0:T(8,128)(2,1)S(1)} %collective-permute-done.refs_0_.refs_1_), channel_id=1, source_target_pairs={{0,2},{2,0},{4,6},{6,4},{8,10},{10,8},{12,14},{14,12},{1,3},{3,1},... | collective-permute-start | bytes 786440 | tf_op jit(solution)/shard_map/ppermute | solution.py:460
  23.2 8.3 %collective-permute-start.5 = (bf16[32,4096]{1,0:T(8,128)(2,1)S(1)}, bf16[32,4096]{1,0:T(8,128)(2,1)S(1)}, u32[]{:S(2)}, u32[]{:S(2)}) collective-permute-start(bf16[32,4096]{1,0:T(8,128)(2,1)S(1)} %join.2.refs_0_.refs_4_), channel_id=1, source_target_pairs={{0,2},{2,0},{4,6},{6,4},{8,10},{10,8},{12,14},{14,12},{1,3},{3,1},... | collective-permute-start | bytes 786440 | tf_op jit(solution)/shard_map/ppermute | solution.py:460
  30.9 8.9 %collective-permute-start.9 = (bf16[32,4096]{1,0:T(8,128)(2,1)S(1)}, bf16[32,4096]{1,0:T(8,128)(2,1)S(1)}, u32[]{:S(2)}, u32[]{:S(2)}) collective-permute-start(bf16[32,4096]{1,0:T(8,128)(2,1)S(1)} %join.3.refs_0_), channel_id=1, source_target_pairs={{0,2},{2,0},{4,6},{6,4},{8,10},{10,8},{12,14},{14,12},{1,3},{3,1},... | collective-permute-start | bytes 786440 | tf_op jit(solution)/shard_map/ppermute | solution.py:460
  38.2 6.3 %collective-permute-start.6 = (bf16[32,2176]{1,0:T(8,128)(2,1)S(1)}, bf16[32,2176]{1,0:T(8,128)(2,1)S(1)}, u32[]{:S(2)}, u32[]{:S(2)}) collective-permute-start(bf16[32,2176]{1,0:T(8,128)(2,1)S(1)} %get-tuple-element.51), channel_id=1, source_target_pairs={{0,2},{2,0},{4,6},{6,4},{8,10},{10,8},{12,14},{14,12},{1,3},{3,1},... | collective-permute-start | bytes 417800 | tf_op jit(solution)/shard_map/ppermute | solution.py:460
  43.9 6.1 %collective-permute-start.10 = (bf16[32,2176]{1,0:T(8,128)(2,1)S(1)}, bf16[32,2176]{1,0:T(8,128)(2,1)S(1)}, u32[]{:S(2)}, u32[]{:S(2)}) collective-permute-start(bf16[32,2176]{1,0:T(8,128)(2,1)S(1)} %get-tuple-element.66), channel_id=1, source_target_pairs={{0,2},{2,0},{4,6},{6,4},{8,10},{10,8},{12,14},{14,12},{1,3},{3,1},... | collective-permute-start | bytes 417800 | tf_op jit(solution)/shard_map/ppermute | solution.py:460
  44.5 17.3 %copy-start = (s32[128,2]{0,1:T(2,128)S(1)}, s32[128,2]{0,1:T(2,128)}, u32[]{:S(2)}) copy-start(s32[128,2]{0,1:T(2,128)} %param.11) | copy-start | bytes 3076
  44.5 17.3 %copy-start.1 = (s32[128]{0:T(128)S(1)}, s32[128]{0:T(128)}, u32[]{:S(2)}) copy-start(s32[128]{0:T(128)} %param.10) | copy-start | bytes 1540
  44.5 17.3 %copy-start.2 = (f32[128,2]{0,1:T(2,128)S(1)}, f32[128,2]{0,1:T(2,128)}, u32[]{:S(2)}) copy-start(f32[128,2]{0,1:T(2,128)} %param.12) | copy-start | bytes 3076
  47.5 7.2 %collective-permute-start.16 = (bf16[32,2176]{1,0:T(8,128)(2,1)S(1)}, bf16[32,2176]{1,0:T(8,128)(2,1)S(1)}, u32[]{:S(2)}, u32[]{:S(2)}) collective-permute-start(bf16[32,2176]{1,0:T(8,128)(2,1)S(1)} %get-tuple-element.74), channel_id=1, source_target_pairs={{0,2},{2,0},{4,6},{6,4},{8,10},{10,8},{12,14},{14,12},{1,3},{3,1},... | collective-permute-start | bytes 417800 | tf_op jit(solution)/shard_map/ppermute | solution.py:460
  50.0 6.5 %collective-permute-start.11 = (bf16[32,2176]{1,0:T(8,128)(2,1)S(1)}, bf16[32,2176]{1,0:T(8,128)(2,1)S(1)}, u32[]{:S(2)}, u32[]{:S(2)}) collective-permute-start(bf16[32,2176]{1,0:T(8,128)(2,1)S(1)} %pass_after.4), channel_id=1, source_target_pairs={{0,2},{2,0},{4,6},{6,4},{8,10},{10,8},{12,14},{14,12},{1,3},{3,1},... | collective-permute-start | bytes 417800 | tf_op jit(solution)/shard_map/ppermute | solution.py:460
  50.1 8.4 %collective-permute-start.14 = (bf16[16,2176]{1,0:T(8,128)(2,1)S(1)}, bf16[16,2176]{1,0:T(8,128)(2,1)S(1)}, u32[]{:S(2)}, u32[]{:S(2)}) collective-permute-start(bf16[16,2176]{1,0:T(8,128)(2,1)S(1)} %get-tuple-element.71), channel_id=1, source_target_pairs={{0,13},{1,12},{2,15},{3,14},{4,9},{5,8},{6,11},{7,10},{8,5},{9,4},... | collective-permute-start | bytes 208904 | tf_op jit(solution)/shard_map/ppermute | solution.py:474
  50.1 11.6 %collective-permute-start.15 = (bf16[16,2176]{1,0:T(8,128)(2,1)S(1)}, bf16[16,2176]{1,0:T(8,128)(2,1)S(1)}, u32[]{:S(2)}, u32[]{:S(2)}) collective-permute-start(bf16[16,2176]{1,0:T(8,128)(2,1)S(1)} %get-tuple-element.72), channel_id=1, source_target_pairs={{0,9},{1,8},{2,11},{3,10},{4,13},{5,12},{6,15},{7,14},{8,1},{9,0},... | collective-permute-start | bytes 208904 | tf_op jit(solution)/shard_map/ppermute | solution.py:474
  54.9 7.2 %collective-permute-start.17 = (bf16[16,2176]{1,0:T(8,128)(2,1)S(1)}, bf16[16,2176]{1,0:T(8,128)(2,1)S(1)}, u32[]{:S(2)}, u32[]{:S(2)}) collective-permute-start(bf16[16,2176]{1,0:T(8,128)(2,1)S(1)} %get-tuple-element.75), channel_id=1, source_target_pairs={{0,4},{1,5},{2,6},{3,7},{4,0},{5,1},{6,2},{7,3},{8,12},{9,13},{10,... | collective-permute-start | bytes 208904 | tf_op jit(solution)/shard_map/ppermute | solution.py:474
  56.6 6.2 %collective-permute-start.12 = (bf16[16,2176]{1,0:T(8,128)(2,1)S(1)}, bf16[16,2176]{1,0:T(8,128)(2,1)S(1)}, u32[]{:S(2)}, u32[]{:S(2)}) collective-permute-start(bf16[16,2176]{1,0:T(8,128)(2,1)S(1)} %get-tuple-element.68), channel_id=1, source_target_pairs={{0,5},{1,4},{2,7},{3,6},{4,1},{5,0},{6,3},{7,2},{8,13},{9,12},{10,... | collective-permute-start | bytes 208904 | tf_op jit(solution)/shard_map/ppermute | solution.py:474
  58.5 4.3 %collective-permute-start.13 = (bf16[16,2176]{1,0:T(8,128)(2,1)S(1)}, bf16[16,2176]{1,0:T(8,128)(2,1)S(1)}, u32[]{:S(2)}, u32[]{:S(2)}) collective-permute-start(bf16[16,2176]{1,0:T(8,128)(2,1)S(1)} %get-tuple-element.69), channel_id=1, source_target_pairs={{0,1},{1,0},{2,3},{3,2},{4,5},{5,4},{6,7},{7,6},{8,9},{9,8},{10,11... | collective-permute-start | bytes 208904 | tf_op jit(solution)/shard_map/ppermute | solution.py:474
  58.5 6.9 %collective-permute-start.18 = (bf16[16,2176]{1,0:T(8,128)(2,1)S(1)}, bf16[16,2176]{1,0:T(8,128)(2,1)S(1)}, u32[]{:S(2)}, u32[]{:S(2)}) collective-permute-start(bf16[16,2176]{1,0:T(8,128)(2,1)S(1)} %get-tuple-element.76), channel_id=1, source_target_pairs={{0,12},{1,13},{2,14},{3,15},{4,8},{5,9},{6,10},{7,11},{8,4},{9,5},... | collective-permute-start | bytes 208904 | tf_op jit(solution)/shard_map/ppermute | solution.py:474
  61.7 6.5 %collective-permute-start.19 = (bf16[16,2176]{1,0:T(8,128)(2,1)S(1)}, bf16[16,2176]{1,0:T(8,128)(2,1)S(1)}, u32[]{:S(2)}, u32[]{:S(2)}) collective-permute-start(bf16[16,2176]{1,0:T(8,128)(2,1)S(1)} %get-tuple-element.67.refs_2_), channel_id=1, source_target_pairs={{0,8},{1,9},{2,10},{3,11},{4,12},{5,13},{6,14},{7,15},{8,0},{9,1},... | collective-permute-start | bytes 208904 | tf_op jit(solution)/shard_map/ppermute | solution.py:474

commit v12 on v10

--- a/solution.py
+++ b/solution.py
@@ -22,10 +22,6 @@
 
 def whole(shape):
     return pl.BlockSpec(shape, lambda *_: (0,) * len(shape))
-
-
-def nt_dot(lhs, rhs):
-    return lax.dot_general(lhs, rhs, (((1,), (1,)), ((), ())), preferred_element_type=F32)
 
 
 def position(groups):
@@ -268,11 +264,13 @@
     half = jnp.bitwise_xor(position(groups)[1], flip)
     wide = outs[0].shape[1] - EXT
     own_rows = outs[0].shape[0]
+    dgate, dup = dgate_ref[...].T, dup_ref[...].T
     chunk = 512
     for step in range(wide // chunk):
         rows = pl.ds(pl.multiple_of(half * wide + step * chunk, chunk), chunk)
-        grad = nt_dot(dgate_ref[...], gate_ref[0, rows, :]) + nt_dot(dup_ref[...], up_ref[0, rows, :])
-        grad = grad.astype(BF16)
+        grad = jnp.dot(gate_ref[0, rows, :], dgate, preferred_element_type=F32)
+        grad = grad + jnp.dot(up_ref[0, rows, :], dup, preferred_element_type=F32)
+        grad = grad.T.astype(BF16)
         for t in range(groups):
             outs[t][:, step * chunk : (step + 1) * chunk] = grad[t * own_rows : (t + 1) * own_rows, :]
     for t in range(groups):

time: 68.3 us -> 67.9 us (level)
  Pallas kernels: 25 us -> 24.1 us
where the time goes in v12:
time: 67.9 us; the launch traced here: 67.7 us
  starting transfers between devices  25.4 us (37%)
  Pallas kernels  24.1 us (35%)
  waiting for transfers between devices  17.5 us (26%)
  between operations  0.76 us (1%)
    ppermute x11, starting transfers between devices, to_expert(): lax.ppermute(x, 'ep', [(e * groups + j, (e ^ s) * groups + (j + t) % grou...  13.9 us
    ppermute x11, waiting for transfers between devices, to_expert(): lax.ppermute(x, 'ep', [(e * groups + j, (e ^ s) * groups + (j + t) % grou...  12.8 us
    ppermute x7, starting transfers between devices, to_source(): lax.ppermute(x, ('ep', 'mod'), [((e * groups + j) * 2 + m, ((e ^ s) * gro...  11.5 us
    pallas_call x2, Pallas kernels, load(): pl.pallas_call(functools.partial(load_kernel, parts), in_specs=[pl.BlockS...  6.94 us
    ppermute x7, waiting for transfers between devices, to_source(): lax.ppermute(x, ('ep', 'mod'), [((e * groups + j) * 2 + m, ((e ^ s) * gro...  4.66 us
    pallas_call x1, Pallas kernels, load_turned(): pl.pallas_call(functools.partial(load_turned_kernel, parts), in_specs=[pl...  4.29 us
    pallas_call x1, Pallas kernels, hidden_grads(): pl.pallas_call(functools.partial(hidden_kernel, count, places, groups), i...  3.62 us
    pallas_call x1, Pallas kernels, pre_activations(): pl.pallas_call(functools.partial(pre_kernel, count, places), in_specs=[vm...  2.61 us
  transfers between devices with their start and end apart: 18, of which 9 were waited for; matrix products, arithmetic and copies ran while one was open for 0% of the time, Pallas kernels for 25%

profile of v12, /device:TPU:0, one launch (start us, length us, event | category | flops | bytes accessed | tf_op | source)
XLA Modules:
  0.0 67.7 jit_solution(11305251472498327093)
XLA Ops:
  0.6 2.5 %gather_slots.1 = (bf16[32,4096]{1,0:T(8,128)(2,1)S(1)}, bf16[32,4096]{1,0:T(8,128)(2,1)S(1)}, bf16[16,4096]{1,0:T(8,128)(2,1)S(1)}, bf16[16,4096]{1,0:T(8,128)(...) custom-call(s32[1,128]{1,0:T(1,128)} %bitcast.6, s32[2,128]{1,0:T(2,128)} %bitcast.4, ...), custom_call_target="tpu_custom_call" | custom-call | flops 134217728 | bytes 3145728 | tf_op jit(solution)/shard_map/gather_slots/pallas_call | solution.py:93
  3.1 3.0 %collective-permute-start.1 = (bf16[32,4096]{1,0:T(8,128)(2,1)S(1)}, bf16[32,4096]{1,0:T(8,128)(2,1)S(1)}, u32[]{:S(2)}, u32[]{:S(2)}) collective-permute-start(bf16[32,4096]{1,0:T(8,128)(2,1)S(1)} %get-tuple-element.34.refs_0_), channel_id=1, source_target_pairs={{0,2},{2,0},{4,6},{6,4},{8,10},{10,8},{12,14},{14,12},{1,3},{3,1},... | collective-permute-start | bytes 786440 | tf_op jit(solution)/shard_map/ppermute | solution.py:446
  6.2 1.6 %collective-permute-start = (bf16[32,4096]{1,0:T(8,128)(2,1)S(1)}, bf16[32,4096]{1,0:T(8,128)(2,1)S(1)}, u32[]{:S(2)}, u32[]{:S(2)}) collective-permute-start(bf16[32,4096]{1,0:T(8,128)(2,1)S(1)} %get-tuple-element.35), channel_id=1, source_target_pairs={{0,4},{2,6},{4,0},{6,2},{8,12},{10,14},{12,8},{14,10},{1,5},{3,7},... | collective-permute-start | bytes 786440 | tf_op jit(solution)/shard_map/ppermute | solution.py:446
  7.7 2.6 %collective-permute-start.5 = (bf16[16,4096]{1,0:T(8,128)(2,1)S(1)}, bf16[16,4096]{1,0:T(8,128)(2,1)S(1)}, u32[]{:S(2)}, u32[]{:S(2)}) collective-permute-start(bf16[16,4096]{1,0:T(8,128)(2,1)S(1)} %get-tuple-element.40), channel_id=1, source_target_pairs={{0,8},{2,10},{4,12},{6,14},{8,0},{10,2},{12,4},{14,6},{1,9},{3,11}... | collective-permute-start | bytes 393224 | tf_op jit(solution)/shard_map/ppermute | solution.py:446
  10.3 0.2 collective-permute-start.6
  10.6 3.5 %load.2.refs_2_.refs_1_.refs_3_.refs_6_.refs_10_.gate_ref = bf16[1,4096,1024]{2,1,0:T(8,128)(2,1)S(1)} custom-call(bf16[1,4096,1024]{2,1,0:T(8,128)(2,1)} %src.3, bf16[32,4096]{1,0:T(8,128)(2,1)S(1)} %get-tuple-element.34.refs_0_), custom_call_target="tpu_custom_call" | custom-call | bytes 1024 | tf_op jit(solution)/shard_map/load/pallas_call | solution.py:128
  14.0 0.0 collective-permute-done.1.refs_3_.refs_1_.refs_2_
  14.1 1.8 %collective-permute-start.3 = (bf16[16,4096]{1,0:T(8,128)(2,1)S(1)}, bf16[16,4096]{1,0:T(8,128)(2,1)S(1)}, u32[]{:S(2)}, u32[]{:S(2)}) collective-permute-start(bf16[16,4096]{1,0:T(8,128)(2,1)S(1)} %get-tuple-element.38), channel_id=1, source_target_pairs={{0,8},{2,10},{4,12},{6,14},{8,0},{10,2},{12,4},{14,6},{1,9},{3,11}... | collective-permute-start | bytes 393224 | tf_op jit(solution)/shard_map/ppermute | solution.py:446
  15.8 2.0 %collective-permute-start.4 = (bf16[16,4096]{1,0:T(8,128)(2,1)S(1)}, bf16[16,4096]{1,0:T(8,128)(2,1)S(1)}, u32[]{:S(2)}, u32[]{:S(2)}) collective-permute-start(bf16[16,4096]{1,0:T(8,128)(2,1)S(1)} %get-tuple-element.39), channel_id=1, source_target_pairs={{0,12},{2,14},{4,8},{6,10},{8,4},{10,6},{12,0},{14,2},{1,13},{3,15... | collective-permute-start | bytes 393224 | tf_op jit(solution)/shard_map/ppermute | solution.py:446
  17.8 0.0 collective-permute-done.refs_0_.refs_1_
  17.8 0.5 collective-permute-start.2
  18.3 3.5 %load.3.refs_3_.refs_4_.refs_7_.refs_11_.up_ref = bf16[1,4096,1024]{2,1,0:T(8,128)(2,1)S(1)} custom-call(bf16[1,4096,1024]{2,1,0:T(8,128)(2,1)} %src.4, bf16[32,4096]{1,0:T(8,128)(2,1)S(1)} %collective-permute-done.refs_0_.refs_1_, bf16[1,4096,1024]{2,1,0:T(8,128)(2,1)S(1)} %load.2.refs_2_.refs_1_.refs_3_.refs_6_.refs_10_.gate_ref), custom_call_target="tpu_custom_call" | custom-call | bytes 1024 | tf_op jit(solution)/shard_map/load/pallas_call | solution.py:128
  21.8 0.0 collective-permute-done.5.refs_0_
  21.8 1.3 %collective-permute-done.6.refs_1_ = bf16[16,4096]{1,0:T(8,128)(2,1)S(1)} collective-permute-done((bf16[16,4096]{1,0:T(8,128)(2,1)S(1)}, bf16[16,4096]{1,0:T(8,128)(2,1)S(1)}, u32[]{:S(2)}, u32[]{:S(2)}) %collective-permute-start.6) | collective-permute-done | bytes 131104 | tf_op jit(solution)/shard_map/ppermute | solution.py:446
  23.2 0.6 collective-permute-start.8
  23.7 2.4 %collective-permute-done.2.refs_2_.refs_3_ = bf16[32,4096]{1,0:T(8,128)(2,1)S(1)} collective-permute-done((bf16[32,4096]{1,0:T(8,128)(2,1)S(1)}, bf16[32,4096]{1,0:T(8,128)(2,1)S(1)}, u32[]{:S(2)}, u32[]{:S(2)}) %collective-permute-start.2) | collective-permute-done | bytes 262176 | tf_op jit(solution)/shard_map/ppermute | solution.py:446
  26.2 4.3 %load_turned.1.refs_4_.refs_8_.refs_9_ = bf16[4096,1024]{1,0:T(8,128)(2,1)S(1)} custom-call(bf16[1,1024,4096]{2,1,0:T(8,128)(2,1)} %src.5, bf16[32,4096]{1,0:T(8,128)(2,1)S(1)} %join.2.refs_0_.refs_4_, bf16[32,4096]{1,0:T(8,128)(2,1)S(1)} %collective-permute-done.1.refs_3_.refs_1_.refs_2_, bf16[32,4096]{1,0:T(8,128)(2,1)S(1)} %collective-permute-done.2.refs_2_.refs_3_, ...), custom_call_target="tpu_custom_call" | custom-call | bytes 1024 | tf_op jit(solution)/shard_map/load_turned/pallas_call | solution.py:161
  30.5 0.4 collective-permute-done.3.refs_0_
  30.9 0.0 collective-permute-done.4.refs_1_
  30.9 0.6 collective-permute-start.7
  31.5 0.0 collective-permute-done.8.refs_5_
  31.5 2.6 %pre_activations.1 = (f32[128,1024]{1,0:T(8,128)S(1)}, f32[128,1024]{1,0:T(8,128)S(1)}, f32[128,1024]{1,0:T(8,128)S(1)}) custom-call(bf16[32,4096]{1,0:T(8,128)(2,1)S(1)} %get-tuple-element.34.refs_0_, bf16[32,4096]{1,0:T(8,128)(2,1)S(1)} %collective-permute-done.refs_0_.refs_1_, bf16[32,4096]{1,0:T(8,128)(2,1)S(1)} %collective-permute-done.1.refs_3_.refs_1_.refs_2_, ...), custom_call_target="tpu_custom_call" | custom-call | flops 5000000000 | bytes 1024 | tf_op jit(solution)/shard_map/pre_activations/pallas_call | solution.py:251
  34.1 3.9 %collective-permute-done.7.refs_5_ = bf16[32,4096]{1,0:T(8,128)(2,1)S(1)} collective-permute-done((bf16[32,4096]{1,0:T(8,128)(2,1)S(1)}, bf16[32,4096]{1,0:T(8,128)(2,1)S(1)}, u32[]{:S(2)}, u32[]{:S(2)}) %collective-permute-start.7) | collective-permute-done | bytes 262176 | tf_op jit(solution)/shard_map/ppermute | solution.py:446
  38.0 3.6 %hidden_grads.1 = (bf16[64,2176]{1,0:T(8,128)(2,1)S(1)}, bf16[64,2176]{1,0:T(8,128)(2,1)S(1)}, bf16[128,1024]{1,0:T(8,128)(2,1)S(1)}, bf16[128,1024]{1,0:T(8,128)(2,1)S(1)}, bf16[128,128]{1,0:T(8,128)(2,1)S(1)}) custom-call(bf16[32,4096]{1,0:T(8,128)(2,1)S(1)} %get-tuple-element.34.refs_0_, bf16[32,4096]{1,0:T(8,128)(2,1)S(1)} %collective-permute-done.refs_0_.refs_1_, ...), custom_call_target="tpu_custom_call" | custom-call | flops 2147483648 | bytes 16777216 | tf_op jit(solution)/shard_map/hidden_grads/pallas_call | solution.py:305
  41.6 0.6 collective-permute-start.9
  42.2 0.0 copy-start
  42.2 0.0 copy-start.1
  42.2 0.0 copy-start.2
  42.2 2.4 %back_half.1 = (bf16[64,2176]{1,0:T(8,128)(2,1)S(1)}, bf16[64,2176]{1,0:T(8,128)(2,1)S(1)}) custom-call(bf16[128,1024]{1,0:T(8,128)(2,1)S(1)} %get-tuple-element.51.dgate_ref, bf16[128,1024]{1,0:T(8,128)(2,1)S(1)} %get-tuple-element.52.dup_ref, bf16[128,128]{1,0:T(8,128)(2,1)S(1)} %get-tuple-element.53.part_ref, ...), custom_call_target="tpu_custom_call" | custom-call | flops 1073741824 | bytes 8388608 | tf_op jit(solution)/shard_map/back_half/pallas_call | solution.py:329
  44.6 4.2 %collective-permute-done.9.refs_1_ = bf16[64,2176]{1,0:T(8,128)(2,1)S(1)} collective-permute-done((bf16[64,2176]{1,0:T(8,128)(2,1)S(1)}, bf16[64,2176]{1,0:T(8,128)(2,1)S(1)}, u32[]{:S(2)}, u32[]{:S(2)}) %collective-permute-start.9) | collective-permute-done | bytes 278560 | tf_op jit(solution)/shard_map/ppermute | solution.py:446
  48.8 0.5 collective-permute-start.14
  49.3 0.1 sum_pieces.2
  49.4 0.1 collective-permute-start.10
  49.5 4.2 %collective-permute-start.11 = (bf16[16,2176]{1,0:T(8,128)(2,1)S(1)}, bf16[16,2176]{1,0:T(8,128)(2,1)S(1)}, u32[]{:S(2)}, u32[]{:S(2)}) collective-permute-start(bf16[16,2176]{1,0:T(8,128)(2,1)S(1)} %get-tuple-element.48), channel_id=1, source_target_pairs={{0,9},{1,8},{2,11},{3,10},{4,13},{5,12},{6,15},{7,14},{8,1},{9,0},... | collective-permute-start | bytes 208904 | tf_op jit(solution)/shard_map/ppermute | solution.py:460
  53.7 1.1 %collective-permute-start.12 = (bf16[16,2176]{1,0:T(8,128)(2,1)S(1)}, bf16[16,2176]{1,0:T(8,128)(2,1)S(1)}, u32[]{:S(2)}, u32[]{:S(2)}) collective-permute-start(bf16[16,2176]{1,0:T(8,128)(2,1)S(1)} %get-tuple-element.49), channel_id=1, source_target_pairs={{0,5},{1,4},{2,7},{3,6},{4,1},{5,0},{6,3},{7,2},{8,13},{9,12},{10,... | collective-permute-start | bytes 208904 | tf_op jit(solution)/shard_map/ppermute | solution.py:460
  54.9 0.0 collective-permute-start.13
  54.9 0.5 collective-permute-done.14.refs_1_
  55.4 0.1 sum_pieces.3
  55.5 5.4 %collective-permute-start.15 = (bf16[16,2176]{1,0:T(8,128)(2,1)S(1)}, bf16[16,2176]{1,0:T(8,128)(2,1)S(1)}, u32[]{:S(2)}, u32[]{:S(2)}) collective-permute-start(bf16[16,2176]{1,0:T(8,128)(2,1)S(1)} %get-tuple-element.56), channel_id=1, source_target_pairs={{0,12},{1,13},{2,14},{3,15},{4,8},{5,9},{6,10},{7,11},{8,4},{9,5},... | collective-permute-start | bytes 208904 | tf_op jit(solution)/shard_map/ppermute | solution.py:460
  60.9 0.0 collective-permute-done.10.refs_0_
  60.9 0.0 collective-permute-start.16
  60.9 0.0 collective-permute-done.11.refs_1_
  60.9 0.6 collective-permute-start.17
  61.6 0.0 copy-done
  61.6 0.0 copy-done.1
  61.6 0.0 copy-done.2
  61.6 0.2 mixing.1
  61.8 0.0 collective-permute-done.12.refs_2_
  61.8 0.0 collective-permute-done.13.refs_3_
  61.8 2.0 %collective-permute-done.15.refs_4_ = bf16[16,2176]{1,0:T(8,128)(2,1)S(1)} collective-permute-done((bf16[16,2176]{1,0:T(8,128)(2,1)S(1)}, bf16[16,2176]{1,0:T(8,128)(2,1)S(1)}, u32[]{:S(2)}, u32[]{:S(2)}) %collective-permute-start.15) | collective-permute-done | bytes 69664 | tf_op jit(solution)/shard_map/ppermute | solution.py:460
  63.9 2.5 %collective-permute-done.16.refs_5_ = bf16[16,2176]{1,0:T(8,128)(2,1)S(1)} collective-permute-done((bf16[16,2176]{1,0:T(8,128)(2,1)S(1)}, bf16[16,2176]{1,0:T(8,128)(2,1)S(1)}, u32[]{:S(2)}, u32[]{:S(2)}) %collective-permute-start.16) | collective-permute-done | bytes 69664 | tf_op jit(solution)/shard_map/ppermute | solution.py:460
  66.4 0.1 collective-permute-done.17.refs_6_
  66.5 1.2 %combine.1 = (bf16[128,2048]{1,0:T(8,128)(2,1)}, f32[1,128]{1,0:T(1,128)}) custom-call(bf16[2,128,128]{2,1,0:T(8,128)(2,1)S(1)} %get-tuple-element.32.mix_ref, f32[128,128]{1,0:T(8,128)S(1)} %get-tuple-element.33.hit_ref, bf16[16,2176]{1,0:T(8,128)(2,1)S(1)} %collective-permute-done.10.refs_0_, bf16[16,2176]{1,0:T(8,128)(2,1)S(1)} %collective-permute-done.11.refs_1_, ...), custom_call_target="tpu_custom_call" | custom-call | flops 134217728 | bytes 1048576 | tf_op jit(solution)/shard_map/combine/pallas_call | solution.py:423
  (4 shorter events, 0.0 us)
Async XLA Ops:
  3.1 10.9 %collective-permute-start.1 = (bf16[32,4096]{1,0:T(8,128)(2,1)S(1)}, bf16[32,4096]{1,0:T(8,128)(2,1)S(1)}, u32[]{:S(2)}, u32[]{:S(2)}) collective-permute-start(bf16[32,4096]{1,0:T(8,128)(2,1)S(1)} %get-tuple-element.34.refs_0_), channel_id=1, source_target_pairs={{0,2},{2,0},{4,6},{6,4},{8,10},{10,8},{12,14},{14,12},{1,3},{3,1},... | collective-permute-start | bytes 786440 | tf_op jit(solution)/shard_map/ppermute | solution.py:446
  6.2 11.6 %collective-permute-start = (bf16[32,4096]{1,0:T(8,128)(2,1)S(1)}, bf16[32,4096]{1,0:T(8,128)(2,1)S(1)}, u32[]{:S(2)}, u32[]{:S(2)}) collective-permute-start(bf16[32,4096]{1,0:T(8,128)(2,1)S(1)} %get-tuple-element.35), channel_id=1, source_target_pairs={{0,4},{2,6},{4,0},{6,2},{8,12},{10,14},{12,8},{14,10},{1,5},{3,7},... | collective-permute-start | bytes 786440 | tf_op jit(solution)/shard_map/ppermute | solution.py:446
  7.7 14.1 %collective-permute-start.5 = (bf16[16,4096]{1,0:T(8,128)(2,1)S(1)}, bf16[16,4096]{1,0:T(8,128)(2,1)S(1)}, u32[]{:S(2)}, u32[]{:S(2)}) collective-permute-start(bf16[16,4096]{1,0:T(8,128)(2,1)S(1)} %get-tuple-element.40), channel_id=1, source_target_pairs={{0,8},{2,10},{4,12},{6,14},{8,0},{10,2},{12,4},{14,6},{1,9},{3,11}... | collective-permute-start | bytes 393224 | tf_op jit(solution)/shard_map/ppermute | solution.py:446
  10.3 12.8 %collective-permute-start.6 = (bf16[16,4096]{1,0:T(8,128)(2,1)S(1)}, bf16[16,4096]{1,0:T(8,128)(2,1)S(1)}, u32[]{:S(2)}, u32[]{:S(2)}) collective-permute-start(bf16[16,4096]{1,0:T(8,128)(2,1)S(1)} %get-tuple-element.41), channel_id=1, source_target_pairs={{0,12},{2,14},{4,8},{6,10},{8,4},{10,6},{12,0},{14,2},{1,13},{3,15... | collective-permute-start | bytes 393224 | tf_op jit(solution)/shard_map/ppermute | solution.py:446
  14.1 16.8 %collective-permute-start.3 = (bf16[16,4096]{1,0:T(8,128)(2,1)S(1)}, bf16[16,4096]{1,0:T(8,128)(2,1)S(1)}, u32[]{:S(2)}, u32[]{:S(2)}) collective-permute-start(bf16[16,4096]{1,0:T(8,128)(2,1)S(1)} %get-tuple-element.38), channel_id=1, source_target_pairs={{0,8},{2,10},{4,12},{6,14},{8,0},{10,2},{12,4},{14,6},{1,9},{3,11}... | collective-permute-start | bytes 393224 | tf_op jit(solution)/shard_map/ppermute | solution.py:446
  15.8 15.1 %collective-permute-start.4 = (bf16[16,4096]{1,0:T(8,128)(2,1)S(1)}, bf16[16,4096]{1,0:T(8,128)(2,1)S(1)}, u32[]{:S(2)}, u32[]{:S(2)}) collective-permute-start(bf16[16,4096]{1,0:T(8,128)(2,1)S(1)} %get-tuple-element.39), channel_id=1, source_target_pairs={{0,12},{2,14},{4,8},{6,10},{8,4},{10,6},{12,0},{14,2},{1,13},{3,15... | collective-permute-start | bytes 393224 | tf_op jit(solution)/shard_map/ppermute | solution.py:446
  17.8 8.3 %collective-permute-start.2 = (bf16[32,4096]{1,0:T(8,128)(2,1)S(1)}, bf16[32,4096]{1,0:T(8,128)(2,1)S(1)}, u32[]{:S(2)}, u32[]{:S(2)}) collective-permute-start(bf16[32,4096]{1,0:T(8,128)(2,1)S(1)} %collective-permute-done.refs_0_.refs_1_), channel_id=1, source_target_pairs={{0,2},{2,0},{4,6},{6,4},{8,10},{10,8},{12,14},{14,12},{1,3},{3,1},... | collective-permute-start | bytes 786440 | tf_op jit(solution)/shard_map/ppermute | solution.py:446
  23.2 8.3 %collective-permute-start.8 = (bf16[32,4096]{1,0:T(8,128)(2,1)S(1)}, bf16[32,4096]{1,0:T(8,128)(2,1)S(1)}, u32[]{:S(2)}, u32[]{:S(2)}) collective-permute-start(bf16[32,4096]{1,0:T(8,128)(2,1)S(1)} %join.2.refs_0_.refs_4_), channel_id=1, source_target_pairs={{0,2},{2,0},{4,6},{6,4},{8,10},{10,8},{12,14},{14,12},{1,3},{3,1},... | collective-permute-start | bytes 786440 | tf_op jit(solution)/shard_map/ppermute | solution.py:446
  30.9 7.1 %collective-permute-start.7 = (bf16[32,4096]{1,0:T(8,128)(2,1)S(1)}, bf16[32,4096]{1,0:T(8,128)(2,1)S(1)}, u32[]{:S(2)}, u32[]{:S(2)}) collective-permute-start(bf16[32,4096]{1,0:T(8,128)(2,1)S(1)} %join.3.refs_4_), channel_id=1, source_target_pairs={{0,2},{2,0},{4,6},{6,4},{8,10},{10,8},{12,14},{14,12},{1,3},{3,1},... | collective-permute-start | bytes 786440 | tf_op jit(solution)/shard_map/ppermute | solution.py:446
  41.6 7.2 %collective-permute-start.9 = (bf16[64,2176]{1,0:T(8,128)(2,1)S(1)}, bf16[64,2176]{1,0:T(8,128)(2,1)S(1)}, u32[]{:S(2)}, u32[]{:S(2)}) collective-permute-start(bf16[64,2176]{1,0:T(8,128)(2,1)S(1)} %get-tuple-element.46), channel_id=1, source_target_pairs={{0,2},{2,0},{4,6},{6,4},{8,10},{10,8},{12,14},{14,12},{1,3},{3,1},... | collective-permute-start | bytes 835592 | tf_op jit(solution)/shard_map/ppermute | solution.py:446
  42.2 19.4 %copy-start = (s32[128,2]{0,1:T(2,128)S(1)}, s32[128,2]{0,1:T(2,128)}, u32[]{:S(2)}) copy-start(s32[128,2]{0,1:T(2,128)} %param.11) | copy-start | bytes 3076
  42.2 19.4 %copy-start.1 = (s32[128]{0:T(128)S(1)}, s32[128]{0:T(128)}, u32[]{:S(2)}) copy-start(s32[128]{0:T(128)} %param.10) | copy-start | bytes 1540
  42.2 19.4 %copy-start.2 = (f32[128,2]{0,1:T(2,128)S(1)}, f32[128,2]{0,1:T(2,128)}, u32[]{:S(2)}) copy-start(f32[128,2]{0,1:T(2,128)} %param.12) | copy-start | bytes 3076
  48.8 6.5 %collective-permute-start.14 = (bf16[64,2176]{1,0:T(8,128)(2,1)S(1)}, bf16[64,2176]{1,0:T(8,128)(2,1)S(1)}, u32[]{:S(2)}, u32[]{:S(2)}) collective-permute-start(bf16[64,2176]{1,0:T(8,128)(2,1)S(1)} %pass_after.3), channel_id=1, source_target_pairs={{0,2},{2,0},{4,6},{6,4},{8,10},{10,8},{12,14},{14,12},{1,3},{3,1},... | collective-permute-start | bytes 835592 | tf_op jit(solution)/shard_map/ppermute | solution.py:446
  49.4 11.5 %collective-permute-start.10 = (bf16[16,2176]{1,0:T(8,128)(2,1)S(1)}, bf16[16,2176]{1,0:T(8,128)(2,1)S(1)}, u32[]{:S(2)}, u32[]{:S(2)}) collective-permute-start(bf16[16,2176]{1,0:T(8,128)(2,1)S(1)} %get-tuple-element.47), channel_id=1, source_target_pairs={{0,13},{1,12},{2,15},{3,14},{4,9},{5,8},{6,11},{7,10},{8,5},{9,4},... | collective-permute-start | bytes 208904 | tf_op jit(solution)/shard_map/ppermute | solution.py:460
  49.5 11.4 %collective-permute-start.11 = (bf16[16,2176]{1,0:T(8,128)(2,1)S(1)}, bf16[16,2176]{1,0:T(8,128)(2,1)S(1)}, u32[]{:S(2)}, u32[]{:S(2)}) collective-permute-start(bf16[16,2176]{1,0:T(8,128)(2,1)S(1)} %get-tuple-element.48), channel_id=1, source_target_pairs={{0,9},{1,8},{2,11},{3,10},{4,13},{5,12},{6,15},{7,14},{8,1},{9,0},... | collective-permute-start | bytes 208904 | tf_op jit(solution)/shard_map/ppermute | solution.py:460
  53.7 8.1 %collective-permute-start.12 = (bf16[16,2176]{1,0:T(8,128)(2,1)S(1)}, bf16[16,2176]{1,0:T(8,128)(2,1)S(1)}, u32[]{:S(2)}, u32[]{:S(2)}) collective-permute-start(bf16[16,2176]{1,0:T(8,128)(2,1)S(1)} %get-tuple-element.49), channel_id=1, source_target_pairs={{0,5},{1,4},{2,7},{3,6},{4,1},{5,0},{6,3},{7,2},{8,13},{9,12},{10,... | collective-permute-start | bytes 208904 | tf_op jit(solution)/shard_map/ppermute | solution.py:460
  54.9 7.0 %collective-permute-start.13 = (bf16[16,2176]{1,0:T(8,128)(2,1)S(1)}, bf16[16,2176]{1,0:T(8,128)(2,1)S(1)}, u32[]{:S(2)}, u32[]{:S(2)}) collective-permute-start(bf16[16,2176]{1,0:T(8,128)(2,1)S(1)} %get-tuple-element.50), channel_id=1, source_target_pairs={{0,1},{1,0},{2,3},{3,2},{4,5},{5,4},{6,7},{7,6},{8,9},{9,8},{10,11... | collective-permute-start | bytes 208904 | tf_op jit(solution)/shard_map/ppermute | solution.py:460
  55.5 8.4 %collective-permute-start.15 = (bf16[16,2176]{1,0:T(8,128)(2,1)S(1)}, bf16[16,2176]{1,0:T(8,128)(2,1)S(1)}, u32[]{:S(2)}, u32[]{:S(2)}) collective-permute-start(bf16[16,2176]{1,0:T(8,128)(2,1)S(1)} %get-tuple-element.56), channel_id=1, source_target_pairs={{0,12},{1,13},{2,14},{3,15},{4,8},{5,9},{6,10},{7,11},{8,4},{9,5},... | collective-permute-start | bytes 208904 | tf_op jit(solution)/shard_map/ppermute | solution.py:460
  60.9 5.5 %collective-permute-start.16 = (bf16[16,2176]{1,0:T(8,128)(2,1)S(1)}, bf16[16,2176]{1,0:T(8,128)(2,1)S(1)}, u32[]{:S(2)}, u32[]{:S(2)}) collective-permute-start(bf16[16,2176]{1,0:T(8,128)(2,1)S(1)} %get-tuple-element.57), channel_id=1, source_target_pairs={{0,8},{1,9},{2,10},{3,11},{4,12},{5,13},{6,14},{7,15},{8,0},{9,1},... | collective-permute-start | bytes 208904 | tf_op jit(solution)/shard_map/ppermute | solution.py:460
  60.9 5.6 %collective-permute-start.17 = (bf16[16,2176]{1,0:T(8,128)(2,1)S(1)}, bf16[16,2176]{1,0:T(8,128)(2,1)S(1)}, u32[]{:S(2)}, u32[]{:S(2)}) collective-permute-start(bf16[16,2176]{1,0:T(8,128)(2,1)S(1)} %get-tuple-element.58), channel_id=1, source_target_pairs={{0,4},{1,5},{2,6},{3,7},{4,0},{5,1},{6,2},{7,3},{8,12},{9,13},{10,... | collective-permute-start | bytes 208904 | tf_op jit(solution)/shard_map/ppermute | solution.py:460

commit v13 on v12

--- a/solution.py
+++ b/solution.py
@@ -293,7 +293,7 @@
         dgate[:, cols] = (grad * slope_ref[:, cols]).astype(BF16)
         dup[:, cols] = (grad * act_ref[:, cols]).astype(BF16)
     part_out[...] = two_terms(part)
-    back_columns(groups, 1, dgate, dup, part_out[...], gate_ref, up_ref, outs)
+    back_columns(groups, 0, dgate, dup, part_out[...], gate_ref, up_ref, outs)
 
 
 def hidden_grads(blocks, places, groups, factors, down_piece, gate_piece, up_piece):
@@ -318,7 +318,7 @@
 
 
 def back_kernel(groups, dgate_ref, dup_ref, part_ref, gate_ref, up_ref, *outs):
-    back_columns(groups, 0, dgate_ref, dup_ref, part_ref[...], gate_ref, up_ref, outs)
+    back_columns(groups, 1, dgate_ref, dup_ref, part_ref[...], gate_ref, up_ref, outs)
 
 
 def back_half(groups, dgate, dup, part, gate_piece, up_piece):
@@ -503,7 +503,7 @@
     first = [first[0]] + [to_piece(first[t], groups - t) for t in range(1, groups)]
     waiting = pass_after(second[1:], *first[1:])
     second = [second[0]] + [to_piece(x, groups - t) for t, x in enumerate(waiting, 1)]
-    crossed, kept = sum_pieces(first), sum_pieces(second)
+    kept, crossed = sum_pieces(first), sum_pieces(second)
     arrived = {0: kept[0]}
     for s in range(1, E_MOD):
         arrived[s] = to_source(kept[s], s, 0)

time: 67.9 us -> 68.1 us (level)
  transfers between devices with their start and end apart: 18 -> 18, of which waited for: 9 -> 8; matrix products, arithmetic and copies ran while one was open for 0% -> 0% of each run, Pallas kernels for 25% -> 25%
where the time goes in v13:
time: 68.1 us; the launch traced here: 68 us
  starting transfers between devices  25.4 us (37%)
  Pallas kernels  24.1 us (35%)
  waiting for transfers between devices  17.7 us (26%)
  between operations  0.77 us (1%)
    ppermute x11, starting transfers between devices, to_expert(): lax.ppermute(x, 'ep', [(e * groups + j, (e ^ s) * groups + (j + t) % grou...  13.9 us
    ppermute x11, waiting for transfers between devices, to_expert(): lax.ppermute(x, 'ep', [(e * groups + j, (e ^ s) * groups + (j + t) % grou...  12.5 us
    ppermute x7, starting transfers between devices, to_source(): lax.ppermute(x, ('ep', 'mod'), [((e * groups + j) * 2 + m, ((e ^ s) * gro...  11.5 us
    pallas_call x2, Pallas kernels, load(): pl.pallas_call(functools.partial(load_kernel, parts), in_specs=[pl.BlockS...  6.94 us
    ppermute x7, waiting for transfers between devices, to_source(): lax.ppermute(x, ('ep', 'mod'), [((e * groups + j) * 2 + m, ((e ^ s) * gro...  5.18 us
    pallas_call x1, Pallas kernels, load_turned(): pl.pallas_call(functools.partial(load_turned_kernel, parts), in_specs=[pl...  4.29 us
    pallas_call x1, Pallas kernels, hidden_grads(): pl.pallas_call(functools.partial(hidden_kernel, count, places, groups), i...  3.62 us
    pallas_call x1, Pallas kernels, pre_activations(): pl.pallas_call(functools.partial(pre_kernel, count, places), in_specs=[vm...  2.61 us
  transfers between devices with their start and end apart: 18, of which 8 were waited for; matrix products, arithmetic and copies ran while one was open for 0% of the time, Pallas kernels for 25%

profile of v13, /device:TPU:0, one launch (start us, length us, event | category | flops | bytes accessed | tf_op | source)
XLA Modules:
  0.0 68.0 jit_solution(8238435592574046274)
XLA Ops:
  0.6 2.5 %gather_slots.1 = (bf16[32,4096]{1,0:T(8,128)(2,1)S(1)}, bf16[32,4096]{1,0:T(8,128)(2,1)S(1)}, bf16[16,4096]{1,0:T(8,128)(2,1)S(1)}, bf16[16,4096]{1,0:T(8,128)(...) custom-call(s32[1,128]{1,0:T(1,128)} %bitcast.6, s32[2,128]{1,0:T(2,128)} %bitcast.4, ...), custom_call_target="tpu_custom_call" | custom-call | flops 134217728 | bytes 3145728 | tf_op jit(solution)/shard_map/gather_slots/pallas_call | solution.py:93
  3.1 3.0 %collective-permute-start.1 = (bf16[32,4096]{1,0:T(8,128)(2,1)S(1)}, bf16[32,4096]{1,0:T(8,128)(2,1)S(1)}, u32[]{:S(2)}, u32[]{:S(2)}) collective-permute-start(bf16[32,4096]{1,0:T(8,128)(2,1)S(1)} %get-tuple-element.34.refs_0_), channel_id=1, source_target_pairs={{0,2},{2,0},{4,6},{6,4},{8,10},{10,8},{12,14},{14,12},{1,3},{3,1},... | collective-permute-start | bytes 786440 | tf_op jit(solution)/shard_map/ppermute | solution.py:446
  6.2 1.6 %collective-permute-start = (bf16[32,4096]{1,0:T(8,128)(2,1)S(1)}, bf16[32,4096]{1,0:T(8,128)(2,1)S(1)}, u32[]{:S(2)}, u32[]{:S(2)}) collective-permute-start(bf16[32,4096]{1,0:T(8,128)(2,1)S(1)} %get-tuple-element.35), channel_id=1, source_target_pairs={{0,4},{2,6},{4,0},{6,2},{8,12},{10,14},{12,8},{14,10},{1,5},{3,7},... | collective-permute-start | bytes 786440 | tf_op jit(solution)/shard_map/ppermute | solution.py:446
  7.7 2.6 %collective-permute-start.5 = (bf16[16,4096]{1,0:T(8,128)(2,1)S(1)}, bf16[16,4096]{1,0:T(8,128)(2,1)S(1)}, u32[]{:S(2)}, u32[]{:S(2)}) collective-permute-start(bf16[16,4096]{1,0:T(8,128)(2,1)S(1)} %get-tuple-element.40), channel_id=1, source_target_pairs={{0,8},{2,10},{4,12},{6,14},{8,0},{10,2},{12,4},{14,6},{1,9},{3,11}... | collective-permute-start | bytes 393224 | tf_op jit(solution)/shard_map/ppermute | solution.py:446
  10.3 0.2 collective-permute-start.6
  10.6 3.5 %load.2.refs_2_.refs_1_.refs_3_.refs_6_.refs_10_.gate_ref = bf16[1,4096,1024]{2,1,0:T(8,128)(2,1)S(1)} custom-call(bf16[1,4096,1024]{2,1,0:T(8,128)(2,1)} %src.3, bf16[32,4096]{1,0:T(8,128)(2,1)S(1)} %get-tuple-element.34.refs_0_), custom_call_target="tpu_custom_call" | custom-call | bytes 1024 | tf_op jit(solution)/shard_map/load/pallas_call | solution.py:128
  14.0 0.0 collective-permute-done.1.refs_3_.refs_1_.refs_2_
  14.1 1.8 %collective-permute-start.3 = (bf16[16,4096]{1,0:T(8,128)(2,1)S(1)}, bf16[16,4096]{1,0:T(8,128)(2,1)S(1)}, u32[]{:S(2)}, u32[]{:S(2)}) collective-permute-start(bf16[16,4096]{1,0:T(8,128)(2,1)S(1)} %get-tuple-element.38), channel_id=1, source_target_pairs={{0,8},{2,10},{4,12},{6,14},{8,0},{10,2},{12,4},{14,6},{1,9},{3,11}... | collective-permute-start | bytes 393224 | tf_op jit(solution)/shard_map/ppermute | solution.py:446
  15.8 2.0 %collective-permute-start.4 = (bf16[16,4096]{1,0:T(8,128)(2,1)S(1)}, bf16[16,4096]{1,0:T(8,128)(2,1)S(1)}, u32[]{:S(2)}, u32[]{:S(2)}) collective-permute-start(bf16[16,4096]{1,0:T(8,128)(2,1)S(1)} %get-tuple-element.39), channel_id=1, source_target_pairs={{0,12},{2,14},{4,8},{6,10},{8,4},{10,6},{12,0},{14,2},{1,13},{3,15... | collective-permute-start | bytes 393224 | tf_op jit(solution)/shard_map/ppermute | solution.py:446
  17.8 0.0 collective-permute-done.refs_0_.refs_1_
  17.8 0.5 collective-permute-start.2
  18.3 3.5 %load.3.refs_3_.refs_4_.refs_7_.refs_11_.up_ref = bf16[1,4096,1024]{2,1,0:T(8,128)(2,1)S(1)} custom-call(bf16[1,4096,1024]{2,1,0:T(8,128)(2,1)} %src.4, bf16[32,4096]{1,0:T(8,128)(2,1)S(1)} %collective-permute-done.refs_0_.refs_1_, bf16[1,4096,1024]{2,1,0:T(8,128)(2,1)S(1)} %load.2.refs_2_.refs_1_.refs_3_.refs_6_.refs_10_.gate_ref), custom_call_target="tpu_custom_call" | custom-call | bytes 1024 | tf_op jit(solution)/shard_map/load/pallas_call | solution.py:128
  21.8 0.0 collective-permute-done.5.refs_0_
  21.8 1.3 %collective-permute-done.6.refs_1_ = bf16[16,4096]{1,0:T(8,128)(2,1)S(1)} collective-permute-done((bf16[16,4096]{1,0:T(8,128)(2,1)S(1)}, bf16[16,4096]{1,0:T(8,128)(2,1)S(1)}, u32[]{:S(2)}, u32[]{:S(2)}) %collective-permute-start.6) | collective-permute-done | bytes 131104 | tf_op jit(solution)/shard_map/ppermute | solution.py:446
  23.2 0.6 collective-permute-start.8
  23.7 2.4 %collective-permute-done.2.refs_2_.refs_3_ = bf16[32,4096]{1,0:T(8,128)(2,1)S(1)} collective-permute-done((bf16[32,4096]{1,0:T(8,128)(2,1)S(1)}, bf16[32,4096]{1,0:T(8,128)(2,1)S(1)}, u32[]{:S(2)}, u32[]{:S(2)}) %collective-permute-start.2) | collective-permute-done | bytes 262176 | tf_op jit(solution)/shard_map/ppermute | solution.py:446
  26.2 4.3 %load_turned.1.refs_4_.refs_8_.refs_9_ = bf16[4096,1024]{1,0:T(8,128)(2,1)S(1)} custom-call(bf16[1,1024,4096]{2,1,0:T(8,128)(2,1)} %src.5, bf16[32,4096]{1,0:T(8,128)(2,1)S(1)} %join.2.refs_0_.refs_4_, bf16[32,4096]{1,0:T(8,128)(2,1)S(1)} %collective-permute-done.1.refs_3_.refs_1_.refs_2_, bf16[32,4096]{1,0:T(8,128)(2,1)S(1)} %collective-permute-done.2.refs_2_.refs_3_, ...), custom_call_target="tpu_custom_call" | custom-call | bytes 1024 | tf_op jit(solution)/shard_map/load_turned/pallas_call | solution.py:161
  30.5 0.4 collective-permute-done.3.refs_0_
  30.9 0.0 collective-permute-done.4.refs_1_
  30.9 0.6 collective-permute-start.7
  31.5 0.0 collective-permute-done.8.refs_5_
  31.5 2.6 %pre_activations.1 = (f32[128,1024]{1,0:T(8,128)S(1)}, f32[128,1024]{1,0:T(8,128)S(1)}, f32[128,1024]{1,0:T(8,128)S(1)}) custom-call(bf16[32,4096]{1,0:T(8,128)(2,1)S(1)} %get-tuple-element.34.refs_0_, bf16[32,4096]{1,0:T(8,128)(2,1)S(1)} %collective-permute-done.refs_0_.refs_1_, bf16[32,4096]{1,0:T(8,128)(2,1)S(1)} %collective-permute-done.1.refs_3_.refs_1_.refs_2_, ...), custom_call_target="tpu_custom_call" | custom-call | flops 5000000000 | bytes 1024 | tf_op jit(solution)/shard_map/pre_activations/pallas_call | solution.py:251
  34.1 3.9 %collective-permute-done.7.refs_5_ = bf16[32,4096]{1,0:T(8,128)(2,1)S(1)} collective-permute-done((bf16[32,4096]{1,0:T(8,128)(2,1)S(1)}, bf16[32,4096]{1,0:T(8,128)(2,1)S(1)}, u32[]{:S(2)}, u32[]{:S(2)}) %collective-permute-start.7) | collective-permute-done | bytes 262176 | tf_op jit(solution)/shard_map/ppermute | solution.py:446
  38.0 3.6 %hidden_grads.1 = (bf16[64,2176]{1,0:T(8,128)(2,1)S(1)}, bf16[64,2176]{1,0:T(8,128)(2,1)S(1)}, bf16[128,1024]{1,0:T(8,128)(2,1)S(1)}, bf16[128,1024]{1,0:T(8,128)(2,1)S(1)}, bf16[128,128]{1,0:T(8,128)(2,1)S(1)}) custom-call(bf16[32,4096]{1,0:T(8,128)(2,1)S(1)} %get-tuple-element.34.refs_0_, bf16[32,4096]{1,0:T(8,128)(2,1)S(1)} %collective-permute-done.refs_0_.refs_1_, ...), custom_call_target="tpu_custom_call" | custom-call | flops 2147483648 | bytes 16777216 | tf_op jit(solution)/shard_map/hidden_grads/pallas_call | solution.py:305
  41.6 0.6 collective-permute-start.9
  42.2 0.0 copy-start
  42.2 0.0 copy-start.1
  42.2 0.0 copy-start.2
  42.2 2.4 %back_half.1 = (bf16[64,2176]{1,0:T(8,128)(2,1)S(1)}, bf16[64,2176]{1,0:T(8,128)(2,1)S(1)}) custom-call(bf16[128,1024]{1,0:T(8,128)(2,1)S(1)} %get-tuple-element.45.dgate_ref, bf16[128,1024]{1,0:T(8,128)(2,1)S(1)} %get-tuple-element.46.dup_ref, bf16[128,128]{1,0:T(8,128)(2,1)S(1)} %get-tuple-element.47.part_ref, ...), custom_call_target="tpu_custom_call" | custom-call | flops 1073741824 | bytes 8388608 | tf_op jit(solution)/shard_map/back_half/pallas_call | solution.py:329
  44.6 4.2 %collective-permute-done.9.refs_1_ = bf16[64,2176]{1,0:T(8,128)(2,1)S(1)} collective-permute-done((bf16[64,2176]{1,0:T(8,128)(2,1)S(1)}, bf16[64,2176]{1,0:T(8,128)(2,1)S(1)}, u32[]{:S(2)}, u32[]{:S(2)}) %collective-permute-start.9) | collective-permute-done | bytes 278560 | tf_op jit(solution)/shard_map/ppermute | solution.py:446
  48.8 0.5 collective-permute-start.10
  49.3 0.1 sum_pieces.3
  49.4 4.9 %collective-permute-start.15 = (bf16[16,2176]{1,0:T(8,128)(2,1)S(1)}, bf16[16,2176]{1,0:T(8,128)(2,1)S(1)}, u32[]{:S(2)}, u32[]{:S(2)}) collective-permute-start(bf16[16,2176]{1,0:T(8,128)(2,1)S(1)} %get-tuple-element.56), channel_id=1, source_target_pairs={{0,12},{1,13},{2,14},{3,15},{4,8},{5,9},{6,10},{7,11},{8,4},{9,5},... | collective-permute-start | bytes 208904 | tf_op jit(solution)/shard_map/ppermute | solution.py:460
  54.4 0.3 collective-permute-start.16
  54.6 0.5 collective-permute-start.17
  55.1 0.2 collective-permute-done.10.refs_1_
  55.4 0.1 sum_pieces.2
  55.5 0.1 collective-permute-start.11
  55.6 4.5 %collective-permute-start.12 = (bf16[16,2176]{1,0:T(8,128)(2,1)S(1)}, bf16[16,2176]{1,0:T(8,128)(2,1)S(1)}, u32[]{:S(2)}, u32[]{:S(2)}) collective-permute-start(bf16[16,2176]{1,0:T(8,128)(2,1)S(1)} %get-tuple-element.52), channel_id=1, source_target_pairs={{0,9},{1,8},{2,11},{3,10},{4,13},{5,12},{6,15},{7,14},{8,1},{9,0},... | collective-permute-start | bytes 208904 | tf_op jit(solution)/shard_map/ppermute | solution.py:460
  60.0 0.0 collective-permute-done.15.refs_4_
  60.0 1.3 %collective-permute-start.13 = (bf16[16,2176]{1,0:T(8,128)(2,1)S(1)}, bf16[16,2176]{1,0:T(8,128)(2,1)S(1)}, u32[]{:S(2)}, u32[]{:S(2)}) collective-permute-start(bf16[16,2176]{1,0:T(8,128)(2,1)S(1)} %get-tuple-element.53), channel_id=1, source_target_pairs={{0,5},{1,4},{2,7},{3,6},{4,1},{5,0},{6,3},{7,2},{8,13},{9,12},{10,... | collective-permute-start | bytes 208904 | tf_op jit(solution)/shard_map/ppermute | solution.py:460
  61.3 0.0 collective-permute-done.16.refs_5_
  61.3 0.0 collective-permute-start.14
  61.3 0.0 copy-done
  61.3 0.0 copy-done.1
  61.3 0.0 copy-done.2
  61.3 0.2 mixing.1
  61.6 0.0 collective-permute-done.17.refs_6_
  61.6 0.3 collective-permute-done.11.refs_0_
  61.9 4.8 %collective-permute-done.12.refs_1_ = bf16[16,2176]{1,0:T(8,128)(2,1)S(1)} collective-permute-done((bf16[16,2176]{1,0:T(8,128)(2,1)S(1)}, bf16[16,2176]{1,0:T(8,128)(2,1)S(1)}, u32[]{:S(2)}, u32[]{:S(2)}) %collective-permute-start.12) | collective-permute-done | bytes 69664 | tf_op jit(solution)/shard_map/ppermute | solution.py:460
  66.7 0.0 collective-permute-done.13.refs_2_
  66.7 0.0 collective-permute-done.14.refs_3_
  66.7 1.2 %combine.1 = (bf16[128,2048]{1,0:T(8,128)(2,1)}, f32[1,128]{1,0:T(1,128)}) custom-call(bf16[2,128,128]{2,1,0:T(8,128)(2,1)S(1)} %get-tuple-element.32.mix_ref, f32[128,128]{1,0:T(8,128)S(1)} %get-tuple-element.33.hit_ref, bf16[16,2176]{1,0:T(8,128)(2,1)S(1)} %collective-permute-done.11.refs_0_, bf16[16,2176]{1,0:T(8,128)(2,1)S(1)} %collective-permute-done.12.refs_1_, ...), custom_call_target="tpu_custom_call" | custom-call | flops 134217728 | bytes 1048576 | tf_op jit(solution)/shard_map/combine/pallas_call | solution.py:423
  (4 shorter events, 0.0 us)
Async XLA Ops:
  3.1 10.9 %collective-permute-start.1 = (bf16[32,4096]{1,0:T(8,128)(2,1)S(1)}, bf16[32,4096]{1,0:T(8,128)(2,1)S(1)}, u32[]{:S(2)}, u32[]{:S(2)}) collective-permute-start(bf16[32,4096]{1,0:T(8,128)(2,1)S(1)} %get-tuple-element.34.refs_0_), channel_id=1, source_target_pairs={{0,2},{2,0},{4,6},{6,4},{8,10},{10,8},{12,14},{14,12},{1,3},{3,1},... | collective-permute-start | bytes 786440 | tf_op jit(solution)/shard_map/ppermute | solution.py:446
  6.2 11.6 %collective-permute-start = (bf16[32,4096]{1,0:T(8,128)(2,1)S(1)}, bf16[32,4096]{1,0:T(8,128)(2,1)S(1)}, u32[]{:S(2)}, u32[]{:S(2)}) collective-permute-start(bf16[32,4096]{1,0:T(8,128)(2,1)S(1)} %get-tuple-element.35), channel_id=1, source_target_pairs={{0,4},{2,6},{4,0},{6,2},{8,12},{10,14},{12,8},{14,10},{1,5},{3,7},... | collective-permute-start | bytes 786440 | tf_op jit(solution)/shard_map/ppermute | solution.py:446
  7.7 14.1 %collective-permute-start.5 = (bf16[16,4096]{1,0:T(8,128)(2,1)S(1)}, bf16[16,4096]{1,0:T(8,128)(2,1)S(1)}, u32[]{:S(2)}, u32[]{:S(2)}) collective-permute-start(bf16[16,4096]{1,0:T(8,128)(2,1)S(1)} %get-tuple-element.40), channel_id=1, source_target_pairs={{0,8},{2,10},{4,12},{6,14},{8,0},{10,2},{12,4},{14,6},{1,9},{3,11}... | collective-permute-start | bytes 393224 | tf_op jit(solution)/shard_map/ppermute | solution.py:446
  10.3 12.8 %collective-permute-start.6 = (bf16[16,4096]{1,0:T(8,128)(2,1)S(1)}, bf16[16,4096]{1,0:T(8,128)(2,1)S(1)}, u32[]{:S(2)}, u32[]{:S(2)}) collective-permute-start(bf16[16,4096]{1,0:T(8,128)(2,1)S(1)} %get-tuple-element.41), channel_id=1, source_target_pairs={{0,12},{2,14},{4,8},{6,10},{8,4},{10,6},{12,0},{14,2},{1,13},{3,15... | collective-permute-start | bytes 393224 | tf_op jit(solution)/shard_map/ppermute | solution.py:446
  14.1 16.8 %collective-permute-start.3 = (bf16[16,4096]{1,0:T(8,128)(2,1)S(1)}, bf16[16,4096]{1,0:T(8,128)(2,1)S(1)}, u32[]{:S(2)}, u32[]{:S(2)}) collective-permute-start(bf16[16,4096]{1,0:T(8,128)(2,1)S(1)} %get-tuple-element.38), channel_id=1, source_target_pairs={{0,8},{2,10},{4,12},{6,14},{8,0},{10,2},{12,4},{14,6},{1,9},{3,11}... | collective-permute-start | bytes 393224 | tf_op jit(solution)/shard_map/ppermute | solution.py:446
  15.8 15.1 %collective-permute-start.4 = (bf16[16,4096]{1,0:T(8,128)(2,1)S(1)}, bf16[16,4096]{1,0:T(8,128)(2,1)S(1)}, u32[]{:S(2)}, u32[]{:S(2)}) collective-permute-start(bf16[16,4096]{1,0:T(8,128)(2,1)S(1)} %get-tuple-element.39), channel_id=1, source_target_pairs={{0,12},{2,14},{4,8},{6,10},{8,4},{10,6},{12,0},{14,2},{1,13},{3,15... | collective-permute-start | bytes 393224 | tf_op jit(solution)/shard_map/ppermute | solution.py:446
  17.8 8.3 %collective-permute-start.2 = (bf16[32,4096]{1,0:T(8,128)(2,1)S(1)}, bf16[32,4096]{1,0:T(8,128)(2,1)S(1)}, u32[]{:S(2)}, u32[]{:S(2)}) collective-permute-start(bf16[32,4096]{1,0:T(8,128)(2,1)S(1)} %collective-permute-done.refs_0_.refs_1_), channel_id=1, source_target_pairs={{0,2},{2,0},{4,6},{6,4},{8,10},{10,8},{12,14},{14,12},{1,3},{3,1},... | collective-permute-start | bytes 786440 | tf_op jit(solution)/shard_map/ppermute | solution.py:446
  23.2 8.3 %collective-permute-start.8 = (bf16[32,4096]{1,0:T(8,128)(2,1)S(1)}, bf16[32,4096]{1,0:T(8,128)(2,1)S(1)}, u32[]{:S(2)}, u32[]{:S(2)}) collective-permute-start(bf16[32,4096]{1,0:T(8,128)(2,1)S(1)} %join.2.refs_0_.refs_4_), channel_id=1, source_target_pairs={{0,2},{2,0},{4,6},{6,4},{8,10},{10,8},{12,14},{14,12},{1,3},{3,1},... | collective-permute-start | bytes 786440 | tf_op jit(solution)/shard_map/ppermute | solution.py:446
  30.9 7.1 %collective-permute-start.7 = (bf16[32,4096]{1,0:T(8,128)(2,1)S(1)}, bf16[32,4096]{1,0:T(8,128)(2,1)S(1)}, u32[]{:S(2)}, u32[]{:S(2)}) collective-permute-start(bf16[32,4096]{1,0:T(8,128)(2,1)S(1)} %join.3.refs_4_), channel_id=1, source_target_pairs={{0,2},{2,0},{4,6},{6,4},{8,10},{10,8},{12,14},{14,12},{1,3},{3,1},... | collective-permute-start | bytes 786440 | tf_op jit(solution)/shard_map/ppermute | solution.py:446
  41.6 7.2 %collective-permute-start.9 = (bf16[64,2176]{1,0:T(8,128)(2,1)S(1)}, bf16[64,2176]{1,0:T(8,128)(2,1)S(1)}, u32[]{:S(2)}, u32[]{:S(2)}) collective-permute-start(bf16[64,2176]{1,0:T(8,128)(2,1)S(1)} %get-tuple-element.50), channel_id=1, source_target_pairs={{0,2},{2,0},{4,6},{6,4},{8,10},{10,8},{12,14},{14,12},{1,3},{3,1},... | collective-permute-start | bytes 835592 | tf_op jit(solution)/shard_map/ppermute | solution.py:446
  42.2 19.1 %copy-start = (s32[128,2]{0,1:T(2,128)S(1)}, s32[128,2]{0,1:T(2,128)}, u32[]{:S(2)}) copy-start(s32[128,2]{0,1:T(2,128)} %param.11) | copy-start | bytes 3076
  42.2 19.1 %copy-start.1 = (s32[128]{0:T(128)S(1)}, s32[128]{0:T(128)}, u32[]{:S(2)}) copy-start(s32[128]{0:T(128)} %param.10) | copy-start | bytes 1540
  42.2 19.1 %copy-start.2 = (f32[128,2]{0,1:T(2,128)S(1)}, f32[128,2]{0,1:T(2,128)}, u32[]{:S(2)}) copy-start(f32[128,2]{0,1:T(2,128)} %param.12) | copy-start | bytes 3076
  48.8 6.5 %collective-permute-start.10 = (bf16[64,2176]{1,0:T(8,128)(2,1)S(1)}, bf16[64,2176]{1,0:T(8,128)(2,1)S(1)}, u32[]{:S(2)}, u32[]{:S(2)}) collective-permute-start(bf16[64,2176]{1,0:T(8,128)(2,1)S(1)} %pass_after.3), channel_id=1, source_target_pairs={{0,2},{2,0},{4,6},{6,4},{8,10},{10,8},{12,14},{14,12},{1,3},{3,1},... | collective-permute-start | bytes 835592 | tf_op jit(solution)/shard_map/ppermute | solution.py:446
  49.4 10.6 %collective-permute-start.15 = (bf16[16,2176]{1,0:T(8,128)(2,1)S(1)}, bf16[16,2176]{1,0:T(8,128)(2,1)S(1)}, u32[]{:S(2)}, u32[]{:S(2)}) collective-permute-start(bf16[16,2176]{1,0:T(8,128)(2,1)S(1)} %get-tuple-element.56), channel_id=1, source_target_pairs={{0,12},{1,13},{2,14},{3,15},{4,8},{5,9},{6,10},{7,11},{8,4},{9,5},... | collective-permute-start | bytes 208904 | tf_op jit(solution)/shard_map/ppermute | solution.py:460
  54.4 6.9 %collective-permute-start.16 = (bf16[16,2176]{1,0:T(8,128)(2,1)S(1)}, bf16[16,2176]{1,0:T(8,128)(2,1)S(1)}, u32[]{:S(2)}, u32[]{:S(2)}) collective-permute-start(bf16[16,2176]{1,0:T(8,128)(2,1)S(1)} %get-tuple-element.57), channel_id=1, source_target_pairs={{0,8},{1,9},{2,10},{3,11},{4,12},{5,13},{6,14},{7,15},{8,0},{9,1},... | collective-permute-start | bytes 208904 | tf_op jit(solution)/shard_map/ppermute | solution.py:460
  54.6 6.9 %collective-permute-start.17 = (bf16[16,2176]{1,0:T(8,128)(2,1)S(1)}, bf16[16,2176]{1,0:T(8,128)(2,1)S(1)}, u32[]{:S(2)}, u32[]{:S(2)}) collective-permute-start(bf16[16,2176]{1,0:T(8,128)(2,1)S(1)} %get-tuple-element.58), channel_id=1, source_target_pairs={{0,4},{1,5},{2,6},{3,7},{4,0},{5,1},{6,2},{7,3},{8,12},{9,13},{10,... | collective-permute-start | bytes 208904 | tf_op jit(solution)/shard_map/ppermute | solution.py:460
  55.5 6.4 %collective-permute-start.11 = (bf16[16,2176]{1,0:T(8,128)(2,1)S(1)}, bf16[16,2176]{1,0:T(8,128)(2,1)S(1)}, u32[]{:S(2)}, u32[]{:S(2)}) collective-permute-start(bf16[16,2176]{1,0:T(8,128)(2,1)S(1)} %get-tuple-element.51), channel_id=1, source_target_pairs={{0,13},{1,12},{2,15},{3,14},{4,9},{5,8},{6,11},{7,10},{8,5},{9,4},... | collective-permute-start | bytes 208904 | tf_op jit(solution)/shard_map/ppermute | solution.py:460
  55.6 11.2 %collective-permute-start.12 = (bf16[16,2176]{1,0:T(8,128)(2,1)S(1)}, bf16[16,2176]{1,0:T(8,128)(2,1)S(1)}, u32[]{:S(2)}, u32[]{:S(2)}) collective-permute-start(bf16[16,2176]{1,0:T(8,128)(2,1)S(1)} %get-tuple-element.52), channel_id=1, source_target_pairs={{0,9},{1,8},{2,11},{3,10},{4,13},{5,12},{6,15},{7,14},{8,1},{9,0},... | collective-permute-start | bytes 208904 | tf_op jit(solution)/shard_map/ppermute | solution.py:460
  60.0 6.7 %collective-permute-start.13 = (bf16[16,2176]{1,0:T(8,128)(2,1)S(1)}, bf16[16,2176]{1,0:T(8,128)(2,1)S(1)}, u32[]{:S(2)}, u32[]{:S(2)}) collective-permute-start(bf16[16,2176]{1,0:T(8,128)(2,1)S(1)} %get-tuple-element.53), channel_id=1, source_target_pairs={{0,5},{1,4},{2,7},{3,6},{4,1},{5,0},{6,3},{7,2},{8,13},{9,12},{10,... | collective-permute-start | bytes 208904 | tf_op jit(solution)/shard_map/ppermute | solution.py:460
  61.3 5.5 %collective-permute-start.14 = (bf16[16,2176]{1,0:T(8,128)(2,1)S(1)}, bf16[16,2176]{1,0:T(8,128)(2,1)S(1)}, u32[]{:S(2)}, u32[]{:S(2)}) collective-permute-start(bf16[16,2176]{1,0:T(8,128)(2,1)S(1)} %get-tuple-element.54), channel_id=1, source_target_pairs={{0,1},{1,0},{2,3},{3,2},{4,5},{5,4},{6,7},{7,6},{8,9},{9,8},{10,11... | collective-permute-start | bytes 208904 | tf_op jit(solution)/shard_map/ppermute | solution.py:460

commit v14 on v12

--- a/solution.py
+++ b/solution.py
@@ -345,7 +345,7 @@
 
 
 def sum_kernel(groups, *refs):
-    ins, outs = refs[:groups], refs[groups:]
+    ins, outs = refs[:groups], refs[-E_MOD:]
     wide = ins[0].shape[1] - EXT
     for s in range(E_MOD):
         rows = slice(s * CAP, (s + 1) * CAP)
@@ -356,16 +356,19 @@
         outs[s][:, wide:] = two_terms(jnp.sum(total[:, wide:], axis=1, keepdims=True))
 
 
-def sum_pieces(partials):
+def sum_pieces(partials, *after):
     groups = len(partials)
     own_rows, wide = partials[0].shape
     return pl.pallas_call(
         functools.partial(sum_kernel, groups),
+        in_specs=[pl.BlockSpec(memory_space=pltpu.VMEM)] * groups
+        + [pl.BlockSpec(memory_space=pl.ANY)] * len(after),
+        out_specs=[pl.BlockSpec(memory_space=pltpu.VMEM)] * E_MOD,
         out_shape=[jax.ShapeDtypeStruct((CAP, wide), BF16)] * E_MOD,
         cost_estimate=cost(own_rows * wide, 4 * groups * own_rows * wide),
         compiler_params=pltpu.CompilerParams(vmem_limit_bytes=SCOPED),
         name="sum_pieces",
-    )(*partials)
+    )(*partials, *after)
 
 
 def mix_kernel(groups, modality_ref, picks_ref, weights_ref, mix_out, gate_out):
@@ -501,15 +504,15 @@
     )
     second = back_half(groups, dgate, dup, part, gate_piece, up_piece)
     first = [first[0]] + [to_piece(first[t], groups - t) for t in range(1, groups)]
-    waiting = pass_after(second[1:], *first[1:])
+    crossed = sum_pieces(first, second[0])
+    arrived = {E_MOD + s: to_source(crossed[s], s, 1) for s in range(E_MOD)}
+    waiting = pass_after(second[1:], arrived[E_MOD])
     second = [second[0]] + [to_piece(x, groups - t) for t, x in enumerate(waiting, 1)]
-    crossed, kept = sum_pieces(first), sum_pieces(second)
-    arrived = {0: kept[0]}
+    kept = sum_pieces(second)
+    arrived[0] = kept[0]
     for s in range(1, E_MOD):
         arrived[s] = to_source(kept[s], s, 0)
-    for s in range(E_MOD):
-        arrived[E_MOD + s] = to_source(crossed[s], s, 1)
-    order = tuple(reversed(arrived))
+    order = tuple(reversed(sorted(arrived)))
     token_grad, gate_grad = combine(order, mix, hits, [arrived[i] for i in order])
     return token_grad, gate_grad.reshape(-1, 1)
 

time: 67.9 us -> 70.4 us (1.037)
  waiting for transfers between devices: 17.5 us -> 21.1 us
  starting transfers between devices: 25.4 us -> 24.3 us
    ppermute x11, waiting for transfers between devices: 12.8 us -> 15 us  [to_expert(): lax.ppermute(x, 'ep', [(e * groups + j, (e ^ s) * groups + (j + t) % grou...]
    ppermute x7, waiting for transfers between devices: 4.66 us -> 6.08 us  [to_source(): lax.ppermute(x, ('ep', 'mod'), [((e * groups + j) * 2 + m, ((e ^ s) * gro...]
    ppermute x7, starting transfers between devices: 11.5 us -> 10.4 us  [to_source(): lax.ppermute(x, ('ep', 'mod'), [((e * groups + j) * 2 + m, ((e ^ s) * gro...]
  transfers between devices with their start and end apart: 18 -> 18, of which waited for: 9 -> 9; matrix products, arithmetic and copies ran while one was open for 0% -> 0% of each run, Pallas kernels for 25% -> 24%
where the time goes in v14:
time: 70.4 us; the launch traced here: 70.2 us
  starting transfers between devices  24.3 us (35%)
  Pallas kernels  24.1 us (34%)
  waiting for transfers between devices  21.1 us (30%)
  between operations  0.78 us (1%)
    ppermute x11, waiting for transfers between devices, to_expert(): lax.ppermute(x, 'ep', [(e * groups + j, (e ^ s) * groups + (j + t) % grou...  15 us
    ppermute x11, starting transfers between devices, to_expert(): lax.ppermute(x, 'ep', [(e * groups + j, (e ^ s) * groups + (j + t) % grou...  13.9 us
    ppermute x7, starting transfers between devices, to_source(): lax.ppermute(x, ('ep', 'mod'), [((e * groups + j) * 2 + m, ((e ^ s) * gro...  10.4 us
    pallas_call x2, Pallas kernels, load(): pl.pallas_call(functools.partial(load_kernel, parts), in_specs=[pl.BlockS...  6.94 us
    ppermute x7, waiting for transfers between devices, to_source(): lax.ppermute(x, ('ep', 'mod'), [((e * groups + j) * 2 + m, ((e ^ s) * gro...  6.08 us
    pallas_call x1, Pallas kernels, load_turned(): pl.pallas_call(functools.partial(load_turned_kernel, parts), in_specs=[pl...  4.29 us
    pallas_call x1, Pallas kernels, hidden_grads(): pl.pallas_call(functools.partial(hidden_kernel, count, places, groups), i...  3.62 us
    pallas_call x1, Pallas kernels, pre_activations(): pl.pallas_call(functools.partial(pre_kernel, count, places), in_specs=[vm...  2.61 us
  transfers between devices with their start and end apart: 18, of which 9 were waited for; matrix products, arithmetic and copies ran while one was open for 0% of the time, Pallas kernels for 24%

profile of v14, /device:TPU:0, one launch (start us, length us, event | category | flops | bytes accessed | tf_op | source)
XLA Modules:
  0.0 70.2 jit_solution(1390645949321305499)
XLA Ops:
  0.6 2.5 %gather_slots.1 = (bf16[32,4096]{1,0:T(8,128)(2,1)S(1)}, bf16[32,4096]{1,0:T(8,128)(2,1)S(1)}, bf16[16,4096]{1,0:T(8,128)(2,1)S(1)}, bf16[16,4096]{1,0:T(8,128)(...) custom-call(s32[1,128]{1,0:T(1,128)} %bitcast.6, s32[2,128]{1,0:T(2,128)} %bitcast.4, ...), custom_call_target="tpu_custom_call" | custom-call | flops 134217728 | bytes 3145728 | tf_op jit(solution)/shard_map/gather_slots/pallas_call | solution.py:93
  3.1 3.0 %collective-permute-start.1 = (bf16[32,4096]{1,0:T(8,128)(2,1)S(1)}, bf16[32,4096]{1,0:T(8,128)(2,1)S(1)}, u32[]{:S(2)}, u32[]{:S(2)}) collective-permute-start(bf16[32,4096]{1,0:T(8,128)(2,1)S(1)} %get-tuple-element.34.refs_0_), channel_id=1, source_target_pairs={{0,2},{2,0},{4,6},{6,4},{8,10},{10,8},{12,14},{14,12},{1,3},{3,1},... | collective-permute-start | bytes 786440 | tf_op jit(solution)/shard_map/ppermute | solution.py:449
  6.2 1.6 %collective-permute-start = (bf16[32,4096]{1,0:T(8,128)(2,1)S(1)}, bf16[32,4096]{1,0:T(8,128)(2,1)S(1)}, u32[]{:S(2)}, u32[]{:S(2)}) collective-permute-start(bf16[32,4096]{1,0:T(8,128)(2,1)S(1)} %get-tuple-element.35), channel_id=1, source_target_pairs={{0,4},{2,6},{4,0},{6,2},{8,12},{10,14},{12,8},{14,10},{1,5},{3,7},... | collective-permute-start | bytes 786440 | tf_op jit(solution)/shard_map/ppermute | solution.py:449
  7.7 2.6 %collective-permute-start.5 = (bf16[16,4096]{1,0:T(8,128)(2,1)S(1)}, bf16[16,4096]{1,0:T(8,128)(2,1)S(1)}, u32[]{:S(2)}, u32[]{:S(2)}) collective-permute-start(bf16[16,4096]{1,0:T(8,128)(2,1)S(1)} %get-tuple-element.40), channel_id=1, source_target_pairs={{0,8},{2,10},{4,12},{6,14},{8,0},{10,2},{12,4},{14,6},{1,9},{3,11}... | collective-permute-start | bytes 393224 | tf_op jit(solution)/shard_map/ppermute | solution.py:449
  10.3 0.2 collective-permute-start.6
  10.6 3.5 %load.2.refs_2_.refs_1_.refs_3_.refs_6_.refs_10_.gate_ref = bf16[1,4096,1024]{2,1,0:T(8,128)(2,1)S(1)} custom-call(bf16[1,4096,1024]{2,1,0:T(8,128)(2,1)} %src.3, bf16[32,4096]{1,0:T(8,128)(2,1)S(1)} %get-tuple-element.34.refs_0_), custom_call_target="tpu_custom_call" | custom-call | bytes 1024 | tf_op jit(solution)/shard_map/load/pallas_call | solution.py:128
  14.0 0.0 collective-permute-done.1.refs_3_.refs_1_.refs_2_
  14.1 1.8 %collective-permute-start.3 = (bf16[16,4096]{1,0:T(8,128)(2,1)S(1)}, bf16[16,4096]{1,0:T(8,128)(2,1)S(1)}, u32[]{:S(2)}, u32[]{:S(2)}) collective-permute-start(bf16[16,4096]{1,0:T(8,128)(2,1)S(1)} %get-tuple-element.38), channel_id=1, source_target_pairs={{0,8},{2,10},{4,12},{6,14},{8,0},{10,2},{12,4},{14,6},{1,9},{3,11}... | collective-permute-start | bytes 393224 | tf_op jit(solution)/shard_map/ppermute | solution.py:449
  15.8 2.0 %collective-permute-start.4 = (bf16[16,4096]{1,0:T(8,128)(2,1)S(1)}, bf16[16,4096]{1,0:T(8,128)(2,1)S(1)}, u32[]{:S(2)}, u32[]{:S(2)}) collective-permute-start(bf16[16,4096]{1,0:T(8,128)(2,1)S(1)} %get-tuple-element.39), channel_id=1, source_target_pairs={{0,12},{2,14},{4,8},{6,10},{8,4},{10,6},{12,0},{14,2},{1,13},{3,15... | collective-permute-start | bytes 393224 | tf_op jit(solution)/shard_map/ppermute | solution.py:449
  17.8 0.0 collective-permute-done.refs_0_.refs_1_
  17.8 0.5 collective-permute-start.2
  18.3 3.5 %load.3.refs_3_.refs_4_.refs_7_.refs_11_.up_ref = bf16[1,4096,1024]{2,1,0:T(8,128)(2,1)S(1)} custom-call(bf16[1,4096,1024]{2,1,0:T(8,128)(2,1)} %src.4, bf16[32,4096]{1,0:T(8,128)(2,1)S(1)} %collective-permute-done.refs_0_.refs_1_, bf16[1,4096,1024]{2,1,0:T(8,128)(2,1)S(1)} %load.2.refs_2_.refs_1_.refs_3_.refs_6_.refs_10_.gate_ref), custom_call_target="tpu_custom_call" | custom-call | bytes 1024 | tf_op jit(solution)/shard_map/load/pallas_call | solution.py:128
  21.8 0.0 collective-permute-done.5.refs_0_
  21.8 1.3 %collective-permute-done.6.refs_1_ = bf16[16,4096]{1,0:T(8,128)(2,1)S(1)} collective-permute-done((bf16[16,4096]{1,0:T(8,128)(2,1)S(1)}, bf16[16,4096]{1,0:T(8,128)(2,1)S(1)}, u32[]{:S(2)}, u32[]{:S(2)}) %collective-permute-start.6) | collective-permute-done | bytes 131104 | tf_op jit(solution)/shard_map/ppermute | solution.py:449
  23.2 0.6 collective-permute-start.8
  23.7 2.4 %collective-permute-done.2.refs_2_.refs_3_ = bf16[32,4096]{1,0:T(8,128)(2,1)S(1)} collective-permute-done((bf16[32,4096]{1,0:T(8,128)(2,1)S(1)}, bf16[32,4096]{1,0:T(8,128)(2,1)S(1)}, u32[]{:S(2)}, u32[]{:S(2)}) %collective-permute-start.2) | collective-permute-done | bytes 262176 | tf_op jit(solution)/shard_map/ppermute | solution.py:449
  26.2 4.3 %load_turned.1.refs_4_.refs_8_.refs_9_ = bf16[4096,1024]{1,0:T(8,128)(2,1)S(1)} custom-call(bf16[1,1024,4096]{2,1,0:T(8,128)(2,1)} %src.5, bf16[32,4096]{1,0:T(8,128)(2,1)S(1)} %join.2.refs_0_.refs_4_, bf16[32,4096]{1,0:T(8,128)(2,1)S(1)} %collective-permute-done.1.refs_3_.refs_1_.refs_2_, bf16[32,4096]{1,0:T(8,128)(2,1)S(1)} %collective-permute-done.2.refs_2_.refs_3_, ...), custom_call_target="tpu_custom_call" | custom-call | bytes 1024 | tf_op jit(solution)/shard_map/load_turned/pallas_call | solution.py:161
  30.5 0.4 collective-permute-done.3.refs_0_
  30.9 0.0 collective-permute-done.4.refs_1_
  30.9 0.6 collective-permute-start.7
  31.5 0.0 collective-permute-done.8.refs_5_
  31.5 2.6 %pre_activations.1 = (f32[128,1024]{1,0:T(8,128)S(1)}, f32[128,1024]{1,0:T(8,128)S(1)}, f32[128,1024]{1,0:T(8,128)S(1)}) custom-call(bf16[32,4096]{1,0:T(8,128)(2,1)S(1)} %get-tuple-element.34.refs_0_, bf16[32,4096]{1,0:T(8,128)(2,1)S(1)} %collective-permute-done.refs_0_.refs_1_, bf16[32,4096]{1,0:T(8,128)(2,1)S(1)} %collective-permute-done.1.refs_3_.refs_1_.refs_2_, ...), custom_call_target="tpu_custom_call" | custom-call | flops 5000000000 | bytes 1024 | tf_op jit(solution)/shard_map/pre_activations/pallas_call | solution.py:251
  34.1 3.9 %collective-permute-done.7.refs_5_ = bf16[32,4096]{1,0:T(8,128)(2,1)S(1)} collective-permute-done((bf16[32,4096]{1,0:T(8,128)(2,1)S(1)}, bf16[32,4096]{1,0:T(8,128)(2,1)S(1)}, u32[]{:S(2)}, u32[]{:S(2)}) %collective-permute-start.7) | collective-permute-done | bytes 262176 | tf_op jit(solution)/shard_map/ppermute | solution.py:449
  38.0 3.6 %hidden_grads.1 = (bf16[64,2176]{1,0:T(8,128)(2,1)S(1)}, bf16[64,2176]{1,0:T(8,128)(2,1)S(1)}, bf16[128,1024]{1,0:T(8,128)(2,1)S(1)}, bf16[128,1024]{1,0:T(8,128)(2,1)S(1)}, bf16[128,128]{1,0:T(8,128)(2,1)S(1)}) custom-call(bf16[32,4096]{1,0:T(8,128)(2,1)S(1)} %get-tuple-element.34.refs_0_, bf16[32,4096]{1,0:T(8,128)(2,1)S(1)} %collective-permute-done.refs_0_.refs_1_, ...), custom_call_target="tpu_custom_call" | custom-call | flops 2147483648 | bytes 16777216 | tf_op jit(solution)/shard_map/hidden_grads/pallas_call | solution.py:305
  41.6 0.6 collective-permute-start.9
  42.2 0.0 copy-start
  42.2 0.0 copy-start.1
  42.2 0.0 copy-start.2
  42.2 2.4 %back_half.1 = (bf16[64,2176]{1,0:T(8,128)(2,1)S(1)}, bf16[64,2176]{1,0:T(8,128)(2,1)S(1)}) custom-call(bf16[128,1024]{1,0:T(8,128)(2,1)S(1)} %get-tuple-element.47.dgate_ref, bf16[128,1024]{1,0:T(8,128)(2,1)S(1)} %get-tuple-element.48.dup_ref, bf16[128,128]{1,0:T(8,128)(2,1)S(1)} %get-tuple-element.49.part_ref, ...), custom_call_target="tpu_custom_call" | custom-call | flops 1073741824 | bytes 8388608 | tf_op jit(solution)/shard_map/back_half/pallas_call | solution.py:329
  44.6 3.6 %collective-permute-done.9.refs_1_ = bf16[64,2176]{1,0:T(8,128)(2,1)S(1)} collective-permute-done((bf16[64,2176]{1,0:T(8,128)(2,1)S(1)}, bf16[64,2176]{1,0:T(8,128)(2,1)S(1)}, u32[]{:S(2)}, u32[]{:S(2)}) %collective-permute-start.9) | collective-permute-done | bytes 278560 | tf_op jit(solution)/shard_map/ppermute | solution.py:449
  48.2 0.1 sum_pieces.2
  48.3 0.1 collective-permute-start.13
  48.4 1.2 %collective-permute-done.13.refs_1_.refs_3_ = bf16[16,2176]{1,0:T(8,128)(2,1)S(1)} collective-permute-done((bf16[16,2176]{1,0:T(8,128)(2,1)S(1)}, bf16[16,2176]{1,0:T(8,128)(2,1)S(1)}, u32[]{:S(2)}, u32[]{:S(2)}) %collective-permute-start.13) | collective-permute-done | bytes 69664 | tf_op jit(solution)/shard_map/ppermute | solution.py:463
  49.6 0.5 collective-permute-start.14
  50.1 2.5 %collective-permute-start.10 = (bf16[16,2176]{1,0:T(8,128)(2,1)S(1)}, bf16[16,2176]{1,0:T(8,128)(2,1)S(1)}, u32[]{:S(2)}, u32[]{:S(2)}) collective-permute-start(bf16[16,2176]{1,0:T(8,128)(2,1)S(1)} %get-tuple-element.51), channel_id=1, source_target_pairs={{0,13},{1,12},{2,15},{3,14},{4,9},{5,8},{6,11},{7,10},{8,5},{9,4},... | collective-permute-start | bytes 208904 | tf_op jit(solution)/shard_map/ppermute | solution.py:463
  52.6 2.4 %collective-permute-start.11 = (bf16[16,2176]{1,0:T(8,128)(2,1)S(1)}, bf16[16,2176]{1,0:T(8,128)(2,1)S(1)}, u32[]{:S(2)}, u32[]{:S(2)}) collective-permute-start(bf16[16,2176]{1,0:T(8,128)(2,1)S(1)} %get-tuple-element.52), channel_id=1, source_target_pairs={{0,9},{1,8},{2,11},{3,10},{4,13},{5,12},{6,15},{7,14},{8,1},{9,0},... | collective-permute-start | bytes 208904 | tf_op jit(solution)/shard_map/ppermute | solution.py:463
  55.0 0.0 collective-permute-start.12
  55.0 3.3 %collective-permute-done.14.refs_1_ = bf16[64,2176]{1,0:T(8,128)(2,1)S(1)} collective-permute-done((bf16[64,2176]{1,0:T(8,128)(2,1)S(1)}, bf16[64,2176]{1,0:T(8,128)(2,1)S(1)}, u32[]{:S(2)}, u32[]{:S(2)}) %collective-permute-start.14) | collective-permute-done | bytes 278560 | tf_op jit(solution)/shard_map/ppermute | solution.py:449
  58.3 0.1 sum_pieces.3
  58.4 3.3 %collective-permute-start.15 = (bf16[16,2176]{1,0:T(8,128)(2,1)S(1)}, bf16[16,2176]{1,0:T(8,128)(2,1)S(1)}, u32[]{:S(2)}, u32[]{:S(2)}) collective-permute-start(bf16[16,2176]{1,0:T(8,128)(2,1)S(1)} %get-tuple-element.56), channel_id=1, source_target_pairs={{0,12},{1,13},{2,14},{3,15},{4,8},{5,9},{6,10},{7,11},{8,4},{9,5},... | collective-permute-start | bytes 208904 | tf_op jit(solution)/shard_map/ppermute | solution.py:463
  61.7 2.2 %collective-permute-start.16 = (bf16[16,2176]{1,0:T(8,128)(2,1)S(1)}, bf16[16,2176]{1,0:T(8,128)(2,1)S(1)}, u32[]{:S(2)}, u32[]{:S(2)}) collective-permute-start(bf16[16,2176]{1,0:T(8,128)(2,1)S(1)} %get-tuple-element.57), channel_id=1, source_target_pairs={{0,8},{1,9},{2,10},{3,11},{4,12},{5,13},{6,14},{7,15},{8,0},{9,1},... | collective-permute-start | bytes 208904 | tf_op jit(solution)/shard_map/ppermute | solution.py:463
  63.9 0.0 collective-permute-done.10.refs_0_
  63.9 0.0 collective-permute-start.17
  63.9 0.0 copy-done
  63.9 0.0 copy-done.1
  63.9 0.0 copy-done.2
  63.9 0.2 mixing.1
  64.1 0.0 collective-permute-done.11.refs_1_
  64.2 0.0 collective-permute-done.12.refs_2_
  64.2 0.5 collective-permute-done.15.refs_4_
  64.7 4.3 %collective-permute-done.16.refs_5_ = bf16[16,2176]{1,0:T(8,128)(2,1)S(1)} collective-permute-done((bf16[16,2176]{1,0:T(8,128)(2,1)S(1)}, bf16[16,2176]{1,0:T(8,128)(2,1)S(1)}, u32[]{:S(2)}, u32[]{:S(2)}) %collective-permute-start.16) | collective-permute-done | bytes 69664 | tf_op jit(solution)/shard_map/ppermute | solution.py:463
  69.0 0.0 collective-permute-done.17.refs_6_
  69.0 1.2 %combine.1 = (bf16[128,2048]{1,0:T(8,128)(2,1)}, f32[1,128]{1,0:T(1,128)}) custom-call(bf16[2,128,128]{2,1,0:T(8,128)(2,1)S(1)} %get-tuple-element.32.mix_ref, f32[128,128]{1,0:T(8,128)S(1)} %get-tuple-element.33.hit_ref, bf16[16,2176]{1,0:T(8,128)(2,1)S(1)} %collective-permute-done.10.refs_0_, bf16[16,2176]{1,0:T(8,128)(2,1)S(1)} %collective-permute-done.11.refs_1_, ...), custom_call_target="tpu_custom_call" | custom-call | flops 134217728 | bytes 1048576 | tf_op jit(solution)/shard_map/combine/pallas_call | solution.py:426
  (4 shorter events, 0.0 us)
Async XLA Ops:
  3.1 10.9 %collective-permute-start.1 = (bf16[32,4096]{1,0:T(8,128)(2,1)S(1)}, bf16[32,4096]{1,0:T(8,128)(2,1)S(1)}, u32[]{:S(2)}, u32[]{:S(2)}) collective-permute-start(bf16[32,4096]{1,0:T(8,128)(2,1)S(1)} %get-tuple-element.34.refs_0_), channel_id=1, source_target_pairs={{0,2},{2,0},{4,6},{6,4},{8,10},{10,8},{12,14},{14,12},{1,3},{3,1},... | collective-permute-start | bytes 786440 | tf_op jit(solution)/shard_map/ppermute | solution.py:449
  6.2 11.6 %collective-permute-start = (bf16[32,4096]{1,0:T(8,128)(2,1)S(1)}, bf16[32,4096]{1,0:T(8,128)(2,1)S(1)}, u32[]{:S(2)}, u32[]{:S(2)}) collective-permute-start(bf16[32,4096]{1,0:T(8,128)(2,1)S(1)} %get-tuple-element.35), channel_id=1, source_target_pairs={{0,4},{2,6},{4,0},{6,2},{8,12},{10,14},{12,8},{14,10},{1,5},{3,7},... | collective-permute-start | bytes 786440 | tf_op jit(solution)/shard_map/ppermute | solution.py:449
  7.7 14.1 %collective-permute-start.5 = (bf16[16,4096]{1,0:T(8,128)(2,1)S(1)}, bf16[16,4096]{1,0:T(8,128)(2,1)S(1)}, u32[]{:S(2)}, u32[]{:S(2)}) collective-permute-start(bf16[16,4096]{1,0:T(8,128)(2,1)S(1)} %get-tuple-element.40), channel_id=1, source_target_pairs={{0,8},{2,10},{4,12},{6,14},{8,0},{10,2},{12,4},{14,6},{1,9},{3,11}... | collective-permute-start | bytes 393224 | tf_op jit(solution)/shard_map/ppermute | solution.py:449
  10.3 12.8 %collective-permute-start.6 = (bf16[16,4096]{1,0:T(8,128)(2,1)S(1)}, bf16[16,4096]{1,0:T(8,128)(2,1)S(1)}, u32[]{:S(2)}, u32[]{:S(2)}) collective-permute-start(bf16[16,4096]{1,0:T(8,128)(2,1)S(1)} %get-tuple-element.41), channel_id=1, source_target_pairs={{0,12},{2,14},{4,8},{6,10},{8,4},{10,6},{12,0},{14,2},{1,13},{3,15... | collective-permute-start | bytes 393224 | tf_op jit(solution)/shard_map/ppermute | solution.py:449
  14.1 16.8 %collective-permute-start.3 = (bf16[16,4096]{1,0:T(8,128)(2,1)S(1)}, bf16[16,4096]{1,0:T(8,128)(2,1)S(1)}, u32[]{:S(2)}, u32[]{:S(2)}) collective-permute-start(bf16[16,4096]{1,0:T(8,128)(2,1)S(1)} %get-tuple-element.38), channel_id=1, source_target_pairs={{0,8},{2,10},{4,12},{6,14},{8,0},{10,2},{12,4},{14,6},{1,9},{3,11}... | collective-permute-start | bytes 393224 | tf_op jit(solution)/shard_map/ppermute | solution.py:449
  15.8 15.1 %collective-permute-start.4 = (bf16[16,4096]{1,0:T(8,128)(2,1)S(1)}, bf16[16,4096]{1,0:T(8,128)(2,1)S(1)}, u32[]{:S(2)}, u32[]{:S(2)}) collective-permute-start(bf16[16,4096]{1,0:T(8,128)(2,1)S(1)} %get-tuple-element.39), channel_id=1, source_target_pairs={{0,12},{2,14},{4,8},{6,10},{8,4},{10,6},{12,0},{14,2},{1,13},{3,15... | collective-permute-start | bytes 393224 | tf_op jit(solution)/shard_map/ppermute | solution.py:449
  17.8 8.3 %collective-permute-start.2 = (bf16[32,4096]{1,0:T(8,128)(2,1)S(1)}, bf16[32,4096]{1,0:T(8,128)(2,1)S(1)}, u32[]{:S(2)}, u32[]{:S(2)}) collective-permute-start(bf16[32,4096]{1,0:T(8,128)(2,1)S(1)} %collective-permute-done.refs_0_.refs_1_), channel_id=1, source_target_pairs={{0,2},{2,0},{4,6},{6,4},{8,10},{10,8},{12,14},{14,12},{1,3},{3,1},... | collective-permute-start | bytes 786440 | tf_op jit(solution)/shard_map/ppermute | solution.py:449
  23.2 8.3 %collective-permute-start.8 = (bf16[32,4096]{1,0:T(8,128)(2,1)S(1)}, bf16[32,4096]{1,0:T(8,128)(2,1)S(1)}, u32[]{:S(2)}, u32[]{:S(2)}) collective-permute-start(bf16[32,4096]{1,0:T(8,128)(2,1)S(1)} %join.2.refs_0_.refs_4_), channel_id=1, source_target_pairs={{0,2},{2,0},{4,6},{6,4},{8,10},{10,8},{12,14},{14,12},{1,3},{3,1},... | collective-permute-start | bytes 786440 | tf_op jit(solution)/shard_map/ppermute | solution.py:449
  30.9 7.1 %collective-permute-start.7 = (bf16[32,4096]{1,0:T(8,128)(2,1)S(1)}, bf16[32,4096]{1,0:T(8,128)(2,1)S(1)}, u32[]{:S(2)}, u32[]{:S(2)}) collective-permute-start(bf16[32,4096]{1,0:T(8,128)(2,1)S(1)} %join.3.refs_4_), channel_id=1, source_target_pairs={{0,2},{2,0},{4,6},{6,4},{8,10},{10,8},{12,14},{14,12},{1,3},{3,1},... | collective-permute-start | bytes 786440 | tf_op jit(solution)/shard_map/ppermute | solution.py:449
  41.6 6.6 %collective-permute-start.9 = (bf16[64,2176]{1,0:T(8,128)(2,1)S(1)}, bf16[64,2176]{1,0:T(8,128)(2,1)S(1)}, u32[]{:S(2)}, u32[]{:S(2)}) collective-permute-start(bf16[64,2176]{1,0:T(8,128)(2,1)S(1)} %get-tuple-element.46), channel_id=1, source_target_pairs={{0,2},{2,0},{4,6},{6,4},{8,10},{10,8},{12,14},{14,12},{1,3},{3,1},... | collective-permute-start | bytes 835592 | tf_op jit(solution)/shard_map/ppermute | solution.py:449
  42.2 21.7 %copy-start = (s32[128,2]{0,1:T(2,128)S(1)}, s32[128,2]{0,1:T(2,128)}, u32[]{:S(2)}) copy-start(s32[128,2]{0,1:T(2,128)} %param.11) | copy-start | bytes 3076
  42.2 21.7 %copy-start.1 = (s32[128]{0:T(128)S(1)}, s32[128]{0:T(128)}, u32[]{:S(2)}) copy-start(s32[128]{0:T(128)} %param.10) | copy-start | bytes 1540
  42.2 21.7 %copy-start.2 = (f32[128,2]{0,1:T(2,128)S(1)}, f32[128,2]{0,1:T(2,128)}, u32[]{:S(2)}) copy-start(f32[128,2]{0,1:T(2,128)} %param.12) | copy-start | bytes 3076
  48.3 1.3 %collective-permute-start.13 = (bf16[16,2176]{1,0:T(8,128)(2,1)S(1)}, bf16[16,2176]{1,0:T(8,128)(2,1)S(1)}, u32[]{:S(2)}, u32[]{:S(2)}) collective-permute-start(bf16[16,2176]{1,0:T(8,128)(2,1)S(1)} %get-tuple-element.54), channel_id=1, source_target_pairs={{0,1},{1,0},{2,3},{3,2},{4,5},{5,4},{6,7},{7,6},{8,9},{9,8},{10,11... | collective-permute-start | bytes 208904 | tf_op jit(solution)/shard_map/ppermute | solution.py:463
  49.6 8.7 %collective-permute-start.14 = (bf16[64,2176]{1,0:T(8,128)(2,1)S(1)}, bf16[64,2176]{1,0:T(8,128)(2,1)S(1)}, u32[]{:S(2)}, u32[]{:S(2)}) collective-permute-start(bf16[64,2176]{1,0:T(8,128)(2,1)S(1)} %pass_after.3), channel_id=1, source_target_pairs={{0,2},{2,0},{4,6},{6,4},{8,10},{10,8},{12,14},{14,12},{1,3},{3,1},... | collective-permute-start | bytes 835592 | tf_op jit(solution)/shard_map/ppermute | solution.py:449
  50.1 13.7 %collective-permute-start.10 = (bf16[16,2176]{1,0:T(8,128)(2,1)S(1)}, bf16[16,2176]{1,0:T(8,128)(2,1)S(1)}, u32[]{:S(2)}, u32[]{:S(2)}) collective-permute-start(bf16[16,2176]{1,0:T(8,128)(2,1)S(1)} %get-tuple-element.51), channel_id=1, source_target_pairs={{0,13},{1,12},{2,15},{3,14},{4,9},{5,8},{6,11},{7,10},{8,5},{9,4},... | collective-permute-start | bytes 208904 | tf_op jit(solution)/shard_map/ppermute | solution.py:463
  52.6 11.5 %collective-permute-start.11 = (bf16[16,2176]{1,0:T(8,128)(2,1)S(1)}, bf16[16,2176]{1,0:T(8,128)(2,1)S(1)}, u32[]{:S(2)}, u32[]{:S(2)}) collective-permute-start(bf16[16,2176]{1,0:T(8,128)(2,1)S(1)} %get-tuple-element.52), channel_id=1, source_target_pairs={{0,9},{1,8},{2,11},{3,10},{4,13},{5,12},{6,15},{7,14},{8,1},{9,0},... | collective-permute-start | bytes 208904 | tf_op jit(solution)/shard_map/ppermute | solution.py:463
  55.0 9.2 %collective-permute-start.12 = (bf16[16,2176]{1,0:T(8,128)(2,1)S(1)}, bf16[16,2176]{1,0:T(8,128)(2,1)S(1)}, u32[]{:S(2)}, u32[]{:S(2)}) collective-permute-start(bf16[16,2176]{1,0:T(8,128)(2,1)S(1)} %get-tuple-element.53), channel_id=1, source_target_pairs={{0,5},{1,4},{2,7},{3,6},{4,1},{5,0},{6,3},{7,2},{8,13},{9,12},{10,... | collective-permute-start | bytes 208904 | tf_op jit(solution)/shard_map/ppermute | solution.py:463
  58.4 6.3 %collective-permute-start.15 = (bf16[16,2176]{1,0:T(8,128)(2,1)S(1)}, bf16[16,2176]{1,0:T(8,128)(2,1)S(1)}, u32[]{:S(2)}, u32[]{:S(2)}) collective-permute-start(bf16[16,2176]{1,0:T(8,128)(2,1)S(1)} %get-tuple-element.56), channel_id=1, source_target_pairs={{0,12},{1,13},{2,14},{3,15},{4,8},{5,9},{6,10},{7,11},{8,4},{9,5},... | collective-permute-start | bytes 208904 | tf_op jit(solution)/shard_map/ppermute | solution.py:463
  61.7 7.3 %collective-permute-start.16 = (bf16[16,2176]{1,0:T(8,128)(2,1)S(1)}, bf16[16,2176]{1,0:T(8,128)(2,1)S(1)}, u32[]{:S(2)}, u32[]{:S(2)}) collective-permute-start(bf16[16,2176]{1,0:T(8,128)(2,1)S(1)} %get-tuple-element.57), channel_id=1, source_target_pairs={{0,8},{1,9},{2,10},{3,11},{4,12},{5,13},{6,14},{7,15},{8,0},{9,1},... | collective-permute-start | bytes 208904 | tf_op jit(solution)/shard_map/ppermute | solution.py:463
  63.9 5.1 %collective-permute-start.17 = (bf16[16,2176]{1,0:T(8,128)(2,1)S(1)}, bf16[16,2176]{1,0:T(8,128)(2,1)S(1)}, u32[]{:S(2)}, u32[]{:S(2)}) collective-permute-start(bf16[16,2176]{1,0:T(8,128)(2,1)S(1)} %get-tuple-element.58), channel_id=1, source_target_pairs={{0,4},{1,5},{2,6},{3,7},{4,0},{5,1},{6,2},{7,3},{8,12},{9,13},{10,... | collective-permute-start | bytes 208904 | tf_op jit(solution)/shard_map/ppermute | solution.py:463

commit v15 on v12

--- a/solution.py
+++ b/solution.py
@@ -263,7 +263,10 @@
 def back_columns(groups, flip, dgate_ref, dup_ref, part, gate_ref, up_ref, outs):
     half = jnp.bitwise_xor(position(groups)[1], flip)
     wide = outs[0].shape[1] - EXT
-    own_rows = outs[0].shape[0]
+    places, start = [], 0
+    for out in outs:
+        places.append(slice(start, start + out.shape[0]))
+        start += out.shape[0]
     dgate, dup = dgate_ref[...].T, dup_ref[...].T
     chunk = 512
     for step in range(wide // chunk):
@@ -271,17 +274,17 @@
         grad = jnp.dot(gate_ref[0, rows, :], dgate, preferred_element_type=F32)
         grad = grad + jnp.dot(up_ref[0, rows, :], dup, preferred_element_type=F32)
         grad = grad.T.astype(BF16)
-        for t in range(groups):
-            outs[t][:, step * chunk : (step + 1) * chunk] = grad[t * own_rows : (t + 1) * own_rows, :]
-    for t in range(groups):
-        outs[t][:, wide:] = part[t * own_rows : (t + 1) * own_rows, :]
+        for out, place in zip(outs, places):
+            out[:, step * chunk : (step + 1) * chunk] = grad[place, :]
+    for out, place in zip(outs, places):
+        out[:, wide:] = part[place, :]
 
 
 def hidden_kernel(count, places, groups, *refs):
     blocks = refs[:count]
     act_ref, slope_ref, both_ref, down_ref, gate_ref, up_ref = refs[count : count + 6]
-    outs = refs[count + 6 : count + 6 + groups]
-    dgate, dup, part_out, rows = refs[count + 6 + groups :]
+    outs = refs[count + 6 : -4]
+    dgate, dup, part_out, rows = refs[-4:]
     fill(rows, blocks, places)
     hidden = gate_ref.shape[2]
     chunk = min(256, hidden)
@@ -300,13 +303,13 @@
     count = len(blocks)
     _, width, hidden = gate_piece.shape
     total = len(places) * CAP
-    shape = (total // groups, width // 2 + EXT)
+    shape = (total // groups // 2, width // 2 + EXT)
     vmem = pl.BlockSpec(memory_space=pltpu.VMEM)
     out = pl.pallas_call(
         functools.partial(hidden_kernel, count, places, groups),
         in_specs=[vmem] * (count + 6),
-        out_specs=[vmem] * (groups + 3),
-        out_shape=[jax.ShapeDtypeStruct(shape, BF16)] * groups
+        out_specs=[vmem] * (2 * groups + 3),
+        out_shape=[jax.ShapeDtypeStruct(shape, BF16)] * (2 * groups)
         + [jax.ShapeDtypeStruct((total, hidden), BF16)] * 2
         + [jax.ShapeDtypeStruct((total, EXT), BF16)],
         scratch_shapes=[pltpu.VMEM((total, width), BF16)],
@@ -314,7 +317,7 @@
         cost_estimate=cost(4 * total * width * hidden, 4 * width * hidden),
         name="hidden_grads",
     )(*blocks, *factors, in_vmem(down_piece), in_vmem(gate_piece), in_vmem(up_piece))
-    return out[:groups], out[groups:]
+    return list(out[:-3]), out[-3:]
 
 
 def back_kernel(groups, dgate_ref, dup_ref, part_ref, gate_ref, up_ref, *outs):
@@ -324,13 +327,13 @@
 def back_half(groups, dgate, dup, part, gate_piece, up_piece):
     _, width, hidden = gate_piece.shape
     total = dgate.shape[0]
-    shape = (total // groups, width // 2 + EXT)
+    shape = (total // groups // 2, width // 2 + EXT)
     vmem = pl.BlockSpec(memory_space=pltpu.VMEM)
     return pl.pallas_call(
         functools.partial(back_kernel, groups),
         in_specs=[vmem] * 5,
-        out_specs=[vmem] * groups,
-        out_shape=[jax.ShapeDtypeStruct(shape, BF16)] * groups,
+        out_specs=[vmem] * (2 * groups),
+        out_shape=[jax.ShapeDtypeStruct(shape, BF16)] * (2 * groups),
         compiler_params=pltpu.CompilerParams(vmem_limit_bytes=SCOPED),
         cost_estimate=cost(2 * total * width * hidden, 2 * width * hidden),
         name="back_half",
@@ -345,19 +348,20 @@
 
 
 def sum_kernel(groups, *refs):
-    ins, outs = refs[:groups], refs[groups:]
+    ins, outs = refs[: 2 * groups], refs[2 * groups :]
     wide = ins[0].shape[1] - EXT
     for s in range(E_MOD):
-        rows = slice(s * CAP, (s + 1) * CAP)
-        total = ins[0][rows, :].astype(F32)
+        half, place = divmod(s, 2)
+        rows = slice(place * CAP, (place + 1) * CAP)
+        total = ins[half][rows, :].astype(F32)
         for t in range(1, groups):
-            total = total + ins[t][rows, :].astype(F32)
+            total = total + ins[2 * t + half][rows, :].astype(F32)
         outs[s][:, :wide] = total[:, :wide].astype(BF16)
         outs[s][:, wide:] = two_terms(jnp.sum(total[:, wide:], axis=1, keepdims=True))
 
 
 def sum_pieces(partials):
-    groups = len(partials)
+    groups = len(partials) // 2
     own_rows, wide = partials[0].shape
     return pl.pallas_call(
         functools.partial(sum_kernel, groups),
@@ -499,10 +503,10 @@
     first, (dgate, dup, part) = hidden_grads(
         blocks[1], places[1], groups, factors, down_piece, gate_piece, up_piece
     )
-    second = back_half(groups, dgate, dup, part, gate_piece, up_piece)
-    first = [first[0]] + [to_piece(first[t], groups - t) for t in range(1, groups)]
-    waiting = pass_after(second[1:], *first[1:])
-    second = [second[0]] + [to_piece(x, groups - t) for t, x in enumerate(waiting, 1)]
+    second = list(back_half(groups, dgate, dup, part, gate_piece, up_piece))
+    first = first[:2] + [to_piece(first[i], groups - i // 2) for i in range(2, 2 * groups)]
+    waiting = pass_after(second[2:], *first[2:])
+    second = second[:2] + [to_piece(x, groups - i // 2) for i, x in enumerate(waiting, 2)]
     crossed, kept = sum_pieces(first), sum_pieces(second)
     arrived = {0: kept[0]}
     for s in range(1, E_MOD):

time: 67.9 us -> 69.3 us (1.021)
  starting transfers between devices: 25.4 us -> 28.3 us
  waiting for transfers between devices: 17.5 us -> 16 us
    ppermute x11 -> x13, starting transfers between devices: 13.9 us -> 16.9 us  [to_expert(): lax.ppermute(x, 'ep', [(e * groups + j, (e ^ s) * groups + (j + t) % grou...]
    ppermute x11 -> x13, waiting for transfers between devices: 12.8 us -> 10.8 us  [to_expert(): lax.ppermute(x, 'ep', [(e * groups + j, (e ^ s) * groups + (j + t) % grou...]
  transfers between devices with their start and end apart: 18 -> 20, of which waited for: 9 -> 9; matrix products, arithmetic and copies ran while one was open for 0% -> 0% of each run, Pallas kernels for 25% -> 24%
where the time goes in v15:
time: 69.3 us; the launch traced here: 69.1 us
  starting transfers between devices  28.3 us (41%)
  Pallas kernels  24.1 us (35%)
  waiting for transfers between devices  16 us (23%)
  between operations  0.77 us (1%)
    ppermute x13, starting transfers between devices, to_expert(): lax.ppermute(x, 'ep', [(e * groups + j, (e ^ s) * groups + (j + t) % grou...  16.9 us
    ppermute x7, starting transfers between devices, to_source(): lax.ppermute(x, ('ep', 'mod'), [((e * groups + j) * 2 + m, ((e ^ s) * gro...  11.3 us
    ppermute x13, waiting for transfers between devices, to_expert(): lax.ppermute(x, 'ep', [(e * groups + j, (e ^ s) * groups + (j + t) % grou...  10.8 us
    pallas_call x2, Pallas kernels, load(): pl.pallas_call(functools.partial(load_kernel, parts), in_specs=[pl.BlockS...  6.94 us
    ppermute x7, waiting for transfers between devices, to_source(): lax.ppermute(x, ('ep', 'mod'), [((e * groups + j) * 2 + m, ((e ^ s) * gro...  5.25 us
    pallas_call x1, Pallas kernels, load_turned(): pl.pallas_call(functools.partial(load_turned_kernel, parts), in_specs=[pl...  4.29 us
    pallas_call x1, Pallas kernels, hidden_grads(): pl.pallas_call(functools.partial(hidden_kernel, count, places, groups), i...  3.61 us
    pallas_call x1, Pallas kernels, pre_activations(): pl.pallas_call(functools.partial(pre_kernel, count, places), in_specs=[vm...  2.61 us
  transfers between devices with their start and end apart: 20, of which 9 were waited for; matrix products, arithmetic and copies ran while one was open for 0% of the time, Pallas kernels for 24%

profile of v15, /device:TPU:0, one launch (start us, length us, event | category | flops | bytes accessed | tf_op | source)
XLA Modules:
  0.0 69.1 jit_solution(11606949175575402600)
XLA Ops:
  0.6 2.5 %gather_slots.1 = (bf16[32,4096]{1,0:T(8,128)(2,1)S(1)}, bf16[32,4096]{1,0:T(8,128)(2,1)S(1)}, bf16[16,4096]{1,0:T(8,128)(2,1)S(1)}, bf16[16,4096]{1,0:T(8,128)(...) custom-call(s32[1,128]{1,0:T(1,128)} %bitcast.6, s32[2,128]{1,0:T(2,128)} %bitcast.4, ...), custom_call_target="tpu_custom_call" | custom-call | flops 134217728 | bytes 3145728 | tf_op jit(solution)/shard_map/gather_slots/pallas_call | solution.py:93
  3.1 3.0 %collective-permute-start.1 = (bf16[32,4096]{1,0:T(8,128)(2,1)S(1)}, bf16[32,4096]{1,0:T(8,128)(2,1)S(1)}, u32[]{:S(2)}, u32[]{:S(2)}) collective-permute-start(bf16[32,4096]{1,0:T(8,128)(2,1)S(1)} %get-tuple-element.40.refs_0_), channel_id=1, source_target_pairs={{0,2},{2,0},{4,6},{6,4},{8,10},{10,8},{12,14},{14,12},{1,3},{3,1},... | collective-permute-start | bytes 786440 | tf_op jit(solution)/shard_map/ppermute | solution.py:450
  6.2 1.6 %collective-permute-start = (bf16[32,4096]{1,0:T(8,128)(2,1)S(1)}, bf16[32,4096]{1,0:T(8,128)(2,1)S(1)}, u32[]{:S(2)}, u32[]{:S(2)}) collective-permute-start(bf16[32,4096]{1,0:T(8,128)(2,1)S(1)} %get-tuple-element.41), channel_id=1, source_target_pairs={{0,4},{2,6},{4,0},{6,2},{8,12},{10,14},{12,8},{14,10},{1,5},{3,7},... | collective-permute-start | bytes 786440 | tf_op jit(solution)/shard_map/ppermute | solution.py:450
  7.7 2.6 %collective-permute-start.5 = (bf16[16,4096]{1,0:T(8,128)(2,1)S(1)}, bf16[16,4096]{1,0:T(8,128)(2,1)S(1)}, u32[]{:S(2)}, u32[]{:S(2)}) collective-permute-start(bf16[16,4096]{1,0:T(8,128)(2,1)S(1)} %get-tuple-element.46), channel_id=1, source_target_pairs={{0,8},{2,10},{4,12},{6,14},{8,0},{10,2},{12,4},{14,6},{1,9},{3,11}... | collective-permute-start | bytes 393224 | tf_op jit(solution)/shard_map/ppermute | solution.py:450
  10.3 0.2 collective-permute-start.6
  10.6 3.5 %load.2.refs_2_.refs_1_.refs_3_.refs_6_.refs_10_.gate_ref = bf16[1,4096,1024]{2,1,0:T(8,128)(2,1)S(1)} custom-call(bf16[1,4096,1024]{2,1,0:T(8,128)(2,1)} %src.3, bf16[32,4096]{1,0:T(8,128)(2,1)S(1)} %get-tuple-element.40.refs_0_), custom_call_target="tpu_custom_call" | custom-call | bytes 1024 | tf_op jit(solution)/shard_map/load/pallas_call | solution.py:128
  14.0 0.0 collective-permute-done.1.refs_3_.refs_1_.refs_2_
  14.1 1.8 %collective-permute-start.3 = (bf16[16,4096]{1,0:T(8,128)(2,1)S(1)}, bf16[16,4096]{1,0:T(8,128)(2,1)S(1)}, u32[]{:S(2)}, u32[]{:S(2)}) collective-permute-start(bf16[16,4096]{1,0:T(8,128)(2,1)S(1)} %get-tuple-element.44), channel_id=1, source_target_pairs={{0,8},{2,10},{4,12},{6,14},{8,0},{10,2},{12,4},{14,6},{1,9},{3,11}... | collective-permute-start | bytes 393224 | tf_op jit(solution)/shard_map/ppermute | solution.py:450
  15.8 2.0 %collective-permute-start.4 = (bf16[16,4096]{1,0:T(8,128)(2,1)S(1)}, bf16[16,4096]{1,0:T(8,128)(2,1)S(1)}, u32[]{:S(2)}, u32[]{:S(2)}) collective-permute-start(bf16[16,4096]{1,0:T(8,128)(2,1)S(1)} %get-tuple-element.45), channel_id=1, source_target_pairs={{0,12},{2,14},{4,8},{6,10},{8,4},{10,6},{12,0},{14,2},{1,13},{3,15... | collective-permute-start | bytes 393224 | tf_op jit(solution)/shard_map/ppermute | solution.py:450
  17.8 0.0 collective-permute-done.refs_0_.refs_1_
  17.8 0.5 collective-permute-start.2
  18.3 3.5 %load.3.refs_3_.refs_4_.refs_7_.refs_11_.up_ref = bf16[1,4096,1024]{2,1,0:T(8,128)(2,1)S(1)} custom-call(bf16[1,4096,1024]{2,1,0:T(8,128)(2,1)} %src.4, bf16[32,4096]{1,0:T(8,128)(2,1)S(1)} %collective-permute-done.refs_0_.refs_1_, bf16[1,4096,1024]{2,1,0:T(8,128)(2,1)S(1)} %load.2.refs_2_.refs_1_.refs_3_.refs_6_.refs_10_.gate_ref), custom_call_target="tpu_custom_call" | custom-call | bytes 1024 | tf_op jit(solution)/shard_map/load/pallas_call | solution.py:128
  21.8 0.0 collective-permute-done.5.refs_0_
  21.8 1.3 %collective-permute-done.6.refs_1_ = bf16[16,4096]{1,0:T(8,128)(2,1)S(1)} collective-permute-done((bf16[16,4096]{1,0:T(8,128)(2,1)S(1)}, bf16[16,4096]{1,0:T(8,128)(2,1)S(1)}, u32[]{:S(2)}, u32[]{:S(2)}) %collective-permute-start.6) | collective-permute-done | bytes 131104 | tf_op jit(solution)/shard_map/ppermute | solution.py:450
  23.2 0.6 collective-permute-start.8
  23.7 2.4 %collective-permute-done.2.refs_2_.refs_3_ = bf16[32,4096]{1,0:T(8,128)(2,1)S(1)} collective-permute-done((bf16[32,4096]{1,0:T(8,128)(2,1)S(1)}, bf16[32,4096]{1,0:T(8,128)(2,1)S(1)}, u32[]{:S(2)}, u32[]{:S(2)}) %collective-permute-start.2) | collective-permute-done | bytes 262176 | tf_op jit(solution)/shard_map/ppermute | solution.py:450
  26.2 4.3 %load_turned.1.refs_4_.refs_8_.refs_9_ = bf16[4096,1024]{1,0:T(8,128)(2,1)S(1)} custom-call(bf16[1,1024,4096]{2,1,0:T(8,128)(2,1)} %src.5, bf16[32,4096]{1,0:T(8,128)(2,1)S(1)} %join.2.refs_0_.refs_4_, bf16[32,4096]{1,0:T(8,128)(2,1)S(1)} %collective-permute-done.1.refs_3_.refs_1_.refs_2_, bf16[32,4096]{1,0:T(8,128)(2,1)S(1)} %collective-permute-done.2.refs_2_.refs_3_, ...), custom_call_target="tpu_custom_call" | custom-call | bytes 1024 | tf_op jit(solution)/shard_map/load_turned/pallas_call | solution.py:161
  30.5 0.4 collective-permute-done.3.refs_0_
  30.9 0.0 collective-permute-done.4.refs_1_
  30.9 0.6 collective-permute-start.7
  31.5 0.0 collective-permute-done.8.refs_5_
  31.5 2.6 %pre_activations.1 = (f32[128,1024]{1,0:T(8,128)S(1)}, f32[128,1024]{1,0:T(8,128)S(1)}, f32[128,1024]{1,0:T(8,128)S(1)}) custom-call(bf16[32,4096]{1,0:T(8,128)(2,1)S(1)} %get-tuple-element.40.refs_0_, bf16[32,4096]{1,0:T(8,128)(2,1)S(1)} %collective-permute-done.refs_0_.refs_1_, bf16[32,4096]{1,0:T(8,128)(2,1)S(1)} %collective-permute-done.1.refs_3_.refs_1_.refs_2_, ...), custom_call_target="tpu_custom_call" | custom-call | flops 5000000000 | bytes 1024 | tf_op jit(solution)/shard_map/pre_activations/pallas_call | solution.py:251
  34.1 3.9 %collective-permute-done.7.refs_5_ = bf16[32,4096]{1,0:T(8,128)(2,1)S(1)} collective-permute-done((bf16[32,4096]{1,0:T(8,128)(2,1)S(1)}, bf16[32,4096]{1,0:T(8,128)(2,1)S(1)}, u32[]{:S(2)}, u32[]{:S(2)}) %collective-permute-start.7) | collective-permute-done | bytes 262176 | tf_op jit(solution)/shard_map/ppermute | solution.py:450
  38.0 3.6 %hidden_grads.1 = (bf16[32,2176]{1,0:T(8,128)(2,1)S(1)}, bf16[32,2176]{1,0:T(8,128)(2,1)S(1)}, bf16[32,2176]{1,0:T(8,128)(2,1)S(1)}, bf16[32,2176]{1,0:T(8,128)(...) custom-call(bf16[32,4096]{1,0:T(8,128)(2,1)S(1)} %get-tuple-element.40.refs_0_,, ...), custom_call_target="tpu_custom_call" | custom-call | flops 2147483648 | bytes 16777216 | tf_op jit(solution)/shard_map/hidden_grads/pallas_call | solution.py:308
  41.6 0.6 collective-permute-start.10
  42.2 1.5 %collective-permute-start.9 = (bf16[32,2176]{1,0:T(8,128)(2,1)S(1)}, bf16[32,2176]{1,0:T(8,128)(2,1)S(1)}, u32[]{:S(2)}, u32[]{:S(2)}) collective-permute-start(bf16[32,2176]{1,0:T(8,128)(2,1)S(1)} %get-tuple-element.53), channel_id=1, source_target_pairs={{0,2},{2,0},{4,6},{6,4},{8,10},{10,8},{12,14},{14,12},{1,3},{3,1},... | collective-permute-start | bytes 417800 | tf_op jit(solution)/shard_map/ppermute | solution.py:450
  43.7 0.0 copy-start
  43.7 0.0 copy-start.1
  43.7 0.0 copy-start.2
  43.7 2.4 %back_half.1 = (bf16[32,2176]{1,0:T(8,128)(2,1)S(1)}, bf16[32,2176]{1,0:T(8,128)(2,1)S(1)}, bf16[32,2176]{1,0:T(8,128)(2,1)S(1)}, bf16[32,2176]{1,0:T(8,128)(2,1)S(1)}) custom-call(bf16[128,1024]{1,0:T(8,128)(2,1)S(1)} %get-tuple-element.59.dgate_ref, bf16[128,1024]{1,0:T(8,128)(2,1)S(1)} %get-tuple-element.60.dup_ref, ...), custom_call_target="tpu_custom_call" | custom-call | flops 1073741824 | bytes 8388608 | tf_op jit(solution)/shard_map/back_half/pallas_call | solution.py:332
  46.1 0.6 collective-permute-done.10.refs_3_
  46.7 2.1 %collective-permute-done.9.refs_2_ = bf16[32,2176]{1,0:T(8,128)(2,1)S(1)} collective-permute-done((bf16[32,2176]{1,0:T(8,128)(2,1)S(1)}, bf16[32,2176]{1,0:T(8,128)(2,1)S(1)}, u32[]{:S(2)}, u32[]{:S(2)}) %collective-permute-start.9) | collective-permute-done | bytes 139296 | tf_op jit(solution)/shard_map/ppermute | solution.py:450
  48.8 0.7 collective-permute-start.15
  49.5 1.4 %collective-permute-start.16 = (bf16[32,2176]{1,0:T(8,128)(2,1)S(1)}, bf16[32,2176]{1,0:T(8,128)(2,1)S(1)}, u32[]{:S(2)}, u32[]{:S(2)}) collective-permute-start(bf16[32,2176]{1,0:T(8,128)(2,1)S(1)} %get-tuple-element.67), channel_id=1, source_target_pairs={{0,2},{2,0},{4,6},{6,4},{8,10},{10,8},{12,14},{14,12},{1,3},{3,1},... | collective-permute-start | bytes 417800 | tf_op jit(solution)/shard_map/ppermute | solution.py:450
  50.9 0.1 sum_pieces.2
  50.9 0.1 collective-permute-start.11
  51.0 4.5 %collective-permute-start.12 = (bf16[16,2176]{1,0:T(8,128)(2,1)S(1)}, bf16[16,2176]{1,0:T(8,128)(2,1)S(1)}, u32[]{:S(2)}, u32[]{:S(2)}) collective-permute-start(bf16[16,2176]{1,0:T(8,128)(2,1)S(1)} %get-tuple-element.56), channel_id=1, source_target_pairs={{0,9},{1,8},{2,11},{3,10},{4,13},{5,12},{6,15},{7,14},{8,1},{9,0},... | collective-permute-start | bytes 208904 | tf_op jit(solution)/shard_map/ppermute | solution.py:464
  55.5 1.3 %collective-permute-start.13 = (bf16[16,2176]{1,0:T(8,128)(2,1)S(1)}, bf16[16,2176]{1,0:T(8,128)(2,1)S(1)}, u32[]{:S(2)}, u32[]{:S(2)}) collective-permute-start(bf16[16,2176]{1,0:T(8,128)(2,1)S(1)} %get-tuple-element.57), channel_id=1, source_target_pairs={{0,5},{1,4},{2,7},{3,6},{4,1},{5,0},{6,3},{7,2},{8,13},{9,12},{10,... | collective-permute-start | bytes 208904 | tf_op jit(solution)/shard_map/ppermute | solution.py:464
  56.8 0.0 collective-permute-done.15.refs_2_
  56.8 0.0 collective-permute-start.14
  56.8 0.0 collective-permute-done.16.refs_3_
  56.8 0.1 sum_pieces.3
  56.9 4.1 %collective-permute-start.17 = (bf16[16,2176]{1,0:T(8,128)(2,1)S(1)}, bf16[16,2176]{1,0:T(8,128)(2,1)S(1)}, u32[]{:S(2)}, u32[]{:S(2)}) collective-permute-start(bf16[16,2176]{1,0:T(8,128)(2,1)S(1)} %get-tuple-element.68), channel_id=1, source_target_pairs={{0,12},{1,13},{2,14},{3,15},{4,8},{5,9},{6,10},{7,11},{8,4},{9,5},... | collective-permute-start | bytes 208904 | tf_op jit(solution)/shard_map/ppermute | solution.py:464
  60.9 0.0 collective-permute-done.11.refs_0_
  60.9 0.0 collective-permute-start.18
  60.9 0.9 %collective-permute-done.12.refs_1_ = bf16[16,2176]{1,0:T(8,128)(2,1)S(1)} collective-permute-done((bf16[16,2176]{1,0:T(8,128)(2,1)S(1)}, bf16[16,2176]{1,0:T(8,128)(2,1)S(1)}, u32[]{:S(2)}, u32[]{:S(2)}) %collective-permute-start.12) | collective-permute-done | bytes 69664 | tf_op jit(solution)/shard_map/ppermute | solution.py:464
  61.8 1.5 %collective-permute-start.19 = (bf16[16,2176]{1,0:T(8,128)(2,1)S(1)}, bf16[16,2176]{1,0:T(8,128)(2,1)S(1)}, u32[]{:S(2)}, u32[]{:S(2)}) collective-permute-start(bf16[16,2176]{1,0:T(8,128)(2,1)S(1)} %get-tuple-element.70), channel_id=1, source_target_pairs={{0,4},{1,5},{2,6},{3,7},{4,0},{5,1},{6,2},{7,3},{8,12},{9,13},{10,... | collective-permute-start | bytes 208904 | tf_op jit(solution)/shard_map/ppermute | solution.py:464
  63.3 0.0 copy-done
  63.3 0.0 copy-done.1
  63.3 0.0 copy-done.2
  63.3 0.2 mixing.1
  63.5 0.0 collective-permute-done.13.refs_2_
  63.5 0.0 collective-permute-done.14.refs_3_
  63.5 0.3 collective-permute-done.17.refs_4_
  63.8 4.1 %collective-permute-done.18.refs_5_ = bf16[16,2176]{1,0:T(8,128)(2,1)S(1)} collective-permute-done((bf16[16,2176]{1,0:T(8,128)(2,1)S(1)}, bf16[16,2176]{1,0:T(8,128)(2,1)S(1)}, u32[]{:S(2)}, u32[]{:S(2)}) %collective-permute-start.18) | collective-permute-done | bytes 69664 | tf_op jit(solution)/shard_map/ppermute | solution.py:464
  67.9 0.0 collective-permute-done.19.refs_6_
  67.9 1.2 %combine.1 = (bf16[128,2048]{1,0:T(8,128)(2,1)}, f32[1,128]{1,0:T(1,128)}) custom-call(bf16[2,128,128]{2,1,0:T(8,128)(2,1)S(1)} %get-tuple-element.38.mix_ref, f32[128,128]{1,0:T(8,128)S(1)} %get-tuple-element.39.hit_ref, bf16[16,2176]{1,0:T(8,128)(2,1)S(1)} %collective-permute-done.11.refs_0_, bf16[16,2176]{1,0:T(8,128)(2,1)S(1)} %collective-permute-done.12.refs_1_, ...), custom_call_target="tpu_custom_call" | custom-call | flops 134217728 | bytes 1048576 | tf_op jit(solution)/shard_map/combine/pallas_call | solution.py:427
  (4 shorter events, 0.0 us)
Async XLA Ops:
  3.1 10.9 %collective-permute-start.1 = (bf16[32,4096]{1,0:T(8,128)(2,1)S(1)}, bf16[32,4096]{1,0:T(8,128)(2,1)S(1)}, u32[]{:S(2)}, u32[]{:S(2)}) collective-permute-start(bf16[32,4096]{1,0:T(8,128)(2,1)S(1)} %get-tuple-element.40.refs_0_), channel_id=1, source_target_pairs={{0,2},{2,0},{4,6},{6,4},{8,10},{10,8},{12,14},{14,12},{1,3},{3,1},... | collective-permute-start | bytes 786440 | tf_op jit(solution)/shard_map/ppermute | solution.py:450
  6.2 11.6 %collective-permute-start = (bf16[32,4096]{1,0:T(8,128)(2,1)S(1)}, bf16[32,4096]{1,0:T(8,128)(2,1)S(1)}, u32[]{:S(2)}, u32[]{:S(2)}) collective-permute-start(bf16[32,4096]{1,0:T(8,128)(2,1)S(1)} %get-tuple-element.41), channel_id=1, source_target_pairs={{0,4},{2,6},{4,0},{6,2},{8,12},{10,14},{12,8},{14,10},{1,5},{3,7},... | collective-permute-start | bytes 786440 | tf_op jit(solution)/shard_map/ppermute | solution.py:450
  7.7 14.1 %collective-permute-start.5 = (bf16[16,4096]{1,0:T(8,128)(2,1)S(1)}, bf16[16,4096]{1,0:T(8,128)(2,1)S(1)}, u32[]{:S(2)}, u32[]{:S(2)}) collective-permute-start(bf16[16,4096]{1,0:T(8,128)(2,1)S(1)} %get-tuple-element.46), channel_id=1, source_target_pairs={{0,8},{2,10},{4,12},{6,14},{8,0},{10,2},{12,4},{14,6},{1,9},{3,11}... | collective-permute-start | bytes 393224 | tf_op jit(solution)/shard_map/ppermute | solution.py:450
  10.3 12.8 %collective-permute-start.6 = (bf16[16,4096]{1,0:T(8,128)(2,1)S(1)}, bf16[16,4096]{1,0:T(8,128)(2,1)S(1)}, u32[]{:S(2)}, u32[]{:S(2)}) collective-permute-start(bf16[16,4096]{1,0:T(8,128)(2,1)S(1)} %get-tuple-element.47), channel_id=1, source_target_pairs={{0,12},{2,14},{4,8},{6,10},{8,4},{10,6},{12,0},{14,2},{1,13},{3,15... | collective-permute-start | bytes 393224 | tf_op jit(solution)/shard_map/ppermute | solution.py:450
  14.1 16.8 %collective-permute-start.3 = (bf16[16,4096]{1,0:T(8,128)(2,1)S(1)}, bf16[16,4096]{1,0:T(8,128)(2,1)S(1)}, u32[]{:S(2)}, u32[]{:S(2)}) collective-permute-start(bf16[16,4096]{1,0:T(8,128)(2,1)S(1)} %get-tuple-element.44), channel_id=1, source_target_pairs={{0,8},{2,10},{4,12},{6,14},{8,0},{10,2},{12,4},{14,6},{1,9},{3,11}... | collective-permute-start | bytes 393224 | tf_op jit(solution)/shard_map/ppermute | solution.py:450
  15.8 15.1 %collective-permute-start.4 = (bf16[16,4096]{1,0:T(8,128)(2,1)S(1)}, bf16[16,4096]{1,0:T(8,128)(2,1)S(1)}, u32[]{:S(2)}, u32[]{:S(2)}) collective-permute-start(bf16[16,4096]{1,0:T(8,128)(2,1)S(1)} %get-tuple-element.45), channel_id=1, source_target_pairs={{0,12},{2,14},{4,8},{6,10},{8,4},{10,6},{12,0},{14,2},{1,13},{3,15... | collective-permute-start | bytes 393224 | tf_op jit(solution)/shard_map/ppermute | solution.py:450
  17.8 8.3 %collective-permute-start.2 = (bf16[32,4096]{1,0:T(8,128)(2,1)S(1)}, bf16[32,4096]{1,0:T(8,128)(2,1)S(1)}, u32[]{:S(2)}, u32[]{:S(2)}) collective-permute-start(bf16[32,4096]{1,0:T(8,128)(2,1)S(1)} %collective-permute-done.refs_0_.refs_1_), channel_id=1, source_target_pairs={{0,2},{2,0},{4,6},{6,4},{8,10},{10,8},{12,14},{14,12},{1,3},{3,1},... | collective-permute-start | bytes 786440 | tf_op jit(solution)/shard_map/ppermute | solution.py:450
  23.2 8.3 %collective-permute-start.8 = (bf16[32,4096]{1,0:T(8,128)(2,1)S(1)}, bf16[32,4096]{1,0:T(8,128)(2,1)S(1)}, u32[]{:S(2)}, u32[]{:S(2)}) collective-permute-start(bf16[32,4096]{1,0:T(8,128)(2,1)S(1)} %join.2.refs_0_.refs_4_), channel_id=1, source_target_pairs={{0,2},{2,0},{4,6},{6,4},{8,10},{10,8},{12,14},{14,12},{1,3},{3,1},... | collective-permute-start | bytes 786440 | tf_op jit(solution)/shard_map/ppermute | solution.py:450
  30.9 7.1 %collective-permute-start.7 = (bf16[32,4096]{1,0:T(8,128)(2,1)S(1)}, bf16[32,4096]{1,0:T(8,128)(2,1)S(1)}, u32[]{:S(2)}, u32[]{:S(2)}) collective-permute-start(bf16[32,4096]{1,0:T(8,128)(2,1)S(1)} %join.3.refs_4_), channel_id=1, source_target_pairs={{0,2},{2,0},{4,6},{6,4},{8,10},{10,8},{12,14},{14,12},{1,3},{3,1},... | collective-permute-start | bytes 786440 | tf_op jit(solution)/shard_map/ppermute | solution.py:450
  41.6 5.1 %collective-permute-start.10 = (bf16[32,2176]{1,0:T(8,128)(2,1)S(1)}, bf16[32,2176]{1,0:T(8,128)(2,1)S(1)}, u32[]{:S(2)}, u32[]{:S(2)}) collective-permute-start(bf16[32,2176]{1,0:T(8,128)(2,1)S(1)} %get-tuple-element.54), channel_id=1, source_target_pairs={{0,2},{2,0},{4,6},{6,4},{8,10},{10,8},{12,14},{14,12},{1,3},{3,1},... | collective-permute-start | bytes 417800 | tf_op jit(solution)/shard_map/ppermute | solution.py:450
  42.2 6.7 %collective-permute-start.9 = (bf16[32,2176]{1,0:T(8,128)(2,1)S(1)}, bf16[32,2176]{1,0:T(8,128)(2,1)S(1)}, u32[]{:S(2)}, u32[]{:S(2)}) collective-permute-start(bf16[32,2176]{1,0:T(8,128)(2,1)S(1)} %get-tuple-element.53), channel_id=1, source_target_pairs={{0,2},{2,0},{4,6},{6,4},{8,10},{10,8},{12,14},{14,12},{1,3},{3,1},... | collective-permute-start | bytes 417800 | tf_op jit(solution)/shard_map/ppermute | solution.py:450
  43.7 19.6 %copy-start = (s32[128,2]{0,1:T(2,128)S(1)}, s32[128,2]{0,1:T(2,128)}, u32[]{:S(2)}) copy-start(s32[128,2]{0,1:T(2,128)} %param.11) | copy-start | bytes 3076
  43.7 19.6 %copy-start.1 = (s32[128]{0:T(128)S(1)}, s32[128]{0:T(128)}, u32[]{:S(2)}) copy-start(s32[128]{0:T(128)} %param.10) | copy-start | bytes 1540
  43.7 19.6 %copy-start.2 = (f32[128,2]{0,1:T(2,128)S(1)}, f32[128,2]{0,1:T(2,128)}, u32[]{:S(2)}) copy-start(f32[128,2]{0,1:T(2,128)} %param.12) | copy-start | bytes 3076
  48.8 7.9 %collective-permute-start.15 = (bf16[32,2176]{1,0:T(8,128)(2,1)S(1)}, bf16[32,2176]{1,0:T(8,128)(2,1)S(1)}, u32[]{:S(2)}, u32[]{:S(2)}) collective-permute-start(bf16[32,2176]{1,0:T(8,128)(2,1)S(1)} %get-tuple-element.66), channel_id=1, source_target_pairs={{0,2},{2,0},{4,6},{6,4},{8,10},{10,8},{12,14},{14,12},{1,3},{3,1},... | collective-permute-start | bytes 417800 | tf_op jit(solution)/shard_map/ppermute | solution.py:450
  49.5 7.3 %collective-permute-start.16 = (bf16[32,2176]{1,0:T(8,128)(2,1)S(1)}, bf16[32,2176]{1,0:T(8,128)(2,1)S(1)}, u32[]{:S(2)}, u32[]{:S(2)}) collective-permute-start(bf16[32,2176]{1,0:T(8,128)(2,1)S(1)} %get-tuple-element.67), channel_id=1, source_target_pairs={{0,2},{2,0},{4,6},{6,4},{8,10},{10,8},{12,14},{14,12},{1,3},{3,1},... | collective-permute-start | bytes 417800 | tf_op jit(solution)/shard_map/ppermute | solution.py:450
  50.9 10.0 %collective-permute-start.11 = (bf16[16,2176]{1,0:T(8,128)(2,1)S(1)}, bf16[16,2176]{1,0:T(8,128)(2,1)S(1)}, u32[]{:S(2)}, u32[]{:S(2)}) collective-permute-start(bf16[16,2176]{1,0:T(8,128)(2,1)S(1)} %get-tuple-element.55), channel_id=1, source_target_pairs={{0,13},{1,12},{2,15},{3,14},{4,9},{5,8},{6,11},{7,10},{8,5},{9,4},... | collective-permute-start | bytes 208904 | tf_op jit(solution)/shard_map/ppermute | solution.py:464
  51.0 10.8 %collective-permute-start.12 = (bf16[16,2176]{1,0:T(8,128)(2,1)S(1)}, bf16[16,2176]{1,0:T(8,128)(2,1)S(1)}, u32[]{:S(2)}, u32[]{:S(2)}) collective-permute-start(bf16[16,2176]{1,0:T(8,128)(2,1)S(1)} %get-tuple-element.56), channel_id=1, source_target_pairs={{0,9},{1,8},{2,11},{3,10},{4,13},{5,12},{6,15},{7,14},{8,1},{9,0},... | collective-permute-start | bytes 208904 | tf_op jit(solution)/shard_map/ppermute | solution.py:464
  55.5 8.0 %collective-permute-start.13 = (bf16[16,2176]{1,0:T(8,128)(2,1)S(1)}, bf16[16,2176]{1,0:T(8,128)(2,1)S(1)}, u32[]{:S(2)}, u32[]{:S(2)}) collective-permute-start(bf16[16,2176]{1,0:T(8,128)(2,1)S(1)} %get-tuple-element.57), channel_id=1, source_target_pairs={{0,5},{1,4},{2,7},{3,6},{4,1},{5,0},{6,3},{7,2},{8,13},{9,12},{10,... | collective-permute-start | bytes 208904 | tf_op jit(solution)/shard_map/ppermute | solution.py:464
  56.8 6.8 %collective-permute-start.14 = (bf16[16,2176]{1,0:T(8,128)(2,1)S(1)}, bf16[16,2176]{1,0:T(8,128)(2,1)S(1)}, u32[]{:S(2)}, u32[]{:S(2)}) collective-permute-start(bf16[16,2176]{1,0:T(8,128)(2,1)S(1)} %get-tuple-element.58), channel_id=1, source_target_pairs={{0,1},{1,0},{2,3},{3,2},{4,5},{5,4},{6,7},{7,6},{8,9},{9,8},{10,11... | collective-permute-start | bytes 208904 | tf_op jit(solution)/shard_map/ppermute | solution.py:464
  56.9 6.9 %collective-permute-start.17 = (bf16[16,2176]{1,0:T(8,128)(2,1)S(1)}, bf16[16,2176]{1,0:T(8,128)(2,1)S(1)}, u32[]{:S(2)}, u32[]{:S(2)}) collective-permute-start(bf16[16,2176]{1,0:T(8,128)(2,1)S(1)} %get-tuple-element.68), channel_id=1, source_target_pairs={{0,12},{1,13},{2,14},{3,15},{4,8},{5,9},{6,10},{7,11},{8,4},{9,5},... | collective-permute-start | bytes 208904 | tf_op jit(solution)/shard_map/ppermute | solution.py:464
  60.9 7.0 %collective-permute-start.18 = (bf16[16,2176]{1,0:T(8,128)(2,1)S(1)}, bf16[16,2176]{1,0:T(8,128)(2,1)S(1)}, u32[]{:S(2)}, u32[]{:S(2)}) collective-permute-start(bf16[16,2176]{1,0:T(8,128)(2,1)S(1)} %get-tuple-element.69), channel_id=1, source_target_pairs={{0,8},{1,9},{2,10},{3,11},{4,12},{5,13},{6,14},{7,15},{8,0},{9,1},... | collective-permute-start | bytes 208904 | tf_op jit(solution)/shard_map/ppermute | solution.py:464
  61.8 6.1 %collective-permute-start.19 = (bf16[16,2176]{1,0:T(8,128)(2,1)S(1)}, bf16[16,2176]{1,0:T(8,128)(2,1)S(1)}, u32[]{:S(2)}, u32[]{:S(2)}) collective-permute-start(bf16[16,2176]{1,0:T(8,128)(2,1)S(1)} %get-tuple-element.70), channel_id=1, source_target_pairs={{0,4},{1,5},{2,6},{3,7},{4,0},{5,1},{6,2},{7,3},{8,12},{9,13},{10,... | collective-permute-start | bytes 208904 | tf_op jit(solution)/shard_map/ppermute | solution.py:464

commit v16 on v12

--- a/solution.py
+++ b/solution.py
@@ -132,7 +132,7 @@
         out_shape=pltpu.VMEM(weight.shape, weight.dtype),
         scratch_shapes=[pltpu.SemaphoreType.DMA((parts,))],
         compiler_params=pltpu.CompilerParams(vmem_limit_bytes=SCOPED),
-        cost_estimate=cost(0, 1024),
+        cost_estimate=cost(3 * 10**9, 1024),
         name="load",
     )(in_hbm(weight), *after)
 
@@ -168,7 +168,7 @@
             pltpu.SemaphoreType.DMA((parts,)),
         ],
         compiler_params=pltpu.CompilerParams(vmem_limit_bytes=SCOPED),
-        cost_estimate=cost(0, 1024),
+        cost_estimate=cost(1 * 10**9, 1024),
         name="load_turned",
     )(in_hbm(weight), *after)
 
@@ -186,7 +186,7 @@
         out_shape=[jax.ShapeDtypeStruct(block.shape, block.dtype) for block in blocks],
         input_output_aliases={i: i for i in range(len(blocks))},
         compiler_params=pltpu.CompilerParams(vmem_limit_bytes=SCOPED),
-        cost_estimate=cost(0, 1024),
+        cost_estimate=cost(3 * 10**9, 1024),
         name="pass_after",
     )(*blocks, *need)
 
@@ -209,7 +209,7 @@
         out_specs=vmem,
         out_shape=jax.ShapeDtypeStruct((total, blocks[0].shape[1]), BF16),
         compiler_params=pltpu.CompilerParams(vmem_limit_bytes=SCOPED),
-        cost_estimate=cost(3 * 10**9, 1024),
+        cost_estimate=cost(2 * 10**9, 1024),
         name="join",
     )(*blocks, *need)
 

time: 67.9 us -> 70.4 us (1.037)
  starting transfers between devices: 25.4 us -> 28.3 us
    ppermute x11, starting transfers between devices: 13.9 us -> 19.6 us  [to_expert(): lax.ppermute(x, 'ep', [(e * groups + j, (e ^ s) * groups + (j + t) % grou...]
    ppermute x7, starting transfers between devices: 11.5 us -> 8.73 us  [to_source(): lax.ppermute(x, ('ep', 'mod'), [((e * groups + j) * 2 + m, ((e ^ s) * gro...]
    ppermute x11, waiting for transfers between devices: 12.8 us -> 11.2 us  [to_expert(): lax.ppermute(x, 'ep', [(e * groups + j, (e ^ s) * groups + (j + t) % grou...]
    ppermute x7, waiting for transfers between devices: 4.66 us -> 5.88 us  [to_source(): lax.ppermute(x, ('ep', 'mod'), [((e * groups + j) * 2 + m, ((e ^ s) * gro...]
  transfers between devices with their start and end apart: 18 -> 18, of which waited for: 9 -> 8; matrix products, arithmetic and copies ran while one was open for 0% -> 0% of each run, Pallas kernels for 25% -> 24%
where the time goes in v16:
time: 70.4 us; the launch traced here: 70.2 us
  starting transfers between devices  28.3 us (40%)
  Pallas kernels  24.1 us (34%)
  waiting for transfers between devices  17.1 us (24%)
  between operations  0.8 us (1%)
    ppermute x11, starting transfers between devices, to_expert(): lax.ppermute(x, 'ep', [(e * groups + j, (e ^ s) * groups + (j + t) % grou...  19.6 us
    ppermute x11, waiting for transfers between devices, to_expert(): lax.ppermute(x, 'ep', [(e * groups + j, (e ^ s) * groups + (j + t) % grou...  11.2 us
    ppermute x7, starting transfers between devices, to_source(): lax.ppermute(x, ('ep', 'mod'), [((e * groups + j) * 2 + m, ((e ^ s) * gro...  8.73 us
    pallas_call x2, Pallas kernels, load(): pl.pallas_call(functools.partial(load_kernel, parts), in_specs=[pl.BlockS...  6.94 us
    ppermute x7, waiting for transfers between devices, to_source(): lax.ppermute(x, ('ep', 'mod'), [((e * groups + j) * 2 + m, ((e ^ s) * gro...  5.88 us
    pallas_call x1, Pallas kernels, load_turned(): pl.pallas_call(functools.partial(load_turned_kernel, parts), in_specs=[pl...  4.29 us
    pallas_call x1, Pallas kernels, hidden_grads(): pl.pallas_call(functools.partial(hidden_kernel, count, places, groups), i...  3.62 us
    pallas_call x1, Pallas kernels, pre_activations(): pl.pallas_call(functools.partial(pre_kernel, count, places), in_specs=[vm...  2.6 us
  transfers between devices with their start and end apart: 18, of which 8 were waited for; matrix products, arithmetic and copies ran while one was open for 0% of the time, Pallas kernels for 24%

profile of v16, /device:TPU:0, one launch (start us, length us, event | category | flops | bytes accessed | tf_op | source)
XLA Modules:
  0.0 70.2 jit_solution(10058030600233477677)
XLA Ops:
  0.6 2.5 %gather_slots.1 = (bf16[32,4096]{1,0:T(8,128)(2,1)S(1)}, bf16[32,4096]{1,0:T(8,128)(2,1)S(1)}, bf16[16,4096]{1,0:T(8,128)(2,1)S(1)}, bf16[16,4096]{1,0:T(8,128)(...) custom-call(s32[1,128]{1,0:T(1,128)} %bitcast.6, s32[2,128]{1,0:T(2,128)} %bitcast.4, ...), custom_call_target="tpu_custom_call" | custom-call | flops 134217728 | bytes 3145728 | tf_op jit(solution)/shard_map/gather_slots/pallas_call | solution.py:93
  3.1 3.1 %collective-permute-start = (bf16[32,4096]{1,0:T(8,128)(2,1)S(1)}, bf16[32,4096]{1,0:T(8,128)(2,1)S(1)}, u32[]{:S(2)}, u32[]{:S(2)}) collective-permute-start(bf16[32,4096]{1,0:T(8,128)(2,1)S(1)} %get-tuple-element.35), channel_id=1, source_target_pairs={{0,4},{2,6},{4,0},{6,2},{8,12},{10,14},{12,8},{14,10},{1,5},{3,7},... | collective-permute-start | bytes 786440 | tf_op jit(solution)/shard_map/ppermute | solution.py:446
  6.2 2.6 %collective-permute-start.5 = (bf16[16,4096]{1,0:T(8,128)(2,1)S(1)}, bf16[16,4096]{1,0:T(8,128)(2,1)S(1)}, u32[]{:S(2)}, u32[]{:S(2)}) collective-permute-start(bf16[16,4096]{1,0:T(8,128)(2,1)S(1)} %get-tuple-element.40), channel_id=1, source_target_pairs={{0,8},{2,10},{4,12},{6,14},{8,0},{10,2},{12,4},{14,6},{1,9},{3,11}... | collective-permute-start | bytes 393224 | tf_op jit(solution)/shard_map/ppermute | solution.py:446
  8.8 0.0 collective-permute-start.6
  8.8 1.7 %collective-permute-start.1 = (bf16[32,4096]{1,0:T(8,128)(2,1)S(1)}, bf16[32,4096]{1,0:T(8,128)(2,1)S(1)}, u32[]{:S(2)}, u32[]{:S(2)}) collective-permute-start(bf16[32,4096]{1,0:T(8,128)(2,1)S(1)} %get-tuple-element.34.refs_0_), channel_id=1, source_target_pairs={{0,2},{2,0},{4,6},{6,4},{8,10},{10,8},{12,14},{14,12},{1,3},{3,1},... | collective-permute-start | bytes 786440 | tf_op jit(solution)/shard_map/ppermute | solution.py:446
  10.6 3.5 %load.2.refs_2_.refs_1_.refs_3_.refs_6_.refs_10_.gate_ref = bf16[1,4096,1024]{2,1,0:T(8,128)(2,1)S(1)} custom-call(bf16[1,4096,1024]{2,1,0:T(8,128)(2,1)} %src.3, bf16[32,4096]{1,0:T(8,128)(2,1)S(1)} %get-tuple-element.34.refs_0_), custom_call_target="tpu_custom_call" | custom-call | flops 3000000000 | bytes 1024 | tf_op jit(solution)/shard_map/load/pallas_call | solution.py:128
  14.0 2.3 %collective-permute-done.1.refs_3_.refs_1_.refs_2_ = bf16[32,4096]{1,0:T(8,128)(2,1)S(1)} collective-permute-done((bf16[32,4096]{1,0:T(8,128)(2,1)S(1)}, bf16[32,4096]{1,0:T(8,128)(2,1)S(1)}, u32[]{:S(2)}, u32[]{:S(2)}) %collective-permute-start.1) | collective-permute-done | bytes 262176 | tf_op jit(solution)/shard_map/ppermute | solution.py:446
  16.3 1.6 %collective-permute-start.3 = (bf16[16,4096]{1,0:T(8,128)(2,1)S(1)}, bf16[16,4096]{1,0:T(8,128)(2,1)S(1)}, u32[]{:S(2)}, u32[]{:S(2)}) collective-permute-start(bf16[16,4096]{1,0:T(8,128)(2,1)S(1)} %get-tuple-element.38), channel_id=1, source_target_pairs={{0,8},{2,10},{4,12},{6,14},{8,0},{10,2},{12,4},{14,6},{1,9},{3,11}... | collective-permute-start | bytes 393224 | tf_op jit(solution)/shard_map/ppermute | solution.py:446
  17.9 1.9 %collective-permute-start.4 = (bf16[16,4096]{1,0:T(8,128)(2,1)S(1)}, bf16[16,4096]{1,0:T(8,128)(2,1)S(1)}, u32[]{:S(2)}, u32[]{:S(2)}) collective-permute-start(bf16[16,4096]{1,0:T(8,128)(2,1)S(1)} %get-tuple-element.39), channel_id=1, source_target_pairs={{0,12},{2,14},{4,8},{6,10},{8,4},{10,6},{12,0},{14,2},{1,13},{3,15... | collective-permute-start | bytes 393224 | tf_op jit(solution)/shard_map/ppermute | solution.py:446
  19.9 0.0 collective-permute-done.refs_0_.refs_1_
  19.9 1.5 %collective-permute-start.2 = (bf16[32,4096]{1,0:T(8,128)(2,1)S(1)}, bf16[32,4096]{1,0:T(8,128)(2,1)S(1)}, u32[]{:S(2)}, u32[]{:S(2)}) collective-permute-start(bf16[32,4096]{1,0:T(8,128)(2,1)S(1)} %collective-permute-done.refs_0_.refs_1_), channel_id=1, source_target_pairs={{0,2},{2,0},{4,6},{6,4},{8,10},{10,8},{12,14},{14,12},{1,3},{3,1},... | collective-permute-start | bytes 786440 | tf_op jit(solution)/shard_map/ppermute | solution.py:446
  21.4 3.5 %load.3.refs_3_.refs_4_.refs_7_.refs_11_.up_ref = bf16[1,4096,1024]{2,1,0:T(8,128)(2,1)S(1)} custom-call(bf16[1,4096,1024]{2,1,0:T(8,128)(2,1)} %src.4, bf16[32,4096]{1,0:T(8,128)(2,1)S(1)} %collective-permute-done.refs_0_.refs_1_, bf16[1,4096,1024]{2,1,0:T(8,128)(2,1)S(1)} %load.2.refs_2_.refs_1_.refs_3_.refs_6_.refs_10_.gate_ref), custom_call_target="tpu_custom_call" | custom-call | flops 3000000000 | bytes 1024 | tf_op jit(solution)/shard_map/load/pallas_call | solution.py:128
  24.9 0.0 collective-permute-done.5.refs_0_
  24.9 0.0 collective-permute-done.6.refs_1_
  24.9 0.6 collective-permute-start.8
  25.5 2.0 %collective-permute-done.2.refs_2_.refs_3_ = bf16[32,4096]{1,0:T(8,128)(2,1)S(1)} collective-permute-done((bf16[32,4096]{1,0:T(8,128)(2,1)S(1)}, bf16[32,4096]{1,0:T(8,128)(2,1)S(1)}, u32[]{:S(2)}, u32[]{:S(2)}) %collective-permute-start.2) | collective-permute-done | bytes 262176 | tf_op jit(solution)/shard_map/ppermute | solution.py:446
  27.5 4.3 %load_turned.1.refs_4_.refs_8_.refs_9_ = bf16[4096,1024]{1,0:T(8,128)(2,1)S(1)} custom-call(bf16[1,1024,4096]{2,1,0:T(8,128)(2,1)} %src.5, bf16[32,4096]{1,0:T(8,128)(2,1)S(1)} %join.2.refs_0_.refs_4_, bf16[32,4096]{1,0:T(8,128)(2,1)S(1)} %collective-permute-done.1.refs_3_.refs_1_.refs_2_, bf16[32,4096]{1,0:T(8,128)(2,1)S(1)} %collective-permute-done.2.refs_2_.refs_3_, ...), custom_call_target="tpu_custom_call" | custom-call | flops 1000000000 | bytes 1024 | tf_op jit(solution)/shard_map/load_turned/pallas_call | solution.py:161
  31.8 0.0 collective-permute-done.3.refs_0_
  31.8 0.0 collective-permute-done.4.refs_1_
  31.8 2.5 %collective-permute-start.7 = (bf16[32,4096]{1,0:T(8,128)(2,1)S(1)}, bf16[32,4096]{1,0:T(8,128)(2,1)S(1)}, u32[]{:S(2)}, u32[]{:S(2)}) collective-permute-start(bf16[32,4096]{1,0:T(8,128)(2,1)S(1)} %join.3.refs_4_), channel_id=1, source_target_pairs={{0,2},{2,0},{4,6},{6,4},{8,10},{10,8},{12,14},{14,12},{1,3},{3,1},... | collective-permute-start | bytes 786440 | tf_op jit(solution)/shard_map/ppermute | solution.py:446
  34.4 0.0 collective-permute-done.8.refs_5_
  34.4 2.6 %pre_activations.1 = (f32[128,1024]{1,0:T(8,128)S(1)}, f32[128,1024]{1,0:T(8,128)S(1)}, f32[128,1024]{1,0:T(8,128)S(1)}) custom-call(bf16[32,4096]{1,0:T(8,128)(2,1)S(1)} %get-tuple-element.34.refs_0_, bf16[32,4096]{1,0:T(8,128)(2,1)S(1)} %collective-permute-done.refs_0_.refs_1_, bf16[32,4096]{1,0:T(8,128)(2,1)S(1)} %collective-permute-done.1.refs_3_.refs_1_.refs_2_, ...), custom_call_target="tpu_custom_call" | custom-call | flops 5000000000 | bytes 1024 | tf_op jit(solution)/shard_map/pre_activations/pallas_call | solution.py:251
  37.0 1.7 %collective-permute-done.7.refs_5_ = bf16[32,4096]{1,0:T(8,128)(2,1)S(1)} collective-permute-done((bf16[32,4096]{1,0:T(8,128)(2,1)S(1)}, bf16[32,4096]{1,0:T(8,128)(2,1)S(1)}, u32[]{:S(2)}, u32[]{:S(2)}) %collective-permute-start.7) | collective-permute-done | bytes 262176 | tf_op jit(solution)/shard_map/ppermute | solution.py:446
  38.7 3.6 %hidden_grads.1 = (bf16[64,2176]{1,0:T(8,128)(2,1)S(1)}, bf16[64,2176]{1,0:T(8,128)(2,1)S(1)}, bf16[128,1024]{1,0:T(8,128)(2,1)S(1)}, bf16[128,1024]{1,0:T(8,128)(2,1)S(1)}, bf16[128,128]{1,0:T(8,128)(2,1)S(1)}) custom-call(bf16[32,4096]{1,0:T(8,128)(2,1)S(1)} %get-tuple-element.34.refs_0_, bf16[32,4096]{1,0:T(8,128)(2,1)S(1)} %collective-permute-done.refs_0_.refs_1_, ...), custom_call_target="tpu_custom_call" | custom-call | flops 2147483648 | bytes 16777216 | tf_op jit(solution)/shard_map/hidden_grads/pallas_call | solution.py:305
  42.4 2.1 %collective-permute-start.9 = (bf16[64,2176]{1,0:T(8,128)(2,1)S(1)}, bf16[64,2176]{1,0:T(8,128)(2,1)S(1)}, u32[]{:S(2)}, u32[]{:S(2)}) collective-permute-start(bf16[64,2176]{1,0:T(8,128)(2,1)S(1)} %get-tuple-element.46), channel_id=1, source_target_pairs={{0,2},{2,0},{4,6},{6,4},{8,10},{10,8},{12,14},{14,12},{1,3},{3,1},... | collective-permute-start | bytes 835592 | tf_op jit(solution)/shard_map/ppermute | solution.py:446
  44.4 2.4 %back_half.1 = (bf16[64,2176]{1,0:T(8,128)(2,1)S(1)}, bf16[64,2176]{1,0:T(8,128)(2,1)S(1)}) custom-call(bf16[128,1024]{1,0:T(8,128)(2,1)S(1)} %get-tuple-element.51.dgate_ref, bf16[128,1024]{1,0:T(8,128)(2,1)S(1)} %get-tuple-element.52.dup_ref, bf16[128,128]{1,0:T(8,128)(2,1)S(1)} %get-tuple-element.53.part_ref, ...), custom_call_target="tpu_custom_call" | custom-call | flops 1073741824 | bytes 8388608 | tf_op jit(solution)/shard_map/back_half/pallas_call | solution.py:329
  46.9 0.0 copy-start
  46.9 0.0 copy-start.1
  46.9 0.0 copy-start.2
  46.9 4.9 %collective-permute-done.9.refs_1_ = bf16[64,2176]{1,0:T(8,128)(2,1)S(1)} collective-permute-done((bf16[64,2176]{1,0:T(8,128)(2,1)S(1)}, bf16[64,2176]{1,0:T(8,128)(2,1)S(1)}, u32[]{:S(2)}, u32[]{:S(2)}) %collective-permute-start.9) | collective-permute-done | bytes 278560 | tf_op jit(solution)/shard_map/ppermute | solution.py:446
  51.8 1.9 %collective-permute-start.14 = (bf16[64,2176]{1,0:T(8,128)(2,1)S(1)}, bf16[64,2176]{1,0:T(8,128)(2,1)S(1)}, u32[]{:S(2)}, u32[]{:S(2)}) collective-permute-start(bf16[64,2176]{1,0:T(8,128)(2,1)S(1)} %pass_after.3), channel_id=1, source_target_pairs={{0,2},{2,0},{4,6},{6,4},{8,10},{10,8},{12,14},{14,12},{1,3},{3,1},... | collective-permute-start | bytes 835592 | tf_op jit(solution)/shard_map/ppermute | solution.py:446
  53.6 0.1 sum_pieces.2
  53.7 0.1 collective-permute-start.10
  53.8 0.3 collective-permute-start.11
  54.1 2.0 %collective-permute-start.12 = (bf16[16,2176]{1,0:T(8,128)(2,1)S(1)}, bf16[16,2176]{1,0:T(8,128)(2,1)S(1)}, u32[]{:S(2)}, u32[]{:S(2)}) collective-permute-start(bf16[16,2176]{1,0:T(8,128)(2,1)S(1)} %get-tuple-element.49), channel_id=1, source_target_pairs={{0,5},{1,4},{2,7},{3,6},{4,1},{5,0},{6,3},{7,2},{8,13},{9,12},{10,... | collective-permute-start | bytes 208904 | tf_op jit(solution)/shard_map/ppermute | solution.py:460
  56.1 2.0 %collective-permute-start.13 = (bf16[16,2176]{1,0:T(8,128)(2,1)S(1)}, bf16[16,2176]{1,0:T(8,128)(2,1)S(1)}, u32[]{:S(2)}, u32[]{:S(2)}) collective-permute-start(bf16[16,2176]{1,0:T(8,128)(2,1)S(1)} %get-tuple-element.50), channel_id=1, source_target_pairs={{0,1},{1,0},{2,3},{3,2},{4,5},{5,4},{6,7},{7,6},{8,9},{9,8},{10,11... | collective-permute-start | bytes 208904 | tf_op jit(solution)/shard_map/ppermute | solution.py:460
  58.0 0.3 collective-permute-done.14.refs_1_
  58.3 0.1 sum_pieces.3
  58.4 2.3 %collective-permute-start.15 = (bf16[16,2176]{1,0:T(8,128)(2,1)S(1)}, bf16[16,2176]{1,0:T(8,128)(2,1)S(1)}, u32[]{:S(2)}, u32[]{:S(2)}) collective-permute-start(bf16[16,2176]{1,0:T(8,128)(2,1)S(1)} %get-tuple-element.56), channel_id=1, source_target_pairs={{0,12},{1,13},{2,14},{3,15},{4,8},{5,9},{6,10},{7,11},{8,4},{9,5},... | collective-permute-start | bytes 208904 | tf_op jit(solution)/shard_map/ppermute | solution.py:460
  60.7 0.0 collective-permute-done.10.refs_0_
  60.7 1.8 %collective-permute-start.16 = (bf16[16,2176]{1,0:T(8,128)(2,1)S(1)}, bf16[16,2176]{1,0:T(8,128)(2,1)S(1)}, u32[]{:S(2)}, u32[]{:S(2)}) collective-permute-start(bf16[16,2176]{1,0:T(8,128)(2,1)S(1)} %get-tuple-element.57), channel_id=1, source_target_pairs={{0,8},{1,9},{2,10},{3,11},{4,12},{5,13},{6,14},{7,15},{8,0},{9,1},... | collective-permute-start | bytes 208904 | tf_op jit(solution)/shard_map/ppermute | solution.py:460
  62.5 0.0 collective-permute-done.11.refs_1_
  62.5 0.4 collective-permute-start.17
  62.9 0.0 copy-done
  62.9 0.0 copy-done.1
  62.9 0.0 copy-done.2
  62.9 0.2 mixing.1
  63.1 0.0 collective-permute-done.12.refs_2_
  63.1 0.0 collective-permute-done.13.refs_3_
  63.1 1.5 %collective-permute-done.15.refs_4_ = bf16[16,2176]{1,0:T(8,128)(2,1)S(1)} collective-permute-done((bf16[16,2176]{1,0:T(8,128)(2,1)S(1)}, bf16[16,2176]{1,0:T(8,128)(2,1)S(1)}, u32[]{:S(2)}, u32[]{:S(2)}) %collective-permute-start.15) | collective-permute-done | bytes 69664 | tf_op jit(solution)/shard_map/ppermute | solution.py:460
  64.6 3.8 %collective-permute-done.16.refs_5_ = bf16[16,2176]{1,0:T(8,128)(2,1)S(1)} collective-permute-done((bf16[16,2176]{1,0:T(8,128)(2,1)S(1)}, bf16[16,2176]{1,0:T(8,128)(2,1)S(1)}, u32[]{:S(2)}, u32[]{:S(2)}) %collective-permute-start.16) | collective-permute-done | bytes 69664 | tf_op jit(solution)/shard_map/ppermute | solution.py:460
  68.5 0.5 collective-permute-done.17.refs_6_
  69.0 1.2 %combine.1 = (bf16[128,2048]{1,0:T(8,128)(2,1)}, f32[1,128]{1,0:T(1,128)}) custom-call(bf16[2,128,128]{2,1,0:T(8,128)(2,1)S(1)} %get-tuple-element.32.mix_ref, f32[128,128]{1,0:T(8,128)S(1)} %get-tuple-element.33.hit_ref, bf16[16,2176]{1,0:T(8,128)(2,1)S(1)} %collective-permute-done.10.refs_0_, bf16[16,2176]{1,0:T(8,128)(2,1)S(1)} %collective-permute-done.11.refs_1_, ...), custom_call_target="tpu_custom_call" | custom-call | flops 134217728 | bytes 1048576 | tf_op jit(solution)/shard_map/combine/pallas_call | solution.py:423
  (4 shorter events, 0.0 us)
Async XLA Ops:
  3.1 16.7 %collective-permute-start = (bf16[32,4096]{1,0:T(8,128)(2,1)S(1)}, bf16[32,4096]{1,0:T(8,128)(2,1)S(1)}, u32[]{:S(2)}, u32[]{:S(2)}) collective-permute-start(bf16[32,4096]{1,0:T(8,128)(2,1)S(1)} %get-tuple-element.35), channel_id=1, source_target_pairs={{0,4},{2,6},{4,0},{6,2},{8,12},{10,14},{12,8},{14,10},{1,5},{3,7},... | collective-permute-start | bytes 786440 | tf_op jit(solution)/shard_map/ppermute | solution.py:446
  6.2 18.6 %collective-permute-start.5 = (bf16[16,4096]{1,0:T(8,128)(2,1)S(1)}, bf16[16,4096]{1,0:T(8,128)(2,1)S(1)}, u32[]{:S(2)}, u32[]{:S(2)}) collective-permute-start(bf16[16,4096]{1,0:T(8,128)(2,1)S(1)} %get-tuple-element.40), channel_id=1, source_target_pairs={{0,8},{2,10},{4,12},{6,14},{8,0},{10,2},{12,4},{14,6},{1,9},{3,11}... | collective-permute-start | bytes 393224 | tf_op jit(solution)/shard_map/ppermute | solution.py:446
  8.8 16.1 %collective-permute-start.6 = (bf16[16,4096]{1,0:T(8,128)(2,1)S(1)}, bf16[16,4096]{1,0:T(8,128)(2,1)S(1)}, u32[]{:S(2)}, u32[]{:S(2)}) collective-permute-start(bf16[16,4096]{1,0:T(8,128)(2,1)S(1)} %get-tuple-element.41), channel_id=1, source_target_pairs={{0,12},{2,14},{4,8},{6,10},{8,4},{10,6},{12,0},{14,2},{1,13},{3,15... | collective-permute-start | bytes 393224 | tf_op jit(solution)/shard_map/ppermute | solution.py:446
  8.8 7.5 %collective-permute-start.1 = (bf16[32,4096]{1,0:T(8,128)(2,1)S(1)}, bf16[32,4096]{1,0:T(8,128)(2,1)S(1)}, u32[]{:S(2)}, u32[]{:S(2)}) collective-permute-start(bf16[32,4096]{1,0:T(8,128)(2,1)S(1)} %get-tuple-element.34.refs_0_), channel_id=1, source_target_pairs={{0,2},{2,0},{4,6},{6,4},{8,10},{10,8},{12,14},{14,12},{1,3},{3,1},... | collective-permute-start | bytes 786440 | tf_op jit(solution)/shard_map/ppermute | solution.py:446
  16.3 15.5 %collective-permute-start.3 = (bf16[16,4096]{1,0:T(8,128)(2,1)S(1)}, bf16[16,4096]{1,0:T(8,128)(2,1)S(1)}, u32[]{:S(2)}, u32[]{:S(2)}) collective-permute-start(bf16[16,4096]{1,0:T(8,128)(2,1)S(1)} %get-tuple-element.38), channel_id=1, source_target_pairs={{0,8},{2,10},{4,12},{6,14},{8,0},{10,2},{12,4},{14,6},{1,9},{3,11}... | collective-permute-start | bytes 393224 | tf_op jit(solution)/shard_map/ppermute | solution.py:446
  17.9 13.9 %collective-permute-start.4 = (bf16[16,4096]{1,0:T(8,128)(2,1)S(1)}, bf16[16,4096]{1,0:T(8,128)(2,1)S(1)}, u32[]{:S(2)}, u32[]{:S(2)}) collective-permute-start(bf16[16,4096]{1,0:T(8,128)(2,1)S(1)} %get-tuple-element.39), channel_id=1, source_target_pairs={{0,12},{2,14},{4,8},{6,10},{8,4},{10,6},{12,0},{14,2},{1,13},{3,15... | collective-permute-start | bytes 393224 | tf_op jit(solution)/shard_map/ppermute | solution.py:446
  19.9 7.6 %collective-permute-start.2 = (bf16[32,4096]{1,0:T(8,128)(2,1)S(1)}, bf16[32,4096]{1,0:T(8,128)(2,1)S(1)}, u32[]{:S(2)}, u32[]{:S(2)}) collective-permute-start(bf16[32,4096]{1,0:T(8,128)(2,1)S(1)} %collective-permute-done.refs_0_.refs_1_), channel_id=1, source_target_pairs={{0,2},{2,0},{4,6},{6,4},{8,10},{10,8},{12,14},{14,12},{1,3},{3,1},... | collective-permute-start | bytes 786440 | tf_op jit(solution)/shard_map/ppermute | solution.py:446
  24.9 9.5 %collective-permute-start.8 = (bf16[32,4096]{1,0:T(8,128)(2,1)S(1)}, bf16[32,4096]{1,0:T(8,128)(2,1)S(1)}, u32[]{:S(2)}, u32[]{:S(2)}) collective-permute-start(bf16[32,4096]{1,0:T(8,128)(2,1)S(1)} %join.2.refs_0_.refs_4_), channel_id=1, source_target_pairs={{0,2},{2,0},{4,6},{6,4},{8,10},{10,8},{12,14},{14,12},{1,3},{3,1},... | collective-permute-start | bytes 786440 | tf_op jit(solution)/shard_map/ppermute | solution.py:446
  31.8 6.9 %collective-permute-start.7 = (bf16[32,4096]{1,0:T(8,128)(2,1)S(1)}, bf16[32,4096]{1,0:T(8,128)(2,1)S(1)}, u32[]{:S(2)}, u32[]{:S(2)}) collective-permute-start(bf16[32,4096]{1,0:T(8,128)(2,1)S(1)} %join.3.refs_4_), channel_id=1, source_target_pairs={{0,2},{2,0},{4,6},{6,4},{8,10},{10,8},{12,14},{14,12},{1,3},{3,1},... | collective-permute-start | bytes 786440 | tf_op jit(solution)/shard_map/ppermute | solution.py:446
  42.4 9.4 %collective-permute-start.9 = (bf16[64,2176]{1,0:T(8,128)(2,1)S(1)}, bf16[64,2176]{1,0:T(8,128)(2,1)S(1)}, u32[]{:S(2)}, u32[]{:S(2)}) collective-permute-start(bf16[64,2176]{1,0:T(8,128)(2,1)S(1)} %get-tuple-element.46), channel_id=1, source_target_pairs={{0,2},{2,0},{4,6},{6,4},{8,10},{10,8},{12,14},{14,12},{1,3},{3,1},... | collective-permute-start | bytes 835592 | tf_op jit(solution)/shard_map/ppermute | solution.py:446
  46.9 16.0 %copy-start = (s32[128,2]{0,1:T(2,128)S(1)}, s32[128,2]{0,1:T(2,128)}, u32[]{:S(2)}) copy-start(s32[128,2]{0,1:T(2,128)} %param.11) | copy-start | bytes 3076
  46.9 16.0 %copy-start.1 = (s32[128]{0:T(128)S(1)}, s32[128]{0:T(128)}, u32[]{:S(2)}) copy-start(s32[128]{0:T(128)} %param.10) | copy-start | bytes 1540
  46.9 16.0 %copy-start.2 = (f32[128,2]{0,1:T(2,128)S(1)}, f32[128,2]{0,1:T(2,128)}, u32[]{:S(2)}) copy-start(f32[128,2]{0,1:T(2,128)} %param.12) | copy-start | bytes 3076
  51.8 6.5 %collective-permute-start.14 = (bf16[64,2176]{1,0:T(8,128)(2,1)S(1)}, bf16[64,2176]{1,0:T(8,128)(2,1)S(1)}, u32[]{:S(2)}, u32[]{:S(2)}) collective-permute-start(bf16[64,2176]{1,0:T(8,128)(2,1)S(1)} %pass_after.3), channel_id=1, source_target_pairs={{0,2},{2,0},{4,6},{6,4},{8,10},{10,8},{12,14},{14,12},{1,3},{3,1},... | collective-permute-start | bytes 835592 | tf_op jit(solution)/shard_map/ppermute | solution.py:446
  53.7 7.0 %collective-permute-start.10 = (bf16[16,2176]{1,0:T(8,128)(2,1)S(1)}, bf16[16,2176]{1,0:T(8,128)(2,1)S(1)}, u32[]{:S(2)}, u32[]{:S(2)}) collective-permute-start(bf16[16,2176]{1,0:T(8,128)(2,1)S(1)} %get-tuple-element.47), channel_id=1, source_target_pairs={{0,13},{1,12},{2,15},{3,14},{4,9},{5,8},{6,11},{7,10},{8,5},{9,4},... | collective-permute-start | bytes 208904 | tf_op jit(solution)/shard_map/ppermute | solution.py:460
  53.8 8.7 %collective-permute-start.11 = (bf16[16,2176]{1,0:T(8,128)(2,1)S(1)}, bf16[16,2176]{1,0:T(8,128)(2,1)S(1)}, u32[]{:S(2)}, u32[]{:S(2)}) collective-permute-start(bf16[16,2176]{1,0:T(8,128)(2,1)S(1)} %get-tuple-element.48), channel_id=1, source_target_pairs={{0,9},{1,8},{2,11},{3,10},{4,13},{5,12},{6,15},{7,14},{8,1},{9,0},... | collective-permute-start | bytes 208904 | tf_op jit(solution)/shard_map/ppermute | solution.py:460
  54.1 9.0 %collective-permute-start.12 = (bf16[16,2176]{1,0:T(8,128)(2,1)S(1)}, bf16[16,2176]{1,0:T(8,128)(2,1)S(1)}, u32[]{:S(2)}, u32[]{:S(2)}) collective-permute-start(bf16[16,2176]{1,0:T(8,128)(2,1)S(1)} %get-tuple-element.49), channel_id=1, source_target_pairs={{0,5},{1,4},{2,7},{3,6},{4,1},{5,0},{6,3},{7,2},{8,13},{9,12},{10,... | collective-permute-start | bytes 208904 | tf_op jit(solution)/shard_map/ppermute | solution.py:460
  56.1 7.1 %collective-permute-start.13 = (bf16[16,2176]{1,0:T(8,128)(2,1)S(1)}, bf16[16,2176]{1,0:T(8,128)(2,1)S(1)}, u32[]{:S(2)}, u32[]{:S(2)}) collective-permute-start(bf16[16,2176]{1,0:T(8,128)(2,1)S(1)} %get-tuple-element.50), channel_id=1, source_target_pairs={{0,1},{1,0},{2,3},{3,2},{4,5},{5,4},{6,7},{7,6},{8,9},{9,8},{10,11... | collective-permute-start | bytes 208904 | tf_op jit(solution)/shard_map/ppermute | solution.py:460
  58.4 6.2 %collective-permute-start.15 = (bf16[16,2176]{1,0:T(8,128)(2,1)S(1)}, bf16[16,2176]{1,0:T(8,128)(2,1)S(1)}, u32[]{:S(2)}, u32[]{:S(2)}) collective-permute-start(bf16[16,2176]{1,0:T(8,128)(2,1)S(1)} %get-tuple-element.56), channel_id=1, source_target_pairs={{0,12},{1,13},{2,14},{3,15},{4,8},{5,9},{6,10},{7,11},{8,4},{9,5},... | collective-permute-start | bytes 208904 | tf_op jit(solution)/shard_map/ppermute | solution.py:460
  60.7 7.7 %collective-permute-start.16 = (bf16[16,2176]{1,0:T(8,128)(2,1)S(1)}, bf16[16,2176]{1,0:T(8,128)(2,1)S(1)}, u32[]{:S(2)}, u32[]{:S(2)}) collective-permute-start(bf16[16,2176]{1,0:T(8,128)(2,1)S(1)} %get-tuple-element.57), channel_id=1, source_target_pairs={{0,8},{1,9},{2,10},{3,11},{4,12},{5,13},{6,14},{7,15},{8,0},{9,1},... | collective-permute-start | bytes 208904 | tf_op jit(solution)/shard_map/ppermute | solution.py:460
  62.5 6.5 %collective-permute-start.17 = (bf16[16,2176]{1,0:T(8,128)(2,1)S(1)}, bf16[16,2176]{1,0:T(8,128)(2,1)S(1)}, u32[]{:S(2)}, u32[]{:S(2)}) collective-permute-start(bf16[16,2176]{1,0:T(8,128)(2,1)S(1)} %get-tuple-element.58), channel_id=1, source_target_pairs={{0,4},{1,5},{2,6},{3,7},{4,0},{5,1},{6,2},{7,3},{8,12},{9,13},{10,... | collective-permute-start | bytes 208904 | tf_op jit(solution)/shard_map/ppermute | solution.py:460

commit v17 on v12

--- a/solution.py
+++ b/solution.py
@@ -265,7 +265,7 @@
     wide = outs[0].shape[1] - EXT
     own_rows = outs[0].shape[0]
     dgate, dup = dgate_ref[...].T, dup_ref[...].T
-    chunk = 512
+    chunk = 1024
     for step in range(wide // chunk):
         rows = pl.ds(pl.multiple_of(half * wide + step * chunk, chunk), chunk)
         grad = jnp.dot(gate_ref[0, rows, :], dgate, preferred_element_type=F32)

time: 67.9 us -> 67.8 us (level)
  no operation moved by 1% of the time
where the time goes in v17:
time: 67.8 us; the launch traced here: 67.7 us
  starting transfers between devices  25.4 us (37%)
  Pallas kernels  24 us (35%)
  waiting for transfers between devices  17.5 us (26%)
  between operations  0.76 us (1%)
    ppermute x11, starting transfers between devices, to_expert(): lax.ppermute(x, 'ep', [(e * groups + j, (e ^ s) * groups + (j + t) % grou...  13.9 us
    ppermute x11, waiting for transfers between devices, to_expert(): lax.ppermute(x, 'ep', [(e * groups + j, (e ^ s) * groups + (j + t) % grou...  12.8 us
    ppermute x7, starting transfers between devices, to_source(): lax.ppermute(x, ('ep', 'mod'), [((e * groups + j) * 2 + m, ((e ^ s) * gro...  11.5 us
    pallas_call x2, Pallas kernels, load(): pl.pallas_call(functools.partial(load_kernel, parts), in_specs=[pl.BlockS...  6.94 us
    ppermute x7, waiting for transfers between devices, to_source(): lax.ppermute(x, ('ep', 'mod'), [((e * groups + j) * 2 + m, ((e ^ s) * gro...  4.66 us
    pallas_call x1, Pallas kernels, load_turned(): pl.pallas_call(functools.partial(load_turned_kernel, parts), in_specs=[pl...  4.29 us
    pallas_call x1, Pallas kernels, hidden_grads(): pl.pallas_call(functools.partial(hidden_kernel, count, places, groups), i...  3.56 us
    pallas_call x1, Pallas kernels, pre_activations(): pl.pallas_call(functools.partial(pre_kernel, count, places), in_specs=[vm...  2.61 us
  transfers between devices with their start and end apart: 18, of which 9 were waited for; matrix products, arithmetic and copies ran while one was open for 0% of the time, Pallas kernels for 25%

profile of v17, /device:TPU:0, one launch (start us, length us, event | category | flops | bytes accessed | tf_op | source)
XLA Modules:
  0.0 67.7 jit_solution(1720645149478248717)
XLA Ops:
  0.6 2.5 %gather_slots.1 = (bf16[32,4096]{1,0:T(8,128)(2,1)S(1)}, bf16[32,4096]{1,0:T(8,128)(2,1)S(1)}, bf16[16,4096]{1,0:T(8,128)(2,1)S(1)}, bf16[16,4096]{1,0:T(8,128)(...) custom-call(s32[1,128]{1,0:T(1,128)} %bitcast.6, s32[2,128]{1,0:T(2,128)} %bitcast.4, ...), custom_call_target="tpu_custom_call" | custom-call | flops 134217728 | bytes 3145728 | tf_op jit(solution)/shard_map/gather_slots/pallas_call | solution.py:93
  3.1 3.0 %collective-permute-start.1 = (bf16[32,4096]{1,0:T(8,128)(2,1)S(1)}, bf16[32,4096]{1,0:T(8,128)(2,1)S(1)}, u32[]{:S(2)}, u32[]{:S(2)}) collective-permute-start(bf16[32,4096]{1,0:T(8,128)(2,1)S(1)} %get-tuple-element.34.refs_0_), channel_id=1, source_target_pairs={{0,2},{2,0},{4,6},{6,4},{8,10},{10,8},{12,14},{14,12},{1,3},{3,1},... | collective-permute-start | bytes 786440 | tf_op jit(solution)/shard_map/ppermute | solution.py:446
  6.2 1.6 %collective-permute-start = (bf16[32,4096]{1,0:T(8,128)(2,1)S(1)}, bf16[32,4096]{1,0:T(8,128)(2,1)S(1)}, u32[]{:S(2)}, u32[]{:S(2)}) collective-permute-start(bf16[32,4096]{1,0:T(8,128)(2,1)S(1)} %get-tuple-element.35), channel_id=1, source_target_pairs={{0,4},{2,6},{4,0},{6,2},{8,12},{10,14},{12,8},{14,10},{1,5},{3,7},... | collective-permute-start | bytes 786440 | tf_op jit(solution)/shard_map/ppermute | solution.py:446
  7.7 2.6 %collective-permute-start.5 = (bf16[16,4096]{1,0:T(8,128)(2,1)S(1)}, bf16[16,4096]{1,0:T(8,128)(2,1)S(1)}, u32[]{:S(2)}, u32[]{:S(2)}) collective-permute-start(bf16[16,4096]{1,0:T(8,128)(2,1)S(1)} %get-tuple-element.40), channel_id=1, source_target_pairs={{0,8},{2,10},{4,12},{6,14},{8,0},{10,2},{12,4},{14,6},{1,9},{3,11}... | collective-permute-start | bytes 393224 | tf_op jit(solution)/shard_map/ppermute | solution.py:446
  10.3 0.2 collective-permute-start.6
  10.6 3.5 %load.2.refs_2_.refs_1_.refs_3_.refs_6_.refs_10_.gate_ref = bf16[1,4096,1024]{2,1,0:T(8,128)(2,1)S(1)} custom-call(bf16[1,4096,1024]{2,1,0:T(8,128)(2,1)} %src.3, bf16[32,4096]{1,0:T(8,128)(2,1)S(1)} %get-tuple-element.34.refs_0_), custom_call_target="tpu_custom_call" | custom-call | bytes 1024 | tf_op jit(solution)/shard_map/load/pallas_call | solution.py:128
  14.0 0.0 collective-permute-done.1.refs_3_.refs_1_.refs_2_
  14.1 1.8 %collective-permute-start.3 = (bf16[16,4096]{1,0:T(8,128)(2,1)S(1)}, bf16[16,4096]{1,0:T(8,128)(2,1)S(1)}, u32[]{:S(2)}, u32[]{:S(2)}) collective-permute-start(bf16[16,4096]{1,0:T(8,128)(2,1)S(1)} %get-tuple-element.38), channel_id=1, source_target_pairs={{0,8},{2,10},{4,12},{6,14},{8,0},{10,2},{12,4},{14,6},{1,9},{3,11}... | collective-permute-start | bytes 393224 | tf_op jit(solution)/shard_map/ppermute | solution.py:446
  15.8 2.0 %collective-permute-start.4 = (bf16[16,4096]{1,0:T(8,128)(2,1)S(1)}, bf16[16,4096]{1,0:T(8,128)(2,1)S(1)}, u32[]{:S(2)}, u32[]{:S(2)}) collective-permute-start(bf16[16,4096]{1,0:T(8,128)(2,1)S(1)} %get-tuple-element.39), channel_id=1, source_target_pairs={{0,12},{2,14},{4,8},{6,10},{8,4},{10,6},{12,0},{14,2},{1,13},{3,15... | collective-permute-start | bytes 393224 | tf_op jit(solution)/shard_map/ppermute | solution.py:446
  17.8 0.0 collective-permute-done.refs_0_.refs_1_
  17.8 0.5 collective-permute-start.2
  18.3 3.5 %load.3.refs_3_.refs_4_.refs_7_.refs_11_.up_ref = bf16[1,4096,1024]{2,1,0:T(8,128)(2,1)S(1)} custom-call(bf16[1,4096,1024]{2,1,0:T(8,128)(2,1)} %src.4, bf16[32,4096]{1,0:T(8,128)(2,1)S(1)} %collective-permute-done.refs_0_.refs_1_, bf16[1,4096,1024]{2,1,0:T(8,128)(2,1)S(1)} %load.2.refs_2_.refs_1_.refs_3_.refs_6_.refs_10_.gate_ref), custom_call_target="tpu_custom_call" | custom-call | bytes 1024 | tf_op jit(solution)/shard_map/load/pallas_call | solution.py:128
  21.8 0.0 collective-permute-done.5.refs_0_
  21.8 1.3 %collective-permute-done.6.refs_1_ = bf16[16,4096]{1,0:T(8,128)(2,1)S(1)} collective-permute-done((bf16[16,4096]{1,0:T(8,128)(2,1)S(1)}, bf16[16,4096]{1,0:T(8,128)(2,1)S(1)}, u32[]{:S(2)}, u32[]{:S(2)}) %collective-permute-start.6) | collective-permute-done | bytes 131104 | tf_op jit(solution)/shard_map/ppermute | solution.py:446
  23.2 0.6 collective-permute-start.8
  23.7 2.4 %collective-permute-done.2.refs_2_.refs_3_ = bf16[32,4096]{1,0:T(8,128)(2,1)S(1)} collective-permute-done((bf16[32,4096]{1,0:T(8,128)(2,1)S(1)}, bf16[32,4096]{1,0:T(8,128)(2,1)S(1)}, u32[]{:S(2)}, u32[]{:S(2)}) %collective-permute-start.2) | collective-permute-done | bytes 262176 | tf_op jit(solution)/shard_map/ppermute | solution.py:446
  26.2 4.3 %load_turned.1.refs_4_.refs_8_.refs_9_ = bf16[4096,1024]{1,0:T(8,128)(2,1)S(1)} custom-call(bf16[1,1024,4096]{2,1,0:T(8,128)(2,1)} %src.5, bf16[32,4096]{1,0:T(8,128)(2,1)S(1)} %join.2.refs_0_.refs_4_, bf16[32,4096]{1,0:T(8,128)(2,1)S(1)} %collective-permute-done.1.refs_3_.refs_1_.refs_2_, bf16[32,4096]{1,0:T(8,128)(2,1)S(1)} %collective-permute-done.2.refs_2_.refs_3_, ...), custom_call_target="tpu_custom_call" | custom-call | bytes 1024 | tf_op jit(solution)/shard_map/load_turned/pallas_call | solution.py:161
  30.5 0.4 collective-permute-done.3.refs_0_
  30.9 0.0 collective-permute-done.4.refs_1_
  30.9 0.6 collective-permute-start.7
  31.5 0.0 collective-permute-done.8.refs_5_
  31.5 2.6 %pre_activations.1 = (f32[128,1024]{1,0:T(8,128)S(1)}, f32[128,1024]{1,0:T(8,128)S(1)}, f32[128,1024]{1,0:T(8,128)S(1)}) custom-call(bf16[32,4096]{1,0:T(8,128)(2,1)S(1)} %get-tuple-element.34.refs_0_, bf16[32,4096]{1,0:T(8,128)(2,1)S(1)} %collective-permute-done.refs_0_.refs_1_, bf16[32,4096]{1,0:T(8,128)(2,1)S(1)} %collective-permute-done.1.refs_3_.refs_1_.refs_2_, ...), custom_call_target="tpu_custom_call" | custom-call | flops 5000000000 | bytes 1024 | tf_op jit(solution)/shard_map/pre_activations/pallas_call | solution.py:251
  34.1 3.9 %collective-permute-done.7.refs_5_ = bf16[32,4096]{1,0:T(8,128)(2,1)S(1)} collective-permute-done((bf16[32,4096]{1,0:T(8,128)(2,1)S(1)}, bf16[32,4096]{1,0:T(8,128)(2,1)S(1)}, u32[]{:S(2)}, u32[]{:S(2)}) %collective-permute-start.7) | collective-permute-done | bytes 262176 | tf_op jit(solution)/shard_map/ppermute | solution.py:446
  38.0 3.6 %hidden_grads.1 = (bf16[64,2176]{1,0:T(8,128)(2,1)S(1)}, bf16[64,2176]{1,0:T(8,128)(2,1)S(1)}, bf16[128,1024]{1,0:T(8,128)(2,1)S(1)}, bf16[128,1024]{1,0:T(8,128)(2,1)S(1)}, bf16[128,128]{1,0:T(8,128)(2,1)S(1)}) custom-call(bf16[32,4096]{1,0:T(8,128)(2,1)S(1)} %get-tuple-element.34.refs_0_, bf16[32,4096]{1,0:T(8,128)(2,1)S(1)} %collective-permute-done.refs_0_.refs_1_, ...), custom_call_target="tpu_custom_call" | custom-call | flops 2147483648 | bytes 16777216 | tf_op jit(solution)/shard_map/hidden_grads/pallas_call | solution.py:305
  41.5 0.6 collective-permute-start.9
  42.1 0.0 copy-start
  42.1 0.0 copy-start.1
  42.1 0.0 copy-start.2
  42.1 2.4 %back_half.1 = (bf16[64,2176]{1,0:T(8,128)(2,1)S(1)}, bf16[64,2176]{1,0:T(8,128)(2,1)S(1)}) custom-call(bf16[128,1024]{1,0:T(8,128)(2,1)S(1)} %get-tuple-element.51.dgate_ref, bf16[128,1024]{1,0:T(8,128)(2,1)S(1)} %get-tuple-element.52.dup_ref, bf16[128,128]{1,0:T(8,128)(2,1)S(1)} %get-tuple-element.53.part_ref, ...), custom_call_target="tpu_custom_call" | custom-call | flops 1073741824 | bytes 8388608 | tf_op jit(solution)/shard_map/back_half/pallas_call | solution.py:329
  44.5 4.2 %collective-permute-done.9.refs_1_ = bf16[64,2176]{1,0:T(8,128)(2,1)S(1)} collective-permute-done((bf16[64,2176]{1,0:T(8,128)(2,1)S(1)}, bf16[64,2176]{1,0:T(8,128)(2,1)S(1)}, u32[]{:S(2)}, u32[]{:S(2)}) %collective-permute-start.9) | collective-permute-done | bytes 278560 | tf_op jit(solution)/shard_map/ppermute | solution.py:446
  48.8 0.5 collective-permute-start.14
  49.3 0.1 sum_pieces.2
  49.4 0.1 collective-permute-start.10
  49.5 4.2 %collective-permute-start.11 = (bf16[16,2176]{1,0:T(8,128)(2,1)S(1)}, bf16[16,2176]{1,0:T(8,128)(2,1)S(1)}, u32[]{:S(2)}, u32[]{:S(2)}) collective-permute-start(bf16[16,2176]{1,0:T(8,128)(2,1)S(1)} %get-tuple-element.48), channel_id=1, source_target_pairs={{0,9},{1,8},{2,11},{3,10},{4,13},{5,12},{6,15},{7,14},{8,1},{9,0},... | collective-permute-start | bytes 208904 | tf_op jit(solution)/shard_map/ppermute | solution.py:460
  53.7 1.1 %collective-permute-start.12 = (bf16[16,2176]{1,0:T(8,128)(2,1)S(1)}, bf16[16,2176]{1,0:T(8,128)(2,1)S(1)}, u32[]{:S(2)}, u32[]{:S(2)}) collective-permute-start(bf16[16,2176]{1,0:T(8,128)(2,1)S(1)} %get-tuple-element.49), channel_id=1, source_target_pairs={{0,5},{1,4},{2,7},{3,6},{4,1},{5,0},{6,3},{7,2},{8,13},{9,12},{10,... | collective-permute-start | bytes 208904 | tf_op jit(solution)/shard_map/ppermute | solution.py:460
  54.8 0.0 collective-permute-start.13
  54.8 0.5 collective-permute-done.14.refs_1_
  55.3 0.1 sum_pieces.3
  55.4 5.4 %collective-permute-start.15 = (bf16[16,2176]{1,0:T(8,128)(2,1)S(1)}, bf16[16,2176]{1,0:T(8,128)(2,1)S(1)}, u32[]{:S(2)}, u32[]{:S(2)}) collective-permute-start(bf16[16,2176]{1,0:T(8,128)(2,1)S(1)} %get-tuple-element.56), channel_id=1, source_target_pairs={{0,12},{1,13},{2,14},{3,15},{4,8},{5,9},{6,10},{7,11},{8,4},{9,5},... | collective-permute-start | bytes 208904 | tf_op jit(solution)/shard_map/ppermute | solution.py:460
  60.9 0.0 collective-permute-done.10.refs_0_
  60.9 0.0 collective-permute-start.16
  60.9 0.0 collective-permute-done.11.refs_1_
  60.9 0.6 collective-permute-start.17
  61.5 0.0 copy-done
  61.5 0.0 copy-done.1
  61.5 0.0 copy-done.2
  61.5 0.2 mixing.1
  61.8 0.0 collective-permute-done.12.refs_2_
  61.8 0.0 collective-permute-done.13.refs_3_
  61.8 2.0 %collective-permute-done.15.refs_4_ = bf16[16,2176]{1,0:T(8,128)(2,1)S(1)} collective-permute-done((bf16[16,2176]{1,0:T(8,128)(2,1)S(1)}, bf16[16,2176]{1,0:T(8,128)(2,1)S(1)}, u32[]{:S(2)}, u32[]{:S(2)}) %collective-permute-start.15) | collective-permute-done | bytes 69664 | tf_op jit(solution)/shard_map/ppermute | solution.py:460
  63.8 2.5 %collective-permute-done.16.refs_5_ = bf16[16,2176]{1,0:T(8,128)(2,1)S(1)} collective-permute-done((bf16[16,2176]{1,0:T(8,128)(2,1)S(1)}, bf16[16,2176]{1,0:T(8,128)(2,1)S(1)}, u32[]{:S(2)}, u32[]{:S(2)}) %collective-permute-start.16) | collective-permute-done | bytes 69664 | tf_op jit(solution)/shard_map/ppermute | solution.py:460
  66.3 0.1 collective-permute-done.17.refs_6_
  66.4 1.2 %combine.1 = (bf16[128,2048]{1,0:T(8,128)(2,1)}, f32[1,128]{1,0:T(1,128)}) custom-call(bf16[2,128,128]{2,1,0:T(8,128)(2,1)S(1)} %get-tuple-element.32.mix_ref, f32[128,128]{1,0:T(8,128)S(1)} %get-tuple-element.33.hit_ref, bf16[16,2176]{1,0:T(8,128)(2,1)S(1)} %collective-permute-done.10.refs_0_, bf16[16,2176]{1,0:T(8,128)(2,1)S(1)} %collective-permute-done.11.refs_1_, ...), custom_call_target="tpu_custom_call" | custom-call | flops 134217728 | bytes 1048576 | tf_op jit(solution)/shard_map/combine/pallas_call | solution.py:423
  (4 shorter events, 0.0 us)
Async XLA Ops:
  3.1 10.9 %collective-permute-start.1 = (bf16[32,4096]{1,0:T(8,128)(2,1)S(1)}, bf16[32,4096]{1,0:T(8,128)(2,1)S(1)}, u32[]{:S(2)}, u32[]{:S(2)}) collective-permute-start(bf16[32,4096]{1,0:T(8,128)(2,1)S(1)} %get-tuple-element.34.refs_0_), channel_id=1, source_target_pairs={{0,2},{2,0},{4,6},{6,4},{8,10},{10,8},{12,14},{14,12},{1,3},{3,1},... | collective-permute-start | bytes 786440 | tf_op jit(solution)/shard_map/ppermute | solution.py:446
  6.2 11.6 %collective-permute-start = (bf16[32,4096]{1,0:T(8,128)(2,1)S(1)}, bf16[32,4096]{1,0:T(8,128)(2,1)S(1)}, u32[]{:S(2)}, u32[]{:S(2)}) collective-permute-start(bf16[32,4096]{1,0:T(8,128)(2,1)S(1)} %get-tuple-element.35), channel_id=1, source_target_pairs={{0,4},{2,6},{4,0},{6,2},{8,12},{10,14},{12,8},{14,10},{1,5},{3,7},... | collective-permute-start | bytes 786440 | tf_op jit(solution)/shard_map/ppermute | solution.py:446
  7.7 14.1 %collective-permute-start.5 = (bf16[16,4096]{1,0:T(8,128)(2,1)S(1)}, bf16[16,4096]{1,0:T(8,128)(2,1)S(1)}, u32[]{:S(2)}, u32[]{:S(2)}) collective-permute-start(bf16[16,4096]{1,0:T(8,128)(2,1)S(1)} %get-tuple-element.40), channel_id=1, source_target_pairs={{0,8},{2,10},{4,12},{6,14},{8,0},{10,2},{12,4},{14,6},{1,9},{3,11}... | collective-permute-start | bytes 393224 | tf_op jit(solution)/shard_map/ppermute | solution.py:446
  10.3 12.8 %collective-permute-start.6 = (bf16[16,4096]{1,0:T(8,128)(2,1)S(1)}, bf16[16,4096]{1,0:T(8,128)(2,1)S(1)}, u32[]{:S(2)}, u32[]{:S(2)}) collective-permute-start(bf16[16,4096]{1,0:T(8,128)(2,1)S(1)} %get-tuple-element.41), channel_id=1, source_target_pairs={{0,12},{2,14},{4,8},{6,10},{8,4},{10,6},{12,0},{14,2},{1,13},{3,15... | collective-permute-start | bytes 393224 | tf_op jit(solution)/shard_map/ppermute | solution.py:446
  14.1 16.8 %collective-permute-start.3 = (bf16[16,4096]{1,0:T(8,128)(2,1)S(1)}, bf16[16,4096]{1,0:T(8,128)(2,1)S(1)}, u32[]{:S(2)}, u32[]{:S(2)}) collective-permute-start(bf16[16,4096]{1,0:T(8,128)(2,1)S(1)} %get-tuple-element.38), channel_id=1, source_target_pairs={{0,8},{2,10},{4,12},{6,14},{8,0},{10,2},{12,4},{14,6},{1,9},{3,11}... | collective-permute-start | bytes 393224 | tf_op jit(solution)/shard_map/ppermute | solution.py:446
  15.8 15.1 %collective-permute-start.4 = (bf16[16,4096]{1,0:T(8,128)(2,1)S(1)}, bf16[16,4096]{1,0:T(8,128)(2,1)S(1)}, u32[]{:S(2)}, u32[]{:S(2)}) collective-permute-start(bf16[16,4096]{1,0:T(8,128)(2,1)S(1)} %get-tuple-element.39), channel_id=1, source_target_pairs={{0,12},{2,14},{4,8},{6,10},{8,4},{10,6},{12,0},{14,2},{1,13},{3,15... | collective-permute-start | bytes 393224 | tf_op jit(solution)/shard_map/ppermute | solution.py:446
  17.8 8.3 %collective-permute-start.2 = (bf16[32,4096]{1,0:T(8,128)(2,1)S(1)}, bf16[32,4096]{1,0:T(8,128)(2,1)S(1)}, u32[]{:S(2)}, u32[]{:S(2)}) collective-permute-start(bf16[32,4096]{1,0:T(8,128)(2,1)S(1)} %collective-permute-done.refs_0_.refs_1_), channel_id=1, source_target_pairs={{0,2},{2,0},{4,6},{6,4},{8,10},{10,8},{12,14},{14,12},{1,3},{3,1},... | collective-permute-start | bytes 786440 | tf_op jit(solution)/shard_map/ppermute | solution.py:446
  23.2 8.3 %collective-permute-start.8 = (bf16[32,4096]{1,0:T(8,128)(2,1)S(1)}, bf16[32,4096]{1,0:T(8,128)(2,1)S(1)}, u32[]{:S(2)}, u32[]{:S(2)}) collective-permute-start(bf16[32,4096]{1,0:T(8,128)(2,1)S(1)} %join.2.refs_0_.refs_4_), channel_id=1, source_target_pairs={{0,2},{2,0},{4,6},{6,4},{8,10},{10,8},{12,14},{14,12},{1,3},{3,1},... | collective-permute-start | bytes 786440 | tf_op jit(solution)/shard_map/ppermute | solution.py:446
  30.9 7.1 %collective-permute-start.7 = (bf16[32,4096]{1,0:T(8,128)(2,1)S(1)}, bf16[32,4096]{1,0:T(8,128)(2,1)S(1)}, u32[]{:S(2)}, u32[]{:S(2)}) collective-permute-start(bf16[32,4096]{1,0:T(8,128)(2,1)S(1)} %join.3.refs_4_), channel_id=1, source_target_pairs={{0,2},{2,0},{4,6},{6,4},{8,10},{10,8},{12,14},{14,12},{1,3},{3,1},... | collective-permute-start | bytes 786440 | tf_op jit(solution)/shard_map/ppermute | solution.py:446
  41.5 7.2 %collective-permute-start.9 = (bf16[64,2176]{1,0:T(8,128)(2,1)S(1)}, bf16[64,2176]{1,0:T(8,128)(2,1)S(1)}, u32[]{:S(2)}, u32[]{:S(2)}) collective-permute-start(bf16[64,2176]{1,0:T(8,128)(2,1)S(1)} %get-tuple-element.46), channel_id=1, source_target_pairs={{0,2},{2,0},{4,6},{6,4},{8,10},{10,8},{12,14},{14,12},{1,3},{3,1},... | collective-permute-start | bytes 835592 | tf_op jit(solution)/shard_map/ppermute | solution.py:446
  42.1 19.4 %copy-start = (s32[128,2]{0,1:T(2,128)S(1)}, s32[128,2]{0,1:T(2,128)}, u32[]{:S(2)}) copy-start(s32[128,2]{0,1:T(2,128)} %param.11) | copy-start | bytes 3076
  42.1 19.4 %copy-start.1 = (s32[128]{0:T(128)S(1)}, s32[128]{0:T(128)}, u32[]{:S(2)}) copy-start(s32[128]{0:T(128)} %param.10) | copy-start | bytes 1540
  42.1 19.4 %copy-start.2 = (f32[128,2]{0,1:T(2,128)S(1)}, f32[128,2]{0,1:T(2,128)}, u32[]{:S(2)}) copy-start(f32[128,2]{0,1:T(2,128)} %param.12) | copy-start | bytes 3076
  48.8 6.5 %collective-permute-start.14 = (bf16[64,2176]{1,0:T(8,128)(2,1)S(1)}, bf16[64,2176]{1,0:T(8,128)(2,1)S(1)}, u32[]{:S(2)}, u32[]{:S(2)}) collective-permute-start(bf16[64,2176]{1,0:T(8,128)(2,1)S(1)} %pass_after.3), channel_id=1, source_target_pairs={{0,2},{2,0},{4,6},{6,4},{8,10},{10,8},{12,14},{14,12},{1,3},{3,1},... | collective-permute-start | bytes 835592 | tf_op jit(solution)/shard_map/ppermute | solution.py:446
  49.4 11.5 %collective-permute-start.10 = (bf16[16,2176]{1,0:T(8,128)(2,1)S(1)}, bf16[16,2176]{1,0:T(8,128)(2,1)S(1)}, u32[]{:S(2)}, u32[]{:S(2)}) collective-permute-start(bf16[16,2176]{1,0:T(8,128)(2,1)S(1)} %get-tuple-element.47), channel_id=1, source_target_pairs={{0,13},{1,12},{2,15},{3,14},{4,9},{5,8},{6,11},{7,10},{8,5},{9,4},... | collective-permute-start | bytes 208904 | tf_op jit(solution)/shard_map/ppermute | solution.py:460
  49.5 11.4 %collective-permute-start.11 = (bf16[16,2176]{1,0:T(8,128)(2,1)S(1)}, bf16[16,2176]{1,0:T(8,128)(2,1)S(1)}, u32[]{:S(2)}, u32[]{:S(2)}) collective-permute-start(bf16[16,2176]{1,0:T(8,128)(2,1)S(1)} %get-tuple-element.48), channel_id=1, source_target_pairs={{0,9},{1,8},{2,11},{3,10},{4,13},{5,12},{6,15},{7,14},{8,1},{9,0},... | collective-permute-start | bytes 208904 | tf_op jit(solution)/shard_map/ppermute | solution.py:460
  53.7 8.1 %collective-permute-start.12 = (bf16[16,2176]{1,0:T(8,128)(2,1)S(1)}, bf16[16,2176]{1,0:T(8,128)(2,1)S(1)}, u32[]{:S(2)}, u32[]{:S(2)}) collective-permute-start(bf16[16,2176]{1,0:T(8,128)(2,1)S(1)} %get-tuple-element.49), channel_id=1, source_target_pairs={{0,5},{1,4},{2,7},{3,6},{4,1},{5,0},{6,3},{7,2},{8,13},{9,12},{10,... | collective-permute-start | bytes 208904 | tf_op jit(solution)/shard_map/ppermute | solution.py:460
  54.8 7.0 %collective-permute-start.13 = (bf16[16,2176]{1,0:T(8,128)(2,1)S(1)}, bf16[16,2176]{1,0:T(8,128)(2,1)S(1)}, u32[]{:S(2)}, u32[]{:S(2)}) collective-permute-start(bf16[16,2176]{1,0:T(8,128)(2,1)S(1)} %get-tuple-element.50), channel_id=1, source_target_pairs={{0,1},{1,0},{2,3},{3,2},{4,5},{5,4},{6,7},{7,6},{8,9},{9,8},{10,11... | collective-permute-start | bytes 208904 | tf_op jit(solution)/shard_map/ppermute | solution.py:460
  55.4 8.4 %collective-permute-start.15 = (bf16[16,2176]{1,0:T(8,128)(2,1)S(1)}, bf16[16,2176]{1,0:T(8,128)(2,1)S(1)}, u32[]{:S(2)}, u32[]{:S(2)}) collective-permute-start(bf16[16,2176]{1,0:T(8,128)(2,1)S(1)} %get-tuple-element.56), channel_id=1, source_target_pairs={{0,12},{1,13},{2,14},{3,15},{4,8},{5,9},{6,10},{7,11},{8,4},{9,5},... | collective-permute-start | bytes 208904 | tf_op jit(solution)/shard_map/ppermute | solution.py:460
  60.9 5.5 %collective-permute-start.16 = (bf16[16,2176]{1,0:T(8,128)(2,1)S(1)}, bf16[16,2176]{1,0:T(8,128)(2,1)S(1)}, u32[]{:S(2)}, u32[]{:S(2)}) collective-permute-start(bf16[16,2176]{1,0:T(8,128)(2,1)S(1)} %get-tuple-element.57), channel_id=1, source_target_pairs={{0,8},{1,9},{2,10},{3,11},{4,12},{5,13},{6,14},{7,15},{8,0},{9,1},... | collective-permute-start | bytes 208904 | tf_op jit(solution)/shard_map/ppermute | solution.py:460
  60.9 5.6 %collective-permute-start.17 = (bf16[16,2176]{1,0:T(8,128)(2,1)S(1)}, bf16[16,2176]{1,0:T(8,128)(2,1)S(1)}, u32[]{:S(2)}, u32[]{:S(2)}) collective-permute-start(bf16[16,2176]{1,0:T(8,128)(2,1)S(1)} %get-tuple-element.58), channel_id=1, source_target_pairs={{0,4},{1,5},{2,6},{3,7},{4,0},{5,1},{6,2},{7,3},{8,12},{9,13},{10,... | collective-permute-start | bytes 208904 | tf_op jit(solution)/shard_map/ppermute | solution.py:460

commit v18 on v17

--- a/solution.py
+++ b/solution.py
@@ -231,7 +231,7 @@
     blocks, (gate_ref, up_ref, _, act_out, slope_out, both_out, rows) = refs[:count], refs[count:]
     fill(rows, blocks, places)
     hidden = gate_ref.shape[2]
-    chunk = min(256, hidden)
+    chunk = min(512, hidden)
     for start in range(0, hidden, chunk):
         cols = slice(start, start + chunk)
         gate_pre = jnp.dot(rows[...], gate_ref[0, :, cols], preferred_element_type=F32)
@@ -284,7 +284,7 @@
     dgate, dup, part_out, rows = refs[count + 6 + groups :]
     fill(rows, blocks, places)
     hidden = gate_ref.shape[2]
-    chunk = min(256, hidden)
+    chunk = min(512, hidden)
     part = jnp.zeros((rows.shape[0], 1), F32)
     for start in range(0, hidden, chunk):
         cols = slice(start, start + chunk)

time: 67.8 us -> 67.8 us (level)
  transfers between devices with their start and end apart: 18 -> 18, of which waited for: 9 -> 9; matrix products, arithmetic and copies ran while one was open for 0% -> 0% of each run, Pallas kernels for 25% -> 24%
where the time goes in v18:
time: 67.8 us; the launch traced here: 67.7 us
  starting transfers between devices  25.4 us (37%)
  Pallas kernels  23.8 us (35%)
  waiting for transfers between devices  17.7 us (26%)
  between operations  0.77 us (1%)
    ppermute x11, starting transfers between devices, to_expert(): lax.ppermute(x, 'ep', [(e * groups + j, (e ^ s) * groups + (j + t) % grou...  13.9 us
    ppermute x11, waiting for transfers between devices, to_expert(): lax.ppermute(x, 'ep', [(e * groups + j, (e ^ s) * groups + (j + t) % grou...  13 us
    ppermute x7, starting transfers between devices, to_source(): lax.ppermute(x, ('ep', 'mod'), [((e * groups + j) * 2 + m, ((e ^ s) * gro...  11.5 us
    pallas_call x2, Pallas kernels, load(): pl.pallas_call(functools.partial(load_kernel, parts), in_specs=[pl.BlockS...  6.94 us
    ppermute x7, waiting for transfers between devices, to_source(): lax.ppermute(x, ('ep', 'mod'), [((e * groups + j) * 2 + m, ((e ^ s) * gro...  4.66 us
    pallas_call x1, Pallas kernels, load_turned(): pl.pallas_call(functools.partial(load_turned_kernel, parts), in_specs=[pl...  4.29 us
    pallas_call x1, Pallas kernels, hidden_grads(): pl.pallas_call(functools.partial(hidden_kernel, count, places, groups), i...  3.56 us
    pallas_call x1, Pallas kernels, gather_slots(): pl.pallas_call(functools.partial(gather_kernel, groups, parts), in_specs=...  2.5 us
  transfers between devices with their start and end apart: 18, of which 9 were waited for; matrix products, arithmetic and copies ran while one was open for 0% of the time, Pallas kernels for 24%

profile of v18, /device:TPU:0, one launch (start us, length us, event | category | flops | bytes accessed | tf_op | source)
XLA Modules:
  0.0 67.7 jit_solution(18264267085474099300)
XLA Ops:
  0.6 2.5 %gather_slots.1 = (bf16[32,4096]{1,0:T(8,128)(2,1)S(1)}, bf16[32,4096]{1,0:T(8,128)(2,1)S(1)}, bf16[16,4096]{1,0:T(8,128)(2,1)S(1)}, bf16[16,4096]{1,0:T(8,128)(...) custom-call(s32[1,128]{1,0:T(1,128)} %bitcast.6, s32[2,128]{1,0:T(2,128)} %bitcast.4, ...), custom_call_target="tpu_custom_call" | custom-call | flops 134217728 | bytes 3145728 | tf_op jit(solution)/shard_map/gather_slots/pallas_call | solution.py:93
  3.1 3.0 %collective-permute-start.1 = (bf16[32,4096]{1,0:T(8,128)(2,1)S(1)}, bf16[32,4096]{1,0:T(8,128)(2,1)S(1)}, u32[]{:S(2)}, u32[]{:S(2)}) collective-permute-start(bf16[32,4096]{1,0:T(8,128)(2,1)S(1)} %get-tuple-element.34.refs_0_), channel_id=1, source_target_pairs={{0,2},{2,0},{4,6},{6,4},{8,10},{10,8},{12,14},{14,12},{1,3},{3,1},... | collective-permute-start | bytes 786440 | tf_op jit(solution)/shard_map/ppermute | solution.py:446
  6.2 1.6 %collective-permute-start = (bf16[32,4096]{1,0:T(8,128)(2,1)S(1)}, bf16[32,4096]{1,0:T(8,128)(2,1)S(1)}, u32[]{:S(2)}, u32[]{:S(2)}) collective-permute-start(bf16[32,4096]{1,0:T(8,128)(2,1)S(1)} %get-tuple-element.35), channel_id=1, source_target_pairs={{0,4},{2,6},{4,0},{6,2},{8,12},{10,14},{12,8},{14,10},{1,5},{3,7},... | collective-permute-start | bytes 786440 | tf_op jit(solution)/shard_map/ppermute | solution.py:446
  7.7 2.6 %collective-permute-start.5 = (bf16[16,4096]{1,0:T(8,128)(2,1)S(1)}, bf16[16,4096]{1,0:T(8,128)(2,1)S(1)}, u32[]{:S(2)}, u32[]{:S(2)}) collective-permute-start(bf16[16,4096]{1,0:T(8,128)(2,1)S(1)} %get-tuple-element.40), channel_id=1, source_target_pairs={{0,8},{2,10},{4,12},{6,14},{8,0},{10,2},{12,4},{14,6},{1,9},{3,11}... | collective-permute-start | bytes 393224 | tf_op jit(solution)/shard_map/ppermute | solution.py:446
  10.3 0.2 collective-permute-start.6
  10.6 3.5 %load.2.refs_2_.refs_1_.refs_3_.refs_6_.refs_10_.gate_ref = bf16[1,4096,1024]{2,1,0:T(8,128)(2,1)S(1)} custom-call(bf16[1,4096,1024]{2,1,0:T(8,128)(2,1)} %src.3, bf16[32,4096]{1,0:T(8,128)(2,1)S(1)} %get-tuple-element.34.refs_0_), custom_call_target="tpu_custom_call" | custom-call | bytes 1024 | tf_op jit(solution)/shard_map/load/pallas_call | solution.py:128
  14.0 0.0 collective-permute-done.1.refs_3_.refs_1_.refs_2_
  14.1 1.8 %collective-permute-start.3 = (bf16[16,4096]{1,0:T(8,128)(2,1)S(1)}, bf16[16,4096]{1,0:T(8,128)(2,1)S(1)}, u32[]{:S(2)}, u32[]{:S(2)}) collective-permute-start(bf16[16,4096]{1,0:T(8,128)(2,1)S(1)} %get-tuple-element.38), channel_id=1, source_target_pairs={{0,8},{2,10},{4,12},{6,14},{8,0},{10,2},{12,4},{14,6},{1,9},{3,11}... | collective-permute-start | bytes 393224 | tf_op jit(solution)/shard_map/ppermute | solution.py:446
  15.8 2.0 %collective-permute-start.4 = (bf16[16,4096]{1,0:T(8,128)(2,1)S(1)}, bf16[16,4096]{1,0:T(8,128)(2,1)S(1)}, u32[]{:S(2)}, u32[]{:S(2)}) collective-permute-start(bf16[16,4096]{1,0:T(8,128)(2,1)S(1)} %get-tuple-element.39), channel_id=1, source_target_pairs={{0,12},{2,14},{4,8},{6,10},{8,4},{10,6},{12,0},{14,2},{1,13},{3,15... | collective-permute-start | bytes 393224 | tf_op jit(solution)/shard_map/ppermute | solution.py:446
  17.8 0.0 collective-permute-done.refs_0_.refs_1_
  17.8 0.5 collective-permute-start.2
  18.3 3.5 %load.3.refs_3_.refs_4_.refs_7_.refs_11_.up_ref = bf16[1,4096,1024]{2,1,0:T(8,128)(2,1)S(1)} custom-call(bf16[1,4096,1024]{2,1,0:T(8,128)(2,1)} %src.4, bf16[32,4096]{1,0:T(8,128)(2,1)S(1)} %collective-permute-done.refs_0_.refs_1_, bf16[1,4096,1024]{2,1,0:T(8,128)(2,1)S(1)} %load.2.refs_2_.refs_1_.refs_3_.refs_6_.refs_10_.gate_ref), custom_call_target="tpu_custom_call" | custom-call | bytes 1024 | tf_op jit(solution)/shard_map/load/pallas_call | solution.py:128
  21.8 0.0 collective-permute-done.5.refs_0_
  21.8 1.3 %collective-permute-done.6.refs_1_ = bf16[16,4096]{1,0:T(8,128)(2,1)S(1)} collective-permute-done((bf16[16,4096]{1,0:T(8,128)(2,1)S(1)}, bf16[16,4096]{1,0:T(8,128)(2,1)S(1)}, u32[]{:S(2)}, u32[]{:S(2)}) %collective-permute-start.6) | collective-permute-done | bytes 131104 | tf_op jit(solution)/shard_map/ppermute | solution.py:446
  23.2 0.6 collective-permute-start.8
  23.7 2.4 %collective-permute-done.2.refs_2_.refs_3_ = bf16[32,4096]{1,0:T(8,128)(2,1)S(1)} collective-permute-done((bf16[32,4096]{1,0:T(8,128)(2,1)S(1)}, bf16[32,4096]{1,0:T(8,128)(2,1)S(1)}, u32[]{:S(2)}, u32[]{:S(2)}) %collective-permute-start.2) | collective-permute-done | bytes 262176 | tf_op jit(solution)/shard_map/ppermute | solution.py:446
  26.2 4.3 %load_turned.1.refs_4_.refs_8_.refs_9_ = bf16[4096,1024]{1,0:T(8,128)(2,1)S(1)} custom-call(bf16[1,1024,4096]{2,1,0:T(8,128)(2,1)} %src.5, bf16[32,4096]{1,0:T(8,128)(2,1)S(1)} %join.2.refs_0_.refs_4_, bf16[32,4096]{1,0:T(8,128)(2,1)S(1)} %collective-permute-done.1.refs_3_.refs_1_.refs_2_, bf16[32,4096]{1,0:T(8,128)(2,1)S(1)} %collective-permute-done.2.refs_2_.refs_3_, ...), custom_call_target="tpu_custom_call" | custom-call | bytes 1024 | tf_op jit(solution)/shard_map/load_turned/pallas_call | solution.py:161
  30.5 0.4 collective-permute-done.3.refs_0_
  30.9 0.0 collective-permute-done.4.refs_1_
  30.9 0.6 collective-permute-start.7
  31.5 0.0 collective-permute-done.8.refs_5_
  31.5 2.4 %pre_activations.1 = (f32[128,1024]{1,0:T(8,128)S(1)}, f32[128,1024]{1,0:T(8,128)S(1)}, f32[128,1024]{1,0:T(8,128)S(1)}) custom-call(bf16[32,4096]{1,0:T(8,128)(2,1)S(1)} %get-tuple-element.34.refs_0_, bf16[32,4096]{1,0:T(8,128)(2,1)S(1)} %collective-permute-done.refs_0_.refs_1_, bf16[32,4096]{1,0:T(8,128)(2,1)S(1)} %collective-permute-done.1.refs_3_.refs_1_.refs_2_, ...), custom_call_target="tpu_custom_call" | custom-call | flops 5000000000 | bytes 1024 | tf_op jit(solution)/shard_map/pre_activations/pallas_call | solution.py:251
  33.9 4.1 %collective-permute-done.7.refs_5_ = bf16[32,4096]{1,0:T(8,128)(2,1)S(1)} collective-permute-done((bf16[32,4096]{1,0:T(8,128)(2,1)S(1)}, bf16[32,4096]{1,0:T(8,128)(2,1)S(1)}, u32[]{:S(2)}, u32[]{:S(2)}) %collective-permute-start.7) | collective-permute-done | bytes 262176 | tf_op jit(solution)/shard_map/ppermute | solution.py:446
  38.0 3.6 %hidden_grads.1 = (bf16[64,2176]{1,0:T(8,128)(2,1)S(1)}, bf16[64,2176]{1,0:T(8,128)(2,1)S(1)}, bf16[128,1024]{1,0:T(8,128)(2,1)S(1)}, bf16[128,1024]{1,0:T(8,128)(2,1)S(1)}, bf16[128,128]{1,0:T(8,128)(2,1)S(1)}) custom-call(bf16[32,4096]{1,0:T(8,128)(2,1)S(1)} %get-tuple-element.34.refs_0_, bf16[32,4096]{1,0:T(8,128)(2,1)S(1)} %collective-permute-done.refs_0_.refs_1_, ...), custom_call_target="tpu_custom_call" | custom-call | flops 2147483648 | bytes 16777216 | tf_op jit(solution)/shard_map/hidden_grads/pallas_call | solution.py:305
  41.5 0.6 collective-permute-start.9
  42.1 0.0 copy-start
  42.1 0.0 copy-start.1
  42.1 0.0 copy-start.2
  42.1 2.4 %back_half.1 = (bf16[64,2176]{1,0:T(8,128)(2,1)S(1)}, bf16[64,2176]{1,0:T(8,128)(2,1)S(1)}) custom-call(bf16[128,1024]{1,0:T(8,128)(2,1)S(1)} %get-tuple-element.51.dgate_ref, bf16[128,1024]{1,0:T(8,128)(2,1)S(1)} %get-tuple-element.52.dup_ref, bf16[128,128]{1,0:T(8,128)(2,1)S(1)} %get-tuple-element.53.part_ref, ...), custom_call_target="tpu_custom_call" | custom-call | flops 1073741824 | bytes 8388608 | tf_op jit(solution)/shard_map/back_half/pallas_call | solution.py:329
  44.5 4.2 %collective-permute-done.9.refs_1_ = bf16[64,2176]{1,0:T(8,128)(2,1)S(1)} collective-permute-done((bf16[64,2176]{1,0:T(8,128)(2,1)S(1)}, bf16[64,2176]{1,0:T(8,128)(2,1)S(1)}, u32[]{:S(2)}, u32[]{:S(2)}) %collective-permute-start.9) | collective-permute-done | bytes 278560 | tf_op jit(solution)/shard_map/ppermute | solution.py:446
  48.8 0.5 collective-permute-start.14
  49.3 0.1 sum_pieces.2
  49.4 0.1 collective-permute-start.10
  49.5 4.2 %collective-permute-start.11 = (bf16[16,2176]{1,0:T(8,128)(2,1)S(1)}, bf16[16,2176]{1,0:T(8,128)(2,1)S(1)}, u32[]{:S(2)}, u32[]{:S(2)}) collective-permute-start(bf16[16,2176]{1,0:T(8,128)(2,1)S(1)} %get-tuple-element.48), channel_id=1, source_target_pairs={{0,9},{1,8},{2,11},{3,10},{4,13},{5,12},{6,15},{7,14},{8,1},{9,0},... | collective-permute-start | bytes 208904 | tf_op jit(solution)/shard_map/ppermute | solution.py:460
  53.7 1.1 %collective-permute-start.12 = (bf16[16,2176]{1,0:T(8,128)(2,1)S(1)}, bf16[16,2176]{1,0:T(8,128)(2,1)S(1)}, u32[]{:S(2)}, u32[]{:S(2)}) collective-permute-start(bf16[16,2176]{1,0:T(8,128)(2,1)S(1)} %get-tuple-element.49), channel_id=1, source_target_pairs={{0,5},{1,4},{2,7},{3,6},{4,1},{5,0},{6,3},{7,2},{8,13},{9,12},{10,... | collective-permute-start | bytes 208904 | tf_op jit(solution)/shard_map/ppermute | solution.py:460
  54.8 0.0 collective-permute-start.13
  54.8 0.5 collective-permute-done.14.refs_1_
  55.3 0.1 sum_pieces.3
  55.4 5.4 %collective-permute-start.15 = (bf16[16,2176]{1,0:T(8,128)(2,1)S(1)}, bf16[16,2176]{1,0:T(8,128)(2,1)S(1)}, u32[]{:S(2)}, u32[]{:S(2)}) collective-permute-start(bf16[16,2176]{1,0:T(8,128)(2,1)S(1)} %get-tuple-element.56), channel_id=1, source_target_pairs={{0,12},{1,13},{2,14},{3,15},{4,8},{5,9},{6,10},{7,11},{8,4},{9,5},... | collective-permute-start | bytes 208904 | tf_op jit(solution)/shard_map/ppermute | solution.py:460
  60.9 0.0 collective-permute-done.10.refs_0_
  60.9 0.0 collective-permute-start.16
  60.9 0.0 collective-permute-done.11.refs_1_
  60.9 0.6 collective-permute-start.17
  61.5 0.0 copy-done
  61.5 0.0 copy-done.1
  61.5 0.0 copy-done.2
  61.5 0.2 mixing.1
  61.8 0.0 collective-permute-done.12.refs_2_
  61.8 0.0 collective-permute-done.13.refs_3_
  61.8 2.0 %collective-permute-done.15.refs_4_ = bf16[16,2176]{1,0:T(8,128)(2,1)S(1)} collective-permute-done((bf16[16,2176]{1,0:T(8,128)(2,1)S(1)}, bf16[16,2176]{1,0:T(8,128)(2,1)S(1)}, u32[]{:S(2)}, u32[]{:S(2)}) %collective-permute-start.15) | collective-permute-done | bytes 69664 | tf_op jit(solution)/shard_map/ppermute | solution.py:460
  63.8 2.5 %collective-permute-done.16.refs_5_ = bf16[16,2176]{1,0:T(8,128)(2,1)S(1)} collective-permute-done((bf16[16,2176]{1,0:T(8,128)(2,1)S(1)}, bf16[16,2176]{1,0:T(8,128)(2,1)S(1)}, u32[]{:S(2)}, u32[]{:S(2)}) %collective-permute-start.16) | collective-permute-done | bytes 69664 | tf_op jit(solution)/shard_map/ppermute | solution.py:460
  66.3 0.1 collective-permute-done.17.refs_6_
  66.4 1.2 %combine.1 = (bf16[128,2048]{1,0:T(8,128)(2,1)}, f32[1,128]{1,0:T(1,128)}) custom-call(bf16[2,128,128]{2,1,0:T(8,128)(2,1)S(1)} %get-tuple-element.32.mix_ref, f32[128,128]{1,0:T(8,128)S(1)} %get-tuple-element.33.hit_ref, bf16[16,2176]{1,0:T(8,128)(2,1)S(1)} %collective-permute-done.10.refs_0_, bf16[16,2176]{1,0:T(8,128)(2,1)S(1)} %collective-permute-done.11.refs_1_, ...), custom_call_target="tpu_custom_call" | custom-call | flops 134217728 | bytes 1048576 | tf_op jit(solution)/shard_map/combine/pallas_call | solution.py:423
  (4 shorter events, 0.0 us)
Async XLA Ops:
  3.1 10.9 %collective-permute-start.1 = (bf16[32,4096]{1,0:T(8,128)(2,1)S(1)}, bf16[32,4096]{1,0:T(8,128)(2,1)S(1)}, u32[]{:S(2)}, u32[]{:S(2)}) collective-permute-start(bf16[32,4096]{1,0:T(8,128)(2,1)S(1)} %get-tuple-element.34.refs_0_), channel_id=1, source_target_pairs={{0,2},{2,0},{4,6},{6,4},{8,10},{10,8},{12,14},{14,12},{1,3},{3,1},... | collective-permute-start | bytes 786440 | tf_op jit(solution)/shard_map/ppermute | solution.py:446
  6.2 11.6 %collective-permute-start = (bf16[32,4096]{1,0:T(8,128)(2,1)S(1)}, bf16[32,4096]{1,0:T(8,128)(2,1)S(1)}, u32[]{:S(2)}, u32[]{:S(2)}) collective-permute-start(bf16[32,4096]{1,0:T(8,128)(2,1)S(1)} %get-tuple-element.35), channel_id=1, source_target_pairs={{0,4},{2,6},{4,0},{6,2},{8,12},{10,14},{12,8},{14,10},{1,5},{3,7},... | collective-permute-start | bytes 786440 | tf_op jit(solution)/shard_map/ppermute | solution.py:446
  7.7 14.1 %collective-permute-start.5 = (bf16[16,4096]{1,0:T(8,128)(2,1)S(1)}, bf16[16,4096]{1,0:T(8,128)(2,1)S(1)}, u32[]{:S(2)}, u32[]{:S(2)}) collective-permute-start(bf16[16,4096]{1,0:T(8,128)(2,1)S(1)} %get-tuple-element.40), channel_id=1, source_target_pairs={{0,8},{2,10},{4,12},{6,14},{8,0},{10,2},{12,4},{14,6},{1,9},{3,11}... | collective-permute-start | bytes 393224 | tf_op jit(solution)/shard_map/ppermute | solution.py:446
  10.3 12.8 %collective-permute-start.6 = (bf16[16,4096]{1,0:T(8,128)(2,1)S(1)}, bf16[16,4096]{1,0:T(8,128)(2,1)S(1)}, u32[]{:S(2)}, u32[]{:S(2)}) collective-permute-start(bf16[16,4096]{1,0:T(8,128)(2,1)S(1)} %get-tuple-element.41), channel_id=1, source_target_pairs={{0,12},{2,14},{4,8},{6,10},{8,4},{10,6},{12,0},{14,2},{1,13},{3,15... | collective-permute-start | bytes 393224 | tf_op jit(solution)/shard_map/ppermute | solution.py:446
  14.1 16.8 %collective-permute-start.3 = (bf16[16,4096]{1,0:T(8,128)(2,1)S(1)}, bf16[16,4096]{1,0:T(8,128)(2,1)S(1)}, u32[]{:S(2)}, u32[]{:S(2)}) collective-permute-start(bf16[16,4096]{1,0:T(8,128)(2,1)S(1)} %get-tuple-element.38), channel_id=1, source_target_pairs={{0,8},{2,10},{4,12},{6,14},{8,0},{10,2},{12,4},{14,6},{1,9},{3,11}... | collective-permute-start | bytes 393224 | tf_op jit(solution)/shard_map/ppermute | solution.py:446
  15.8 15.1 %collective-permute-start.4 = (bf16[16,4096]{1,0:T(8,128)(2,1)S(1)}, bf16[16,4096]{1,0:T(8,128)(2,1)S(1)}, u32[]{:S(2)}, u32[]{:S(2)}) collective-permute-start(bf16[16,4096]{1,0:T(8,128)(2,1)S(1)} %get-tuple-element.39), channel_id=1, source_target_pairs={{0,12},{2,14},{4,8},{6,10},{8,4},{10,6},{12,0},{14,2},{1,13},{3,15... | collective-permute-start | bytes 393224 | tf_op jit(solution)/shard_map/ppermute | solution.py:446
  17.8 8.3 %collective-permute-start.2 = (bf16[32,4096]{1,0:T(8,128)(2,1)S(1)}, bf16[32,4096]{1,0:T(8,128)(2,1)S(1)}, u32[]{:S(2)}, u32[]{:S(2)}) collective-permute-start(bf16[32,4096]{1,0:T(8,128)(2,1)S(1)} %collective-permute-done.refs_0_.refs_1_), channel_id=1, source_target_pairs={{0,2},{2,0},{4,6},{6,4},{8,10},{10,8},{12,14},{14,12},{1,3},{3,1},... | collective-permute-start | bytes 786440 | tf_op jit(solution)/shard_map/ppermute | solution.py:446
  23.2 8.3 %collective-permute-start.8 = (bf16[32,4096]{1,0:T(8,128)(2,1)S(1)}, bf16[32,4096]{1,0:T(8,128)(2,1)S(1)}, u32[]{:S(2)}, u32[]{:S(2)}) collective-permute-start(bf16[32,4096]{1,0:T(8,128)(2,1)S(1)} %join.2.refs_0_.refs_4_), channel_id=1, source_target_pairs={{0,2},{2,0},{4,6},{6,4},{8,10},{10,8},{12,14},{14,12},{1,3},{3,1},... | collective-permute-start | bytes 786440 | tf_op jit(solution)/shard_map/ppermute | solution.py:446
  30.9 7.1 %collective-permute-start.7 = (bf16[32,4096]{1,0:T(8,128)(2,1)S(1)}, bf16[32,4096]{1,0:T(8,128)(2,1)S(1)}, u32[]{:S(2)}, u32[]{:S(2)}) collective-permute-start(bf16[32,4096]{1,0:T(8,128)(2,1)S(1)} %join.3.refs_4_), channel_id=1, source_target_pairs={{0,2},{2,0},{4,6},{6,4},{8,10},{10,8},{12,14},{14,12},{1,3},{3,1},... | collective-permute-start | bytes 786440 | tf_op jit(solution)/shard_map/ppermute | solution.py:446
  41.5 7.2 %collective-permute-start.9 = (bf16[64,2176]{1,0:T(8,128)(2,1)S(1)}, bf16[64,2176]{1,0:T(8,128)(2,1)S(1)}, u32[]{:S(2)}, u32[]{:S(2)}) collective-permute-start(bf16[64,2176]{1,0:T(8,128)(2,1)S(1)} %get-tuple-element.46), channel_id=1, source_target_pairs={{0,2},{2,0},{4,6},{6,4},{8,10},{10,8},{12,14},{14,12},{1,3},{3,1},... | collective-permute-start | bytes 835592 | tf_op jit(solution)/shard_map/ppermute | solution.py:446
  42.1 19.4 %copy-start = (s32[128,2]{0,1:T(2,128)S(1)}, s32[128,2]{0,1:T(2,128)}, u32[]{:S(2)}) copy-start(s32[128,2]{0,1:T(2,128)} %param.11) | copy-start | bytes 3076
  42.1 19.4 %copy-start.1 = (s32[128]{0:T(128)S(1)}, s32[128]{0:T(128)}, u32[]{:S(2)}) copy-start(s32[128]{0:T(128)} %param.10) | copy-start | bytes 1540
  42.1 19.4 %copy-start.2 = (f32[128,2]{0,1:T(2,128)S(1)}, f32[128,2]{0,1:T(2,128)}, u32[]{:S(2)}) copy-start(f32[128,2]{0,1:T(2,128)} %param.12) | copy-start | bytes 3076
  48.8 6.5 %collective-permute-start.14 = (bf16[64,2176]{1,0:T(8,128)(2,1)S(1)}, bf16[64,2176]{1,0:T(8,128)(2,1)S(1)}, u32[]{:S(2)}, u32[]{:S(2)}) collective-permute-start(bf16[64,2176]{1,0:T(8,128)(2,1)S(1)} %pass_after.3), channel_id=1, source_target_pairs={{0,2},{2,0},{4,6},{6,4},{8,10},{10,8},{12,14},{14,12},{1,3},{3,1},... | collective-permute-start | bytes 835592 | tf_op jit(solution)/shard_map/ppermute | solution.py:446
  49.4 11.5 %collective-permute-start.10 = (bf16[16,2176]{1,0:T(8,128)(2,1)S(1)}, bf16[16,2176]{1,0:T(8,128)(2,1)S(1)}, u32[]{:S(2)}, u32[]{:S(2)}) collective-permute-start(bf16[16,2176]{1,0:T(8,128)(2,1)S(1)} %get-tuple-element.47), channel_id=1, source_target_pairs={{0,13},{1,12},{2,15},{3,14},{4,9},{5,8},{6,11},{7,10},{8,5},{9,4},... | collective-permute-start | bytes 208904 | tf_op jit(solution)/shard_map/ppermute | solution.py:460
  49.5 11.4 %collective-permute-start.11 = (bf16[16,2176]{1,0:T(8,128)(2,1)S(1)}, bf16[16,2176]{1,0:T(8,128)(2,1)S(1)}, u32[]{:S(2)}, u32[]{:S(2)}) collective-permute-start(bf16[16,2176]{1,0:T(8,128)(2,1)S(1)} %get-tuple-element.48), channel_id=1, source_target_pairs={{0,9},{1,8},{2,11},{3,10},{4,13},{5,12},{6,15},{7,14},{8,1},{9,0},... | collective-permute-start | bytes 208904 | tf_op jit(solution)/shard_map/ppermute | solution.py:460
  53.7 8.1 %collective-permute-start.12 = (bf16[16,2176]{1,0:T(8,128)(2,1)S(1)}, bf16[16,2176]{1,0:T(8,128)(2,1)S(1)}, u32[]{:S(2)}, u32[]{:S(2)}) collective-permute-start(bf16[16,2176]{1,0:T(8,128)(2,1)S(1)} %get-tuple-element.49), channel_id=1, source_target_pairs={{0,5},{1,4},{2,7},{3,6},{4,1},{5,0},{6,3},{7,2},{8,13},{9,12},{10,... | collective-permute-start | bytes 208904 | tf_op jit(solution)/shard_map/ppermute | solution.py:460
  54.8 7.0 %collective-permute-start.13 = (bf16[16,2176]{1,0:T(8,128)(2,1)S(1)}, bf16[16,2176]{1,0:T(8,128)(2,1)S(1)}, u32[]{:S(2)}, u32[]{:S(2)}) collective-permute-start(bf16[16,2176]{1,0:T(8,128)(2,1)S(1)} %get-tuple-element.50), channel_id=1, source_target_pairs={{0,1},{1,0},{2,3},{3,2},{4,5},{5,4},{6,7},{7,6},{8,9},{9,8},{10,11... | collective-permute-start | bytes 208904 | tf_op jit(solution)/shard_map/ppermute | solution.py:460
  55.4 8.4 %collective-permute-start.15 = (bf16[16,2176]{1,0:T(8,128)(2,1)S(1)}, bf16[16,2176]{1,0:T(8,128)(2,1)S(1)}, u32[]{:S(2)}, u32[]{:S(2)}) collective-permute-start(bf16[16,2176]{1,0:T(8,128)(2,1)S(1)} %get-tuple-element.56), channel_id=1, source_target_pairs={{0,12},{1,13},{2,14},{3,15},{4,8},{5,9},{6,10},{7,11},{8,4},{9,5},... | collective-permute-start | bytes 208904 | tf_op jit(solution)/shard_map/ppermute | solution.py:460
  60.9 5.5 %collective-permute-start.16 = (bf16[16,2176]{1,0:T(8,128)(2,1)S(1)}, bf16[16,2176]{1,0:T(8,128)(2,1)S(1)}, u32[]{:S(2)}, u32[]{:S(2)}) collective-permute-start(bf16[16,2176]{1,0:T(8,128)(2,1)S(1)} %get-tuple-element.57), channel_id=1, source_target_pairs={{0,8},{1,9},{2,10},{3,11},{4,12},{5,13},{6,14},{7,15},{8,0},{9,1},... | collective-permute-start | bytes 208904 | tf_op jit(solution)/shard_map/ppermute | solution.py:460
  60.9 5.6 %collective-permute-start.17 = (bf16[16,2176]{1,0:T(8,128)(2,1)S(1)}, bf16[16,2176]{1,0:T(8,128)(2,1)S(1)}, u32[]{:S(2)}, u32[]{:S(2)}) collective-permute-start(bf16[16,2176]{1,0:T(8,128)(2,1)S(1)} %get-tuple-element.58), channel_id=1, source_target_pairs={{0,4},{1,5},{2,6},{3,7},{4,0},{5,1},{6,2},{7,3},{8,12},{9,13},{10,... | collective-permute-start | bytes 208904 | tf_op jit(solution)/shard_map/ppermute | solution.py:460
